TPU v7x, 32 devices: a whole 2x2x4 slice. The times are simulated.
32 devices in a mesh: dp: 8 (over z, x), tm: 4 (over y, core).
Axes of the slice: x: 2, y: 2, z: 4, core: 2. Of those that a mesh axis runs over, the one named last changes fastest.
Arguments:
- mel_pieces: bfloat16 [8, 128, 2048], P('dp', 'tm'), may hold values from -6 to 6
- dest_owner: int32 [8, 128], P('dp', 'tm'), may hold values from 0 to 7, as said below
- dest_slot: int32 [8, 128], P('dp', 'tm'), may hold values from 0 to 31, as said below
- segment_ids: int32 [8, 512], P('dp'), may hold values from 0 to 3, never falling along the last dimension, each value on 1 to 256 neighbouring positions
- out_grad: bfloat16 [8, 512, 1024], P('dp', 'tm'), may hold values from -6 to 6
- stem_weight: bfloat16 [512, 1024], P(('dp', 'tm')), may hold values from -0.25 to 0.25
- up_weight: bfloat16 [1024, 2048], P(('dp', 'tm')), may hold values from -0.1875 to 0.1875
- down_weight: bfloat16 [1024, 1024], P(('dp', 'tm')), may hold values from -0.1875 to 0.1875
- depth_kernel: bfloat16 [1024, 31], P(('dp', 'tm')), may hold values from -1 to 1
- gain_pre: bfloat16 [1024], P(('dp', 'tm')), may hold values from 0.099609375 to 1.8984375
- gain_post: bfloat16 [1024], P(('dp', 'tm')), may hold values from 0.099609375 to 1.8984375
Outputs:
- y_out: bfloat16 [8, 512, 1024], P('dp', 'tm')
- grad_stem: float32 [512, 1024], P(('dp', 'tm'))
- grad_up: float32 [1024, 2048], P('dp', 'tm')
- grad_down: float32 [1024, 1024], P('dp', 'tm')
- grad_kernel: float32 [1024, 31], P(('dp', 'tm'))
- grad_gain_pre: float32 [1024], P(('dp', 'tm'))
- grad_gain_post: float32 [1024], P(('dp', 'tm'))
Inputs may be any that keep to these rules, and one draw needn't show every extreme that they name: `dest_owner`: A loader piece in time block t (columns t * 32 to (t + 1) * 32 - 1) goes to a packed row's time block t. From one loader row and time block, every packed row receives either no piece or exactly 8 pieces, and every packed row receives exactly 32 pieces in each time block. `dest_slot`: for each packed row and time block, the places of the pieces it receives are the numbers 0 to 31, each once.
All inputs are finite; a program needn't handle non-finite values.
Results may differ from a plain program's by a relative error of at most 0.018.
Values may be sent and summed in bfloat16 or wider, within the bound.
No kernel may reach another device: no remote copies, remote signals or barrier semaphores. Data moves between devices by JAX's collectives and lax.ppermute only.
A program may use at most 128 MiB of HBM per device.

v0:
```python
import jax
import jax.numpy as jnp
from jax import lax
from jax.sharding import PartitionSpec as P

NORM_EPS = 1e-05


def with_halo(array, sides, width):
    for axis, dim in sides:
        size, length = (lax.axis_size(axis), array.shape[dim])
        up = [(i, (i + 1) % size) for i in range(size - 1)]
        down = [(j, i) for i, j in up]
        last = lax.slice_in_dim(array, length - width, length, axis=dim)
        leading = lax.slice_in_dim(array, 0, width, axis=dim)
        before = lax.ppermute(last, axis, up)
        after = lax.ppermute(leading, axis, down)
        array = jnp.concatenate([before, array, after], axis=dim)
    return array


def standardize(values):
    centered = values - jnp.mean(values, axis=-1, keepdims=True)
    inverse = lax.rsqrt(jnp.mean(centered * centered, axis=-1, keepdims=True) + NORM_EPS)
    return (centered * inverse, inverse)


def norm_backward(grad_hat, normed_hat, inverse):
    first = jnp.mean(grad_hat, axis=-1, keepdims=True)
    second = jnp.mean(grad_hat * normed_hat, axis=-1, keepdims=True)
    return (grad_hat - first - normed_hat * second) * inverse


def silu_slope(values):
    sigma = jax.nn.sigmoid(values)
    return sigma * (1.0 + values * (1.0 - sigma))


def depth_forward(padded, kernel, seg_window, seg_centre, length):
    weights = kernel.astype(jnp.float32)
    summed = jnp.zeros((length, padded.shape[1]), jnp.float32)
    for offset in range(weights.shape[1]):
        inside = (seg_window[offset : offset + length] == seg_centre)[:, None]
        summed = summed + jnp.where(
            inside, padded[offset : offset + length].astype(jnp.float32) * weights[:, offset], 0.0
        )
    return summed


def depth_backward(padded_grad, padded_in, kernel, seg_window, seg_centre, length):
    margin = (kernel.shape[1] - 1) // 2
    weights = kernel.astype(jnp.float32)
    grad_in = jnp.zeros((length, padded_grad.shape[1]), jnp.float32)
    grad_here = padded_grad[margin : margin + length].astype(jnp.float32)
    columns = []
    for offset in range(weights.shape[1]):
        start = 2 * margin - offset
        inside_back = (seg_window[start : start + length] == seg_centre)[:, None]
        grad_in = grad_in + jnp.where(
            inside_back,
            padded_grad[start : start + length].astype(jnp.float32) * weights[:, offset],
            0.0,
        )
        inside = (seg_window[offset : offset + length] == seg_centre)[:, None]
        columns.append(
            jnp.sum(
                jnp.where(
                    inside, grad_here * padded_in[offset : offset + length].astype(jnp.float32), 0.0
                ),
                axis=0,
            )
        )
    return (grad_in, jnp.stack(columns, axis=1))


def per_device(
    mel_pieces,
    dest_owner,
    dest_slot,
    segment_ids,
    out_grad,
    stem_weight,
    up_weight,
    down_weight,
    depth_kernel,
    gain_pre,
    gain_post,
):
    dp_count = lax.axis_size("dp")
    tm_count = lax.axis_size("tm")
    pieces = mel_pieces.shape[1]
    piece_values = mel_pieces.shape[2]
    length = out_grad.shape[1]
    channels = out_grad.shape[2]
    features = piece_values * pieces // length
    capacity = max(2, 2 * pieces // dp_count)
    owners = dest_owner[0]
    matches = (owners[:, None] == jnp.arange(dp_count, dtype=jnp.int32)[None, :]).astype(jnp.int32)
    before = jnp.cumsum(matches, axis=0) - matches
    ranked = jnp.sum(before * matches, axis=1)
    position = owners * capacity + ranked
    outgoing = (
        jnp.zeros((dp_count * capacity, piece_values), jnp.bfloat16).at[position].set(mel_pieces[0])
    )
    outgoing = outgoing.reshape(dp_count, capacity, piece_values)
    labels = (
        jnp.full((dp_count * capacity,), -1, jnp.int32)
        .at[position]
        .set(dest_slot[0])
        .reshape(dp_count, capacity)
    )
    arrived, arrived_ids = (
        lax.all_to_all(outgoing, "dp", split_axis=0, concat_axis=0, tiled=True),
        lax.all_to_all(labels, "dp", split_axis=0, concat_axis=0, tiled=True),
    )
    found = (arrived_ids.reshape(1, -1) == jnp.arange(pieces, dtype=jnp.int32)[:, None]).astype(
        jnp.int32
    )
    source = jnp.sum(found * jnp.arange(dp_count * capacity, dtype=jnp.int32)[None, :], axis=1)
    frames = arrived.reshape(dp_count * capacity, piece_values)[source].reshape(length, features)
    stem_full, up_full, down_full, kernel_full, gain_one, gain_two = (
        lax.all_gather(stem_weight, ("dp", "tm"), axis=0, tiled=True),
        lax.all_gather(up_weight, ("dp", "tm"), axis=0, tiled=True),
        lax.all_gather(down_weight, ("dp", "tm"), axis=0, tiled=True),
        lax.all_gather(depth_kernel, ("dp", "tm"), axis=0, tiled=True),
        lax.all_gather(gain_pre, ("dp", "tm"), axis=0, tiled=True),
        lax.all_gather(gain_post, ("dp", "tm"), axis=0, tiled=True),
    )
    gain_one = gain_one.astype(jnp.float32)
    gain_two = gain_two.astype(jnp.float32)
    margin = (kernel_full.shape[1] - 1) // 2
    seg_padded = jnp.pad(segment_ids[0], (margin, margin), constant_values=-1)
    seg_window = lax.dynamic_slice_in_dim(
        seg_padded, lax.axis_index("tm") * length, length + 2 * margin
    )
    seg_centre = seg_window[margin : margin + length]
    stem_pre = jnp.dot(frames, stem_full, preferred_element_type=jnp.float32)
    stem_out = jax.nn.silu(stem_pre).astype(jnp.bfloat16)
    stem_hat, inverse_one = standardize(stem_out.astype(jnp.float32))
    normed = (stem_hat * gain_one).astype(jnp.bfloat16)
    proj = jnp.dot(normed, up_full, preferred_element_type=jnp.float32)
    linear = proj[:, :channels]
    gate_sig = jax.nn.sigmoid(proj[:, channels:])
    gated = (linear * gate_sig).astype(jnp.bfloat16)
    gated_ext = with_halo(gated, (("tm", 0),), margin)
    conv = depth_forward(gated_ext, kernel_full, seg_window, seg_centre, length)
    conv_hat, inverse_two = standardize(conv)
    conv_scaled = conv_hat * gain_two
    activated = jax.nn.silu(conv_scaled).astype(jnp.bfloat16)
    grad_out = out_grad[0]
    y_full = stem_out.astype(jnp.float32) + jnp.dot(
        activated, down_full, preferred_element_type=jnp.float32
    )
    y_out = y_full.astype(jnp.bfloat16)
    grad_act = jnp.dot(grad_out, down_full.T, preferred_element_type=jnp.float32)
    grad_scaled = grad_act * silu_slope(conv_scaled)
    gain_post_term = jnp.sum(grad_scaled * conv_hat, axis=0)
    grad_conv = norm_backward(grad_scaled * gain_two, conv_hat, inverse_two).astype(jnp.bfloat16)
    grad_ext = with_halo(grad_conv, (("tm", 0),), margin)
    grad_gated, kernel_term = depth_backward(
        grad_ext, gated_ext, kernel_full, seg_window, seg_centre, length
    )
    grad_proj = jnp.concatenate(
        [grad_gated * gate_sig, grad_gated * linear * gate_sig * (1.0 - gate_sig)], axis=1
    ).astype(jnp.bfloat16)
    grad_normed = jnp.dot(grad_proj, up_full.T, preferred_element_type=jnp.float32)
    gain_pre_term = jnp.sum(grad_normed * stem_hat, axis=0)
    grad_stem_out = grad_out.astype(jnp.float32) + norm_backward(
        grad_normed * gain_one, stem_hat, inverse_one
    )
    grad_stem_pre = (grad_stem_out * silu_slope(stem_pre)).astype(jnp.bfloat16)
    stem_term = jnp.dot(frames.T, grad_stem_pre, preferred_element_type=jnp.float32)
    up_share = 2 * channels // tm_count
    down_share = channels // tm_count
    normed_all, active_all, proj_all, out_all = (
        lax.all_gather(normed, "tm", axis=0, tiled=True),
        lax.all_gather(activated, "tm", axis=0, tiled=True),
        lax.all_gather(grad_proj, "tm", axis=0, tiled=True),
        lax.all_gather(grad_out, "tm", axis=0, tiled=True),
    )
    column = lax.axis_index("tm")
    proj_part = lax.dynamic_slice_in_dim(proj_all, column * up_share, up_share, 1)
    out_part = lax.dynamic_slice_in_dim(out_all, column * down_share, down_share, 1)
    proj_grads = lax.psum_scatter(
        jnp.concatenate(
            [
                jnp.dot(normed_all.T, proj_part, preferred_element_type=jnp.float32),
                jnp.dot(active_all.T, out_part, preferred_element_type=jnp.float32),
            ],
            axis=1,
        ),
        "dp",
        scatter_dimension=0,
        tiled=True,
    )
    grad_stem, grad_kernel, grad_gain_pre, grad_gain_post = (
        lax.psum_scatter(stem_term, ("dp", "tm"), scatter_dimension=0, tiled=True),
        lax.psum_scatter(kernel_term, ("dp", "tm"), scatter_dimension=0, tiled=True),
        lax.psum_scatter(gain_pre_term, ("dp", "tm"), scatter_dimension=0, tiled=True),
        lax.psum_scatter(gain_post_term, ("dp", "tm"), scatter_dimension=0, tiled=True),
    )
    grad_up = proj_grads[:, :up_share]
    grad_down = proj_grads[:, up_share:]
    return (y_out[None], grad_stem, grad_up, grad_down, grad_kernel, grad_gain_pre, grad_gain_post)


def solution(mesh):
    return jax.shard_map(
        per_device,
        mesh=mesh,
        in_specs=(
            P("dp", "tm", None),
            P("dp", "tm"),
            P("dp", "tm"),
            P("dp", None),
            P("dp", "tm", None),
            P(("dp", "tm"), None),
            P(("dp", "tm"), None),
            P(("dp", "tm"), None),
            P(("dp", "tm"), None),
            P(("dp", "tm")),
            P(("dp", "tm")),
        ),
        out_specs=(
            P("dp", "tm", None),
            P(("dp", "tm"), None),
            P("dp", "tm"),
            P("dp", "tm"),
            P(("dp", "tm"), None),
            P(("dp", "tm")),
            P(("dp", "tm")),
        ),
        check_vma=False,
    )
```

profile of v0, /device:TPU:0, one launch (start us, length us, event | category | flops | bytes accessed | tf_op | source)
XLA Modules:
  0.0 626.8 jit_solution(2573294284970404835)
XLA Ops:
  13.2 7.3 %all-to-all-start.1 = ((s32[8,1,8]{2,1,0:T(1,128)}), s32[8,1,8]{2,1,0:T(1,128)S(1)}, u32[]{:S(2)}, u32[]{:S(2)}) async-start(s32[8,1,8]{2,1,0:T(1,128)} %bitcast.8), calls=%async_computation.1 | async-start | bytes 8192 | tf_op jit(solution)/shard_map/all_to_all | solution.py:114
  23.1 43.1 %all_gather.33 = bf16[1024,31]{1,0:T(8,128)(2,1)S(1)} all-gather(bf16[32,31]{1,0:T(8,128)(2,1)} %param.19), channel_id=1, replica_groups=mesh['dp'=8,'tm'=4] {'dp','tm'}, dimensions={0}, use_global_device_ids=true | all-gather | bytes 65472 | tf_op jit(solution)/shard_map/all_gather | solution.py:125
  66.3 5.1 slice_reduce_fusion.30
  73.6 3.4 all-to-all-start
  78.1 40.2 %all-reduce.6 = (bf16[1024]{0:T(1024)(128)(2,1)S(1)}, bf16[1024]{0:T(1024)(128)(2,1)S(1)}) all-reduce(bf16[1024]{0:T(1024)(128)(2,1)S(1)} %dynamic-update-slice, bf16[1024]{0:T(1024)(128)(2,1)S(1)} %dynamic-update-slice.1), channel_id=1, replica_groups=mesh['dp'=8,'tm'=4] {'dp','tm'}, use_global_device_ids=true, to_apply=%add.1 | all-reduce | flops 2048 | bytes 8192
  120.5 2.4 convert_reduce_fusion
  123.4 8.8 %all-gather.11.cloned.1.call-done = bf16[1024,2048]{1,0:T(8,128)(2,1)} async-done(((bf16[32,2048]{1,0:T(8,128)(2,1)}), bf16[1024,2048]{1,0:T(8,128)(2,1)}) %all-gather.11.cloned.1.call-update) | async-done | bytes 4194320 | tf_op jit(solution)/shard_map/all_gather | solution.py:123
  132.1 2.9 fusion.245
  136.5 3.3 collective-permute-start
  139.9 3.3 slice_reduce_fusion.29
  143.6 3.9 fusion.241
  147.9 42.2 %all-gather.13.cloned.1.call-done = bf16[1024,1024]{1,0:T(8,128)(2,1)} async-done(((bf16[32,1024]{1,0:T(8,128)(2,1)}), bf16[1024,1024]{1,0:T(8,128)(2,1)}) %all-gather.13.cloned.1.call-update) | async-done | bytes 2097168 | tf_op jit(solution)/shard_map/all_gather | solution.py:124
  190.1 3.8 multiply_reduce_fusion
  194.6 3.0 fusion.151
  201.2 2.7 collective-permute-done.2
  203.8 5.9 multiply_convert_fusion.1
  211.0 15.2 %all-gather.19.cloned.1.call-done = bf16[512,1024]{1,0:T(8,128)(2,1)} async-done(((bf16[128,1024]{1,0:T(8,128)(2,1)}), bf16[512,1024]{1,0:T(8,128)(2,1)}) %all-gather.19.cloned.1.call-update) | async-done | bytes 1048592 | tf_op jit(solution)/shard_map/all_gather | solution.py:177
  228.0 17.0 %all-gather.15.cloned.1.call-done = bf16[512,1024]{1,0:T(8,128)(2,1)} async-done(((bf16[128,1024]{1,0:T(8,128)(2,1)}), bf16[512,1024]{1,0:T(8,128)(2,1)}) %all-gather.15.cloned.1.call-update) | async-done | bytes 1048592 | tf_op jit(solution)/shard_map/all_gather | solution.py:176
  245.0 24.2 %all-gather.17.cloned.1.call-done = bf16[512,2048]{1,0:T(8,128)(2,1)} async-done(((bf16[128,2048]{1,0:T(8,128)(2,1)}), bf16[512,2048]{1,0:T(8,128)(2,1)}) %all-gather.17.cloned.1.call-update) | async-done | bytes 2097168 | tf_op jit(solution)/shard_map/all_gather | solution.py:178
  279.3 4.2 fusion.15
  288.3 40.2 %all-reduce.5 = (f32[1024]{0:T(1024)S(1)}, f32[1024]{0:T(1024)S(1)}) all-reduce(f32[1024]{0:T(1024)S(1)} %get-tuple-element.37, f32[1024]{0:T(1024)S(1)} %copy-done.69), channel_id=6, replica_groups=mesh['dp'=8,'tm'=4] {'dp','tm'}, use_global_device_ids=true, to_apply=%region_48.49.clone | all-reduce | flops 2048 | bytes 16384
  329.6 19.3 %reduce-scatter.8.cloned.1.call-done = f32[128,768]{0,1:T(8,128)} async-done(((f32[1024,768]{0,1:T(8,128)}), f32[128,768]{0,1:T(8,128)}) %reduce-scatter.8.cloned.1.call-update) | async-done | bytes 393232 | tf_op jit(solution)/shard_map/reduce_scatter | solution.py:184
  352.4 132.1 %reduce-scatter.10.cloned.1.call-done = f32[32,31]{1,0:T(8,128)} async-done(((f32[1024,31]{1,0:T(8,128)}), f32[32,31]{1,0:T(8,128)}) %reduce-scatter.10.cloned.1.call-update) | async-done | bytes 3984
  484.5 135.4 %reduce-scatter.6.cloned.1.call-done = f32[16,1024]{1,0:T(8,128)} async-done(((f32[512,1024]{1,0:T(8,128)}), f32[16,1024]{1,0:T(8,128)}) %reduce-scatter.6.cloned.1.call-update) | async-done | bytes 65552 | tf_op jit(solution)/shard_map/reduce_scatter | solution.py:197
  (248 shorter events, 42.5 us)
Async XLA Ops:
  7.2 113.3 %all-gather.9.cloned.1.call-start = ((), (), s32[]{:S(2)}) async-start(), calls=%async_computation.5 | async-start | bytes 1081344 | tf_op jit(solution)/shard_map/all_gather | solution.py:122
  7.9 124.2 %all-gather.11.cloned.1.call-start = ((), (), s32[]{:S(2)}) async-start(), calls=%async_computation.6 | async-start | bytes 4325376 | tf_op jit(solution)/shard_map/all_gather | solution.py:123
  8.7 181.4 %all-gather.13.cloned.1.call-start = ((), (), s32[]{:S(2)}) async-start(), calls=%async_computation.7 | async-start | bytes 2162688 | tf_op jit(solution)/shard_map/all_gather | solution.py:124
  13.2 60.4 %all-to-all-start.1 = ((s32[8,1,8]{2,1,0:T(1,128)}), s32[8,1,8]{2,1,0:T(1,128)S(1)}, u32[]{:S(2)}, u32[]{:S(2)}) async-start(s32[8,1,8]{2,1,0:T(1,128)} %bitcast.8), calls=%async_computation.1 | async-start | bytes 8192 | tf_op jit(solution)/shard_map/all_to_all | solution.py:114
  20.4 190.6 %all-gather.21.cloned.1.call-start = ((), (), s32[]{:S(2)}) async-start(), calls=%async_computation.13 | async-start | bytes 1310720 | tf_op jit(solution)/shard_map/all_gather | solution.py:179
  22.4 121.0 %copy-start.25 = (pred[128]{0:T(512)(128)(4,1)}, pred[128]{0:T(512)(128)(4,1)S(1)}, u32[]{:S(2)}) copy-start(pred[128]{0:T(512)(128)(4,1)S(1)} %get-tuple-element.119) | copy-start | bytes 388
  22.4 121.0 %copy-start.61 = (pred[128]{0:T(512)(128)(4,1)}, pred[128]{0:T(512)(128)(4,1)S(1)}, u32[]{:S(2)}) copy-start(pred[128]{0:T(512)(128)(4,1)S(1)} %get-tuple-element.120) | copy-start | bytes 388
  22.4 121.0 %copy-start.62 = (pred[128]{0:T(512)(128)(4,1)}, pred[128]{0:T(512)(128)(4,1)S(1)}, u32[]{:S(2)}) copy-start(pred[128]{0:T(512)(128)(4,1)S(1)} %get-tuple-element.124) | copy-start | bytes 388
  22.4 121.0 %copy-start.63 = (pred[128]{0:T(512)(128)(4,1)}, pred[128]{0:T(512)(128)(4,1)S(1)}, u32[]{:S(2)}) copy-start(pred[128]{0:T(512)(128)(4,1)S(1)} %get-tuple-element.125) | copy-start | bytes 388
  22.4 121.0 %copy-start.64 = (pred[128]{0:T(512)(128)(4,1)}, pred[128]{0:T(512)(128)(4,1)S(1)}, u32[]{:S(2)}) copy-start(pred[128]{0:T(512)(128)(4,1)S(1)} %get-tuple-element.126) | copy-start | bytes 388
  22.4 121.0 %copy-start.65 = (pred[128]{0:T(512)(128)(4,1)}, pred[128]{0:T(512)(128)(4,1)S(1)}, u32[]{:S(2)}) copy-start(pred[128]{0:T(512)(128)(4,1)S(1)} %get-tuple-element.127) | copy-start | bytes 388
  22.4 121.0 %copy-start.67 = (pred[128]{0:T(512)(128)(4,1)}, pred[128]{0:T(512)(128)(4,1)S(1)}, u32[]{:S(2)}) copy-start(pred[128]{0:T(512)(128)(4,1)S(1)} %get-tuple-element.121) | copy-start | bytes 388
  23.0 120.4 %copy-start.35 = (pred[128]{0:T(512)(128)(4,1)}, pred[128]{0:T(512)(128)(4,1)S(1)}, u32[]{:S(2)}) copy-start(pred[128]{0:T(512)(128)(4,1)S(1)} %get-tuple-element.133) | copy-start | bytes 388
  73.6 46.1 %all-to-all-start = ((bf16[8,8,2048]{2,1,0:T(8,128)(2,1)}), bf16[8,8,2048]{2,1,0:T(8,128)(2,1)S(1)}, u32[]{:S(2)}, u32[]{:S(2)}) async-start(bf16[8,8,2048]{2,1,0:T(8,128)(2,1)} %bitcast.5), calls=%async_computation | async-start | bytes 524288 | tf_op jit(solution)/shard_map/all_to_all | solution.py:113
  77.0 149.2 %all-gather.19.cloned.1.call-start = ((), (), s32[]{:S(2)}) async-start(), calls=%async_computation.11 | async-start | bytes 1310720 | tf_op jit(solution)/shard_map/all_gather | solution.py:177
  135.2 8.1 %collective-permute-start.1 = (bf16[15,1024]{1,0:T(8,128)(2,1)S(1)}, bf16[15,1024]{1,0:T(8,128)(2,1)S(1)}, u32[]{:S(2)}, u32[]{:S(2)}) collective-permute-start(bf16[15,1024]{1,0:T(8,128)(2,1)S(1)} %get-tuple-element.118), channel_id=1, source_target_pairs={{1,0},{2,1},{3,2},{5,4},{6,5},{7,6},{9,8},{10,9},{11,10},{13,12},{... | collective-permute-start | bytes 92168 | tf_op jit(solution)/shard_map/ppermute | solution.py:17
  136.5 6.8 %collective-permute-start = (bf16[15,1024]{1,0:T(8,128)(2,1)S(1)}, bf16[15,1024]{1,0:T(8,128)(2,1)S(1)}, u32[]{:S(2)}, u32[]{:S(2)}) collective-permute-start(bf16[15,1024]{1,0:T(8,128)(2,1)S(1)} %get-tuple-element.117), channel_id=1, source_target_pairs={{0,1},{1,2},{2,3},{4,5},{5,6},{6,7},{8,9},{9,10},{10,11},{12,13},{... | collective-permute-start | bytes 92168 | tf_op jit(solution)/shard_map/ppermute | solution.py:16
  194.0 51.0 %all-gather.15.cloned.1.call-start = ((), (), s32[]{:S(2)}) async-start(), calls=%async_computation.9 | async-start | bytes 1310720 | tf_op jit(solution)/shard_map/all_gather | solution.py:176
  194.6 74.6 %all-gather.17.cloned.1.call-start = ((), (), s32[]{:S(2)}) async-start(), calls=%async_computation.10 | async-start | bytes 2621440 | tf_op jit(solution)/shard_map/all_gather | solution.py:178
  197.7 3.5 collective-permute-start.3
  199.8 4.0 collective-permute-start.2
  210.7 138.2 %reduce-scatter.8.cloned.1.call-start = ((), (), s32[]{:S(2)}) async-start(), calls=%async_computation.12 | async-start | bytes 3538944 | tf_op jit(solution)/shard_map/reduce_scatter | solution.py:184
  273.4 211.1 %reduce-scatter.10.cloned.1.call-start = ((), (), s32[]{:S(2)}) async-start(), calls=%async_computation.14 | async-start | bytes 540672
  279.2 340.7 %reduce-scatter.6.cloned.1.call-start = ((), (), s32[]{:S(2)}) async-start(), calls=%async_computation.8 | async-start | bytes 2162688 | tf_op jit(solution)/shard_map/reduce_scatter | solution.py:197
  (71 other events, 2034.3 us)
Sparse Core Ops, SparseCore 0:
  10.9 56.3 all-gather.8
  70.2 61.8 all-gather.10
  135.0 55.0 all-gather.12
  191.5 15.5 all-gather.20
  209.1 17.0 all-gather.18
  228.2 16.7 all-gather.14
  246.5 22.5 all-gather.16
  273.5 75.3 reduce-scatter.7
  351.7 132.7 reduce-scatter.9
  487.3 132.5 reduce-scatter.5
where the time goes:
time: 628 us; the launch traced here: 627 us
  waiting for transfers between devices  400 us (64%)
  blocking collectives  123 us (20%)
  other arithmetic  26.3 us (4%)
  local copies, waits for them, and re-layouts  21.8 us (3%)
  matrix products  20.3 us (3%)
  starting transfers between devices  19.4 us (3%)
  between operations  15.5 us (2%)
    reduce_scatter x1, waiting for transfers between devices, per_device(): lax.psum_scatter(stem_term, ('dp', 'tm'), scatter_dimension=0, tiled=True)  135 us
    unnamed x11, waiting for transfers between devices  135 us
    unnamed x2, blocking collectives  80.3 us
    all_gather x1, blocking collectives, per_device(): lax.all_gather(depth_kernel, ('dp', 'tm'), axis=0, tiled=True)  43.1 us
    all_gather x1, waiting for transfers between devices, per_device(): lax.all_gather(down_weight, ('dp', 'tm'), axis=0, tiled=True)  42.2 us
    all_gather x1, waiting for transfers between devices, per_device(): lax.all_gather(grad_proj, 'tm', axis=0, tiled=True)  24.2 us
    reduce_scatter x1, waiting for transfers between devices, per_device(): lax.psum_scatter(jnp.concatenate([jnp.dot(normed_all.T, proj_part, prefer...  19.3 us
    all_gather x1, waiting for transfers between devices, per_device(): lax.all_gather(normed, 'tm', axis=0, tiled=True)  17 us
  transfers between devices with their start and end apart: 16, of which 9 were waited for; matrix products, arithmetic and copies ran while one was open for 10% of the time, Pallas kernels for 0%

commit v1 on v0

v1 whole, which is shorter than its diff:
```python
import jax
import jax.numpy as jnp
from jax import lax
from jax.sharding import PartitionSpec as P

NORM_EPS = 1e-05
BF16 = jnp.bfloat16
F32 = jnp.float32


def stages_of(sizes):
    if sizes["dp"] == 8 and sizes["tm"] == 4:
        return {"dp": ((2, 4), (1, 2)), "tm": ((2, 2), (1, 2))}
    if sizes["dp"] == 64 and sizes["tm"] == 4:
        return {"dp": ((8, 8), (2, 4), (1, 2)), "tm": ((1, 4),)}
    return {axis: ((1, size),) for axis, size in sizes.items()}


def swap(value, axis, mask):
    size = lax.axis_size(axis)
    return lax.ppermute(value, axis, [(i, i ^ mask) for i in range(size)])


def gather_stage(value, axis, stride, size):
    place = (lax.axis_index(axis) // stride) % size
    out = jnp.zeros((size,) + value.shape, value.dtype)
    for k in range(size):
        part = value if k == 0 else swap(value, axis, k * stride)
        out = lax.dynamic_update_slice_in_dim(out, part[None], place ^ k, 0)
    return out


def gather(value, axis, chains):
    shape = value.shape
    sizes = []
    for stride, size in chains:
        value = gather_stage(value, axis, stride, size)
        sizes.insert(0, size)
    count = len(sizes)
    order = tuple(reversed(range(count))) + tuple(range(count, value.ndim))
    return value.transpose(order).reshape((-1,) + shape)


def scatter_sum(value, axis, chains):
    index = lax.axis_index(axis)
    sizes = [size for _, size in chains]
    value = value.reshape(tuple(sizes) + value.shape[1:])
    for depth in reversed(range(len(chains))):
        stride, size = chains[depth]
        place = (index // stride) % size
        total = lax.dynamic_index_in_dim(value, place, depth, keepdims=False)
        for k in range(1, size):
            part = lax.dynamic_index_in_dim(value, place ^ k, depth, keepdims=False)
            total = total + swap(part.astype(BF16), axis, k * stride).astype(F32)
        value = total
    return value


def all_sum(value, axis):
    size = lax.axis_size(axis)
    mask = 1
    while mask < size:
        value = value + swap(value, axis, mask)
        mask *= 2
    return value


def standardize(values):
    centered = values - jnp.mean(values, axis=-1, keepdims=True)
    inverse = lax.rsqrt(jnp.mean(centered * centered, axis=-1, keepdims=True) + NORM_EPS)
    return (centered * inverse, inverse)


def shared_standardize(values, axis):
    count = values.shape[-1]
    mean = jnp.mean(values, axis=-1)
    centered = values - mean[:, None]
    squares = jnp.sum(centered * centered, axis=-1)
    both = jnp.stack([mean, squares])
    mask, held = 1, count
    while mask < lax.axis_size(axis):
        other = swap(both, axis, mask)
        gap = both[0] - other[0]
        both = jnp.stack([0.5 * (both[0] + other[0]), both[1] + other[1] + gap * gap * (0.5 * held)])
        mask *= 2
        held *= 2
    inverse = lax.rsqrt(both[1] / held + NORM_EPS)[:, None]
    return ((values - both[0][:, None]) * inverse, inverse)


def silu_slope(values):
    sigma = jax.nn.sigmoid(values)
    return sigma * (1.0 + values * (1.0 - sigma))


def depth_forward(padded, weights, seg_window, seg_centre, length):
    summed = jnp.zeros((length, padded.shape[1]), F32)
    for offset in range(weights.shape[0]):
        inside = (seg_window[offset : offset + length] == seg_centre)[:, None]
        summed = summed + jnp.where(
            inside, padded[offset : offset + length].astype(F32) * weights[offset][None, :], 0.0
        )
    return summed


def depth_backward(padded_grad, padded_in, weights, seg_window, seg_centre, length):
    taps = weights.shape[0]
    margin = (taps - 1) // 2
    grad_in = jnp.zeros((length, padded_grad.shape[1]), F32)
    grad_here = padded_grad[margin : margin + length].astype(F32)
    columns = []
    for offset in range(taps):
        start = 2 * margin - offset
        inside_back = (seg_window[start : start + length] == seg_centre)[:, None]
        grad_in = grad_in + jnp.where(
            inside_back,
            padded_grad[start : start + length].astype(F32) * weights[offset][None, :],
            0.0,
        )
        inside = (seg_window[offset : offset + length] == seg_centre)[:, None]
        columns.append(
            jnp.sum(
                jnp.where(inside, grad_here * padded_in[offset : offset + length].astype(F32), 0.0),
                axis=0,
            )
        )
    return (grad_in, jnp.stack(columns, axis=0))


def one_hot(rows, columns):
    return (rows[:, None] == columns[None, :]).astype(BF16)


def route_frames(mel_pieces, dest_owner, dest_slot, dp_count):
    pieces, piece_values = mel_pieces.shape
    capacity = max(2, 2 * pieces // dp_count)
    matches = (dest_owner[:, None] == jnp.arange(dp_count, dtype=jnp.int32)[None, :]).astype(jnp.int32)
    earlier = jnp.cumsum(matches, axis=0) - matches
    position = dest_owner * capacity + jnp.sum(earlier * matches, axis=1)
    pick = one_hot(jnp.arange(dp_count * capacity, dtype=jnp.int32), position)
    label = jnp.broadcast_to((dest_slot + 1).astype(BF16)[:, None], (pieces, 128))
    outgoing = jnp.dot(
        pick, jnp.concatenate([mel_pieces, label], axis=1), preferred_element_type=F32
    ).astype(BF16)
    arrived = lax.all_to_all(
        outgoing.reshape(dp_count, capacity, -1), "dp", split_axis=0, concat_axis=0, tiled=True
    ).reshape(dp_count * capacity, -1)
    labels = arrived[:, piece_values].astype(jnp.int32)
    put = one_hot(jnp.arange(1, pieces + 1, dtype=jnp.int32), labels)
    return jnp.dot(put, arrived[:, :piece_values], preferred_element_type=F32).astype(BF16)


def per_device(
    mel_pieces,
    dest_owner,
    dest_slot,
    segment_ids,
    out_grad,
    stem_weight,
    up_weight,
    down_weight,
    depth_kernel,
    gain_pre,
    gain_post,
):
    dp_count = lax.axis_size("dp")
    tm_count = lax.axis_size("tm")
    chains = stages_of({"dp": dp_count, "tm": tm_count})
    dp_chains, tm_chains = chains["dp"], chains["tm"]
    column = lax.axis_index("tm")
    taps = depth_kernel.shape[1]
    margin = (taps - 1) // 2
    block = out_grad.shape[1]
    channels = out_grad.shape[2]
    held = channels // tm_count
    rows = down_weight.shape[0]
    stem_rows = stem_weight.shape[0]
    features = stem_rows * dp_count * tm_count
    length = block * tm_count

    pieces = route_frames(mel_pieces[0], dest_owner[0], dest_slot[0], dp_count)
    frames = gather(pieces, "tm", tm_chains).reshape(length, features)

    gain_row = jnp.zeros((stem_rows, 128), BF16).at[0, :rows].set(gain_pre)
    stem_all = gather(jnp.concatenate([stem_weight, gain_row], axis=1), "dp", dp_chains)
    stem_all = gather(stem_all, "tm", tm_chains)
    stem_all = stem_all.transpose(1, 0, 2, 3)
    stem_full = stem_all[..., :channels].reshape(features, channels)
    gain_one = stem_all[:, :, 0, channels : channels + rows].reshape(channels).astype(F32)

    span = 128 * tm_count
    lane = jnp.arange(span, dtype=jnp.int32)
    grouped = (lane // rows) % tm_count * 128 + lane // (rows * tm_count) * rows + lane % rows
    regroup = one_hot(grouped, lane)
    groups = 2 * channels // span
    up_parts = jnp.dot(
        up_weight.reshape(rows, groups, span).transpose(1, 0, 2).reshape(groups * rows, span),
        regroup,
        preferred_element_type=F32,
    ).astype(BF16)
    up_parts = up_parts.reshape(groups, rows, tm_count, 128).transpose(2, 1, 0, 3)
    up_parts = up_parts.reshape(tm_count, rows, groups * 128)
    up_mine = lax.all_to_all(up_parts, "tm", split_axis=0, concat_axis=0, tiled=True)
    up_full = gather(up_mine.reshape(tm_count * rows, groups * 128), "dp", dp_chains)
    up_full = up_full.reshape(channels, 2 * held)

    small = jnp.concatenate(
        [depth_kernel, gain_post[:, None], jnp.zeros((rows, 128 - taps - 1), BF16)], axis=1
    )
    down_all = gather(jnp.concatenate([down_weight, small], axis=1), "dp", dp_chains)
    down_all = down_all.reshape(held, channels + 128)
    down_full = down_all[:, :channels]
    small_all = down_all[:, channels:].astype(F32).T
    taps_full = small_all[:taps]
    gain_two = small_all[taps][None, :]

    grad_out = out_grad[0]
    grad_out_all = gather(grad_out, "tm", tm_chains).reshape(length, channels)

    seg_centre = segment_ids[0]
    seg_window = jnp.pad(seg_centre, (margin, margin), constant_values=-1)

    stem_pre = jnp.dot(frames, stem_full, preferred_element_type=F32)
    stem_out = jax.nn.silu(stem_pre).astype(BF16)
    stem_hat, inverse_one = standardize(stem_out.astype(F32))
    normed = (stem_hat * gain_one).astype(BF16)
    proj = jnp.dot(normed, up_full, preferred_element_type=F32)
    linear = proj[:, :held]
    gate_sig = jax.nn.sigmoid(proj[:, held:])
    gated = (linear * gate_sig).astype(BF16)
    gated_ext = jnp.pad(gated, ((margin, margin), (0, 0)))
    conv = depth_forward(gated_ext, taps_full, seg_window, seg_centre, length)
    conv_hat, inverse_two = shared_standardize(conv, "tm")
    conv_scaled = conv_hat * gain_two
    activated = jax.nn.silu(conv_scaled).astype(BF16)
    y_terms = jnp.dot(activated, down_full, preferred_element_type=F32)
    y_part = scatter_sum(y_terms.reshape(tm_count, block, channels), "tm", tm_chains)

    def mine(value):
        return lax.dynamic_slice_in_dim(value, column * block, block, 0)

    y_out = (mine(stem_out).astype(F32) + y_part).astype(BF16)

    down_terms = jnp.dot(activated.T, grad_out_all, preferred_element_type=F32).astype(BF16)
    down_terms = down_terms.reshape(dp_count, rows, tm_count, held).transpose(0, 2, 1, 3)
    down_terms = down_terms.reshape(dp_count * tm_count, rows, held)
    down_terms = lax.all_to_all(down_terms, ("dp", "tm"), split_axis=0, concat_axis=0, tiled=True)
    grad_down = jnp.sum(
        down_terms.reshape(dp_count, tm_count * rows, held).astype(F32), axis=0
    )

    grad_act = lax.dot_general(
        grad_out_all, down_full, (((1,), (1,)), ((), ())), preferred_element_type=F32
    )
    grad_scaled = grad_act * silu_slope(conv_scaled)
    gain_post_term = jnp.sum(grad_scaled * conv_hat, axis=0)
    grad_hat = grad_scaled * gain_two
    means = all_sum(
        jnp.stack([jnp.sum(grad_hat, axis=-1), jnp.sum(grad_hat * conv_hat, axis=-1)]), "tm"
    ) * (1.0 / channels)
    grad_conv = (
        (grad_hat - means[0][:, None] - conv_hat * means[1][:, None]) * inverse_two
    ).astype(BF16)
    grad_ext = jnp.pad(grad_conv, ((margin, margin), (0, 0)))
    grad_gated, kernel_term = depth_backward(
        grad_ext, gated_ext, taps_full, seg_window, seg_centre, length
    )
    grad_proj = jnp.concatenate(
        [grad_gated * gate_sig, grad_gated * linear * gate_sig * (1.0 - gate_sig)], axis=1
    ).astype(BF16)

    up_terms = jnp.dot(normed.T, grad_proj, preferred_element_type=F32).astype(BF16)
    share = up_terms.shape[1] // tm_count
    up_terms = up_terms.reshape(dp_count, tm_count * rows, tm_count, share).transpose(0, 2, 1, 3)
    up_terms = up_terms.reshape(dp_count * tm_count, tm_count * rows, share)
    up_terms = lax.all_to_all(up_terms, ("dp", "tm"), split_axis=0, concat_axis=0, tiled=True)
    up_terms = up_terms.reshape(dp_count, tm_count, tm_count * rows, share)
    spread = one_hot(lane, grouped).reshape(tm_count, share, span)
    grad_up = jnp.einsum(
        "ijab,jbc->ac", up_terms, spread, preferred_element_type=F32
    )

    small_term = jnp.concatenate([kernel_term, gain_post_term[None, :]], axis=0)
    small_term = small_term.reshape(taps + 1, dp_count, rows).transpose(1, 2, 0)
    small_term = lax.all_to_all(small_term, "dp", split_axis=0, concat_axis=0, tiled=True)
    small_sum = jnp.sum(small_term, axis=0)
    grad_kernel, grad_gain_post = small_sum[:, :taps], small_sum[:, taps]

    normed_terms = lax.dot_general(
        grad_proj, up_full, (((1,), (1,)), ((), ())), preferred_element_type=F32
    )
    grad_normed = scatter_sum(normed_terms.reshape(tm_count, block, channels), "tm", tm_chains)
    my_hat = mine(stem_hat)
    gain_pre_term = jnp.sum(grad_normed * my_hat, axis=0).reshape(dp_count * tm_count, rows)
    gain_pre_term = lax.all_to_all(
        gain_pre_term, ("dp", "tm"), split_axis=0, concat_axis=0, tiled=True
    )
    grad_gain_pre = jnp.sum(gain_pre_term, axis=0)
    back = grad_normed * gain_one
    first = jnp.mean(back, axis=-1, keepdims=True)
    second = jnp.mean(back * my_hat, axis=-1, keepdims=True)
    grad_stem_out = grad_out.astype(F32) + (back - first - my_hat * second) * mine(inverse_one)
    grad_stem_pre = (grad_stem_out * silu_slope(mine(stem_pre))).astype(BF16)
    grad_stem_all = gather(grad_stem_pre, "tm", tm_chains).reshape(length, channels)
    chosen = jnp.arange(features // tm_count, dtype=jnp.int32)
    chosen = (chosen // stem_rows * tm_count + column) * stem_rows + chosen % stem_rows
    frames_part = jnp.dot(
        frames, one_hot(jnp.arange(features, dtype=jnp.int32), chosen), preferred_element_type=F32
    ).astype(BF16)
    stem_terms = jnp.dot(frames_part.T, grad_stem_all, preferred_element_type=F32).astype(BF16)
    stem_terms = lax.all_to_all(
        stem_terms.reshape(dp_count, stem_rows, channels),
        "dp",
        split_axis=0,
        concat_axis=0,
        tiled=True,
    )
    grad_stem = jnp.sum(stem_terms.astype(F32), axis=0)
    return (y_out[None], grad_stem, grad_up, grad_down, grad_kernel, grad_gain_pre, grad_gain_post)


def solution(mesh):
    return jax.shard_map(
        per_device,
        mesh=mesh,
        in_specs=(
            P("dp", "tm", None),
            P("dp", "tm"),
            P("dp", "tm"),
            P("dp", None),
            P("dp", "tm", None),
            P(("dp", "tm"), None),
            P(("dp", "tm"), None),
            P(("dp", "tm"), None),
            P(("dp", "tm"), None),
            P(("dp", "tm")),
            P(("dp", "tm")),
        ),
        out_specs=(
            P("dp", "tm", None),
            P(("dp", "tm"), None),
            P("dp", "tm"),
            P("dp", "tm"),
            P(("dp", "tm"), None),
            P(("dp", "tm")),
            P(("dp", "tm")),
        ),
        check_vma=False,
    )
```

time: 628 us -> 221 us (0.35)
  waiting for transfers between devices: 400 us -> 63.7 us
  blocking collectives: 123 us -> 0 us
  starting transfers between devices: 19.4 us -> 54.7 us
  local copies, waits for them, and re-layouts: 21.8 us -> 40.8 us
  between operations: 15.5 us -> 2.48 us
  other arithmetic: 26.3 us -> 37.2 us
    reduce_scatter x2 -> x0, waiting for transfers between devices: 155 us -> none  [the longest x1 135 us: per_device(): lax.psum_scatter(stem_term, ('dp', 'tm'), scatter_dimension=0, tiled=True)]
    unnamed x11 -> x0, waiting for transfers between devices: 135 us -> none
    all_gather x7 -> x0, waiting for transfers between devices: 107 us -> none  [the longest x1 42.2 us: per_device(): lax.all_gather(down_weight, ('dp', 'tm'), axis=0, tiled=True)]
    unnamed x2 -> x0, blocking collectives: 80.3 us -> none
    all_gather x1 -> x0, blocking collectives: 43.1 us -> none  [per_device(): lax.all_gather(depth_kernel, ('dp', 'tm'), axis=0, tiled=True)]
    ppermute x4 -> x28, waiting for transfers between devices: 2.66 us -> 39 us  [swap(): return lax.ppermute(value, axis, [(i, i ^ mask) for i in range(size)])]
    all_to_all x2 -> x7, waiting for transfers between devices: 0.01 us -> 24.7 us  [the longest x1 10.6 us: per_device(): lax.all_to_all(down_terms, ('dp', 'tm'), split_axis=0, concat_axis=0, til...]
    ppermute x4 -> x28, starting transfers between devices: 8.1 us -> 31.7 us  [swap(): return lax.ppermute(value, axis, [(i, i ^ mask) for i in range(size)])]
  transfers between devices with their start and end apart: 16 -> 35, of which waited for: 9 -> 13; matrix products, arithmetic and copies ran while one was open for 10% -> 34% of each run, Pallas kernels for 0% -> 0%
where the time goes in v1:
time: 221 us; the launch traced here: 219 us
  waiting for transfers between devices  63.7 us (29%)
  starting transfers between devices  54.7 us (25%)
  local copies, waits for them, and re-layouts  40.8 us (18%)
  other arithmetic  37.2 us (17%)
  matrix products  20.3 us (9%)
  between operations  2.48 us (1%)
    ppermute x28, waiting for transfers between devices, swap(): return lax.ppermute(value, axis, [(i, i ^ mask) for i in range(size)])  39 us
    ppermute x28, starting transfers between devices, swap(): return lax.ppermute(value, axis, [(i, i ^ mask) for i in range(size)])  31.7 us
    dynamic_update_slice x31, local copies, waits for them, and re-layouts, gather_stage(): out = lax.dynamic_update_slice_in_dim(out, part[None], place ^ k, 0)  14.3 us
    all_to_all x1, waiting for transfers between devices, per_device(): lax.all_to_all(down_terms, ('dp', 'tm'), split_axis=0, concat_axis=0, til...  10.6 us
    reduce_sum x6, other arithmetic, depth_backward(): jnp.sum(jnp.where(inside, grad_here * padded_in[offset:offset + length].a...  7.11 us
    another operation x2, other arithmetic  6.37 us
    all_to_all x1, waiting for transfers between devices, per_device(): lax.all_to_all(small_term, 'dp', split_axis=0, concat_axis=0, tiled=True)  5.2 us
    all_to_all x1, waiting for transfers between devices, per_device(): lax.all_to_all(gain_pre_term, ('dp', 'tm'), split_axis=0, concat_axis=0,...  5.08 us
  transfers between devices with their start and end apart: 35, of which 13 were waited for; matrix products, arithmetic and copies ran while one was open for 34% of the time, Pallas kernels for 0%

profile of v1, /device:TPU:0, one launch (start us, length us, event | category | flops | bytes accessed | tf_op | source)
XLA Modules:
  0.0 219.2 jit_solution(7120896891129736055)
XLA Ops:
  1.5 3.0 %collective-permute-start.2 = (bf16[16,1152]{1,0:T(8,128)(2,1)S(1)}, bf16[16,1152]{1,0:T(8,128)(2,1)S(1)}, u32[]{:S(2)}, u32[]{:S(2)}) collective-permute-start(bf16[16,1152]{1,0:T(8,128)(2,1)S(1)} %fusion.176), channel_id=1, source_target_pairs={{0,8},{4,12},{8,0},{12,4},{16,24},{20,28},{24,16},{28,20},{1,9},{5... | collective-permute-start | bytes 110600 | tf_op jit(solution)/shard_map/ppermute | solution.py:21
  4.5 2.6 %collective-permute-start.3 = (bf16[16,1152]{1,0:T(8,128)(2,1)S(1)}, bf16[16,1152]{1,0:T(8,128)(2,1)S(1)}, u32[]{:S(2)}, u32[]{:S(2)}) collective-permute-start(bf16[16,1152]{1,0:T(8,128)(2,1)S(1)} %fusion.176), channel_id=1, source_target_pairs={{0,16},{4,20},{8,24},{12,28},{16,0},{20,4},{24,8},{28,12},{1,17},{... | collective-permute-start | bytes 110600 | tf_op jit(solution)/shard_map/ppermute | solution.py:21
  9.8 3.5 %collective-permute-start.13 = (bf16[32,1152]{1,0:T(8,128)(2,1)S(1)}, bf16[32,1152]{1,0:T(8,128)(2,1)S(1)}, u32[]{:S(2)}, u32[]{:S(2)}) collective-permute-start(bf16[32,1152]{1,0:T(8,128)(2,1)S(1)} %concatenate.93), channel_id=1, source_target_pairs={{0,16},{4,20},{8,24},{12,28},{16,0},{20,4},{24,8},{28,12},{1,17},{... | collective-permute-start | bytes 221192 | tf_op jit(solution)/shard_map/ppermute | solution.py:21
  15.8 3.3 %all-to-all-start.1 = ((bf16[4,32,512]{2,1,0:T(8,128)(2,1)}), bf16[4,32,512]{2,1,0:T(8,128)(2,1)S(1)}, u32[]{:S(2)}, u32[]{:S(2)}) async-start(bf16[4,32,512]{2,1,0:T(8,128)(2,1)} %reshape.467), calls=%async_computation.1 | async-start | bytes 262144 | tf_op jit(solution)/shard_map/all_to_all | solution.py:203
  33.3 3.6 %all-to-all-start = ((bf16[8,8,2176]{2,1,0:T(8,128)(2,1)}), bf16[8,8,2176]{2,1,0:T(8,128)(2,1)S(1)}, u32[]{:S(2)}, u32[]{:S(2)}) async-start(bf16[8,8,2176]{2,1,0:T(8,128)(2,1)} %fusion), calls=%async_computation | async-start | bytes 557056 | tf_op jit(solution)/shard_map/all_to_all | solution.py:145
  41.6 5.3 %collective-permute-done.8 = bf16[128,512]{1,0:T(8,128)(2,1)S(1)} collective-permute-done((bf16[128,512]{1,0:T(8,128)(2,1)S(1)}, bf16[128,512]{1,0:T(8,128)(2,1)S(1)}, u32[]{:S(2)}, u32[]{:S(2)}) %collective-permute-start.8) | collective-permute-done | bytes 131104 | tf_op jit(solution)/shard_map/ppermute | solution.py:21
  48.0 7.5 %collective-permute-done.9 = bf16[128,512]{1,0:T(8,128)(2,1)S(1)} collective-permute-done((bf16[128,512]{1,0:T(8,128)(2,1)S(1)}, bf16[128,512]{1,0:T(8,128)(2,1)S(1)}, u32[]{:S(2)}, u32[]{:S(2)}) %collective-permute-start.9) | collective-permute-done | bytes 131104 | tf_op jit(solution)/shard_map/ppermute | solution.py:21
  66.3 4.1 %collective-permute-done = bf16[32,2048]{1,0:T(8,128)(2,1)S(1)} collective-permute-done((bf16[32,2048]{1,0:T(8,128)(2,1)S(1)}, bf16[32,2048]{1,0:T(8,128)(2,1)S(1)}, u32[]{:S(2)}, u32[]{:S(2)}) %collective-permute-start) | collective-permute-done | bytes 131104 | tf_op jit(solution)/shard_map/ppermute | solution.py:21
  82.9 4.7 %fusion.237 = (f32[512]{0:T(512)S(1)}, f32[512,256]{1,0:T(8,128)S(1)}) fusion(f32[256]{0:T(256)S(1)} %get-tuple-element.84, pred[512]{0:T(512)(128)(4,1)S(1)} %get-tuple-element.163, f32[256]{0:T(256)S(1)} %get-tuple-element.85, pred[512]{0:T(512)(128)(4,1)S(1)} %get-tuple-element.135, f32[256]{0:T(256)S(1)} %get-tuple-element.86, ...), kind=kLoop, calls=%fused_computation.480 | loop fusion | flops 16121344 | bytes 835584 | tf_op jit(solution)/shard_map/reduce_sum | solution.py:76
  93.4 3.0 %multiply_reduce_fusion.1 = (f32[256]{0:T(256)}, f32[512]{0:T(512)S(1)}, f32[512]{0:T(512)S(1)}, f32[512,256]{1,0:T(8,128)}) fusion(f32[512,256]{1,0:T(8,128)S(1)} %get-tuple-element.121, f32[512]{0:T(512)S(1)} %get-tuple-element.125, f32[512]{0:T(512)S(1)} %get-tuple-element.124, f32[256]{0:T(256)S(1)} %copy-done.71, bf16[512,1024]{1,0:T(8,128)(2,1)S(1)} %bitcast.246, ...), kind=kOutput, calls=%fused_computation.254 | convolution fusion | flops 270662400 | bytes 2631680 | tf_op jit(solution)/shard_map/dot_general | solution.py:252
  101.4 3.4 %fusion.138 = (f32[256]{0:T(256)}, f32[256]{0:T(256)}, f32[256]{0:T(256)}, f32[256]{0:T(256)}, f32[256]{0:T(256)}, /*index=5*/f32[256]{0:T(256)}, bf16[512,256]{1,0:T(8,128)(2,1)S(1)}) fusion(pred[512]{0:T(512)(128)(4,1)S(1)} %get-tuple-element.138, bf16[512,256]{1,0:T(8,128)(2,1)S(1)} %multiply_convert_fusion.7, pred[512]{0:T(512)(128)(4,1)S(1)} %get-tuple-element.143, ...), kind=kLoop, calls=%fused_computation.223 | loop fusion | flops 4323840 | bytes 1591296 | tf_op jit(solution)/shard_map/reduce_sum | solution.py:122
  104.8 6.2 %multiply_convert_fusion.4 = (bf16[512,256]{1,0:T(8,128)(2,1)S(1)}, f32[512,256]{1,0:T(8,128)S(1)}) fusion(f32[512,512]{1,0:T(8,128)S(1)} %fusion.165, f32[256]{0:T(256)S(1)} %get-tuple-element.84, pred[512]{0:T(512)(128)(4,1)S(1)} %get-tuple-element.134, f32[256]{0:T(256)S(1)} %get-tuple-element.85, pred[512]{0:T(512)(128)(4,1)} %copy-done.28, ...), kind=kLoop, calls=%fused_computation.262 | loop fusion | flops 16646144 | bytes 1619968 | tf_op jit(solution)/shard_map/convert.10
  121.8 5.7 %collective-permute-done.25 = bf16[128,1024]{1,0:T(8,128)(2,1)S(1)} collective-permute-done((bf16[128,1024]{1,0:T(8,128)(2,1)S(1)}, bf16[128,1024]{1,0:T(8,128)(2,1)S(1)}, u32[]{:S(2)}, u32[]{:S(2)}) %collective-permute-start.25) | collective-permute-done | bytes 262176 | tf_op jit(solution)/shard_map/ppermute | solution.py:21
  135.8 3.3 %all-to-all-start.5 = ((f32[8,1,1024]{2,1,0:T(1,128)}), f32[8,1,1024]{2,1,0:T(1,128)S(1)}, u32[]{:S(2)}, u32[]{:S(2)}) async-start(f32[8,1,1024]{2,1,0:T(1,128)} %reshape.513), calls=%async_computation.5 | async-start | bytes 65536 | tf_op jit(solution)/shard_map/all_to_all | solution.py:285
  140.6 5.2 %all-to-all-done.5 = f32[8,1,1024]{2,1,0:T(1,128)S(1)} async-done(((f32[8,1,1024]{2,1,0:T(1,128)}), f32[8,1,1024]{2,1,0:T(1,128)S(1)}, u32[]{:S(2)}, u32[]{:S(2)}) %all-to-all-start.5) | async-done | bytes 32800 | tf_op jit(solution)/shard_map/all_to_all | solution.py:285
  150.3 5.1 %all-to-all-done.6 = f32[32,1,32]{2,1,0:T(1,128)S(1)} async-done(((f32[32,1,32]{2,1,0:T(1,128)}), f32[32,1,32]{2,1,0:T(1,128)S(1)}, u32[]{:S(2)}, u32[]{:S(2)}) %all-to-all-start.6) | async-done | bytes 4128 | tf_op jit(solution)/shard_map/all_to_all | solution.py:295
  156.0 2.6 %all-to-all-start.4 = ((bf16[32,32,256]{2,1,0:T(8,128)(2,1)}), bf16[32,32,256]{2,1,0:T(8,128)(2,1)S(1)}, u32[]{:S(2)}, u32[]{:S(2)}) async-start(bf16[32,32,256]{2,1,0:T(8,128)(2,1)} %bitcast.106), calls=%async_computation.4 | async-start | bytes 1048576 | tf_op jit(solution)/shard_map/all_to_all | solution.py:247
  163.6 10.6 %all-to-all-done.4 = bf16[32,32,256]{2,1,0:T(8,128)(2,1)S(1)} async-done(((bf16[32,32,256]{2,1,0:T(8,128)(2,1)}), bf16[32,32,256]{2,1,0:T(8,128)(2,1)S(1)}, u32[]{:S(2)}, u32[]{:S(2)}) %all-to-all-start.4) | async-done | bytes 524320 | tf_op jit(solution)/shard_map/all_to_all | solution.py:247
  174.2 4.0 %all-to-all-start.2 = ((bf16[8,16,1024]{2,1,0:T(8,128)(2,1)}), bf16[8,16,1024]{2,1,0:T(8,128)(2,1)}, u32[]{:S(2)}, u32[]{:S(2)}) async-start(bf16[8,16,1024]{2,1,0:T(8,128)(2,1)} %bitcast.248), calls=%async_computation.2 | async-start | bytes 524288 | tf_op jit(solution)/shard_map/all_to_all | solution.py:311
  178.2 2.8 %convolution_convert_fusion.2 = bf16[1024,512]{1,0:T(8,128)(2,1)} fusion(bf16[512,256]{1,0:T(8,128)(2,1)} %copy-done.8, bf16[512,256]{1,0:T(8,128)(2,1)S(1)} %get-tuple-element.118, f32[1024]{0:T(1024)S(1)} %reshape.475, bf16[512,1024]{1,0:T(8,128)(2,1)S(1)} %copy-done.2, f32[512]{0:T(512)S(1)} %copy-done.65, f32[512]{0:T(512)S(1)} %broadcast_multiply_fusion.1), kind=kOutput, calls=%fused_computation.43 | convolution fusion | flops 541065216 | bytes 2629632 | tf_op jit(solution)/shard_map/dot_general | solution.py:272
  183.7 3.8 %all-to-all-done.2 = bf16[8,16,1024]{2,1,0:T(8,128)(2,1)} async-done(((bf16[8,16,1024]{2,1,0:T(8,128)(2,1)}), bf16[8,16,1024]{2,1,0:T(8,128)(2,1)}, u32[]{:S(2)}, u32[]{:S(2)}) %all-to-all-start.2) | async-done | bytes 262176 | tf_op jit(solution)/shard_map/all_to_all | solution.py:311
  187.5 3.5 %all-to-all-start.3 = ((bf16[32,128,128]{2,1,0:T(8,128)(2,1)}), bf16[32,128,128]{2,1,0:T(8,128)(2,1)S(1)}, u32[]{:S(2)}, u32[]{:S(2)}) async-start(bf16[32,128,128]{2,1,0:T(8,128)(2,1)} %bitcast.101), calls=%async_computation.3 | async-start | bytes 2097152 | tf_op jit(solution)/shard_map/all_to_all | solution.py:276
  191.0 2.9 %fusion.163 = f32[512,1024]{1,0:T(8,128)} fusion(bf16[256,1152]{1,0:T(8,128)(2,1)} %bitcast.56, f32[512,256]{1,0:T(8,128)S(1)} %get-tuple-element.121, f32[256]{0:T(256)S(1)} %copy-done.72, f32[512]{0:T(512)S(1)} %copy-done.69, f32[512]{0:T(512)S(1)} %copy-done.67), kind=kOutput, calls=%fused_computation.273 | convolution fusion | flops 269484032 | bytes 3150848 | tf_op jit(solution)/shard_map/dot_general | solution.py:236
  202.0 8.8 %collective-permute-done.19 = bf16[128,1024]{1,0:T(8,128)(2,1)} collective-permute-done((bf16[128,1024]{1,0:T(8,128)(2,1)S(1)}, bf16[128,1024]{1,0:T(8,128)(2,1)}, u32[]{:S(2)}, u32[]{:S(2)}) %collective-permute-start.19) | collective-permute-done | bytes 262176 | tf_op jit(solution)/shard_map/ppermute | solution.py:21
  (393 shorter events, 108.0 us)
Async XLA Ops:
  1.5 22.2 %collective-permute-start.2 = (bf16[16,1152]{1,0:T(8,128)(2,1)S(1)}, bf16[16,1152]{1,0:T(8,128)(2,1)S(1)}, u32[]{:S(2)}, u32[]{:S(2)}) collective-permute-start(bf16[16,1152]{1,0:T(8,128)(2,1)S(1)} %fusion.176), channel_id=1, source_target_pairs={{0,8},{4,12},{8,0},{12,4},{16,24},{20,28},{24,16},{28,20},{1,9},{5... | collective-permute-start | bytes 110600 | tf_op jit(solution)/shard_map/ppermute | solution.py:21
  4.5 19.2 %collective-permute-start.3 = (bf16[16,1152]{1,0:T(8,128)(2,1)S(1)}, bf16[16,1152]{1,0:T(8,128)(2,1)S(1)}, u32[]{:S(2)}, u32[]{:S(2)}) collective-permute-start(bf16[16,1152]{1,0:T(8,128)(2,1)S(1)} %fusion.176), channel_id=1, source_target_pairs={{0,16},{4,20},{8,24},{12,28},{16,0},{20,4},{24,8},{28,12},{1,17},{... | collective-permute-start | bytes 110600 | tf_op jit(solution)/shard_map/ppermute | solution.py:21
  7.1 18.7 %collective-permute-start.4 = (bf16[16,1152]{1,0:T(8,128)(2,1)S(1)}, bf16[16,1152]{1,0:T(8,128)(2,1)S(1)}, u32[]{:S(2)}, u32[]{:S(2)}) collective-permute-start(bf16[16,1152]{1,0:T(8,128)(2,1)S(1)} %fusion.176), channel_id=1, source_target_pairs={{0,24},{4,28},{8,16},{12,20},{16,8},{20,12},{24,0},{28,4},{1,25},{... | collective-permute-start | bytes 110600 | tf_op jit(solution)/shard_map/ppermute | solution.py:21
  8.8 18.8 %collective-permute-start.12 = (bf16[32,1152]{1,0:T(8,128)(2,1)S(1)}, bf16[32,1152]{1,0:T(8,128)(2,1)S(1)}, u32[]{:S(2)}, u32[]{:S(2)}) collective-permute-start(bf16[32,1152]{1,0:T(8,128)(2,1)S(1)} %concatenate.93), channel_id=1, source_target_pairs={{0,8},{4,12},{8,0},{12,4},{16,24},{20,28},{24,16},{28,20},{1,9},{5... | collective-permute-start | bytes 221192 | tf_op jit(solution)/shard_map/ppermute | solution.py:21
  9.8 17.9 %collective-permute-start.13 = (bf16[32,1152]{1,0:T(8,128)(2,1)S(1)}, bf16[32,1152]{1,0:T(8,128)(2,1)S(1)}, u32[]{:S(2)}, u32[]{:S(2)}) collective-permute-start(bf16[32,1152]{1,0:T(8,128)(2,1)S(1)} %concatenate.93), channel_id=1, source_target_pairs={{0,16},{4,20},{8,24},{12,28},{16,0},{20,4},{24,8},{28,12},{1,17},{... | collective-permute-start | bytes 221192 | tf_op jit(solution)/shard_map/ppermute | solution.py:21
  15.8 17.5 %all-to-all-start.1 = ((bf16[4,32,512]{2,1,0:T(8,128)(2,1)}), bf16[4,32,512]{2,1,0:T(8,128)(2,1)S(1)}, u32[]{:S(2)}, u32[]{:S(2)}) async-start(bf16[4,32,512]{2,1,0:T(8,128)(2,1)} %reshape.467), calls=%async_computation.1 | async-start | bytes 262144 | tf_op jit(solution)/shard_map/all_to_all | solution.py:203
  23.8 33.4 %collective-permute-start.20 = (bf16[128,1024]{1,0:T(8,128)(2,1)S(1)}, bf16[128,1024]{1,0:T(8,128)(2,1)}, u32[]{:S(2)}, u32[]{:S(2)}) collective-permute-start(bf16[128,1024]{1,0:T(8,128)(2,1)S(1)} %bitcast.244), channel_id=1, source_target_pairs={{0,2},{1,3},{2,0},{3,1},{4,6},{5,7},{6,4},{7,5},{8,10},{9,11},{10,... | collective-permute-start | bytes 786440 | tf_op jit(solution)/shard_map/ppermute | solution.py:21
  25.8 15.3 %collective-permute-start.5 = (bf16[4,16,1152]{2,1,0:T(8,128)(2,1)S(1)}, bf16[4,16,1152]{2,1,0:T(8,128)(2,1)S(1)}, u32[]{:S(2)}, u32[]{:S(2)}) collective-permute-start(bf16[4,16,1152]{2,1,0:T(8,128)(2,1)S(1)} %bitcast_dynamic-update-slice_fusion.28), channel_id=1, source_target_pairs={{0,4},{4,0},{8,12},{12,8},{16,20},{20,16},{24,28},{28,24},{1,5},{5... | collective-permute-start | bytes 442376 | tf_op jit(solution)/shard_map/ppermute | solution.py:21
  30.1 28.8 %collective-permute-start.15 = (bf16[4,32,1152]{2,1,0:T(8,128)(2,1)S(1)}, bf16[4,32,1152]{2,1,0:T(8,128)(2,1)}, u32[]{:S(2)}, u32[]{:S(2)}) collective-permute-start(bf16[4,32,1152]{2,1,0:T(8,128)(2,1)S(1)} %bitcast_dynamic-update-slice_fusion.24), channel_id=1, source_target_pairs={{0,4},{4,0},{8,12},{12,8},{16,20},{20,16},{24,28},{28,24},{1,5},{5... | collective-permute-start | bytes 884744 | tf_op jit(solution)/shard_map/ppermute | solution.py:21
  33.3 31.3 %all-to-all-start = ((bf16[8,8,2176]{2,1,0:T(8,128)(2,1)}), bf16[8,8,2176]{2,1,0:T(8,128)(2,1)S(1)}, u32[]{:S(2)}, u32[]{:S(2)}) async-start(bf16[8,8,2176]{2,1,0:T(8,128)(2,1)} %fusion), calls=%async_computation | async-start | bytes 557056 | tf_op jit(solution)/shard_map/all_to_all | solution.py:145
  36.9 10.0 %collective-permute-start.8 = (bf16[128,512]{1,0:T(8,128)(2,1)S(1)}, bf16[128,512]{1,0:T(8,128)(2,1)S(1)}, u32[]{:S(2)}, u32[]{:S(2)}) collective-permute-start(bf16[128,512]{1,0:T(8,128)(2,1)S(1)} %bitcast.249), channel_id=1, source_target_pairs={{0,8},{4,12},{8,0},{12,4},{16,24},{20,28},{24,16},{28,20},{1,9},{5... | collective-permute-start | bytes 393224 | tf_op jit(solution)/shard_map/ppermute | solution.py:21
  38.7 16.9 %collective-permute-start.9 = (bf16[128,512]{1,0:T(8,128)(2,1)S(1)}, bf16[128,512]{1,0:T(8,128)(2,1)S(1)}, u32[]{:S(2)}, u32[]{:S(2)}) collective-permute-start(bf16[128,512]{1,0:T(8,128)(2,1)S(1)} %bitcast.250), channel_id=1, source_target_pairs={{0,16},{4,20},{8,24},{12,28},{16,0},{20,4},{24,8},{28,12},{1,17},{... | collective-permute-start | bytes 393224 | tf_op jit(solution)/shard_map/ppermute | solution.py:21
  41.1 14.4 %collective-permute-start.10 = (bf16[128,512]{1,0:T(8,128)(2,1)S(1)}, bf16[128,512]{1,0:T(8,128)(2,1)S(1)}, u32[]{:S(2)}, u32[]{:S(2)}) collective-permute-start(bf16[128,512]{1,0:T(8,128)(2,1)S(1)} %bitcast.252), channel_id=1, source_target_pairs={{0,24},{4,28},{8,16},{12,20},{16,8},{20,12},{24,0},{28,4},{1,25},{... | collective-permute-start | bytes 393224 | tf_op jit(solution)/shard_map/ppermute | solution.py:21
  47.0 17.0 %collective-permute-start.6 = (bf16[8,16,1152]{2,1,0:T(8,128)(2,1)S(1)}, bf16[8,16,1152]{2,1,0:T(8,128)(2,1)S(1)}, u32[]{:S(2)}, u32[]{:S(2)}) collective-permute-start(bf16[8,16,1152]{2,1,0:T(8,128)(2,1)S(1)} %bitcast.239), channel_id=1, source_target_pairs={{0,2},{1,3},{2,0},{3,1},{4,6},{5,7},{6,4},{7,5},{8,10},{9,11},{10,... | collective-permute-start | bytes 884744 | tf_op jit(solution)/shard_map/ppermute | solution.py:21
  55.6 16.6 %collective-permute-start.11 = (bf16[4,128,512]{2,1,0:T(8,128)(2,1)S(1)}, bf16[4,128,512]{2,1,0:T(8,128)(2,1)}, u32[]{:S(2)}, u32[]{:S(2)}) collective-permute-start(bf16[4,128,512]{2,1,0:T(8,128)(2,1)S(1)} %bitcast_dynamic-update-slice_fusion.18), channel_id=1, source_target_pairs={{0,4},{4,0},{8,12},{12,8},{16,20},{20,16},{24,28},{28,24},{1,5},{5... | collective-permute-start | bytes 1572872 | tf_op jit(solution)/shard_map/ppermute | solution.py:21
  58.9 32.0 %collective-permute-start.21 = (bf16[2,128,1024]{2,1,0:T(8,128)(2,1)}, bf16[2,128,1024]{2,1,0:T(8,128)(2,1)}, u32[]{:S(2)}, u32[]{:S(2)}) collective-permute-start(bf16[2,128,1024]{2,1,0:T(8,128)(2,1)} %bitcast_dynamic-update-slice_fusion.14), channel_id=1, source_target_pairs={{0,1},{1,0},{2,3},{3,2},{4,5},{5,4},{6,7},{7,6},{8,9},{9,8},{10,11... | collective-permute-start | bytes 1572872 | tf_op jit(solution)/shard_map/ppermute | solution.py:21
  64.0 11.4 %collective-permute-start.7 = (bf16[2,8,16,1152]{3,2,1,0:T(8,128)(2,1)S(1)}, bf16[2,8,16,1152]{3,2,1,0:T(8,128)(2,1)}, u32[]{:S(2)}, u32[]{:S(2)}) collective-permute-start(bf16[2,8,16,1152]{3,2,1,0:T(8,128)(2,1)S(1)} %bitcast_dynamic-update-slice_fusion.10), channel_id=1, source_target_pairs={{0,1},{1,0},{2,3},{3,2},{4,5},{5,4},{6,7},{7,6},{8,9},{9,8},{10,11... | collective-permute-start | bytes 1769480 | tf_op jit(solution)/shard_map/ppermute | solution.py:21
  135.8 10.0 %all-to-all-start.5 = ((f32[8,1,1024]{2,1,0:T(1,128)}), f32[8,1,1024]{2,1,0:T(1,128)S(1)}, u32[]{:S(2)}, u32[]{:S(2)}) async-start(f32[8,1,1024]{2,1,0:T(1,128)} %reshape.513), calls=%async_computation.5 | async-start | bytes 65536 | tf_op jit(solution)/shard_map/all_to_all | solution.py:285
  140.6 19.4 %collective-permute-start.27 = (bf16[2,128,1024]{2,1,0:T(8,128)(2,1)}, bf16[2,128,1024]{2,1,0:T(8,128)(2,1)}, u32[]{:S(2)}, u32[]{:S(2)}) collective-permute-start(bf16[2,128,1024]{2,1,0:T(8,128)(2,1)} %bitcast_dynamic-update-slice_fusion.12), channel_id=1, source_target_pairs={{0,1},{1,0},{2,3},{3,2},{4,5},{5,4},{6,7},{7,6},{8,9},{9,8},{10,11... | collective-permute-start | bytes 1572872 | tf_op jit(solution)/shard_map/ppermute | solution.py:21
  145.8 9.6 %all-to-all-start.6 = ((f32[32,1,32]{2,1,0:T(1,128)}), f32[32,1,32]{2,1,0:T(1,128)S(1)}, u32[]{:S(2)}, u32[]{:S(2)}) async-start(f32[32,1,32]{2,1,0:T(1,128)} %all_to_all.30), calls=%async_computation.6 | async-start | bytes 32768 | tf_op jit(solution)/shard_map/all_to_all | solution.py:295
  156.0 18.2 %all-to-all-start.4 = ((bf16[32,32,256]{2,1,0:T(8,128)(2,1)}), bf16[32,32,256]{2,1,0:T(8,128)(2,1)S(1)}, u32[]{:S(2)}, u32[]{:S(2)}) async-start(bf16[32,32,256]{2,1,0:T(8,128)(2,1)} %bitcast.106), calls=%async_computation.4 | async-start | bytes 1048576 | tf_op jit(solution)/shard_map/all_to_all | solution.py:247
  174.2 13.3 %all-to-all-start.2 = ((bf16[8,16,1024]{2,1,0:T(8,128)(2,1)}), bf16[8,16,1024]{2,1,0:T(8,128)(2,1)}, u32[]{:S(2)}, u32[]{:S(2)}) async-start(bf16[8,16,1024]{2,1,0:T(8,128)(2,1)} %bitcast.248), calls=%async_computation.2 | async-start | bytes 524288 | tf_op jit(solution)/shard_map/all_to_all | solution.py:311
  187.5 29.8 %all-to-all-start.3 = ((bf16[32,128,128]{2,1,0:T(8,128)(2,1)}), bf16[32,128,128]{2,1,0:T(8,128)(2,1)S(1)}, u32[]{:S(2)}, u32[]{:S(2)}) async-start(bf16[32,128,128]{2,1,0:T(8,128)(2,1)} %bitcast.101), calls=%async_computation.3 | async-start | bytes 2097152 | tf_op jit(solution)/shard_map/all_to_all | solution.py:276
  199.1 11.8 %collective-permute-start.19 = (bf16[128,1024]{1,0:T(8,128)(2,1)S(1)}, bf16[128,1024]{1,0:T(8,128)(2,1)}, u32[]{:S(2)}, u32[]{:S(2)}) collective-permute-start(bf16[128,1024]{1,0:T(8,128)(2,1)S(1)} %fusion.166), channel_id=1, source_target_pairs={{0,2},{1,3},{2,0},{3,1},{4,6},{5,7},{6,4},{7,5},{8,10},{9,11},{10,... | collective-permute-start | bytes 786440 | tf_op jit(solution)/shard_map/ppermute | solution.py:21
  (96 other events, 1654.1 us)

commit v2 on v1

v2 whole, which is shorter than its diff:
```python
import jax
import jax.numpy as jnp
from jax import lax
from jax.experimental import pallas as pl
from jax.experimental.pallas import tpu as pltpu
from jax.sharding import PartitionSpec as P

NORM_EPS = 1e-05
BF16 = jnp.bfloat16
F32 = jnp.float32


def stages_of(sizes):
    if sizes["dp"] == 8 and sizes["tm"] == 4:
        return {"dp": ((2, 4), (1, 2)), "tm": ((2, 2), (1, 2))}
    if sizes["dp"] == 64 and sizes["tm"] == 4:
        return {"dp": ((8, 8), (2, 4), (1, 2)), "tm": ((1, 4),)}
    return {axis: ((1, size),) for axis, size in sizes.items()}


def swap(value, axis, mask):
    size = lax.axis_size(axis)
    return lax.ppermute(value, axis, [(i, i ^ mask) for i in range(size)])


VMEM_LIMIT = 48 << 20


def kernel_params():
    return pltpu.CompilerParams(vmem_limit_bytes=VMEM_LIMIT)


def costs(flops, moved):
    return pl.CostEstimate(flops=flops, bytes_accessed=moved, transcendentals=0)


def after(value, *others):
    return lax.optimization_barrier((value,) + others)[0]


def place_parts(parts, axis, stride, size, dim):
    shape = parts[0].shape
    out_shape = shape[:dim] + (size,) + shape[dim:]

    def kernel(*refs):
        place = (lax.axis_index(axis) // stride) % size
        for k in range(size):
            refs[size][(slice(None),) * dim + (place ^ k,)] = refs[k][...]

    return pl.pallas_call(
        kernel,
        out_shape=jax.ShapeDtypeStruct(out_shape, parts[0].dtype),
        compiler_params=kernel_params(),
        cost_estimate=pl.CostEstimate(
            flops=0, bytes_accessed=2 * size * parts[0].size * 2, transcendentals=0
        ),
    )(*parts)


def gather_stage(value, axis, stride, size, dim):
    parts = [value] + [swap(value, axis, k * stride) for k in range(1, size)]
    return place_parts(parts, axis, stride, size, dim)


def gather(value, axis, chains):
    shape = value.shape
    for dim, (stride, size) in enumerate(chains):
        value = gather_stage(value, axis, stride, size, dim)
    return value.reshape((-1,) + shape)


def block_terms(left, right, transposed, axis, count):
    block = left.shape[0] // count
    width = right.shape[0] if transposed else right.shape[1]
    dims = (((1,), (1 if transposed else 0,)), ((), ()))

    def kernel(left_ref, right_ref, own, others):
        place = lax.axis_index(axis)
        for k in range(count):
            start = pl.multiple_of((place ^ k) * block, block)
            term = lax.dot_general(
                left_ref[pl.ds(start, block), :], right_ref[...], dims, preferred_element_type=F32
            )
            if k == 0:
                own[...] = term
            else:
                others[k - 1] = term.astype(BF16)

    return pl.pallas_call(
        kernel,
        out_shape=(
            jax.ShapeDtypeStruct((block, width), F32),
            jax.ShapeDtypeStruct((count - 1, block, width), BF16),
        ),
        compiler_params=kernel_params(),
        cost_estimate=pl.CostEstimate(
            flops=2 * left.size * width,
            bytes_accessed=2 * (left.size + right.size) + 10 * block * width,
            transcendentals=0,
        ),
    )(left, right)


def block_sum(own, others, axis, chains):
    if list(chains) == [(2, 2), (1, 2)]:
        near = swap(others[0], axis, 1)
        passed = swap(others[2], axis, 1)
        far = swap((others[1].astype(F32) + passed.astype(F32)).astype(BF16), axis, 2)
        return own + near.astype(F32) + far.astype(F32)
    for k in range(others.shape[0]):
        own = own + swap(others[k], axis, k + 1).astype(F32)
    return own


def message_terms(left, right, parts, sides):
    rows, columns = left.shape[1] // parts, right.shape[1] // sides
    if rows % 16:
        terms = jnp.dot(left.T, right, preferred_element_type=F32).astype(BF16)
        terms = terms.reshape(parts, rows, sides, columns).transpose(0, 2, 1, 3)
        return terms.reshape(parts * sides, rows, columns)
    step = max(1, 128 // rows)

    def kernel(left_ref, right_ref, out):
        for i in range(0, parts, step):
            term = lax.dot_general(
                left_ref[:, i * rows : (i + step) * rows],
                right_ref[...],
                (((0,), (0,)), ((), ())),
                preferred_element_type=F32,
            ).astype(BF16)
            for k in range(step):
                for j in range(sides):
                    out[(i + k) * sides + j] = term[
                        k * rows : (k + 1) * rows, j * columns : (j + 1) * columns
                    ]

    return pl.pallas_call(
        kernel,
        out_shape=jax.ShapeDtypeStruct((parts * sides, rows, columns), BF16),
        compiler_params=kernel_params(),
        cost_estimate=pl.CostEstimate(
            flops=2 * left.size * right.shape[1],
            bytes_accessed=2 * (left.size + right.size + left.shape[1] * right.shape[1]),
            transcendentals=0,
        ),
    )(left, right)


def regroup_columns(weight, lane, grouped, axis, count):
    rows, columns = weight.shape
    span = lane.shape[0]
    groups = columns // span
    if rows % 16:
        parts = jnp.dot(
            weight.reshape(rows * groups, span), one_hot(grouped, lane), preferred_element_type=F32
        ).astype(BF16)
        parts = parts.reshape(rows, groups, count, 128).transpose(2, 0, 1, 3)
        parts = parts.reshape(count, rows, groups * 128)
        return [
            lax.dynamic_index_in_dim(parts, lax.axis_index(axis) ^ k, 0, keepdims=False)
            for k in range(count)
        ]
    small = rows

    def kernel(weight_ref, *outs):
        place = lax.axis_index(axis)
        at = lax.broadcasted_iota(jnp.int32, (span, 128), 0)
        to = lax.broadcasted_iota(jnp.int32, (span, 128), 1)
        for k in range(count):
            want = to // small * (small * count) + (place ^ k) * small + to % small
            pick = jnp.where(at == want, 1.0, 0.0).astype(BF16)
            for g in range(groups):
                outs[k][:, g * 128 : (g + 1) * 128] = jnp.dot(
                    weight_ref[:, g * span : (g + 1) * span], pick, preferred_element_type=F32
                ).astype(BF16)

    return pl.pallas_call(
        kernel,
        out_shape=[jax.ShapeDtypeStruct((rows, columns // count), BF16)] * count,
        cost_estimate=pl.CostEstimate(
            flops=2 * weight.size * span, bytes_accessed=4 * weight.size, transcendentals=0
        ),
    )(weight)


def stem_backward(grad_normed, stem_pre, grad_out, gain, extra):
    block, channels = grad_normed.shape

    def kernel(grad_ref, pre_ref, out_grad_ref, gain_ref, out):
        pre = pre_ref[...]
        sigma = jax.nn.sigmoid(pre)
        hat, inverse = standardize((pre * sigma).astype(BF16).astype(F32))
        grad = grad_ref[...]
        out[block:, :] = jnp.concatenate(
            [jnp.sum(grad * hat, axis=0, keepdims=True), jnp.zeros((extra - 1, channels), F32)]
        ).astype(BF16)
        back = grad * gain_ref[...]
        first = jnp.mean(back, axis=-1, keepdims=True)
        second = jnp.mean(back * hat, axis=-1, keepdims=True)
        stem_out = out_grad_ref[...].astype(F32) + (back - first - hat * second) * inverse
        out[:block, :] = (stem_out * (sigma * (1.0 + pre * (1.0 - sigma)))).astype(BF16)

    return pl.pallas_call(
        kernel,
        out_shape=jax.ShapeDtypeStruct((block + extra, channels), BF16),
        compiler_params=kernel_params(),
        cost_estimate=pl.CostEstimate(
            flops=30 * grad_normed.size, bytes_accessed=12 * grad_normed.size, transcendentals=0
        ),
    )(grad_normed, stem_pre, grad_out, gain)


def standardize(values):
    centered = values - jnp.mean(values, axis=-1, keepdims=True)
    inverse = lax.rsqrt(jnp.mean(centered * centered, axis=-1, keepdims=True) + NORM_EPS)
    return (centered * inverse, inverse)


def gather_parts(value, axis, chains):
    if list(chains) == [(2, 2), (1, 2)]:
        far = swap(value, axis, 2)
        return [value, swap(value, axis, 1), far, swap(far, axis, 1)]
    return [value] + [swap(value, axis, k) for k in range(1, lax.axis_size(axis))]


def swap_all(value, axis):
    return [value] + [swap(value, axis, k) for k in range(1, lax.axis_size(axis))]


def split_parts(parts, axis, stride, size, dim, cut):
    shape = parts[0].shape
    lead = shape[:dim] + (size,) + shape[dim:-2]
    rows = (cut, shape[-2] - cut)

    def kernel(*refs):
        place = (lax.axis_index(axis) // stride) % size
        for k in range(size):
            target = (slice(None),) * dim + (place ^ k,)
            refs[size][target] = refs[k][..., :cut, :]
            refs[size + 1][target] = refs[k][..., cut:, :]

    return pl.pallas_call(
        kernel,
        out_shape=[
            jax.ShapeDtypeStruct(lead + (count, shape[-1]), parts[0].dtype) for count in rows
        ],
        compiler_params=kernel_params(),
        cost_estimate=costs(0, 4 * size * parts[0].size),
    )(*parts)


def split_gather(value, axis, chains, cut):
    for dim, (stride, size) in enumerate(chains):
        parts = [value] + [swap(value, axis, k * stride) for k in range(1, size)]
        if dim == len(chains) - 1:
            upper, lower = split_parts(parts, axis, stride, size, dim, cut)
        else:
            value = place_parts(parts, axis, stride, size, dim)
    return (
        upper.reshape((-1,) + upper.shape[-2:]),
        lower.reshape((-1, lower.shape[-1])),
    )


def prepare(mel, owner, slot, stem, up, down, taps, gain_one, gain_two, dp_count, tm_count):
    pieces, values = mel.shape
    capacity = max(2, 2 * pieces // dp_count)
    slots = dp_count * capacity
    stem_rows, channels = stem.shape
    rows = down.shape[0]
    tap_count = taps.shape[1]
    span = 128 * tm_count
    groups = up.shape[1] // span

    def kernel(
        mel_ref, owner_ref, slot_ref, stem_ref, up_ref, down_ref, taps_ref, one_ref, two_ref,
        sent, pack, *up_parts
    ):
        def iota(shape, dim):
            return lax.broadcasted_iota(jnp.int32, shape, dim)

        def table(flags):
            return jnp.where(flags, 1.0, 0.0).astype(BF16)

        pack[:stem_rows, :channels] = stem_ref[...]
        pack[stem_rows:, :channels] = down_ref[...]
        lane = iota((rows, 128), 1)
        spread = table(lane % rows == iota((rows, 128), 0))
        gain = jnp.broadcast_to(one_ref[...].astype(F32), (stem_rows, rows)).astype(BF16)
        pack[:stem_rows, channels:] = jnp.dot(gain, spread, preferred_element_type=F32).astype(BF16)
        tap_lane = table(iota((tap_count, 128), 1) == iota((tap_count, 128), 0))
        square = iota((rows, rows), 0) == iota((rows, rows), 1)
        diagonal = jnp.where(
            square, jnp.broadcast_to(two_ref[...].astype(F32), (rows, rows)), 0.0
        ).astype(BF16)
        small = jnp.dot(taps_ref[...], tap_lane, preferred_element_type=F32)
        small = small + jnp.dot(diagonal, table(lane == tap_count), preferred_element_type=F32)
        pack[stem_rows:, channels:] = small.astype(BF16)

        place = lax.axis_index("tm")
        at = iota((span, 128), 0)
        to = iota((span, 128), 1)
        for k in range(tm_count):
            want = to // rows * (rows * tm_count) + (place ^ k) * rows + to % rows
            pick = table(at == want)
            for g in range(groups):
                up_parts[k][:, g * 128 : (g + 1) * 128] = jnp.dot(
                    up_ref[:, g * span : (g + 1) * span], pick, preferred_element_type=F32
                ).astype(BF16)

        owners = jnp.broadcast_to(owner_ref[...].astype(F32), (pieces, pieces))
        earlier = iota((pieces, pieces), 0) < iota((pieces, pieces), 1)
        same = jnp.where(owners.T == owners, jnp.where(earlier, 1.0, 0.0), 0.0)
        target = owners[:1] * float(capacity) + jnp.sum(same, axis=0, keepdims=True)
        target = jnp.broadcast_to(target, (slots, pieces)).astype(jnp.int32)
        chosen = target == iota((slots, pieces), 0)
        pick = table(chosen)
        sent[:, :values] = jnp.dot(pick, mel_ref[...], preferred_element_type=F32).astype(BF16)
        labels = jnp.broadcast_to(slot_ref[...].astype(F32) + 1.0, (slots, pieces))
        label = jnp.sum(jnp.where(chosen, labels, 0.0), axis=1, keepdims=True)
        sent[:, values:] = jnp.broadcast_to(label, (slots, 128)).astype(BF16)

    outs = pl.pallas_call(
        kernel,
        out_shape=[
            jax.ShapeDtypeStruct((slots, values + 128), BF16),
            jax.ShapeDtypeStruct((stem_rows + rows, channels + 128), BF16),
        ]
        + [jax.ShapeDtypeStruct((rows, up.shape[1] // tm_count), BF16)] * tm_count,
        compiler_params=kernel_params(),
        cost_estimate=costs(1 << 27, 2 << 20),
    )(
        mel, owner[None, :], slot[None, :], stem, up, down, taps, gain_one[None, :],
        gain_two[None, :],
    )
    return outs[0], outs[1], list(outs[2:])


def place_frames(arrived, pieces, features):
    slots, width = arrived.shape
    steps = (width - 128) // features

    def kernel(arrived_ref, out):
        labels = arrived_ref[:, steps * features :].astype(F32).T[:1]
        want = jnp.broadcast_to(labels, (pieces * steps, slots)).astype(jnp.int32)
        row = lax.broadcasted_iota(jnp.int32, (pieces * steps, slots), 0)
        total = jnp.zeros((pieces * steps, features), F32)
        for q in range(steps):
            put = jnp.where(row == (want - 1) * steps + q, 1.0, 0.0).astype(BF16)
            total = total + jnp.dot(
                put, arrived_ref[:, q * features : (q + 1) * features], preferred_element_type=F32
            )
        out[...] = total.astype(BF16)

    return pl.pallas_call(
        kernel,
        out_shape=jax.ShapeDtypeStruct((pieces * steps, features), BF16),
        compiler_params=kernel_params(),
        cost_estimate=costs(2 * arrived.size * pieces * steps, 4 * arrived.size),
    )(arrived)


def stem_forward(frames, stem_all, count, axis, rows):
    length = frames.shape[0]
    features, width = stem_all.shape
    channels = width - 128
    block = length // count
    stem_rows = features * rows // channels

    def kernel(frames_ref, stem_ref, normed, pre_own, gain_out):
        place = lax.axis_index(axis)
        beside = stem_ref[:, channels:].astype(F32)
        gains = []
        for g in range(channels // 128):
            row = lax.broadcasted_iota(jnp.int32, (features, 128), 0)
            lane = lax.broadcasted_iota(jnp.int32, (features, 128), 1) + g * 128
            gains.append(
                jnp.sum(
                    jnp.where(row == lane // rows * stem_rows, beside, 0.0), axis=0, keepdims=True
                )
            )
        gain_out[...] = jnp.concatenate(gains, axis=1)
        for b in range(count):
            pre = jnp.dot(
                frames_ref[b * block : (b + 1) * block, :],
                stem_ref[:, :channels],
                preferred_element_type=F32,
            )
            hat, _ = standardize((pre * jax.nn.sigmoid(pre)).astype(BF16).astype(F32))
            normed[b * block : (b + 1) * block, :] = (hat * gain_out[...]).astype(BF16)

            @pl.when(place == b)
            def _():
                pre_own[...] = pre

    return pl.pallas_call(
        kernel,
        out_shape=[
            jax.ShapeDtypeStruct((length, channels), BF16),
            jax.ShapeDtypeStruct((block, channels), F32),
            jax.ShapeDtypeStruct((1, channels), F32),
        ],
        compiler_params=kernel_params(),
        cost_estimate=costs(2 * frames.size * channels, 2 * stem_all.size + 4 * frames.size),
    )(frames, stem_all)


PAD = 16


def up_forward(normed, up):
    length = normed.shape[0]
    held = up.shape[1] // 2
    step = min(128, length)

    def kernel(normed_ref, up_ref, linear, gate, gated):
        edge = jnp.zeros((PAD, held), F32)
        gated[:PAD, :] = edge
        gated[PAD + length :, :] = edge
        for b in range(0, length, step):
            proj = jnp.dot(normed_ref[b : b + step, :], up_ref[...], preferred_element_type=F32)
            sigma = jax.nn.sigmoid(proj[:, held:])
            linear[b : b + step, :] = proj[:, :held]
            gate[b : b + step, :] = sigma
            gated[PAD + b : PAD + b + step, :] = (proj[:, :held] * sigma).astype(BF16).astype(F32)

    return pl.pallas_call(
        kernel,
        out_shape=[
            jax.ShapeDtypeStruct((length, held), F32),
            jax.ShapeDtypeStruct((length, held), F32),
            jax.ShapeDtypeStruct((length + 2 * PAD, held), F32),
        ],
        compiler_params=kernel_params(),
        cost_estimate=costs(4 * normed.size * held, 2 * normed.size + 2 * up.size),
    )(normed, up)


def columns_of(first, second):
    rows = first.shape[0]
    lane = lax.broadcasted_iota(jnp.int32, (rows, 128), 1)
    both = jnp.where(lane == 0, first, jnp.where(lane == 1, second, 0.0))
    return both.T[:8]


def rows_of(table):
    rows = table.shape[1]
    turned = jnp.concatenate([table, jnp.zeros((120, rows), F32)], axis=0).T
    return turned[:, :1], turned[:, 1:2]


TILE = 64


def conv_forward(gated, small, segments, taps):
    length, held = gated.shape[0] - 2 * PAD, gated.shape[1]
    margin = (taps - 1) // 2

    def kernel(gated_ref, small_ref, seg_ref, conv, stats, turned, gated_near, seg_near):
        turned[...] = small_ref[...].astype(F32).T

        def tile(t, carry):
            base = pl.multiple_of(t * TILE, TILE)
            gated_near[...] = gated_ref[pl.ds(base, TILE + 2 * PAD), :]
            seg_near[...] = seg_ref[pl.ds(base, TILE + 2 * PAD), :]
            centre = seg_near[PAD : PAD + TILE, :]
            sums = [jnp.zeros((TILE, 128), F32) for _ in range(held // 128)]
            for k in range(taps):
                shift = PAD + k - margin
                inside = seg_near[shift : shift + TILE, :] == centre
                for g in range(held // 128):
                    lanes = slice(g * 128, (g + 1) * 128)
                    value = gated_near[shift : shift + TILE, lanes]
                    sums[g] = sums[g] + jnp.where(inside, value, 0.0) * turned[k : k + 1, lanes]
            conv[pl.ds(base, TILE), :] = jnp.concatenate(sums, axis=1)
            return carry

        lax.fori_loop(0, length // TILE, tile, 0)
        value = conv[...]
        mean = jnp.mean(value, axis=-1, keepdims=True)
        centered = value - mean
        stats[...] = columns_of(mean, jnp.sum(centered * centered, axis=-1, keepdims=True))

    return pl.pallas_call(
        kernel,
        out_shape=[
            jax.ShapeDtypeStruct((length, held), F32),
            jax.ShapeDtypeStruct((8, length), F32),
            jax.ShapeDtypeStruct((128, held), F32),
        ],
        scratch_shapes=[
            pltpu.VMEM((TILE + 2 * PAD, held), F32),
            pltpu.VMEM((TILE + 2 * PAD, 128), jnp.int32),
        ],
        compiler_params=kernel_params(),
        cost_estimate=costs(4 * taps * gated.size, 8 * gated.size),
    )(gated, small, segments)


def activate(conv, stats, turned, grad_act, taps):
    length, held = conv.shape
    count = len(stats)

    def kernel(conv_ref, turned_ref, grad_ref, *refs):
        tables, (active, hat_out, grad_hat_out, inverse_out, sums, gain_term) = (
            refs[:count], refs[count:],
        )
        means = [table[0:1, :] for table in tables]
        mean = sum(means) * (1.0 / count)
        squares = sum(table[1:2, :] for table in tables)
        squares = squares + held * sum((one - mean) * (one - mean) for one in means)
        inverse = lax.rsqrt(squares * (1.0 / (held * count)) + NORM_EPS)
        both = jnp.concatenate([mean, inverse, jnp.zeros((6, length), F32)], axis=0)
        mean, inverse = rows_of(both)
        inverse_out[...] = jnp.broadcast_to(inverse, (length, 128))
        gain = turned_ref[taps : taps + 1, :]
        hat = (conv_ref[...] - mean) * inverse
        scaled = hat * gain
        sigma = jax.nn.sigmoid(scaled)
        active[...] = (scaled * sigma).astype(BF16)
        grad_scaled = grad_ref[...] * (sigma * (1.0 + scaled * (1.0 - sigma)))
        gain_term[...] = jnp.sum(grad_scaled * hat, axis=0, keepdims=True)
        grad_hat = grad_scaled * gain
        hat_out[...] = hat
        grad_hat_out[...] = grad_hat
        sums[...] = columns_of(
            jnp.sum(grad_hat, axis=-1, keepdims=True),
            jnp.sum(grad_hat * hat, axis=-1, keepdims=True),
        )

    return pl.pallas_call(
        kernel,
        out_shape=[
            jax.ShapeDtypeStruct((length, held), BF16),
            jax.ShapeDtypeStruct((length, held), F32),
            jax.ShapeDtypeStruct((length, held), F32),
            jax.ShapeDtypeStruct((length, 128), F32),
            jax.ShapeDtypeStruct((8, length), F32),
            jax.ShapeDtypeStruct((1, held), F32),
        ],
        compiler_params=kernel_params(),
        cost_estimate=costs(40 * conv.size, 20 * conv.size),
    )(conv, turned, grad_act, *stats)


def conv_backward(grad_hat, hat, inverse, sums, gated, segments, linear, gate, turned, taps, gain_term):
    length, held = hat.shape
    count = len(sums)
    margin = (taps - 1) // 2
    groups = held // 128

    def kernel(
        grad_ref, hat_ref, inverse_ref, gated_ref, seg_ref, linear_ref, gate_ref, turned_ref,
        gain_ref, *refs
    ):
        tables, (proj, terms), (grad_conv, partial, grad_near, gated_near, seg_near) = (
            refs[:count], refs[count : count + 2], refs[count + 2 :],
        )
        total = sum(table[...] for table in tables) * (1.0 / (held * count))
        first, second = rows_of(total)
        edge = jnp.zeros((PAD, held), F32)
        grad_conv[:PAD, :] = edge
        grad_conv[PAD + length :, :] = edge
        value = (grad_ref[...] - first - hat_ref[...] * second) * inverse_ref[:, :1]
        grad_conv[PAD : PAD + length, :] = value.astype(BF16).astype(F32)
        partial[...] = jnp.zeros_like(partial)

        def tile(t, carry):
            base = pl.multiple_of(t * TILE, TILE)
            grad_near[...] = grad_conv[pl.ds(base, TILE + 2 * PAD), :]
            gated_near[...] = gated_ref[pl.ds(base, TILE + 2 * PAD), :]
            seg_near[...] = seg_ref[pl.ds(base, TILE + 2 * PAD), :]
            centre = seg_near[PAD : PAD + TILE, :]
            lanes = [slice(g * 128, (g + 1) * 128) for g in range(groups)]
            here = [grad_near[PAD : PAD + TILE, lanes[g]] for g in range(groups)]
            back = [jnp.zeros((TILE, 128), F32) for _ in range(groups)]
            for k in range(taps):
                shift = PAD + k - margin
                inside = seg_near[shift : shift + TILE, :] == centre
                for g in range(groups):
                    near = grad_near[shift : shift + TILE, lanes[g]]
                    weight = turned_ref[taps - 1 - k : taps - k, lanes[g]]
                    back[g] = back[g] + jnp.where(inside, near, 0.0) * weight
                    source = gated_near[shift : shift + TILE, lanes[g]]
                    product = jnp.where(inside, source, 0.0) * here[g]
                    partial[k, :, lanes[g]] += jnp.sum(
                        product.reshape(TILE // 8, 8, 128), axis=0
                    )
            for g in range(groups):
                sigma = gate_ref[pl.ds(base, TILE), lanes[g]]
                part = back[g] * sigma
                proj[pl.ds(base, TILE), lanes[g]] = part.astype(BF16)
                far = slice(held + g * 128, held + (g + 1) * 128)
                proj[pl.ds(base, TILE), far] = (
                    part * linear_ref[pl.ds(base, TILE), lanes[g]] * (1.0 - sigma)
                ).astype(BF16)
            return carry

        lax.fori_loop(0, length // TILE, tile, 0)
        terms[:taps, :] = jnp.sum(partial[...], axis=1)
        terms[taps : taps + 1, :] = gain_ref[...]

    return pl.pallas_call(
        kernel,
        out_shape=[
            jax.ShapeDtypeStruct((length, 2 * held), BF16),
            jax.ShapeDtypeStruct((taps + 1, held), F32),
        ],
        scratch_shapes=[
            pltpu.VMEM((length + 2 * PAD, held), F32),
            pltpu.VMEM((taps, 8, held), F32),
            pltpu.VMEM((TILE + 2 * PAD, held), F32),
            pltpu.VMEM((TILE + 2 * PAD, held), F32),
            pltpu.VMEM((TILE + 2 * PAD, 128), jnp.int32),
        ],
        compiler_params=kernel_params(),
        cost_estimate=costs(8 * taps * hat.size, 24 * hat.size),
    )(grad_hat, hat, inverse, gated, segments, linear, gate, turned, gain_term, *sums)


def one_hot(rows, columns):
    return (rows[:, None] == columns[None, :]).astype(BF16)


def order_pieces(mel_pieces, dest_owner, dest_slot, dp_count):
    pieces, piece_values = mel_pieces.shape
    capacity = max(2, 2 * pieces // dp_count)
    matches = (dest_owner[:, None] == jnp.arange(dp_count, dtype=jnp.int32)[None, :]).astype(jnp.int32)
    earlier = jnp.cumsum(matches, axis=0) - matches
    position = dest_owner * capacity + jnp.sum(earlier * matches, axis=1)
    pick = one_hot(jnp.arange(dp_count * capacity, dtype=jnp.int32), position)
    label = jnp.broadcast_to((dest_slot + 1).astype(BF16)[:, None], (pieces, 128))
    return jnp.dot(
        pick, jnp.concatenate([mel_pieces, label], axis=1), preferred_element_type=F32
    ).astype(BF16)


def per_device(
    mel_pieces,
    dest_owner,
    dest_slot,
    segment_ids,
    out_grad,
    stem_weight,
    up_weight,
    down_weight,
    depth_kernel,
    gain_pre,
    gain_post,
):
    dp_count = lax.axis_size("dp")
    tm_count = lax.axis_size("tm")
    chains = stages_of({"dp": dp_count, "tm": tm_count})
    dp_chains, tm_chains = chains["dp"], chains["tm"]
    column = lax.axis_index("tm")
    taps = depth_kernel.shape[1]
    margin = (taps - 1) // 2
    block = out_grad.shape[1]
    channels = out_grad.shape[2]
    held = channels // tm_count
    rows = down_weight.shape[0]
    stem_rows = stem_weight.shape[0]
    features = stem_rows * dp_count * tm_count
    length = block * tm_count

    span = 128 * tm_count
    lane = jnp.arange(span, dtype=jnp.int32)
    grouped = (lane // rows) % tm_count * 128 + lane // (rows * tm_count) * rows + lane % rows
    if stem_rows % 16 == 0 and rows % 16 == 0:
        sent, pack, up_parts = prepare(
            mel_pieces[0], dest_owner[0], dest_slot[0], stem_weight, up_weight, down_weight,
            depth_kernel, gain_pre, gain_post, dp_count, tm_count,
        )
    else:
        sent = order_pieces(mel_pieces[0], dest_owner[0], dest_slot[0], dp_count)
        up_parts = regroup_columns(up_weight, lane, grouped, "tm", tm_count)
        beside = jnp.broadcast_to(jnp.tile(gain_pre, 128 // rows)[None, :], (stem_rows, 128))
        small = jnp.concatenate(
            [depth_kernel, gain_post[:, None], jnp.zeros((rows, 128 - taps - 1), BF16)], axis=1
        )
        pack = jnp.concatenate(
            [
                jnp.concatenate([stem_weight, beside], axis=1),
                jnp.concatenate([down_weight, small], axis=1),
            ]
        )

    up_parts = [up_parts[0]] + [swap(up_parts[k], "tm", k) for k in range(1, tm_count)]
    up_mine = place_parts(up_parts, "tm", 1, tm_count, 0)
    stem_mine, down_all = split_gather(pack, "dp", dp_chains, stem_rows)
    up_full = gather(up_mine.reshape(tm_count * rows, 2 * held), "dp", dp_chains)
    up_full = up_full.reshape(channels, 2 * held)
    down_full = down_all[:, :channels]
    small_all = down_all[:, channels:]
    stem_all = place_parts(gather_parts(stem_mine, "tm", tm_chains), "tm", 1, tm_count, 1)
    stem_all = stem_all.reshape(features, channels + 128)

    pieces = mel_pieces.shape[1]
    capacity = max(2, 2 * pieces // dp_count)
    arrived = lax.all_to_all(
        sent.reshape(dp_count, capacity, -1), "dp", split_axis=0, concat_axis=0, tiled=True
    ).reshape(dp_count * capacity, -1)
    frames = place_frames(arrived, pieces, features)
    frames = place_parts(gather_parts(frames, "tm", tm_chains), "tm", 1, tm_count, 0)
    frames = frames.reshape(length, features)
    grad_out = out_grad[0]
    grad_out_all = gather_parts(after(grad_out, stem_mine), "tm", tm_chains)
    grad_out_all = place_parts(grad_out_all, "tm", 1, tm_count, 0).reshape(length, channels)
    segments = jnp.pad(segment_ids[0], (PAD, PAD), constant_values=-1)
    segments = jnp.broadcast_to(segments[:, None], (length + 2 * PAD, 128))

    normed, stem_pre, gain_one = stem_forward(frames, stem_all, tm_count, "tm", rows)
    linear, gate_sig, gated = up_forward(normed, up_full)
    conv, stats, turned = conv_forward(gated, small_all, segments, taps)
    grad_act = lax.dot_general(
        grad_out_all, down_full, (((1,), (1,)), ((), ())), preferred_element_type=F32
    )
    activated, conv_hat, grad_hat, inverse, sums, gain_post_term = activate(
        conv, swap_all(stats, "tm"), turned, grad_act, taps
    )
    sums = swap_all(sums, "tm")
    late = after(activated, *sums[:2])
    down_terms = message_terms(late, grad_out_all, dp_count, tm_count)
    y_terms = block_terms(late, down_full, False, "tm", tm_count)
    down_sums = lax.all_to_all(down_terms, ("dp", "tm"), split_axis=0, concat_axis=0, tiled=True)

    grad_hat = after(grad_hat, down_terms, *y_terms)
    grad_proj, kernel_term = conv_backward(
        grad_hat, conv_hat, inverse, sums, gated, segments, linear, gate_sig, turned, taps,
        gain_post_term,
    )
    y_part = block_sum(*y_terms, "tm", tm_chains)

    normed_terms = block_terms(after(grad_proj, y_part), up_full, True, "tm", tm_count)
    grad_normed = block_sum(*normed_terms, "tm", tm_chains)
    up_terms = message_terms(
        after(normed, down_sums, *normed_terms), grad_proj, dp_count, tm_count
    )
    up_sums = lax.all_to_all(up_terms, ("dp", "tm"), split_axis=0, concat_axis=0, tiled=True)
    y_out = (jax.nn.silu(stem_pre).astype(BF16).astype(F32) + after(y_part, up_terms)).astype(BF16)
    grad_down = jnp.sum(
        after(down_sums, up_terms).reshape(dp_count, tm_count * rows, held).astype(F32), axis=0
    )

    extra = 16
    grad_stem_pre = stem_backward(
        grad_normed, stem_pre, grad_out, gain_one, extra
    )
    chosen = jnp.arange(features // tm_count, dtype=jnp.int32)
    chosen = (chosen // stem_rows * tm_count + column) * stem_rows + chosen % stem_rows
    frames_part = jnp.dot(
        frames, one_hot(jnp.arange(features, dtype=jnp.int32), chosen), preferred_element_type=F32
    ).astype(BF16)
    frames_part = frames_part.reshape(tm_count, block, features // tm_count)
    frames_part = jnp.pad(frames_part, ((0, 0), (0, extra), (0, extra)))
    frames_part = frames_part.at[:, block, features // tm_count].set(1)
    grad_stem_parts = gather_parts(grad_stem_pre, "tm", tm_chains)
    stem_sum = 0.0
    for k in range(tm_count):
        frames_k = lax.dynamic_index_in_dim(frames_part, column ^ k, 0, keepdims=False)
        stem_sum = stem_sum + jnp.dot(
            frames_k.T, grad_stem_parts[k], preferred_element_type=F32
        )
    small_term = kernel_term.reshape(taps + 1, dp_count, rows).transpose(1, 0, 2)
    small_term = small_term.reshape(dp_count, 1, (taps + 1) * rows).astype(BF16)
    small_term = jnp.pad(small_term, ((0, 0), (0, 0), (0, channels - (taps + 1) * rows)))
    gain_term = stem_sum[features // tm_count].astype(BF16).reshape(dp_count, 1, tm_count * rows)
    gain_term = jnp.pad(gain_term, ((0, 0), (0, 0), (0, channels - tm_count * rows)))
    stem_terms = stem_sum[: features // tm_count].astype(BF16)
    stem_terms = stem_terms.reshape(dp_count, stem_rows, channels)
    stem_terms = jnp.concatenate([stem_terms, small_term, gain_term], axis=1)
    stem_terms = after(stem_terms, up_sums)
    stem_sums = lax.all_to_all(stem_terms, "dp", split_axis=0, concat_axis=0, tiled=True)
    up_sums = up_sums.reshape(dp_count, tm_count, tm_count * rows, 128)
    spread = one_hot(lane, grouped).reshape(tm_count, 128, span)
    grad_up = jnp.einsum("ijab,jbc->ac", up_sums, spread, preferred_element_type=F32)
    stem_sums = jnp.sum(stem_sums.astype(F32), axis=0)
    grad_stem = stem_sums[:stem_rows]
    small_sum = stem_sums[stem_rows, : (taps + 1) * rows].reshape(taps + 1, rows)
    grad_kernel, grad_gain_post = small_sum[:taps].T, small_sum[taps]
    grad_gain_pre = lax.dynamic_slice_in_dim(stem_sums[stem_rows + 1], column * rows, rows, 0)
    return (y_out[None], grad_stem, grad_up, grad_down, grad_kernel, grad_gain_pre, grad_gain_post)


def solution(mesh):
    return jax.shard_map(
        per_device,
        mesh=mesh,
        in_specs=(
            P("dp", "tm", None),
            P("dp", "tm"),
            P("dp", "tm"),
            P("dp", None),
            P("dp", "tm", None),
            P(("dp", "tm"), None),
            P(("dp", "tm"), None),
            P(("dp", "tm"), None),
            P(("dp", "tm"), None),
            P(("dp", "tm")),
            P(("dp", "tm")),
        ),
        out_specs=(
            P("dp", "tm", None),
            P(("dp", "tm"), None),
            P("dp", "tm"),
            P("dp", "tm"),
            P(("dp", "tm"), None),
            P(("dp", "tm")),
            P(("dp", "tm")),
        ),
        check_vma=False,
    )
```

time: 221 us -> 171 us (0.77)
  other arithmetic: 37.2 us -> 8.35 us
  Pallas kernels: 0 us -> 21.1 us
  local copies, waits for them, and re-layouts: 40.8 us -> 21.6 us
  matrix products: 20.3 us -> 3 us
  starting transfers between devices: 54.7 us -> 41.8 us
  waiting for transfers between devices: 63.7 us -> 73.3 us
    pallas_call x0 -> x20, Pallas kernels: none -> 21.1 us  [the longest x1 6.18 us: conv_backward(): pl.pallas_call(kernel, out_shape=[jax.ShapeDtypeStruct((length, 2 * held)...]
    ppermute x28 -> x35, waiting for transfers between devices: 39 us -> 59.6 us  [swap(): return lax.ppermute(value, axis, [(i, i ^ mask) for i in range(size)])]
    unnamed x174 -> x82, local copies, waits for them, and re-layouts: 2.49 us -> 18.1 us
    reduce_sum x16 -> x3, other arithmetic: 17.6 us -> 1.98 us  [the longest x1 1.78 us: per_device(): jnp.sum(after(down_sums, up_terms).reshape(dp_count, tm_count * rows, hel...]
    dot_general x11 -> x6, matrix products: 17.3 us -> 2.53 us  [the longest x4 1.12 us: per_device(): jnp.dot(frames_k.T, grad_stem_parts[k], preferred_element_type=F32)]
    dynamic_update_slice x31 -> x0, local copies, waits for them, and re-layouts: 14.3 us -> none  [gather_stage(): out = lax.dynamic_update_slice_in_dim(out, part[None], place ^ k, 0)]
    all_to_all x1, waiting for transfers between devices: 10.6 us -> 0.01 us  [per_device(): lax.all_to_all(down_terms, ('dp', 'tm'), split_axis=0, concat_axis=0, til...]
    all_to_all x5 -> x2, starting transfers between devices: 16.9 us -> 7.41 us  [the longest x1 3.75 us: per_device(): lax.all_to_all(sent.reshape(dp_count, capacity, -1), 'dp', split_axis=0,...]
  transfers between devices with their start and end apart: 35 -> 39, of which waited for: 13 -> 20; matrix products, arithmetic and copies ran while one was open for 34% -> 7% of each run, Pallas kernels for 0% -> 7%
where the time goes in v2:
time: 171 us; the launch traced here: 170 us
  waiting for transfers between devices  73.3 us (43%)
  starting transfers between devices  41.8 us (24%)
  local copies, waits for them, and re-layouts  21.6 us (13%)
  Pallas kernels  21.1 us (12%)
  other arithmetic  8.35 us (5%)
  matrix products  3 us (2%)
    ppermute x35, waiting for transfers between devices, swap(): return lax.ppermute(value, axis, [(i, i ^ mask) for i in range(size)])  59.6 us
    ppermute x35, starting transfers between devices, swap(): return lax.ppermute(value, axis, [(i, i ^ mask) for i in range(size)])  27.9 us
    unnamed x82, local copies, waits for them, and re-layouts  18.1 us
    all_to_all x1, waiting for transfers between devices, per_device(): lax.all_to_all(stem_terms, 'dp', split_axis=0, concat_axis=0, tiled=True)  9.8 us
    pallas_call x1, Pallas kernels, conv_backward(): pl.pallas_call(kernel, out_shape=[jax.ShapeDtypeStruct((length, 2 * held)...  6.18 us
    all_to_all x1, waiting for transfers between devices, per_device(): lax.all_to_all(up_terms, ('dp', 'tm'), split_axis=0, concat_axis=0, tiled...  3.96 us
    all_to_all x1, starting transfers between devices, per_device(): lax.all_to_all(sent.reshape(dp_count, capacity, -1), 'dp', split_axis=0,...  3.75 us
    all_to_all x1, starting transfers between devices, per_device(): lax.all_to_all(stem_terms, 'dp', split_axis=0, concat_axis=0, tiled=True)  3.66 us
  transfers between devices with their start and end apart: 39, of which 20 were waited for; matrix products, arithmetic and copies ran while one was open for 7% of the time, Pallas kernels for 7%

profile of v2, /device:TPU:0, one launch (start us, length us, event | category | flops | bytes accessed | tf_op | source)
XLA Modules:
  0.0 170.4 jit_solution(13780450081053477347)
XLA Ops:
  8.6 5.0 %collective-permute-start.5 = (bf16[48,1152]{1,0:T(8,128)(2,1)S(1)}, bf16[48,1152]{1,0:T(8,128)(2,1)S(1)}, u32[]{:S(2)}, u32[]{:S(2)}) collective-permute-start(bf16[48,1152]{1,0:T(8,128)(2,1)S(1)} %get-tuple-element.57.refs_0_), channel_id=1, source_target_pairs={{0,24},{4,28},{8,16},{12,20},{16,8},{20,12},{24,0},{28,4},{1,25},{... | collective-permute-start | bytes 331784 | tf_op jit(solution)/shard_map/ppermute | solution.py:23
  14.2 3.4 %collective-permute-done.5.refs_3_ = bf16[48,1152]{1,0:T(8,128)(2,1)S(1)} collective-permute-done((bf16[48,1152]{1,0:T(8,128)(2,1)S(1)}, bf16[48,1152]{1,0:T(8,128)(2,1)S(1)}, u32[]{:S(2)}, u32[]{:S(2)}) %collective-permute-start.5) | collective-permute-done | bytes 110624 | tf_op jit(solution)/shard_map/ppermute | solution.py:23
  17.6 5.3 %collective-permute-done.4.refs_2_ = bf16[48,1152]{1,0:T(8,128)(2,1)S(1)} collective-permute-done((bf16[48,1152]{1,0:T(8,128)(2,1)S(1)}, bf16[48,1152]{1,0:T(8,128)(2,1)S(1)}, u32[]{:S(2)}, u32[]{:S(2)}) %collective-permute-start.4) | collective-permute-done | bytes 110624 | tf_op jit(solution)/shard_map/ppermute | solution.py:23
  24.6 3.8 %all-to-all-start = ((bf16[8,8,2176]{2,1,0:T(8,128)(2,1)}), bf16[8,8,2176]{2,1,0:T(8,128)(2,1)S(1)}, u32[]{:S(2)}, u32[]{:S(2)}) async-start(bf16[8,8,2176]{2,1,0:T(8,128)(2,1)} %bitcast.3), calls=%async_computation | async-start | bytes 557056 | tf_op jit(solution)/shard_map/all_to_all | solution.py:700
  30.3 2.1 %collective-permute-done.11.refs_2_ = bf16[32,512]{1,0:T(8,128)(2,1)S(1)} collective-permute-done((bf16[32,512]{1,0:T(8,128)(2,1)S(1)}, bf16[32,512]{1,0:T(8,128)(2,1)S(1)}, u32[]{:S(2)}, u32[]{:S(2)}) %collective-permute-start.11) | collective-permute-done | bytes 32800 | tf_op jit(solution)/shard_map/ppermute | solution.py:23
  33.4 3.8 %collective-permute-start.15 = (bf16[128,512]{1,0:T(8,128)(2,1)S(1)}, bf16[128,512]{1,0:T(8,128)(2,1)S(1)}, u32[]{:S(2)}, u32[]{:S(2)}) collective-permute-start(bf16[128,512]{1,0:T(8,128)(2,1)S(1)} %bitcast.83), channel_id=1, source_target_pairs={{0,24},{4,28},{8,16},{12,20},{16,8},{20,12},{24,0},{28,4},{1,25},{... | collective-permute-start | bytes 393224 | tf_op jit(solution)/shard_map/ppermute | solution.py:23
  37.8 3.9 %collective-permute-done.15.refs_3_ = bf16[128,512]{1,0:T(8,128)(2,1)S(1)} collective-permute-done((bf16[128,512]{1,0:T(8,128)(2,1)S(1)}, bf16[128,512]{1,0:T(8,128)(2,1)S(1)}, u32[]{:S(2)}, u32[]{:S(2)}) %collective-permute-start.15) | collective-permute-done | bytes 131104 | tf_op jit(solution)/shard_map/ppermute | solution.py:23
  41.7 7.4 %collective-permute-done.14.refs_2_ = bf16[128,512]{1,0:T(8,128)(2,1)S(1)} collective-permute-done((bf16[128,512]{1,0:T(8,128)(2,1)S(1)}, bf16[128,512]{1,0:T(8,128)(2,1)S(1)}, u32[]{:S(2)}, u32[]{:S(2)}) %collective-permute-start.14) | collective-permute-done | bytes 131104 | tf_op jit(solution)/shard_map/ppermute | solution.py:23
  54.2 13.4 %collective-permute-done.1.refs_2_ = bf16[128,512]{1,0:T(8,128)(2,1)S(1)} collective-permute-done((bf16[128,512]{1,0:T(8,128)(2,1)S(1)}, bf16[128,512]{1,0:T(8,128)(2,1)S(1)}, u32[]{:S(2)}, u32[]{:S(2)}) %collective-permute-start.1) | collective-permute-done | bytes 131104 | tf_op jit(solution)/shard_map/ppermute | solution.py:23
  68.9 1.7 collective-permute-done.2.refs_3_
  72.0 2.5 %shard_map.168 = (bf16[512,1024]{1,0:T(8,128)(2,1)S(1)}, f32[128,1024]{1,0:T(8,128)S(1)}, f32[1,1024]{1,0:T(1,128)S(1)}) custom-call(bf16[512,512]{1,0:T(8,128)(2,1)S(1)} %bitcast.72, bf16[512,1152]{1,0:T(8,128)(2,1)S(1)} %bitcast.74), custom_call_target="tpu_custom_call" | custom-call | flops 536870912 | bytes 2228224 | tf_op jit(solution)/shard_map/pallas_call | solution.py:396
  77.0 3.0 %shard_map.173 = (f32[512,256]{1,0:T(8,128)S(1)}, f32[8,512]{1,0:T(8,128)S(1)}, f32[128,256]{1,0:T(8,128)S(1)}) custom-call(f32[544,256]{1,0:T(8,128)S(1)} %get-tuple-element.65.gated_ref, bf16[256,128]{1,0:T(8,128)(2,1)S(1)} %slice.86.small_ref, s32[544,128]{1,0:T(8,128)S(1)} %broadcast_in_dim.10.seg_ref), custom_call_target="tpu_custom_call" | custom-call | flops 17268736 | bytes 1114112 | tf_op jit(solution)/shard_map/pallas_call | solution.py:484
  94.6 3.5 %all-to-all-start.1 = ((bf16[32,32,256]{2,1,0:T(8,128)(2,1)}), bf16[32,32,256]{2,1,0:T(8,128)(2,1)}, u32[]{:S(2)}, u32[]{:S(2)}) async-start(bf16[32,32,256]{2,1,0:T(8,128)(2,1)} %copy-done), calls=%async_computation.1 | async-start | bytes 1048576 | tf_op jit(solution)/shard_map/all_to_all | solution.py:725
  106.6 6.2 %shard_map.178 = (bf16[512,512]{1,0:T(8,128)(2,1)S(1)}, f32[32,256]{1,0:T(8,128)S(1)}) custom-call(f32[512,256]{1,0:T(8,128)S(1)} %copy-done.16, f32[512,256]{1,0:T(8,128)S(1)} %copy-done.14, f32[512,128]{1,0:T(8,128)S(1)} %copy-done.24, f32[544,256]{1,0:T(8,128)S(1)} %get-tuple-element.65.gated_ref, s32[544,128]{1,0:T(8,128)S(1)} %broadcast_in_dim.10.seg_ref, ...), custom_call_target="tpu_custom_call" | custom-call | flops 32505856 | bytes 3145728 | tf_op jit(solution)/shard_map/pallas_call | solution.py:603
  112.9 2.1 %convert_add_fusion.3 = f32[128,1024]{1,0:T(8,128)} fusion(bf16[128,1024]{1,0:T(8,128)(2,1)} %collective-permute-done.26, f32[128,1024]{1,0:T(8,128)S(1)} %copy-done.18, bf16[128,1024]{1,0:T(8,128)(2,1)} %collective-permute-done.24), kind=kLoop, calls=%fused_computation.20 | loop fusion | flops 524288 | bytes 1572864 | tf_op jit(solution)/shard_map/add | solution.py:109
  121.7 1.7 %shard_map.180 = bf16[32,128,128]{2,1,0:T(8,128)(2,1)} custom-call(bf16[512,1024]{1,0:T(8,128)(2,1)S(1)} %get-tuple-element.87.normed_ref.left_ref, bf16[512,512]{1,0:T(8,128)(2,1)S(1)} %copy-done.20), custom_call_target="tpu_custom_call" | custom-call | flops 536870912 | bytes 2621440 | tf_op jit(solution)/shard_map/pallas_call | solution.py:137
  123.5 3.0 %all-to-all-start.2 = ((bf16[32,128,128]{2,1,0:T(8,128)(2,1)}), bf16[32,128,128]{2,1,0:T(8,128)(2,1)S(1)}, u32[]{:S(2)}, u32[]{:S(2)}) async-start(bf16[32,128,128]{2,1,0:T(8,128)(2,1)} %shard_map.180), calls=%async_computation.2 | async-start | bytes 2097152 | tf_op jit(solution)/shard_map/all_to_all | solution.py:739
  126.6 2.5 %collective-permute-done.31 = bf16[128,1024]{1,0:T(8,128)(2,1)S(1)} collective-permute-done((bf16[128,1024]{1,0:T(8,128)(2,1)}, bf16[128,1024]{1,0:T(8,128)(2,1)S(1)}, u32[]{:S(2)}, u32[]{:S(2)}) %collective-permute-start.31) | collective-permute-done | bytes 262176 | tf_op jit(solution)/shard_map/ppermute | solution.py:23
  130.8 1.7 %collective-permute-start.33 = (bf16[144,1024]{1,0:T(8,128)(2,1)S(1)}, bf16[144,1024]{1,0:T(8,128)(2,1)S(1)}, u32[]{:S(2)}, u32[]{:S(2)}) collective-permute-start(bf16[144,1024]{1,0:T(8,128)(2,1)S(1)} %shard_map.181), channel_id=1, source_target_pairs={{0,2},{1,3},{2,0},{3,1},{4,6},{5,7},{6,4},{7,5},{8,10},{9,11},{10,... | collective-permute-start | bytes 884744 | tf_op jit(solution)/shard_map/ppermute | solution.py:23
  133.3 1.8 %convert_reduce_fusion.1 = f32[128,256]{1,0:T(8,128)} fusion(bf16[8,128,256]{2,1,0:T(8,128)(2,1)} %bitcast.67), kind=kLoop, calls=%fused_computation.7 | loop fusion | flops 491520 | bytes 655360 | tf_op jit(solution)/shard_map/reduce_sum | solution.py:741
  135.1 11.0 %collective-permute-done.33 = bf16[144,1024]{1,0:T(8,128)(2,1)S(1)} collective-permute-done((bf16[144,1024]{1,0:T(8,128)(2,1)S(1)}, bf16[144,1024]{1,0:T(8,128)(2,1)S(1)}, u32[]{:S(2)}, u32[]{:S(2)}) %collective-permute-start.33) | collective-permute-done | bytes 294944 | tf_op jit(solution)/shard_map/ppermute | solution.py:23
  148.8 4.0 %all-to-all-done.2 = bf16[32,128,128]{2,1,0:T(8,128)(2,1)S(1)} async-done(((bf16[32,128,128]{2,1,0:T(8,128)(2,1)}), bf16[32,128,128]{2,1,0:T(8,128)(2,1)S(1)}, u32[]{:S(2)}, u32[]{:S(2)}) %all-to-all-start.2) | async-done | bytes 1048608 | tf_op jit(solution)/shard_map/all_to_all | solution.py:739
  152.8 3.7 %all-to-all-start.3 = ((bf16[8,18,1024]{2,1,0:T(8,128)(2,1)}), bf16[8,18,1024]{2,1,0:T(8,128)(2,1)S(1)}, u32[]{:S(2)}, u32[]{:S(2)}) async-start(bf16[8,18,1024]{2,1,0:T(8,128)(2,1)} %fusion.8), calls=%async_computation.3 | async-start | bytes 786432 | tf_op jit(solution)/shard_map/all_to_all | solution.py:773
  158.5 9.8 %all-to-all-done.3 = bf16[8,18,1024]{2,1,0:T(8,128)(2,1)S(1)} async-done(((bf16[8,18,1024]{2,1,0:T(8,128)(2,1)}), bf16[8,18,1024]{2,1,0:T(8,128)(2,1)S(1)}, u32[]{:S(2)}, u32[]{:S(2)}) %all-to-all-start.3) | async-done | bytes 294944 | tf_op jit(solution)/shard_map/all_to_all | solution.py:773
  (195 shorter events, 62.9 us)
Async XLA Ops:
  8.6 9.0 %collective-permute-start.5 = (bf16[48,1152]{1,0:T(8,128)(2,1)S(1)}, bf16[48,1152]{1,0:T(8,128)(2,1)S(1)}, u32[]{:S(2)}, u32[]{:S(2)}) collective-permute-start(bf16[48,1152]{1,0:T(8,128)(2,1)S(1)} %get-tuple-element.57.refs_0_), channel_id=1, source_target_pairs={{0,24},{4,28},{8,16},{12,20},{16,8},{20,12},{24,0},{28,4},{1,25},{... | collective-permute-start | bytes 331784 | tf_op jit(solution)/shard_map/ppermute | solution.py:23
  13.6 9.3 %collective-permute-start.4 = (bf16[48,1152]{1,0:T(8,128)(2,1)S(1)}, bf16[48,1152]{1,0:T(8,128)(2,1)S(1)}, u32[]{:S(2)}, u32[]{:S(2)}) collective-permute-start(bf16[48,1152]{1,0:T(8,128)(2,1)S(1)} %get-tuple-element.57.refs_0_), channel_id=1, source_target_pairs={{0,16},{4,20},{8,24},{12,28},{16,0},{20,4},{24,8},{28,12},{1,17},{... | collective-permute-start | bytes 331784 | tf_op jit(solution)/shard_map/ppermute | solution.py:23
  13.6 9.3 %collective-permute-start.3 = (bf16[48,1152]{1,0:T(8,128)(2,1)S(1)}, bf16[48,1152]{1,0:T(8,128)(2,1)S(1)}, u32[]{:S(2)}, u32[]{:S(2)}) collective-permute-start(bf16[48,1152]{1,0:T(8,128)(2,1)S(1)} %get-tuple-element.57.refs_0_), channel_id=1, source_target_pairs={{0,8},{4,12},{8,0},{12,4},{16,24},{20,28},{24,16},{28,20},{1,9},{5... | collective-permute-start | bytes 331784 | tf_op jit(solution)/shard_map/ppermute | solution.py:23
  23.0 27.7 %collective-permute-start.6 = (bf16[4,48,1152]{2,1,0:T(8,128)(2,1)S(1)}, bf16[4,48,1152]{2,1,0:T(8,128)(2,1)S(1)}, u32[]{:S(2)}, u32[]{:S(2)}) collective-permute-start(bf16[4,48,1152]{2,1,0:T(8,128)(2,1)S(1)} %shard_map.165.refs_0_), channel_id=1, source_target_pairs={{0,4},{4,0},{8,12},{12,8},{16,20},{20,16},{24,28},{28,24},{1,5},{5... | collective-permute-start | bytes 1327112 | tf_op jit(solution)/shard_map/ppermute | solution.py:23
  24.6 28.3 %all-to-all-start = ((bf16[8,8,2176]{2,1,0:T(8,128)(2,1)}), bf16[8,8,2176]{2,1,0:T(8,128)(2,1)S(1)}, u32[]{:S(2)}, u32[]{:S(2)}) async-start(bf16[8,8,2176]{2,1,0:T(8,128)(2,1)} %bitcast.3), calls=%async_computation | async-start | bytes 557056 | tf_op jit(solution)/shard_map/all_to_all | solution.py:700
  33.4 8.3 %collective-permute-start.15 = (bf16[128,512]{1,0:T(8,128)(2,1)S(1)}, bf16[128,512]{1,0:T(8,128)(2,1)S(1)}, u32[]{:S(2)}, u32[]{:S(2)}) collective-permute-start(bf16[128,512]{1,0:T(8,128)(2,1)S(1)} %bitcast.83), channel_id=1, source_target_pairs={{0,24},{4,28},{8,16},{12,20},{16,8},{20,12},{24,0},{28,4},{1,25},{... | collective-permute-start | bytes 393224 | tf_op jit(solution)/shard_map/ppermute | solution.py:23
  37.2 11.9 %collective-permute-start.14 = (bf16[128,512]{1,0:T(8,128)(2,1)S(1)}, bf16[128,512]{1,0:T(8,128)(2,1)S(1)}, u32[]{:S(2)}, u32[]{:S(2)}) collective-permute-start(bf16[128,512]{1,0:T(8,128)(2,1)S(1)} %bitcast.84), channel_id=1, source_target_pairs={{0,16},{4,20},{8,24},{12,28},{16,0},{20,4},{24,8},{28,12},{1,17},{... | collective-permute-start | bytes 393224 | tf_op jit(solution)/shard_map/ppermute | solution.py:23
  37.2 11.9 %collective-permute-start.13 = (bf16[128,512]{1,0:T(8,128)(2,1)S(1)}, bf16[128,512]{1,0:T(8,128)(2,1)S(1)}, u32[]{:S(2)}, u32[]{:S(2)}) collective-permute-start(bf16[128,512]{1,0:T(8,128)(2,1)S(1)} %bitcast.85), channel_id=1, source_target_pairs={{0,8},{4,12},{8,0},{12,4},{16,24},{20,28},{24,16},{28,20},{1,9},{5... | collective-permute-start | bytes 393224 | tf_op jit(solution)/shard_map/ppermute | solution.py:23
  49.2 19.5 %collective-permute-start.16 = (bf16[4,128,512]{2,1,0:T(8,128)(2,1)S(1)}, bf16[4,128,512]{2,1,0:T(8,128)(2,1)S(1)}, u32[]{:S(2)}, u32[]{:S(2)}) collective-permute-start(bf16[4,128,512]{2,1,0:T(8,128)(2,1)S(1)} %shard_map.170.refs_0_), channel_id=1, source_target_pairs={{0,4},{4,0},{8,12},{12,8},{16,20},{20,16},{24,28},{28,24},{1,5},{5... | collective-permute-start | bytes 1572872 | tf_op jit(solution)/shard_map/ppermute | solution.py:23
  50.8 16.8 %collective-permute-start.8 = (bf16[8,16,1152]{2,1,0:T(8,128)(2,1)S(1)}, bf16[8,16,1152]{2,1,0:T(8,128)(2,1)S(1)}, u32[]{:S(2)}, u32[]{:S(2)}) collective-permute-start(bf16[8,16,1152]{2,1,0:T(8,128)(2,1)S(1)} %bitcast.87), channel_id=1, source_target_pairs={{0,2},{1,3},{2,0},{3,1},{4,6},{5,7},{6,4},{7,5},{8,10},{9,11},{10,... | collective-permute-start | bytes 884744 | tf_op jit(solution)/shard_map/ppermute | solution.py:23
  51.7 16.5 %collective-permute-start.18 = (bf16[128,1024]{1,0:T(8,128)(2,1)S(1)}, bf16[128,1024]{1,0:T(8,128)(2,1)}, u32[]{:S(2)}, u32[]{:S(2)}) collective-permute-start(bf16[128,1024]{1,0:T(8,128)(2,1)S(1)} %bitcast.76), channel_id=1, source_target_pairs={{0,2},{1,3},{2,0},{3,1},{4,6},{5,7},{6,4},{7,5},{8,10},{9,11},{10,... | collective-permute-start | bytes 786440 | tf_op jit(solution)/shard_map/ppermute | solution.py:23
  53.2 14.3 %collective-permute-start.1 = (bf16[128,512]{1,0:T(8,128)(2,1)S(1)}, bf16[128,512]{1,0:T(8,128)(2,1)S(1)}, u32[]{:S(2)}, u32[]{:S(2)}) collective-permute-start(bf16[128,512]{1,0:T(8,128)(2,1)S(1)} %shard_map.163.refs_0_), channel_id=1, source_target_pairs={{0,2},{1,3},{2,0},{3,1},{4,6},{5,7},{6,4},{7,5},{8,10},{9,11},{10,... | collective-permute-start | bytes 393224 | tf_op jit(solution)/shard_map/ppermute | solution.py:23
  54.2 13.9 %collective-permute-start = (bf16[128,512]{1,0:T(8,128)(2,1)S(1)}, bf16[128,512]{1,0:T(8,128)(2,1)S(1)}, u32[]{:S(2)}, u32[]{:S(2)}) collective-permute-start(bf16[128,512]{1,0:T(8,128)(2,1)S(1)} %shard_map.163.refs_0_), channel_id=1, source_target_pairs={{0,1},{1,0},{2,3},{3,2},{4,5},{5,4},{6,7},{7,6},{8,9},{9,8},{10,11... | collective-permute-start | bytes 393224 | tf_op jit(solution)/shard_map/ppermute | solution.py:23
  88.5 24.3 %collective-permute-start.24 = (bf16[128,1024]{1,0:T(8,128)(2,1)}, bf16[128,1024]{1,0:T(8,128)(2,1)}, u32[]{:S(2)}, u32[]{:S(2)}) collective-permute-start(bf16[128,1024]{1,0:T(8,128)(2,1)} %get-tuple-element.102), channel_id=1, source_target_pairs={{0,1},{1,0},{2,3},{3,2},{4,5},{5,4},{6,7},{7,6},{8,9},{9,8},{10,11... | collective-permute-start | bytes 786440 | tf_op jit(solution)/shard_map/ppermute | solution.py:23
  90.6 22.2 %collective-permute-start.26 = (bf16[128,1024]{1,0:T(8,128)(2,1)}, bf16[128,1024]{1,0:T(8,128)(2,1)}, u32[]{:S(2)}, u32[]{:S(2)}) collective-permute-start(bf16[128,1024]{1,0:T(8,128)(2,1)} %fusion.5), channel_id=1, source_target_pairs={{0,2},{1,3},{2,0},{3,1},{4,6},{5,7},{6,4},{7,5},{8,10},{9,11},{10,... | collective-permute-start | bytes 786440 | tf_op jit(solution)/shard_map/ppermute | solution.py:23
  91.8 7.0 %collective-permute-start.28 = (f32[8,512]{1,0:T(8,128)S(1)}, f32[8,512]{1,0:T(8,128)S(1)}, u32[]{:S(2)}, u32[]{:S(2)}) collective-permute-start(f32[8,512]{1,0:T(8,128)S(1)} %get-tuple-element.72.refs_0_), channel_id=1, source_target_pairs={{0,3},{1,2},{2,1},{3,0},{4,7},{5,6},{6,5},{7,4},{8,11},{9,10},{10,... | collective-permute-start | bytes 49160 | tf_op jit(solution)/shard_map/ppermute | solution.py:23
  92.2 7.8 %collective-permute-start.27 = (f32[8,512]{1,0:T(8,128)S(1)}, f32[8,512]{1,0:T(8,128)S(1)}, u32[]{:S(2)}, u32[]{:S(2)}) collective-permute-start(f32[8,512]{1,0:T(8,128)S(1)} %get-tuple-element.72.refs_0_), channel_id=1, source_target_pairs={{0,2},{1,3},{2,0},{3,1},{4,6},{5,7},{6,4},{7,5},{8,10},{9,11},{10,... | collective-permute-start | bytes 49160 | tf_op jit(solution)/shard_map/ppermute | solution.py:23
  94.6 27.1 %all-to-all-start.1 = ((bf16[32,32,256]{2,1,0:T(8,128)(2,1)}), bf16[32,32,256]{2,1,0:T(8,128)(2,1)}, u32[]{:S(2)}, u32[]{:S(2)}) async-start(bf16[32,32,256]{2,1,0:T(8,128)(2,1)} %copy-done), calls=%async_computation.1 | async-start | bytes 1048576 | tf_op jit(solution)/shard_map/all_to_all | solution.py:725
  118.0 8.6 %collective-permute-start.29 = (bf16[128,1024]{1,0:T(8,128)(2,1)}, bf16[128,1024]{1,0:T(8,128)(2,1)}, u32[]{:S(2)}, u32[]{:S(2)}) collective-permute-start(bf16[128,1024]{1,0:T(8,128)(2,1)} %get-tuple-element.100), channel_id=1, source_target_pairs={{0,1},{1,0},{2,3},{3,2},{4,5},{5,4},{6,7},{7,6},{8,9},{9,8},{10,11... | collective-permute-start | bytes 786440 | tf_op jit(solution)/shard_map/ppermute | solution.py:23
  120.6 8.6 %collective-permute-start.31 = (bf16[128,1024]{1,0:T(8,128)(2,1)}, bf16[128,1024]{1,0:T(8,128)(2,1)S(1)}, u32[]{:S(2)}, u32[]{:S(2)}) collective-permute-start(bf16[128,1024]{1,0:T(8,128)(2,1)} %fusion.4), channel_id=1, source_target_pairs={{0,2},{1,3},{2,0},{3,1},{4,6},{5,7},{6,4},{7,5},{8,10},{9,11},{10,... | collective-permute-start | bytes 786440 | tf_op jit(solution)/shard_map/ppermute | solution.py:23
  123.5 29.3 %all-to-all-start.2 = ((bf16[32,128,128]{2,1,0:T(8,128)(2,1)}), bf16[32,128,128]{2,1,0:T(8,128)(2,1)S(1)}, u32[]{:S(2)}, u32[]{:S(2)}) async-start(bf16[32,128,128]{2,1,0:T(8,128)(2,1)} %shard_map.180), calls=%async_computation.2 | async-start | bytes 2097152 | tf_op jit(solution)/shard_map/all_to_all | solution.py:739
  130.8 15.2 %collective-permute-start.33 = (bf16[144,1024]{1,0:T(8,128)(2,1)S(1)}, bf16[144,1024]{1,0:T(8,128)(2,1)S(1)}, u32[]{:S(2)}, u32[]{:S(2)}) collective-permute-start(bf16[144,1024]{1,0:T(8,128)(2,1)S(1)} %shard_map.181), channel_id=1, source_target_pairs={{0,2},{1,3},{2,0},{3,1},{4,6},{5,7},{6,4},{7,5},{8,10},{9,11},{10,... | collective-permute-start | bytes 884744 | tf_op jit(solution)/shard_map/ppermute | solution.py:23
  133.2 13.2 %collective-permute-start.32 = (bf16[144,1024]{1,0:T(8,128)(2,1)S(1)}, bf16[144,1024]{1,0:T(8,128)(2,1)S(1)}, u32[]{:S(2)}, u32[]{:S(2)}) collective-permute-start(bf16[144,1024]{1,0:T(8,128)(2,1)S(1)} %shard_map.181), channel_id=1, source_target_pairs={{0,1},{1,0},{2,3},{3,2},{4,5},{5,4},{6,7},{7,6},{8,9},{9,8},{10,11... | collective-permute-start | bytes 884744 | tf_op jit(solution)/shard_map/ppermute | solution.py:23
  152.8 15.6 %all-to-all-start.3 = ((bf16[8,18,1024]{2,1,0:T(8,128)(2,1)}), bf16[8,18,1024]{2,1,0:T(8,128)(2,1)S(1)}, u32[]{:S(2)}, u32[]{:S(2)}) async-start(bf16[8,18,1024]{2,1,0:T(8,128)(2,1)} %fusion.8), calls=%async_computation.3 | async-start | bytes 786432 | tf_op jit(solution)/shard_map/all_to_all | solution.py:773
  (55 other events, 198.5 us)

commit v3 on v2

--- a/solution.py
+++ b/solution.py
@@ -23,7 +23,7 @@
     return lax.ppermute(value, axis, [(i, i ^ mask) for i in range(size)])
 
 
-VMEM_LIMIT = 48 << 20
+VMEM_LIMIT = 16 << 20
 
 
 def kernel_params():
@@ -62,9 +62,9 @@
     return place_parts(parts, axis, stride, size, dim)
 
 
-def gather(value, axis, chains):
-    shape = value.shape
-    for dim, (stride, size) in enumerate(chains):
+def gather_rest(value, axis, chains):
+    shape = value.shape[1:]
+    for dim, (stride, size) in enumerate(chains[1:], 1):
         value = gather_stage(value, axis, stride, size, dim)
     return value.reshape((-1,) + shape)
 
@@ -74,7 +74,7 @@
     width = right.shape[0] if transposed else right.shape[1]
     dims = (((1,), (1 if transposed else 0,)), ((), ()))
 
-    def kernel(left_ref, right_ref, own, others):
+    def kernel(left_ref, right_ref, own, *others):
         place = lax.axis_index(axis)
         for k in range(count):
             start = pl.multiple_of((place ^ k) * block, block)
@@ -84,14 +84,12 @@
             if k == 0:
                 own[...] = term
             else:
-                others[k - 1] = term.astype(BF16)
-
-    return pl.pallas_call(
-        kernel,
-        out_shape=(
-            jax.ShapeDtypeStruct((block, width), F32),
-            jax.ShapeDtypeStruct((count - 1, block, width), BF16),
-        ),
+                others[k - 1][...] = term.astype(BF16)
+
+    return pl.pallas_call(
+        kernel,
+        out_shape=[jax.ShapeDtypeStruct((block, width), F32)]
+        + [jax.ShapeDtypeStruct((block, width), BF16)] * (count - 1),
         compiler_params=kernel_params(),
         cost_estimate=pl.CostEstimate(
             flops=2 * left.size * width,
@@ -101,15 +99,173 @@
     )(left, right)
 
 
-def block_sum(own, others, axis, chains):
+def block_sum(others, axis, chains, first=None):
     if list(chains) == [(2, 2), (1, 2)]:
-        near = swap(others[0], axis, 1)
-        passed = swap(others[2], axis, 1)
-        far = swap((others[1].astype(F32) + passed.astype(F32)).astype(BF16), axis, 2)
-        return own + near.astype(F32) + far.astype(F32)
-    for k in range(others.shape[0]):
-        own = own + swap(others[k], axis, k + 1).astype(F32)
-    return own
+        near, passed = swap(others[0], axis, 1), swap(others[2], axis, 1)
+        passed = add_pair(others[1], passed)
+        if first is not None:
+            passed = after(passed, first)
+        return swap(passed, axis, 2), [near], passed
+    parts = [swap(other, axis, k) for k, other in enumerate(others, 1)]
+    return parts[-1], parts[:-1], others[-1]
+
+
+def add_pair(one, other):
+    def kernel(one_ref, other_ref, out):
+        out[...] = (one_ref[...].astype(F32) + other_ref[...].astype(F32)).astype(BF16)
+
+    return pl.pallas_call(
+        kernel,
+        out_shape=jax.ShapeDtypeStruct(one.shape, BF16),
+        compiler_params=kernel_params(),
+        cost_estimate=costs(one.size, 6 * one.size),
+    )(one, other)
+
+
+def finish_rows(stem_pre, own, parts):
+    def kernel(pre_ref, own_ref, *refs):
+        total = own_ref[...]
+        for part in refs[:-1]:
+            total = total + part[...].astype(F32)
+        pre = pre_ref[...]
+        stem_out = (pre * jax.nn.sigmoid(pre)).astype(BF16).astype(F32)
+        refs[-1][...] = (stem_out + total).astype(BF16)
+
+    return pl.pallas_call(
+        kernel,
+        out_shape=jax.ShapeDtypeStruct(own.shape, BF16),
+        compiler_params=kernel_params(),
+        cost_estimate=costs(8 * own.size, 14 * own.size),
+    )(stem_pre, own, *parts)
+
+
+def part_terms(left, right, axis, chains):
+    total = lax.axis_size(axis)
+    stride, size = chains[-1]
+    rows, columns = left.shape[1] // total, right.shape[1]
+    step = max(1, 128 // rows)
+
+    def kernel(left_ref, right_ref, *outs):
+        place = (lax.axis_index(axis) // stride) % size
+        for i in range(0, total, step):
+            term = lax.dot_general(
+                left_ref[:, i * rows : (i + step) * rows],
+                right_ref[...],
+                (((0,), (0,)), ((), ())),
+                preferred_element_type=F32,
+            ).astype(BF16)
+            for n in range(step):
+                for k in range(size):
+
+                    @pl.when((i + n) % size ^ place == k)
+                    def _():
+                        outs[k][(i + n) // size] = term[n * rows : (n + 1) * rows]
+
+    return pl.pallas_call(
+        kernel,
+        out_shape=[jax.ShapeDtypeStruct((total // size, rows, columns), BF16)] * size,
+        compiler_params=kernel_params(),
+        cost_estimate=costs(
+            2 * left.size * columns, 2 * (left.size + right.size + left.shape[1] * columns)
+        ),
+    )(left, right)
+
+
+def add_parts(parts, axis, chain):
+    stride, size = chain
+    shape = (parts[0].shape[0] // size,) + parts[0].shape[1:]
+
+    def kernel(*refs):
+        place = (lax.axis_index(axis) // stride) % size
+        for a in range(shape[0]):
+            for k in range(size):
+                at = a * size + (place ^ k)
+                total = sum(part[at].astype(F32) for part in refs[: len(parts)])
+                refs[len(parts) + k][a] = total.astype(BF16)
+
+    return pl.pallas_call(
+        kernel,
+        out_shape=[jax.ShapeDtypeStruct(shape, BF16)] * size,
+        compiler_params=kernel_params(),
+        cost_estimate=costs(len(parts) * parts[0].size, 4 * len(parts) * parts[0].size),
+    )(*parts)
+
+
+def swap_parts(parts, axis, chain):
+    stride, _ = chain
+    return [parts[0]] + [swap(part, axis, k * stride) for k, part in enumerate(parts[1:], 1)]
+
+
+def reduce_parts(parts, axis, chains):
+    parts = swap_parts(parts, axis, chains[-1])
+    for chain in reversed(chains[:-1]):
+        parts = swap_parts(add_parts(parts, axis, chain), axis, chain)
+    return parts
+
+
+def cut_columns(parts, axis):
+    count = lax.axis_size(axis)
+    rows, columns = parts[0].shape[1:]
+    share = columns // count
+
+    def kernel(*refs):
+        place = lax.axis_index(axis)
+        total = sum(part[0].astype(F32) for part in refs[: len(parts)]).astype(BF16)
+        for j in range(count):
+            for k in range(count):
+
+                @pl.when(place ^ j == k)
+                def _():
+                    refs[len(parts) + k][...] = total[:, j * share : (j + 1) * share]
+
+    return pl.pallas_call(
+        kernel,
+        out_shape=[jax.ShapeDtypeStruct((rows, share), BF16)] * count,
+        compiler_params=kernel_params(),
+        cost_estimate=costs(len(parts) * parts[0].size, 4 * len(parts) * parts[0].size),
+    )(*parts)
+
+
+def stack_rows(parts, axis):
+    count = len(parts)
+    rows, columns = parts[0].shape
+
+    def kernel(*refs):
+        place = lax.axis_index(axis)
+        for k in range(count):
+            start = pl.multiple_of((place ^ k) * rows, rows)
+            refs[count][pl.ds(start, rows), :] = refs[k][...].astype(F32)
+
+    return pl.pallas_call(
+        kernel,
+        out_shape=jax.ShapeDtypeStruct((count * rows, columns), F32),
+        compiler_params=kernel_params(),
+        cost_estimate=costs(0, 6 * count * parts[0].size),
+    )(*parts)
+
+
+def mix_columns(parts, axis, small):
+    count = len(parts)
+    rows = parts[0].shape[0]
+    span = 128 * count
+
+    def kernel(*refs):
+        place = lax.axis_index(axis)
+        at = lax.broadcasted_iota(jnp.int32, (128, span), 0)
+        to = lax.broadcasted_iota(jnp.int32, (128, span), 1)
+        total = jnp.zeros((rows, span), F32)
+        for k in range(count):
+            want = at // small * (small * count) + (place ^ k) * small + at % small
+            spread = jnp.where(to == want, 1.0, 0.0).astype(BF16)
+            total = total + jnp.dot(refs[k][...], spread, preferred_element_type=F32)
+        refs[count][...] = total
+
+    return pl.pallas_call(
+        kernel,
+        out_shape=jax.ShapeDtypeStruct((rows, span), F32),
+        compiler_params=kernel_params(),
+        cost_estimate=costs(2 * rows * span * span, 8 * rows * span),
+    )(*parts)
 
 
 def message_terms(left, right, parts, sides):
@@ -183,14 +339,17 @@
     )(weight)
 
 
-def stem_backward(grad_normed, stem_pre, grad_out, gain, extra):
-    block, channels = grad_normed.shape
-
-    def kernel(grad_ref, pre_ref, out_grad_ref, gain_ref, out):
+def stem_backward(own, parts, stem_pre, grad_out, gain, extra):
+    block, channels = own.shape
+
+    def kernel(own_ref, pre_ref, out_grad_ref, gain_ref, *refs):
+        out = refs[-1]
         pre = pre_ref[...]
         sigma = jax.nn.sigmoid(pre)
         hat, inverse = standardize((pre * sigma).astype(BF16).astype(F32))
-        grad = grad_ref[...]
+        grad = own_ref[...]
+        for part in refs[:-1]:
+            grad = grad + part[...].astype(F32)
         out[block:, :] = jnp.concatenate(
             [jnp.sum(grad * hat, axis=0, keepdims=True), jnp.zeros((extra - 1, channels), F32)]
         ).astype(BF16)
@@ -205,9 +364,9 @@
         out_shape=jax.ShapeDtypeStruct((block + extra, channels), BF16),
         compiler_params=kernel_params(),
         cost_estimate=pl.CostEstimate(
-            flops=30 * grad_normed.size, bytes_accessed=12 * grad_normed.size, transcendentals=0
+            flops=30 * own.size, bytes_accessed=14 * own.size, transcendentals=0
         ),
-    )(grad_normed, stem_pre, grad_out, gain)
+    )(own, stem_pre, grad_out, gain, *parts)
 
 
 def standardize(values):
@@ -230,19 +389,24 @@
 def split_parts(parts, axis, stride, size, dim, cut):
     shape = parts[0].shape
     lead = shape[:dim] + (size,) + shape[dim:-2]
-    rows = (cut, shape[-2] - cut)
+    rows, width = shape[-2:]
+    chunks = (width - cut) // 128
 
     def kernel(*refs):
         place = (lax.axis_index(axis) // stride) % size
         for k in range(size):
             target = (slice(None),) * dim + (place ^ k,)
-            refs[size][target] = refs[k][..., :cut, :]
-            refs[size + 1][target] = refs[k][..., cut:, :]
+            refs[size][target] = refs[k][..., :cut]
+            for q in range(chunks):
+                inner = (slice(None),) * (len(lead) - dim - 1) + (q,)
+                lanes = slice(cut + q * 128, cut + (q + 1) * 128)
+                refs[size + 1][target + inner] = refs[k][..., lanes]
 
     return pl.pallas_call(
         kernel,
         out_shape=[
-            jax.ShapeDtypeStruct(lead + (count, shape[-1]), parts[0].dtype) for count in rows
+            jax.ShapeDtypeStruct(lead + (rows, cut), parts[0].dtype),
+            jax.ShapeDtypeStruct(lead + (chunks, rows, 128), parts[0].dtype),
         ],
         compiler_params=kernel_params(),
         cost_estimate=costs(0, 4 * size * parts[0].size),
@@ -253,41 +417,51 @@
     for dim, (stride, size) in enumerate(chains):
         parts = [value] + [swap(value, axis, k * stride) for k in range(1, size)]
         if dim == len(chains) - 1:
-            upper, lower = split_parts(parts, axis, stride, size, dim, cut)
+            left, beyond = split_parts(parts, axis, stride, size, dim, cut)
         else:
             value = place_parts(parts, axis, stride, size, dim)
-    return (
-        upper.reshape((-1,) + upper.shape[-2:]),
-        lower.reshape((-1, lower.shape[-1])),
-    )
-
-
-def prepare(mel, owner, slot, stem, up, down, taps, gain_one, gain_two, dp_count, tm_count):
+    return left.reshape((-1,) + left.shape[-2:]), beyond.reshape(-1, 128)
+
+
+def prepare(mel, owner, slot, stem, up, taps, gain_one, gain_two, dp_count, tm_count):
     pieces, values = mel.shape
     capacity = max(2, 2 * pieces // dp_count)
     slots = dp_count * capacity
     stem_rows, channels = stem.shape
-    rows = down.shape[0]
-    tap_count = taps.shape[1]
+    rows, tap_count = taps.shape
+    chunks = rows // stem_rows
     span = 128 * tm_count
     groups = up.shape[1] // span
-
-    def kernel(
-        mel_ref, owner_ref, slot_ref, stem_ref, up_ref, down_ref, taps_ref, one_ref, two_ref,
-        sent, pack, *up_parts
-    ):
+    inputs = (
+        up, stem, taps, gain_one[None, :], gain_two[None, :], owner[None, :], slot[None, :], mel
+    )
+    count = len(inputs)
+
+    def kernel(*refs):
+        sent, pack, *up_parts = refs[count : count + 2 + tm_count]
+        held = refs[count + 2 + tm_count : -1]
+        copies = [
+            pltpu.make_async_copy(refs[k], held[k], refs[-1].at[k]) for k in range(count)
+        ]
+        for copy in copies:
+            copy.start()
+        up_ref, stem_ref, taps_ref, one_ref, two_ref, owner_ref, slot_ref, mel_ref = held
+
         def iota(shape, dim):
             return lax.broadcasted_iota(jnp.int32, shape, dim)
 
         def table(flags):
             return jnp.where(flags, 1.0, 0.0).astype(BF16)
 
-        pack[:stem_rows, :channels] = stem_ref[...]
-        pack[stem_rows:, :channels] = down_ref[...]
+        for copy in copies:
+            copy.wait()
+        pack[:, :channels] = stem_ref[...]
         lane = iota((rows, 128), 1)
         spread = table(lane % rows == iota((rows, 128), 0))
         gain = jnp.broadcast_to(one_ref[...].astype(F32), (stem_rows, rows)).astype(BF16)
-        pack[:stem_rows, channels:] = jnp.dot(gain, spread, preferred_element_type=F32).astype(BF16)
+        pack[:, channels : channels + 128] = jnp.dot(
+            gain, spread, preferred_element_type=F32
+        ).astype(BF16)
         tap_lane = table(iota((tap_count, 128), 1) == iota((tap_count, 128), 0))
         square = iota((rows, rows), 0) == iota((rows, rows), 1)
         diagonal = jnp.where(
@@ -295,7 +469,9 @@
         ).astype(BF16)
         small = jnp.dot(taps_ref[...], tap_lane, preferred_element_type=F32)
         small = small + jnp.dot(diagonal, table(lane == tap_count), preferred_element_type=F32)
-        pack[stem_rows:, channels:] = small.astype(BF16)
+        for q in range(chunks):
+            lanes = slice(channels + 128 * (q + 1), channels + 128 * (q + 2))
+            pack[:, lanes] = small[q * stem_rows : (q + 1) * stem_rows].astype(BF16)
 
         place = lax.axis_index("tm")
         at = iota((span, 128), 0)
@@ -324,15 +500,14 @@
         kernel,
         out_shape=[
             jax.ShapeDtypeStruct((slots, values + 128), BF16),
-            jax.ShapeDtypeStruct((stem_rows + rows, channels + 128), BF16),
+            jax.ShapeDtypeStruct((stem_rows, channels + 128 * (chunks + 1)), BF16),
         ]
         + [jax.ShapeDtypeStruct((rows, up.shape[1] // tm_count), BF16)] * tm_count,
-        compiler_params=kernel_params(),
+        in_specs=[pl.BlockSpec(memory_space=pl.ANY)] * count,
+        scratch_shapes=[pltpu.VMEM(value.shape, value.dtype) for value in inputs]
+        + [pltpu.SemaphoreType.DMA((count,))],
         cost_estimate=costs(1 << 27, 2 << 20),
-    )(
-        mel, owner[None, :], slot[None, :], stem, up, down, taps, gain_one[None, :],
-        gain_two[None, :],
-    )
+    )(*inputs)
     return outs[0], outs[1], list(outs[2:])
 
 
@@ -360,15 +535,34 @@
     )(arrived)
 
 
-def stem_forward(frames, stem_all, count, axis, rows):
+def stem_forward(frames, stem_all, count, axis, rows, extra):
     length = frames.shape[0]
     features, width = stem_all.shape
     channels = width - 128
     block = length // count
     stem_rows = features * rows // channels
-
-    def kernel(frames_ref, stem_ref, normed, pre_own, gain_out):
+    share = features // count
+
+    def kernel(frames_ref, stem_ref, normed, pre_own, gain_out, turned):
         place = lax.axis_index(axis)
+        feature = lax.broadcasted_iota(jnp.int32, (features, share), 0)
+        chosen = lax.broadcasted_iota(jnp.int32, (features, share), 1)
+        chosen = (chosen // stem_rows * count + place) * stem_rows + chosen % stem_rows
+        pick = jnp.where(feature == chosen, 1.0, 0.0).astype(BF16)
+        corner = lax.broadcasted_iota(jnp.int32, (extra, extra), 0)
+        corner = corner + lax.broadcasted_iota(jnp.int32, (extra, extra), 1)
+        corner = jnp.where(corner == 0, 1.0, 0.0).astype(BF16)
+        for k in range(count):
+            start = pl.multiple_of((place ^ k) * block, block)
+            turned[k, :share, :block] = lax.dot_general(
+                pick,
+                frames_ref[pl.ds(start, block), :],
+                (((0,), (1,)), ((), ())),
+                preferred_element_type=F32,
+            ).astype(BF16)
+            turned[k, share:, :block] = jnp.zeros((extra, block), BF16)
+            turned[k, :share, block:] = jnp.zeros((share, extra), BF16)
+            turned[k, share:, block:] = corner
         beside = stem_ref[:, channels:].astype(F32)
         gains = []
         for g in range(channels // 128):
@@ -399,6 +593,7 @@
             jax.ShapeDtypeStruct((length, channels), BF16),
             jax.ShapeDtypeStruct((block, channels), F32),
             jax.ShapeDtypeStruct((1, channels), F32),
+            jax.ShapeDtypeStruct((count, share + extra, block + extra), BF16),
         ],
         compiler_params=kernel_params(),
         cost_estimate=costs(2 * frames.size * channels, 2 * stem_all.size + 4 * frames.size),
@@ -618,6 +813,88 @@
     )(grad_hat, hat, inverse, gated, segments, linear, gate, turned, gain_term, *sums)
 
 
+def stem_message(turned, parts, small, axis, chains, stem_rows):
+    dp_count = lax.axis_size(axis)
+    stride, size = chains[-1]
+    count, share, width = turned.shape
+    channels = parts[0].shape[1]
+    rows = dp_count * stem_rows
+    own = channels // dp_count
+    height = stem_rows + 8
+
+    def kernel(turned_ref, small_ref, *refs):
+        outs = refs[count:]
+        place = (lax.axis_index(axis) // stride) % size
+        total = jnp.zeros((share, channels), F32)
+        for k in range(count):
+            total = total + jnp.dot(turned_ref[k], refs[k][...], preferred_element_type=F32)
+        for i in range(dp_count):
+            gain = jnp.concatenate(
+                [total[rows : rows + 1, i * own : (i + 1) * own], jnp.zeros((1, channels - own), F32)],
+                axis=1,
+            )
+            block = jnp.concatenate(
+                [
+                    total[i * stem_rows : (i + 1) * stem_rows],
+                    small_ref[i : i + 1, :],
+                    gain,
+                    jnp.zeros((6, channels), F32),
+                ],
+                axis=0,
+            ).astype(BF16)
+            for k in range(size):
+
+                @pl.when(i % size ^ place == k)
+                def _():
+                    outs[k][i // size] = block
+
+    return pl.pallas_call(
+        kernel,
+        out_shape=[jax.ShapeDtypeStruct((dp_count // size, height, channels), BF16)] * size,
+        compiler_params=kernel_params(),
+        cost_estimate=costs(2 * turned.size * channels, 4 * count * width * channels),
+    )(turned, small, *parts)
+
+
+def stem_finish(parts, stem_rows, rows, taps, axis):
+    channels = parts[0].shape[2]
+    count = len(parts)
+
+    def kernel(*refs):
+        stem, kernel_out, post, pre = refs[count:]
+        total = sum(jnp.sum(part[...].astype(F32), axis=0) for part in refs[:count])
+        stem[...] = total[:stem_rows]
+        lane = lax.broadcasted_iota(jnp.int32, (taps + 1, channels), 1)
+        tap = lax.broadcasted_iota(jnp.int32, (taps + 1, channels), 0)
+        spread = jnp.where(lane // rows == tap, total[stem_rows : stem_rows + 1], 0.0)
+        at = lax.broadcasted_iota(jnp.int32, (channels, rows), 0)
+        to = lax.broadcasted_iota(jnp.int32, (channels, rows), 1)
+        fold = jnp.where(at % rows == to, 1.0, 0.0)
+        table = jnp.dot(
+            spread, fold, preferred_element_type=F32, precision=lax.Precision.HIGHEST
+        )
+        kernel_out[...] = table.T[:, :taps]
+        post[...] = table[taps : taps + 1]
+        mine = lax.axis_index(axis) * rows
+        own = jnp.where(at == to + mine, 1.0, 0.0)
+        line = jnp.broadcast_to(total[stem_rows + 1 : stem_rows + 2], (8, channels))
+        pre[...] = jnp.dot(
+            line, own, preferred_element_type=F32, precision=lax.Precision.HIGHEST
+        )[:1]
+
+    return pl.pallas_call(
+        kernel,
+        out_shape=[
+            jax.ShapeDtypeStruct((stem_rows, channels), F32),
+            jax.ShapeDtypeStruct((rows, taps), F32),
+            jax.ShapeDtypeStruct((1, rows), F32),
+            jax.ShapeDtypeStruct((1, rows), F32),
+        ],
+        compiler_params=kernel_params(),
+        cost_estimate=costs(1 << 24, 2 * count * parts[0].size),
+    )(*parts)
+
+
 def one_hot(rows, columns):
     return (rows[:, None] == columns[None, :]).astype(BF16)
 
@@ -668,8 +945,8 @@
     grouped = (lane // rows) % tm_count * 128 + lane // (rows * tm_count) * rows + lane % rows
     if stem_rows % 16 == 0 and rows % 16 == 0:
         sent, pack, up_parts = prepare(
-            mel_pieces[0], dest_owner[0], dest_slot[0], stem_weight, up_weight, down_weight,
-            depth_kernel, gain_pre, gain_post, dp_count, tm_count,
+            mel_pieces[0], dest_owner[0], dest_slot[0], stem_weight, up_weight, depth_kernel,
+            gain_pre, gain_post, dp_count, tm_count,
         )
     else:
         sent = order_pieces(mel_pieces[0], dest_owner[0], dest_slot[0], dp_count)
@@ -678,38 +955,38 @@
         small = jnp.concatenate(
             [depth_kernel, gain_post[:, None], jnp.zeros((rows, 128 - taps - 1), BF16)], axis=1
         )
-        pack = jnp.concatenate(
-            [
-                jnp.concatenate([stem_weight, beside], axis=1),
-                jnp.concatenate([down_weight, small], axis=1),
-            ]
-        )
-
+        small = [small[q : q + stem_rows] for q in range(0, rows, stem_rows)]
+        pack = jnp.concatenate([stem_weight, beside] + small, axis=1)
+
+    stem_mine, small_all = split_gather(pack, "dp", dp_chains, channels + 128)
     up_parts = [up_parts[0]] + [swap(up_parts[k], "tm", k) for k in range(1, tm_count)]
-    up_mine = place_parts(up_parts, "tm", 1, tm_count, 0)
-    stem_mine, down_all = split_gather(pack, "dp", dp_chains, stem_rows)
-    up_full = gather(up_mine.reshape(tm_count * rows, 2 * held), "dp", dp_chains)
-    up_full = up_full.reshape(channels, 2 * held)
-    down_full = down_all[:, :channels]
-    small_all = down_all[:, channels:]
-    stem_all = place_parts(gather_parts(stem_mine, "tm", tm_chains), "tm", 1, tm_count, 1)
+    up_mine = place_parts(up_parts, "tm", 1, tm_count, 0).reshape(tm_count * rows, 2 * held)
+    up_near = gather_stage(up_mine, "dp", *dp_chains[0], 0)
+    up_full = gather_rest(up_near, "dp", dp_chains).reshape(channels, 2 * held)
+    down_near = gather_stage(after(down_weight, up_near), "dp", *dp_chains[0], 0)
+    down_full = gather_rest(down_near, "dp", dp_chains).reshape(held, channels)
+    stem_parts = gather_parts(stem_mine, "tm", tm_chains)
+    stem_all = place_parts(stem_parts, "tm", 1, tm_count, 1)
     stem_all = stem_all.reshape(features, channels + 128)
 
     pieces = mel_pieces.shape[1]
     capacity = max(2, 2 * pieces // dp_count)
     arrived = lax.all_to_all(
-        sent.reshape(dp_count, capacity, -1), "dp", split_axis=0, concat_axis=0, tiled=True
+        after(sent, up_mine, stem_mine).reshape(dp_count, capacity, -1), "dp", split_axis=0, concat_axis=0, tiled=True
     ).reshape(dp_count * capacity, -1)
     frames = place_frames(arrived, pieces, features)
     frames = place_parts(gather_parts(frames, "tm", tm_chains), "tm", 1, tm_count, 0)
     frames = frames.reshape(length, features)
     grad_out = out_grad[0]
-    grad_out_all = gather_parts(after(grad_out, stem_mine), "tm", tm_chains)
+    grad_out_all = gather_parts(after(grad_out, stem_parts[2]), "tm", tm_chains)
     grad_out_all = place_parts(grad_out_all, "tm", 1, tm_count, 0).reshape(length, channels)
     segments = jnp.pad(segment_ids[0], (PAD, PAD), constant_values=-1)
     segments = jnp.broadcast_to(segments[:, None], (length + 2 * PAD, 128))
 
-    normed, stem_pre, gain_one = stem_forward(frames, stem_all, tm_count, "tm", rows)
+    extra = 16
+    normed, stem_pre, gain_one, frames_turned = stem_forward(
+        frames, stem_all, tm_count, "tm", rows, extra
+    )
     linear, gate_sig, gated = up_forward(normed, up_full)
     conv, stats, turned = conv_forward(gated, small_all, segments, taps)
     grad_act = lax.dot_general(
@@ -719,66 +996,90 @@
         conv, swap_all(stats, "tm"), turned, grad_act, taps
     )
     sums = swap_all(sums, "tm")
-    late = after(activated, *sums[:2])
-    down_terms = message_terms(late, grad_out_all, dp_count, tm_count)
-    y_terms = block_terms(late, down_full, False, "tm", tm_count)
-    down_sums = lax.all_to_all(down_terms, ("dp", "tm"), split_axis=0, concat_axis=0, tiled=True)
-
-    grad_hat = after(grad_hat, down_terms, *y_terms)
+    by_parts = stem_rows % 16 == 0 and rows % 16 == 0
+    if by_parts:
+        down_terms = part_terms(activated, grad_out_all, "dp", dp_chains)
+    else:
+        down_terms = [message_terms(activated, grad_out_all, dp_count, tm_count)]
+    y_own, *y_others = block_terms(activated, down_full, False, "tm", tm_count)
+    down_terms, y_others = lax.optimization_barrier((down_terms, y_others, *sums))[:2]
+    y_far, y_parts, y_passed = block_sum(y_others, "tm", tm_chains)
+    if by_parts:
+        down_parts = swap_parts(down_terms, "dp", dp_chains[-1])
+
+    grad_hat = after(grad_hat, *down_terms, y_passed)
     grad_proj, kernel_term = conv_backward(
         grad_hat, conv_hat, inverse, sums, gated, segments, linear, gate_sig, turned, taps,
         gain_post_term,
     )
-    y_part = block_sum(*y_terms, "tm", tm_chains)
-
-    normed_terms = block_terms(after(grad_proj, y_part), up_full, True, "tm", tm_count)
-    grad_normed = block_sum(*normed_terms, "tm", tm_chains)
-    up_terms = message_terms(
-        after(normed, down_sums, *normed_terms), grad_proj, dp_count, tm_count
+
+    own_terms, *other_terms = block_terms(
+        after(grad_proj, y_far), up_full, True, "tm", tm_count
     )
-    up_sums = lax.all_to_all(up_terms, ("dp", "tm"), split_axis=0, concat_axis=0, tiled=True)
-    y_out = (jax.nn.silu(stem_pre).astype(BF16).astype(F32) + after(y_part, up_terms)).astype(BF16)
-    grad_down = jnp.sum(
-        after(down_sums, up_terms).reshape(dp_count, tm_count * rows, held).astype(F32), axis=0
+    small_term = kernel_term.reshape(taps + 1, dp_count, rows).transpose(1, 0, 2)
+    small_term = small_term.reshape(dp_count, (taps + 1) * rows)
+    small_term = jnp.pad(small_term, ((0, 0), (0, channels - (taps + 1) * rows)))
+    if by_parts:
+        up_terms = part_terms(after(normed, *other_terms), grad_proj, "dp", dp_chains)
+    else:
+        up_terms = [message_terms(normed, grad_proj, dp_count, tm_count)]
+    grad_far, grad_parts, grad_passed = block_sum(other_terms, "tm", tm_chains, up_terms[-1])
+    if by_parts:
+        down_parts = add_parts(
+            [after(down_parts[0], grad_passed)] + down_parts[1:], "dp", dp_chains[0]
+        )
+        down_parts = swap_parts(down_parts, "dp", dp_chains[0])
+        up_parts = reduce_parts(up_terms, "dp", dp_chains)
+    grad_stem_pre = stem_backward(
+        own_terms, grad_parts + [grad_far], stem_pre, grad_out, gain_one, extra
     )
-
-    extra = 16
-    grad_stem_pre = stem_backward(
-        grad_normed, stem_pre, grad_out, gain_one, extra
+    grad_stem_parts = gather_parts(grad_stem_pre, "tm", tm_chains)
+    y_out = finish_rows(after(stem_pre, grad_stem_pre), y_own, y_parts + [y_far])
+    if by_parts:
+        stem_terms = stem_message(
+            frames_turned, grad_stem_parts, small_term, "dp", dp_chains, stem_rows
+        )
+        stem_sums = reduce_parts(stem_terms, "dp", dp_chains)
+        down_parts = cut_columns([after(down_parts[0], grad_stem_pre)] + down_parts[1:], "tm")
+        down_parts = [down_parts[0]] + [
+            swap(part, "tm", k) for k, part in enumerate(down_parts[1:], 1)
+        ]
+        grad_down = stack_rows(down_parts, "tm")
+        up_parts = cut_columns(up_parts, "tm")
+        up_parts = [up_parts[0]] + [
+            swap(part, "tm", k) for k, part in enumerate(up_parts[1:], 1)
+        ]
+        grad_up = mix_columns(up_parts, "tm", rows)
+    else:
+        down_sums = lax.all_to_all(
+            down_terms[0], ("dp", "tm"), split_axis=0, concat_axis=0, tiled=True
+        )
+        grad_down = jnp.sum(
+            down_sums.reshape(dp_count, tm_count * rows, held).astype(F32), axis=0
+        )
+        up_sums = lax.all_to_all(
+            up_terms[0], ("dp", "tm"), split_axis=0, concat_axis=0, tiled=True
+        )
+        up_sums = up_sums.reshape(dp_count, tm_count, tm_count * rows, 128)
+        spread = one_hot(lane, grouped).reshape(tm_count, 128, span)
+        grad_up = jnp.einsum("ijab,jbc->ac", up_sums, spread, preferred_element_type=F32)
+        stem_sum = sum(
+            jnp.dot(frames_turned[k], grad_stem_parts[k], preferred_element_type=F32)
+            for k in range(tm_count)
+        )
+        share = features // tm_count
+        gain_term = stem_sum[share].reshape(dp_count, 1, tm_count * rows)
+        gain_term = jnp.pad(gain_term, ((0, 0), (0, 0), (0, channels - tm_count * rows)))
+        stem_terms = stem_sum[:share].reshape(dp_count, stem_rows, channels)
+        stem_terms = jnp.concatenate([stem_terms, small_term[:, None, :], gain_term], axis=1)
+        stem_terms = jnp.pad(stem_terms.astype(BF16), ((0, 0), (0, 6), (0, 0)))
+        stem_sums = [
+            lax.all_to_all(stem_terms, "dp", split_axis=0, concat_axis=0, tiled=True)
+        ]
+    grad_stem, grad_kernel, grad_gain_post, grad_gain_pre = stem_finish(
+        stem_sums, stem_rows, rows, taps, "tm"
     )
-    chosen = jnp.arange(features // tm_count, dtype=jnp.int32)
-    chosen = (chosen // stem_rows * tm_count + column) * stem_rows + chosen % stem_rows
-    frames_part = jnp.dot(
-        frames, one_hot(jnp.arange(features, dtype=jnp.int32), chosen), preferred_element_type=F32
-    ).astype(BF16)
-    frames_part = frames_part.reshape(tm_count, block, features // tm_count)
-    frames_part = jnp.pad(frames_part, ((0, 0), (0, extra), (0, extra)))
-    frames_part = frames_part.at[:, block, features // tm_count].set(1)
-    grad_stem_parts = gather_parts(grad_stem_pre, "tm", tm_chains)
-    stem_sum = 0.0
-    for k in range(tm_count):
-        frames_k = lax.dynamic_index_in_dim(frames_part, column ^ k, 0, keepdims=False)
-        stem_sum = stem_sum + jnp.dot(
-            frames_k.T, grad_stem_parts[k], preferred_element_type=F32
-        )
-    small_term = kernel_term.reshape(taps + 1, dp_count, rows).transpose(1, 0, 2)
-    small_term = small_term.reshape(dp_count, 1, (taps + 1) * rows).astype(BF16)
-    small_term = jnp.pad(small_term, ((0, 0), (0, 0), (0, channels - (taps + 1) * rows)))
-    gain_term = stem_sum[features // tm_count].astype(BF16).reshape(dp_count, 1, tm_count * rows)
-    gain_term = jnp.pad(gain_term, ((0, 0), (0, 0), (0, channels - tm_count * rows)))
-    stem_terms = stem_sum[: features // tm_count].astype(BF16)
-    stem_terms = stem_terms.reshape(dp_count, stem_rows, channels)
-    stem_terms = jnp.concatenate([stem_terms, small_term, gain_term], axis=1)
-    stem_terms = after(stem_terms, up_sums)
-    stem_sums = lax.all_to_all(stem_terms, "dp", split_axis=0, concat_axis=0, tiled=True)
-    up_sums = up_sums.reshape(dp_count, tm_count, tm_count * rows, 128)
-    spread = one_hot(lane, grouped).reshape(tm_count, 128, span)
-    grad_up = jnp.einsum("ijab,jbc->ac", up_sums, spread, preferred_element_type=F32)
-    stem_sums = jnp.sum(stem_sums.astype(F32), axis=0)
-    grad_stem = stem_sums[:stem_rows]
-    small_sum = stem_sums[stem_rows, : (taps + 1) * rows].reshape(taps + 1, rows)
-    grad_kernel, grad_gain_post = small_sum[:taps].T, small_sum[taps]
-    grad_gain_pre = lax.dynamic_slice_in_dim(stem_sums[stem_rows + 1], column * rows, rows, 0)
+    grad_gain_post, grad_gain_pre = grad_gain_post[0], grad_gain_pre[0]
     return (y_out[None], grad_stem, grad_up, grad_down, grad_kernel, grad_gain_pre, grad_gain_post)
 
 

time: 171 us -> 154 us (0.901)
  local copies, waits for them, and re-layouts: 21.6 us -> 5.56 us
  waiting for transfers between devices: 73.3 us -> 59.1 us
  starting transfers between devices: 41.8 us -> 54.7 us
  Pallas kernels: 21.1 us -> 32.2 us
  other arithmetic: 8.35 us -> 0 us
  matrix products: 3 us -> 0.48 us
    ppermute x35 -> x57, starting transfers between devices: 27.9 us -> 51.2 us  [swap(): return lax.ppermute(value, axis, [(i, i ^ mask) for i in range(size)])]
    unnamed x82 -> x20, local copies, waits for them, and re-layouts: 18.1 us -> 2.9 us
    all_to_all x4 -> x1, waiting for transfers between devices: 13.8 us -> 0.01 us  [per_device(): lax.all_to_all(after(sent, up_mine, stem_mine).reshape(dp_count, capacity...]
    pallas_call x5 -> x17, Pallas kernels: 4.22 us -> 14.9 us  [the longest x2 4.61 us: part_terms(): pl.pallas_call(kernel, out_shape=[jax.ShapeDtypeStruct((total // size, ro...]
    all_to_all x4 -> x1, starting transfers between devices: 13.9 us -> 3.42 us  [per_device(): lax.all_to_all(after(sent, up_mine, stem_mine).reshape(dp_count, capacity...]
    add x4 -> x0, other arithmetic: 3.16 us -> none  [the longest x2 3.14 us: block_sum(): return own + near.astype(F32) + far.astype(F32)]
    dot_general x6 -> x0, matrix products: 2.53 us -> none  [the longest x4 1.12 us: per_device(): jnp.dot(frames_k.T, grad_stem_parts[k], preferred_element_type=F32)]
    reduce_sum x3 -> x0, other arithmetic: 1.98 us -> none  [the longest x1 1.78 us: per_device(): jnp.sum(after(down_sums, up_terms).reshape(dp_count, tm_count * rows, hel...]
  transfers between devices with their start and end apart: 39 -> 58, of which waited for: 20 -> 23; matrix products, arithmetic and copies ran while one was open for 7% -> 2% of each run, Pallas kernels for 7% -> 17%
where the time goes in v3:
time: 154 us; the launch traced here: 153 us
  waiting for transfers between devices  59.1 us (38%)
  starting transfers between devices  54.7 us (36%)
  Pallas kernels  32.2 us (21%)
  local copies, waits for them, and re-layouts  5.56 us (4%)
    ppermute x57, waiting for transfers between devices, swap(): return lax.ppermute(value, axis, [(i, i ^ mask) for i in range(size)])  59.1 us
    ppermute x57, starting transfers between devices, swap(): return lax.ppermute(value, axis, [(i, i ^ mask) for i in range(size)])  51.2 us
    pallas_call x1, Pallas kernels, conv_backward(): pl.pallas_call(kernel, out_shape=[jax.ShapeDtypeStruct((length, 2 * held)...  6.26 us
    pallas_call x2, Pallas kernels, part_terms(): pl.pallas_call(kernel, out_shape=[jax.ShapeDtypeStruct((total // size, ro...  4.61 us
    all_to_all x1, starting transfers between devices, per_device(): lax.all_to_all(after(sent, up_mine, stem_mine).reshape(dp_count, capacity...  3.42 us
  transfers between devices with their start and end apart: 58, of which 23 were waited for; matrix products, arithmetic and copies ran while one was open for 2% of the time, Pallas kernels for 17%

profile of v3, /device:TPU:0, one launch (start us, length us, event | category | flops | bytes accessed | tf_op | source)
XLA Modules:
  0.0 153.0 jit_solution(12069080620091316874)
XLA Ops:
  0.6 2.3 %shard_map.162 = (bf16[64,2176]{1,0:T(8,128)(2,1)}, bf16[16,1408]{1,0:T(8,128)(2,1)}, bf16[32,512]{1,0:T(8,128)(2,1)}, bf16[32,512]{1,0:T(8,128)(2,1)}, bf16[32,...) custom-call(bf16[32,2048]{1,0:T(8,128)(2,1)} %refs_0_.1, bf16[16,1024]{1,0:T(8,128)(2,1)} %refs_1_.1, bf16[32,31]{1,0:T(8,128)(2,1)} %refs_2_.1, ...), custom_call_target="tpu_custom_call" | custom-call | flops 134217728 | bytes 2097152 | tf_op jit(solution)/shard_map/pallas_call | solution.py:499
  3.0 5.1 %collective-permute-start.5 = (bf16[16,1408]{1,0:T(8,128)(2,1)}, bf16[16,1408]{1,0:T(8,128)(2,1)S(1)}, u32[]{:S(2)}, u32[]{:S(2)}) collective-permute-start(bf16[16,1408]{1,0:T(8,128)(2,1)} %get-tuple-element.91.refs_0_), channel_id=1, source_target_pairs={{0,24},{4,28},{8,16},{12,20},{16,8},{20,12},{24,0},{28,4},{1,25},{... | collective-permute-start | bytes 135176 | tf_op jit(solution)/shard_map/ppermute | solution.py:23
  10.4 2.9 %collective-permute-done.4.refs_2_ = bf16[16,1408]{1,0:T(8,128)(2,1)S(1)} collective-permute-done((bf16[16,1408]{1,0:T(8,128)(2,1)}, bf16[16,1408]{1,0:T(8,128)(2,1)S(1)}, u32[]{:S(2)}, u32[]{:S(2)}) %collective-permute-start.4) | collective-permute-done | bytes 45088 | tf_op jit(solution)/shard_map/ppermute | solution.py:23
  17.5 2.3 %collective-permute-done.1.refs_2_ = bf16[32,512]{1,0:T(8,128)(2,1)S(1)} collective-permute-done((bf16[32,512]{1,0:T(8,128)(2,1)}, bf16[32,512]{1,0:T(8,128)(2,1)S(1)}, u32[]{:S(2)}, u32[]{:S(2)}) %collective-permute-start.1) | collective-permute-done | bytes 32800 | tf_op jit(solution)/shard_map/ppermute | solution.py:23
  23.7 2.3 %collective-permute-start.13 = (bf16[128,512]{1,0:T(8,128)(2,1)S(1)}, bf16[128,512]{1,0:T(8,128)(2,1)S(1)}, u32[]{:S(2)}, u32[]{:S(2)}) collective-permute-start(bf16[128,512]{1,0:T(8,128)(2,1)S(1)} %bitcast.38), channel_id=1, source_target_pairs={{0,8},{4,12},{8,0},{12,4},{16,24},{20,28},{24,16},{28,20},{1,9},{5... | collective-permute-start | bytes 393224 | tf_op jit(solution)/shard_map/ppermute | solution.py:23
  26.7 3.4 %all-to-all-start = ((bf16[8,8,2176]{2,1,0:T(8,128)(2,1)}), bf16[8,8,2176]{2,1,0:T(8,128)(2,1)S(1)}, u32[]{:S(2)}, u32[]{:S(2)}) async-start(bf16[8,8,2176]{2,1,0:T(8,128)(2,1)} %bitcast.45), calls=%async_computation | async-start | bytes 557056 | tf_op jit(solution)/shard_map/all_to_all | solution.py:974
  31.0 8.3 %collective-permute-done.14.refs_2_ = bf16[128,512]{1,0:T(8,128)(2,1)S(1)} collective-permute-done((bf16[128,512]{1,0:T(8,128)(2,1)S(1)}, bf16[128,512]{1,0:T(8,128)(2,1)S(1)}, u32[]{:S(2)}, u32[]{:S(2)}) %collective-permute-start.14) | collective-permute-done | bytes 131104 | tf_op jit(solution)/shard_map/ppermute | solution.py:23
  39.5 3.4 %collective-permute-start.22 = (bf16[32,1024]{1,0:T(8,128)(2,1)S(1)}, bf16[32,1024]{1,0:T(8,128)(2,1)S(1)}, u32[]{:S(2)}, u32[]{:S(2)}) collective-permute-start(bf16[32,1024]{1,0:T(8,128)(2,1)S(1)} %copy-done.7), channel_id=1, source_target_pairs={{0,24},{4,28},{8,16},{12,20},{16,8},{20,12},{24,0},{28,4},{1,25},{... | collective-permute-start | bytes 196616 | tf_op jit(solution)/shard_map/ppermute | solution.py:23
  43.9 2.0 %collective-permute-done.22.refs_3_ = bf16[32,1024]{1,0:T(8,128)(2,1)S(1)} collective-permute-done((bf16[32,1024]{1,0:T(8,128)(2,1)S(1)}, bf16[32,1024]{1,0:T(8,128)(2,1)S(1)}, u32[]{:S(2)}, u32[]{:S(2)}) %collective-permute-start.22) | collective-permute-done | bytes 65568 | tf_op jit(solution)/shard_map/ppermute | solution.py:23
  45.9 2.1 %collective-permute-done.21.refs_2_ = bf16[32,1024]{1,0:T(8,128)(2,1)S(1)} collective-permute-done((bf16[32,1024]{1,0:T(8,128)(2,1)S(1)}, bf16[32,1024]{1,0:T(8,128)(2,1)S(1)}, u32[]{:S(2)}, u32[]{:S(2)}) %collective-permute-start.21) | collective-permute-done | bytes 65568 | tf_op jit(solution)/shard_map/ppermute | solution.py:23
  51.1 5.1 %collective-permute-done.23.refs_1_ = bf16[4,32,1024]{2,1,0:T(8,128)(2,1)S(1)} collective-permute-done((bf16[4,32,1024]{2,1,0:T(8,128)(2,1)S(1)}, bf16[4,32,1024]{2,1,0:T(8,128)(2,1)S(1)}, u32[]{:S(2)}, u32[]{:S(2)}) %collective-permute-start.23) | collective-permute-done | bytes 262176 | tf_op jit(solution)/shard_map/ppermute | solution.py:23
  62.7 2.7 %shard_map.169 = (bf16[512,1024]{1,0:T(8,128)(2,1)S(1)}, f32[128,1024]{1,0:T(8,128)S(1)}, f32[1,1024]{1,0:T(1,128)S(1)}, bf16[4,144,144]{2,1,0:T(8,128)(2,1)S(1)}) custom-call(bf16[512,512]{1,0:T(8,128)(2,1)S(1)} %bitcast.35, bf16[512,1152]{1,0:T(8,128)(2,1)S(1)} %bitcast.29), custom_call_target="tpu_custom_call" | custom-call | flops 536870912 | bytes 2228224 | tf_op jit(solution)/shard_map/pallas_call | solution.py:590
  66.3 3.0 %shard_map.173 = (f32[512,256]{1,0:T(8,128)S(1)}, f32[8,512]{1,0:T(8,128)S(1)}, f32[128,256]{1,0:T(8,128)S(1)}) custom-call(f32[544,256]{1,0:T(8,128)S(1)} %get-tuple-element.96.gated_ref, bf16[256,128]{1,0:T(8,128)(2,1)S(1)} %bitcast.43, s32[544,128]{1,0:T(8,128)S(1)} %broadcast_in_dim.17.seg_ref), custom_call_target="tpu_custom_call" | custom-call | flops 17268736 | bytes 1114112 | tf_op jit(solution)/shard_map/pallas_call | solution.py:679
  82.5 6.3 %shard_map.181 = (bf16[512,512]{1,0:T(8,128)(2,1)S(1)}, f32[32,256]{1,0:T(8,128)S(1)}) custom-call(f32[512,256]{1,0:T(8,128)S(1)} %get-tuple-element.115.grad_ref, f32[512,256]{1,0:T(8,128)S(1)} %get-tuple-element.116.hat_ref, f32[512,128]{1,0:T(8,128)S(1)} %get-tuple-element.117.inverse_ref, f32[544,256]{1,0:T(8,128)S(1)} %get-tuple-element.96.gated_ref, ...), custom_call_target="tpu_custom_call" | custom-call | flops 32505856 | bytes 3145728 | tf_op jit(solution)/shard_map/pallas_call | solution.py:798
  92.2 3.2 %shard_map.184 = (bf16[4,128,512]{2,1,0:T(8,128)(2,1)S(1)}, bf16[4,128,512]{2,1,0:T(8,128)(2,1)}) custom-call(bf16[512,1024]{1,0:T(8,128)(2,1)S(1)} %get-tuple-element.128.normed_ref.left_ref, bf16[512,512]{1,0:T(8,128)(2,1)S(1)} %get-tuple-element.122.left_ref.right_ref), custom_call_target="tpu_custom_call" | custom-call | flops 536870912 | bytes 2621440 | tf_op jit(solution)/shard_map/pallas_call | solution.py:164
  96.2 7.6 %collective-permute-done.34.refs_1_ = bf16[128,1024]{1,0:T(8,128)(2,1)S(1)} collective-permute-done((bf16[128,1024]{1,0:T(8,128)(2,1)S(1)}, bf16[128,1024]{1,0:T(8,128)(2,1)S(1)}, u32[]{:S(2)}, u32[]{:S(2)}) %collective-permute-start.34) | collective-permute-done | bytes 262176 | tf_op jit(solution)/shard_map/ppermute | solution.py:23
  107.2 5.5 %collective-permute-done.37.refs_2_ = bf16[144,1024]{1,0:T(8,128)(2,1)S(1)} collective-permute-done((bf16[144,1024]{1,0:T(8,128)(2,1)S(1)}, bf16[144,1024]{1,0:T(8,128)(2,1)S(1)}, u32[]{:S(2)}, u32[]{:S(2)}) %collective-permute-start.37) | collective-permute-done | bytes 294944 | tf_op jit(solution)/shard_map/ppermute | solution.py:23
  112.7 2.1 %collective-permute-start.50 = (bf16[4,32,1024]{2,1,0:T(8,128)(2,1)}, bf16[4,32,1024]{2,1,0:T(8,128)(2,1)}, u32[]{:S(2)}, u32[]{:S(2)}) collective-permute-start(bf16[4,32,1024]{2,1,0:T(8,128)(2,1)} %get-tuple-element.112), channel_id=1, source_target_pairs={{0,4},{4,0},{8,12},{12,8},{16,20},{20,16},{24,28},{28,24},{1,5},{5... | collective-permute-start | bytes 786440 | tf_op jit(solution)/shard_map/ppermute | solution.py:23
  116.8 3.5 %collective-permute-done.43.refs_1_ = bf16[4,128,512]{2,1,0:T(8,128)(2,1)S(1)} collective-permute-done((bf16[4,128,512]{2,1,0:T(8,128)(2,1)}, bf16[4,128,512]{2,1,0:T(8,128)(2,1)S(1)}, u32[]{:S(2)}, u32[]{:S(2)}) %collective-permute-start.43) | collective-permute-done | bytes 524320 | tf_op jit(solution)/shard_map/ppermute | solution.py:23
  121.0 3.4 %collective-permute-start.45 = (bf16[1,128,512]{2,1,0:T(8,128)(2,1)S(1)}, bf16[1,128,512]{2,1,0:T(8,128)(2,1)S(1)}, u32[]{:S(2)}, u32[]{:S(2)}) collective-permute-start(bf16[1,128,512]{2,1,0:T(8,128)(2,1)S(1)} %get-tuple-element.146), channel_id=1, source_target_pairs={{0,16},{4,20},{8,24},{12,28},{16,0},{20,4},{24,8},{28,12},{1,17},{... | collective-permute-start | bytes 393224 | tf_op jit(solution)/shard_map/ppermute | solution.py:23
  126.4 2.1 %collective-permute-start.39 = (bf16[4,24,1024]{2,1,0:T(8,128)(2,1)S(1)}, bf16[4,24,1024]{2,1,0:T(8,128)(2,1)S(1)}, u32[]{:S(2)}, u32[]{:S(2)}) collective-permute-start(bf16[4,24,1024]{2,1,0:T(8,128)(2,1)S(1)} %get-tuple-element.137), channel_id=1, source_target_pairs={{0,4},{4,0},{8,12},{12,8},{16,20},{20,16},{24,28},{28,24},{1,5},{5... | collective-permute-start | bytes 589832 | tf_op jit(solution)/shard_map/ppermute | solution.py:23
  129.6 4.0 %collective-permute-done.45.refs_2_ = bf16[1,128,512]{2,1,0:T(8,128)(2,1)S(1)} collective-permute-done((bf16[1,128,512]{2,1,0:T(8,128)(2,1)S(1)}, bf16[1,128,512]{2,1,0:T(8,128)(2,1)S(1)}, u32[]{:S(2)}, u32[]{:S(2)}) %collective-permute-start.45) | collective-permute-done | bytes 131104 | tf_op jit(solution)/shard_map/ppermute | solution.py:23
  133.5 2.5 %collective-permute-start.53 = (bf16[1,32,1024]{2,1,0:T(8,128)(2,1)S(1)}, bf16[1,32,1024]{2,1,0:T(8,128)(2,1)S(1)}, u32[]{:S(2)}, u32[]{:S(2)}) collective-permute-start(bf16[1,32,1024]{2,1,0:T(8,128)(2,1)S(1)} %get-tuple-element.157), channel_id=1, source_target_pairs={{0,24},{4,28},{8,16},{12,20},{16,8},{20,12},{24,0},{28,4},{1,25},{... | collective-permute-start | bytes 196616 | tf_op jit(solution)/shard_map/ppermute | solution.py:23
  136.2 2.7 %collective-permute-done.52.refs_2_ = bf16[1,32,1024]{2,1,0:T(8,128)(2,1)S(1)} collective-permute-done((bf16[1,32,1024]{2,1,0:T(8,128)(2,1)S(1)}, bf16[1,32,1024]{2,1,0:T(8,128)(2,1)S(1)}, u32[]{:S(2)}, u32[]{:S(2)}) %collective-permute-start.52) | collective-permute-done | bytes 65568 | tf_op jit(solution)/shard_map/ppermute | solution.py:23
  (152 shorter events, 64.2 us)
Async XLA Ops:
  14.1 11.9 %collective-permute-start.6 = (bf16[4,16,1408]{2,1,0:T(8,128)(2,1)S(1)}, bf16[4,16,1408]{2,1,0:T(8,128)(2,1)S(1)}, u32[]{:S(2)}, u32[]{:S(2)}) collective-permute-start(bf16[4,16,1408]{2,1,0:T(8,128)(2,1)S(1)} %shard_map.164.refs_0_), channel_id=1, source_target_pairs={{0,4},{4,0},{8,12},{12,8},{16,20},{20,16},{24,28},{28,24},{1,5},{5... | collective-permute-start | bytes 540680 | tf_op jit(solution)/shard_map/ppermute | solution.py:23
  21.5 9.5 %collective-permute-start.15 = (bf16[128,512]{1,0:T(8,128)(2,1)S(1)}, bf16[128,512]{1,0:T(8,128)(2,1)S(1)}, u32[]{:S(2)}, u32[]{:S(2)}) collective-permute-start(bf16[128,512]{1,0:T(8,128)(2,1)S(1)} %bitcast.36), channel_id=1, source_target_pairs={{0,24},{4,28},{8,16},{12,20},{16,8},{20,12},{24,0},{28,4},{1,25},{... | collective-permute-start | bytes 393224 | tf_op jit(solution)/shard_map/ppermute | solution.py:23
  23.4 15.9 %collective-permute-start.14 = (bf16[128,512]{1,0:T(8,128)(2,1)S(1)}, bf16[128,512]{1,0:T(8,128)(2,1)S(1)}, u32[]{:S(2)}, u32[]{:S(2)}) collective-permute-start(bf16[128,512]{1,0:T(8,128)(2,1)S(1)} %bitcast.37), channel_id=1, source_target_pairs={{0,16},{4,20},{8,24},{12,28},{16,0},{20,4},{24,8},{28,12},{1,17},{... | collective-permute-start | bytes 393224 | tf_op jit(solution)/shard_map/ppermute | solution.py:23
  23.7 15.7 %collective-permute-start.13 = (bf16[128,512]{1,0:T(8,128)(2,1)S(1)}, bf16[128,512]{1,0:T(8,128)(2,1)S(1)}, u32[]{:S(2)}, u32[]{:S(2)}) collective-permute-start(bf16[128,512]{1,0:T(8,128)(2,1)S(1)} %bitcast.38), channel_id=1, source_target_pairs={{0,8},{4,12},{8,0},{12,4},{16,24},{20,28},{24,16},{28,20},{1,9},{5... | collective-permute-start | bytes 393224 | tf_op jit(solution)/shard_map/ppermute | solution.py:23
  26.7 24.1 %all-to-all-start = ((bf16[8,8,2176]{2,1,0:T(8,128)(2,1)}), bf16[8,8,2176]{2,1,0:T(8,128)(2,1)S(1)}, u32[]{:S(2)}, u32[]{:S(2)}) async-start(bf16[8,8,2176]{2,1,0:T(8,128)(2,1)} %bitcast.45), calls=%async_computation | async-start | bytes 557056 | tf_op jit(solution)/shard_map/all_to_all | solution.py:974
  30.1 19.6 %collective-permute-start.11 = (bf16[8,16,1152]{2,1,0:T(8,128)(2,1)S(1)}, bf16[8,16,1152]{2,1,0:T(8,128)(2,1)S(1)}, u32[]{:S(2)}, u32[]{:S(2)}) collective-permute-start(bf16[8,16,1152]{2,1,0:T(8,128)(2,1)S(1)} %bitcast.40), channel_id=1, source_target_pairs={{0,2},{1,3},{2,0},{3,1},{4,6},{5,7},{6,4},{7,5},{8,10},{9,11},{10,... | collective-permute-start | bytes 884744 | tf_op jit(solution)/shard_map/ppermute | solution.py:23
  39.4 19.5 %collective-permute-start.16 = (bf16[4,128,512]{2,1,0:T(8,128)(2,1)S(1)}, bf16[4,128,512]{2,1,0:T(8,128)(2,1)S(1)}, u32[]{:S(2)}, u32[]{:S(2)}) collective-permute-start(bf16[4,128,512]{2,1,0:T(8,128)(2,1)S(1)} %shard_map.170.refs_0_), channel_id=1, source_target_pairs={{0,4},{4,0},{8,12},{12,8},{16,20},{20,16},{24,28},{28,24},{1,5},{5... | collective-permute-start | bytes 1572872 | tf_op jit(solution)/shard_map/ppermute | solution.py:23
  49.7 9.2 %collective-permute-start.18 = (bf16[128,1024]{1,0:T(8,128)(2,1)S(1)}, bf16[128,1024]{1,0:T(8,128)(2,1)S(1)}, u32[]{:S(2)}, u32[]{:S(2)}) collective-permute-start(bf16[128,1024]{1,0:T(8,128)(2,1)S(1)} %bitcast.31), channel_id=1, source_target_pairs={{0,2},{1,3},{2,0},{3,1},{4,6},{5,7},{6,4},{7,5},{8,10},{9,11},{10,... | collective-permute-start | bytes 786440 | tf_op jit(solution)/shard_map/ppermute | solution.py:23
  50.6 11.5 %collective-permute-start.12 = (bf16[8,16,1152]{2,1,0:T(8,128)(2,1)S(1)}, bf16[8,16,1152]{2,1,0:T(8,128)(2,1)S(1)}, u32[]{:S(2)}, u32[]{:S(2)}) collective-permute-start(bf16[8,16,1152]{2,1,0:T(8,128)(2,1)S(1)} %collective-permute-done.11.refs_2_), channel_id=1, source_target_pairs={{0,1},{1,0},{2,3},{3,2},{4,5},{5,4},{6,7},{7,6},{8,9},{9,8},{10,11... | collective-permute-start | bytes 884744 | tf_op jit(solution)/shard_map/ppermute | solution.py:23
  57.6 13.6 %collective-permute-start.17 = (bf16[128,1024]{1,0:T(8,128)(2,1)S(1)}, bf16[128,1024]{1,0:T(8,128)(2,1)S(1)}, u32[]{:S(2)}, u32[]{:S(2)}) collective-permute-start(bf16[128,1024]{1,0:T(8,128)(2,1)S(1)} %bitcast.32), channel_id=1, source_target_pairs={{0,1},{1,0},{2,3},{3,2},{4,5},{5,4},{6,7},{7,6},{8,9},{9,8},{10,11... | collective-permute-start | bytes 786440 | tf_op jit(solution)/shard_map/ppermute | solution.py:23
  58.9 12.4 %collective-permute-start.19 = (bf16[128,1024]{1,0:T(8,128)(2,1)S(1)}, bf16[128,1024]{1,0:T(8,128)(2,1)S(1)}, u32[]{:S(2)}, u32[]{:S(2)}) collective-permute-start(bf16[128,1024]{1,0:T(8,128)(2,1)S(1)} %collective-permute-done.18.refs_2_), channel_id=1, source_target_pairs={{0,1},{1,0},{2,3},{3,2},{4,5},{5,4},{6,7},{7,6},{8,9},{9,8},{10,11... | collective-permute-start | bytes 786440 | tf_op jit(solution)/shard_map/ppermute | solution.py:23
  81.7 8.4 %collective-permute-start.31 = (bf16[128,1024]{1,0:T(8,128)(2,1)S(1)}, bf16[128,1024]{1,0:T(8,128)(2,1)S(1)}, u32[]{:S(2)}, u32[]{:S(2)}) collective-permute-start(bf16[128,1024]{1,0:T(8,128)(2,1)S(1)} %shard_map.180), channel_id=1, source_target_pairs={{0,2},{1,3},{2,0},{3,1},{4,6},{5,7},{6,4},{7,5},{8,10},{9,11},{10,... | collective-permute-start | bytes 786440 | tf_op jit(solution)/shard_map/ppermute | solution.py:23
  105.2 15.1 %collective-permute-start.43 = (bf16[4,128,512]{2,1,0:T(8,128)(2,1)}, bf16[4,128,512]{2,1,0:T(8,128)(2,1)S(1)}, u32[]{:S(2)}, u32[]{:S(2)}) collective-permute-start(bf16[4,128,512]{2,1,0:T(8,128)(2,1)} %get-tuple-element.129), channel_id=1, source_target_pairs={{0,4},{4,0},{8,12},{12,8},{16,20},{20,16},{24,28},{28,24},{1,5},{5... | collective-permute-start | bytes 1572872 | tf_op jit(solution)/shard_map/ppermute | solution.py:23
  107.2 13.8 %collective-permute-start.36 = (bf16[144,1024]{1,0:T(8,128)(2,1)S(1)}, bf16[144,1024]{1,0:T(8,128)(2,1)S(1)}, u32[]{:S(2)}, u32[]{:S(2)}) collective-permute-start(bf16[144,1024]{1,0:T(8,128)(2,1)S(1)} %shard_map.185.refs_0_), channel_id=1, source_target_pairs={{0,1},{1,0},{2,3},{3,2},{4,5},{5,4},{6,7},{7,6},{8,9},{9,8},{10,11... | collective-permute-start | bytes 884744 | tf_op jit(solution)/shard_map/ppermute | solution.py:23
  112.7 11.8 %collective-permute-start.38 = (bf16[144,1024]{1,0:T(8,128)(2,1)S(1)}, bf16[144,1024]{1,0:T(8,128)(2,1)}, u32[]{:S(2)}, u32[]{:S(2)}) collective-permute-start(bf16[144,1024]{1,0:T(8,128)(2,1)S(1)} %collective-permute-done.37.refs_2_), channel_id=1, source_target_pairs={{0,1},{1,0},{2,3},{3,2},{4,5},{5,4},{6,7},{7,6},{8,9},{9,8},{10,11... | collective-permute-start | bytes 884744 | tf_op jit(solution)/shard_map/ppermute | solution.py:23
  112.7 13.7 %collective-permute-start.50 = (bf16[4,32,1024]{2,1,0:T(8,128)(2,1)}, bf16[4,32,1024]{2,1,0:T(8,128)(2,1)}, u32[]{:S(2)}, u32[]{:S(2)}) collective-permute-start(bf16[4,32,1024]{2,1,0:T(8,128)(2,1)} %get-tuple-element.112), channel_id=1, source_target_pairs={{0,4},{4,0},{8,12},{12,8},{16,20},{20,16},{24,28},{28,24},{1,5},{5... | collective-permute-start | bytes 786440 | tf_op jit(solution)/shard_map/ppermute | solution.py:23
  114.8 27.0 %collective-permute-start.35 = (bf16[128,1024]{1,0:T(8,128)(2,1)}, bf16[128,1024]{1,0:T(8,128)(2,1)}, u32[]{:S(2)}, u32[]{:S(2)}) collective-permute-start(bf16[128,1024]{1,0:T(8,128)(2,1)} %get-tuple-element.133), channel_id=1, source_target_pairs={{0,1},{1,0},{2,3},{3,2},{4,5},{5,4},{6,7},{7,6},{8,9},{9,8},{10,11... | collective-permute-start | bytes 786440 | tf_op jit(solution)/shard_map/ppermute | solution.py:23
  120.4 9.1 %collective-permute-start.44 = (bf16[1,128,512]{2,1,0:T(8,128)(2,1)S(1)}, bf16[1,128,512]{2,1,0:T(8,128)(2,1)S(1)}, u32[]{:S(2)}, u32[]{:S(2)}) collective-permute-start(bf16[1,128,512]{2,1,0:T(8,128)(2,1)S(1)} %get-tuple-element.145), channel_id=1, source_target_pairs={{0,8},{4,12},{8,0},{12,4},{16,24},{20,28},{24,16},{28,20},{1,9},{5... | collective-permute-start | bytes 393224 | tf_op jit(solution)/shard_map/ppermute | solution.py:23
  121.0 12.5 %collective-permute-start.45 = (bf16[1,128,512]{2,1,0:T(8,128)(2,1)S(1)}, bf16[1,128,512]{2,1,0:T(8,128)(2,1)S(1)}, u32[]{:S(2)}, u32[]{:S(2)}) collective-permute-start(bf16[1,128,512]{2,1,0:T(8,128)(2,1)S(1)} %get-tuple-element.146), channel_id=1, source_target_pairs={{0,16},{4,20},{8,24},{12,28},{16,0},{20,4},{24,8},{28,12},{1,17},{... | collective-permute-start | bytes 393224 | tf_op jit(solution)/shard_map/ppermute | solution.py:23
  124.5 9.0 %collective-permute-start.46 = (bf16[1,128,512]{2,1,0:T(8,128)(2,1)S(1)}, bf16[1,128,512]{2,1,0:T(8,128)(2,1)S(1)}, u32[]{:S(2)}, u32[]{:S(2)}) collective-permute-start(bf16[1,128,512]{2,1,0:T(8,128)(2,1)S(1)} %get-tuple-element.147), channel_id=1, source_target_pairs={{0,24},{4,28},{8,16},{12,20},{16,8},{20,12},{24,0},{28,4},{1,25},{... | collective-permute-start | bytes 393224 | tf_op jit(solution)/shard_map/ppermute | solution.py:23
  126.4 14.6 %collective-permute-start.39 = (bf16[4,24,1024]{2,1,0:T(8,128)(2,1)S(1)}, bf16[4,24,1024]{2,1,0:T(8,128)(2,1)S(1)}, u32[]{:S(2)}, u32[]{:S(2)}) collective-permute-start(bf16[4,24,1024]{2,1,0:T(8,128)(2,1)S(1)} %get-tuple-element.137), channel_id=1, source_target_pairs={{0,4},{4,0},{8,12},{12,8},{16,20},{20,16},{24,28},{28,24},{1,5},{5... | collective-permute-start | bytes 589832 | tf_op jit(solution)/shard_map/ppermute | solution.py:23
  136.1 11.2 %collective-permute-start.47 = (bf16[128,128]{1,0:T(8,128)(2,1)S(1)}, bf16[128,128]{1,0:T(8,128)(2,1)S(1)}, u32[]{:S(2)}, u32[]{:S(2)}) collective-permute-start(bf16[128,128]{1,0:T(8,128)(2,1)S(1)} %get-tuple-element.149), channel_id=1, source_target_pairs={{0,1},{1,0},{2,3},{3,2},{4,5},{5,4},{6,7},{7,6},{8,9},{9,8},{10,11... | collective-permute-start | bytes 98312 | tf_op jit(solution)/shard_map/ppermute | solution.py:23
  141.7 10.1 %collective-permute-start.40 = (bf16[1,24,1024]{2,1,0:T(8,128)(2,1)S(1)}, bf16[1,24,1024]{2,1,0:T(8,128)(2,1)S(1)}, u32[]{:S(2)}, u32[]{:S(2)}) collective-permute-start(bf16[1,24,1024]{2,1,0:T(8,128)(2,1)S(1)} %get-tuple-element.139), channel_id=1, source_target_pairs={{0,8},{4,12},{8,0},{12,4},{16,24},{20,28},{24,16},{28,20},{1,9},{5... | collective-permute-start | bytes 147464 | tf_op jit(solution)/shard_map/ppermute | solution.py:23
  143.1 8.8 %collective-permute-start.41 = (bf16[1,24,1024]{2,1,0:T(8,128)(2,1)S(1)}, bf16[1,24,1024]{2,1,0:T(8,128)(2,1)S(1)}, u32[]{:S(2)}, u32[]{:S(2)}) collective-permute-start(bf16[1,24,1024]{2,1,0:T(8,128)(2,1)S(1)} %get-tuple-element.140), channel_id=1, source_target_pairs={{0,16},{4,20},{8,24},{12,28},{16,0},{20,4},{24,8},{28,12},{1,17},{... | collective-permute-start | bytes 147464 | tf_op jit(solution)/shard_map/ppermute | solution.py:23
  (44 other events, 258.4 us)

commit v4 on v3

--- a/solution.py
+++ b/solution.py
@@ -30,8 +30,10 @@
     return pltpu.CompilerParams(vmem_limit_bytes=VMEM_LIMIT)
 
 
-def costs(flops, moved):
-    return pl.CostEstimate(flops=flops, bytes_accessed=moved, transcendentals=0)
+def costs(microseconds):
+    return pl.CostEstimate(
+        flops=int(microseconds * 2e10), bytes_accessed=1 << 16, transcendentals=0
+    )
 
 
 def after(value, *others):
@@ -51,9 +53,7 @@
         kernel,
         out_shape=jax.ShapeDtypeStruct(out_shape, parts[0].dtype),
         compiler_params=kernel_params(),
-        cost_estimate=pl.CostEstimate(
-            flops=0, bytes_accessed=2 * size * parts[0].size * 2, transcendentals=0
-        ),
+        cost_estimate=costs(0.8),
     )(*parts)
 
 
@@ -74,28 +74,26 @@
     width = right.shape[0] if transposed else right.shape[1]
     dims = (((1,), (1 if transposed else 0,)), ((), ()))
 
-    def kernel(left_ref, right_ref, own, *others):
+    def kernel(left_ref, right_ref, own, *refs):
+        others, terms = refs[:-1], refs[-1]
         place = lax.axis_index(axis)
+        terms[...] = lax.dot_general(
+            left_ref[...], right_ref[...], dims, preferred_element_type=F32
+        )
         for k in range(count):
             start = pl.multiple_of((place ^ k) * block, block)
-            term = lax.dot_general(
-                left_ref[pl.ds(start, block), :], right_ref[...], dims, preferred_element_type=F32
-            )
             if k == 0:
-                own[...] = term
+                own[...] = terms[pl.ds(start, block), :]
             else:
-                others[k - 1][...] = term.astype(BF16)
+                others[k - 1][...] = terms[pl.ds(start, block), :].astype(BF16)
 
     return pl.pallas_call(
         kernel,
         out_shape=[jax.ShapeDtypeStruct((block, width), F32)]
         + [jax.ShapeDtypeStruct((block, width), BF16)] * (count - 1),
-        compiler_params=kernel_params(),
-        cost_estimate=pl.CostEstimate(
-            flops=2 * left.size * width,
-            bytes_accessed=2 * (left.size + right.size) + 10 * block * width,
-            transcendentals=0,
-        ),
+        scratch_shapes=[pltpu.VMEM((count * block, width), F32)],
+        compiler_params=kernel_params(),
+        cost_estimate=costs(1.2),
     )(left, right)
 
 
@@ -118,7 +116,7 @@
         kernel,
         out_shape=jax.ShapeDtypeStruct(one.shape, BF16),
         compiler_params=kernel_params(),
-        cost_estimate=costs(one.size, 6 * one.size),
+        cost_estimate=costs(0.5),
     )(one, other)
 
 
@@ -135,25 +133,45 @@
         kernel,
         out_shape=jax.ShapeDtypeStruct(own.shape, BF16),
         compiler_params=kernel_params(),
-        cost_estimate=costs(8 * own.size, 14 * own.size),
+        cost_estimate=costs(0.6),
     )(stem_pre, own, *parts)
 
 
-def part_terms(left, right, axis, chains):
+def turn(value):
+    rows, columns = value.shape
+
+    def kernel(source, out):
+        for c in range(0, columns, 128):
+            out[c : c + 128, :] = source[:, c : c + 128].astype(F32).T.astype(BF16)
+
+    return pl.pallas_call(
+        kernel,
+        out_shape=jax.ShapeDtypeStruct((columns, rows), value.dtype),
+        compiler_params=kernel_params(),
+        cost_estimate=costs(1.0),
+    )(value)
+
+
+def part_terms(left, right, turned, axis, chains):
     total = lax.axis_size(axis)
     stride, size = chains[-1]
-    rows, columns = left.shape[1] // total, right.shape[1]
-    step = max(1, 128 // rows)
+    rows, columns = left.shape[0 if turned else 1] // total, right.shape[1]
+    step = max(1, 512 // rows) if turned else max(1, 128 // rows)
 
     def kernel(left_ref, right_ref, *outs):
         place = (lax.axis_index(axis) // stride) % size
         for i in range(0, total, step):
-            term = lax.dot_general(
-                left_ref[:, i * rows : (i + step) * rows],
-                right_ref[...],
-                (((0,), (0,)), ((), ())),
-                preferred_element_type=F32,
-            ).astype(BF16)
+            block = slice(i * rows, (i + step) * rows)
+            if turned:
+                term = jnp.dot(left_ref[block, :], right_ref[...], preferred_element_type=F32)
+            else:
+                term = lax.dot_general(
+                    left_ref[:, block],
+                    right_ref[...],
+                    (((0,), (0,)), ((), ())),
+                    preferred_element_type=F32,
+                )
+            term = term.astype(BF16)
             for n in range(step):
                 for k in range(size):
 
@@ -165,10 +183,47 @@
         kernel,
         out_shape=[jax.ShapeDtypeStruct((total // size, rows, columns), BF16)] * size,
         compiler_params=kernel_params(),
-        cost_estimate=costs(
-            2 * left.size * columns, 2 * (left.size + right.size + left.shape[1] * columns)
-        ),
+        cost_estimate=costs(1.5),
     )(left, right)
+
+
+def join_parts(first, second, axis, chain):
+    stride, size = chain
+    count = len(first)
+    lead, rows, columns = first[0].shape
+    _, below, wide = second[0].shape
+    folds = wide // columns
+
+    def kernel(*refs):
+        place = (lax.axis_index(axis) // stride) % size
+        outs = refs[2 * count :]
+        for a in range(lead // size):
+            for k in range(size):
+                at = a * size + (place ^ k)
+                total = sum(part[at].astype(F32) for part in refs[:count])
+                outs[k][a, :rows, :] = total.astype(BF16)
+                total = sum(part[at].astype(F32) for part in refs[count : 2 * count]).astype(BF16)
+                for f in range(folds):
+                    outs[k][a, rows + f * below : rows + (f + 1) * below, :] = total[
+                        :, f * columns : (f + 1) * columns
+                    ]
+
+    shape = (lead // size, rows + folds * below, columns)
+    return pl.pallas_call(
+        kernel,
+        out_shape=[jax.ShapeDtypeStruct(shape, BF16)] * size,
+        compiler_params=kernel_params(),
+        cost_estimate=costs(0.8),
+    )(*first, *second)
+
+
+def swap_all_parts(parts, axis):
+    return [parts[0]] + [swap(part, axis, k) for k, part in enumerate(parts[1:], 1)]
+
+
+def swap_parts(parts, axis, chain):
+    stride, _ = chain
+    return [parts[0]] + [swap(part, axis, k * stride) for k, part in enumerate(parts[1:], 1)]
 
 
 def add_parts(parts, axis, chain):
@@ -187,156 +242,102 @@
         kernel,
         out_shape=[jax.ShapeDtypeStruct(shape, BF16)] * size,
         compiler_params=kernel_params(),
-        cost_estimate=costs(len(parts) * parts[0].size, 4 * len(parts) * parts[0].size),
+        cost_estimate=costs(0.6),
     )(*parts)
 
 
-def swap_parts(parts, axis, chain):
-    stride, _ = chain
-    return [parts[0]] + [swap(part, axis, k * stride) for k, part in enumerate(parts[1:], 1)]
-
-
-def reduce_parts(parts, axis, chains):
+def reduce_rest(parts, axis, chains):
     parts = swap_parts(parts, axis, chains[-1])
     for chain in reversed(chains[:-1]):
         parts = swap_parts(add_parts(parts, axis, chain), axis, chain)
     return parts
 
 
-def cut_columns(parts, axis):
+def cut_columns(parts, axis, rows, below):
     count = lax.axis_size(axis)
-    rows, columns = parts[0].shape[1:]
+    _, height, columns = parts[0].shape
     share = columns // count
+    folds = (height - rows) // below
+    wide = folds * columns // count
 
     def kernel(*refs):
         place = lax.axis_index(axis)
         total = sum(part[0].astype(F32) for part in refs[: len(parts)]).astype(BF16)
         for j in range(count):
+            fold, start = divmod(wide * j, columns)
             for k in range(count):
 
                 @pl.when(place ^ j == k)
                 def _():
-                    refs[len(parts) + k][...] = total[:, j * share : (j + 1) * share]
-
-    return pl.pallas_call(
-        kernel,
-        out_shape=[jax.ShapeDtypeStruct((rows, share), BF16)] * count,
-        compiler_params=kernel_params(),
-        cost_estimate=costs(len(parts) * parts[0].size, 4 * len(parts) * parts[0].size),
+                    out = refs[len(parts) + k]
+                    out[:rows, :] = total[:rows, j * share : (j + 1) * share]
+                    for f in range(folds):
+                        lanes = slice(start + f * share, start + (f + 1) * share)
+                        out[rows + f * below : rows + (f + 1) * below, :] = total[
+                            rows + fold * below : rows + (fold + 1) * below, lanes
+                        ]
+
+    return pl.pallas_call(
+        kernel,
+        out_shape=[jax.ShapeDtypeStruct((height, share), BF16)] * count,
+        compiler_params=kernel_params(),
+        cost_estimate=costs(0.6),
     )(*parts)
 
 
-def stack_rows(parts, axis):
+def mix_columns(parts, axis, rows, small):
     count = len(parts)
-    rows, columns = parts[0].shape
+    height, share = parts[0].shape
+    span = share * count
+    folds = (height - rows) // small
 
     def kernel(*refs):
         place = lax.axis_index(axis)
-        for k in range(count):
-            start = pl.multiple_of((place ^ k) * rows, rows)
-            refs[count][pl.ds(start, rows), :] = refs[k][...].astype(F32)
-
-    return pl.pallas_call(
-        kernel,
-        out_shape=jax.ShapeDtypeStruct((count * rows, columns), F32),
-        compiler_params=kernel_params(),
-        cost_estimate=costs(0, 6 * count * parts[0].size),
-    )(*parts)
-
-
-def mix_columns(parts, axis, small):
-    count = len(parts)
-    rows = parts[0].shape[0]
-    span = 128 * count
-
-    def kernel(*refs):
-        place = lax.axis_index(axis)
-        at = lax.broadcasted_iota(jnp.int32, (128, span), 0)
-        to = lax.broadcasted_iota(jnp.int32, (128, span), 1)
+        upper, lower = refs[count:]
+        at, to = iota((share, span), 0), iota((share, span), 1)
         total = jnp.zeros((rows, span), F32)
         for k in range(count):
             want = at // small * (small * count) + (place ^ k) * small + at % small
-            spread = jnp.where(to == want, 1.0, 0.0).astype(BF16)
-            total = total + jnp.dot(refs[k][...], spread, preferred_element_type=F32)
-        refs[count][...] = total
-
-    return pl.pallas_call(
-        kernel,
-        out_shape=jax.ShapeDtypeStruct((rows, span), F32),
-        compiler_params=kernel_params(),
-        cost_estimate=costs(2 * rows * span * span, 8 * rows * span),
+            spread = table(to == want)
+            total = total + jnp.dot(refs[k][:rows, :], spread, preferred_element_type=F32)
+            start = pl.multiple_of((place ^ k) * small, small)
+            for f in range(folds):
+                lower[pl.ds(start, small), f * share : (f + 1) * share] = refs[k][
+                    rows + f * small : rows + (f + 1) * small, :
+                ].astype(F32)
+        upper[...] = total
+
+    return pl.pallas_call(
+        kernel,
+        out_shape=[
+            jax.ShapeDtypeStruct((rows, span), F32),
+            jax.ShapeDtypeStruct((count * small, folds * share), F32),
+        ],
+        compiler_params=kernel_params(),
+        cost_estimate=costs(0.8),
     )(*parts)
 
 
 def message_terms(left, right, parts, sides):
     rows, columns = left.shape[1] // parts, right.shape[1] // sides
-    if rows % 16:
-        terms = jnp.dot(left.T, right, preferred_element_type=F32).astype(BF16)
-        terms = terms.reshape(parts, rows, sides, columns).transpose(0, 2, 1, 3)
-        return terms.reshape(parts * sides, rows, columns)
-    step = max(1, 128 // rows)
-
-    def kernel(left_ref, right_ref, out):
-        for i in range(0, parts, step):
-            term = lax.dot_general(
-                left_ref[:, i * rows : (i + step) * rows],
-                right_ref[...],
-                (((0,), (0,)), ((), ())),
-                preferred_element_type=F32,
-            ).astype(BF16)
-            for k in range(step):
-                for j in range(sides):
-                    out[(i + k) * sides + j] = term[
-                        k * rows : (k + 1) * rows, j * columns : (j + 1) * columns
-                    ]
-
-    return pl.pallas_call(
-        kernel,
-        out_shape=jax.ShapeDtypeStruct((parts * sides, rows, columns), BF16),
-        compiler_params=kernel_params(),
-        cost_estimate=pl.CostEstimate(
-            flops=2 * left.size * right.shape[1],
-            bytes_accessed=2 * (left.size + right.size + left.shape[1] * right.shape[1]),
-            transcendentals=0,
-        ),
-    )(left, right)
+    terms = jnp.dot(left.T, right, preferred_element_type=F32).astype(BF16)
+    terms = terms.reshape(parts, rows, sides, columns).transpose(0, 2, 1, 3)
+    return terms.reshape(parts * sides, rows, columns)
 
 
 def regroup_columns(weight, lane, grouped, axis, count):
     rows, columns = weight.shape
     span = lane.shape[0]
     groups = columns // span
-    if rows % 16:
-        parts = jnp.dot(
-            weight.reshape(rows * groups, span), one_hot(grouped, lane), preferred_element_type=F32
-        ).astype(BF16)
-        parts = parts.reshape(rows, groups, count, 128).transpose(2, 0, 1, 3)
-        parts = parts.reshape(count, rows, groups * 128)
-        return [
-            lax.dynamic_index_in_dim(parts, lax.axis_index(axis) ^ k, 0, keepdims=False)
-            for k in range(count)
-        ]
-    small = rows
-
-    def kernel(weight_ref, *outs):
-        place = lax.axis_index(axis)
-        at = lax.broadcasted_iota(jnp.int32, (span, 128), 0)
-        to = lax.broadcasted_iota(jnp.int32, (span, 128), 1)
-        for k in range(count):
-            want = to // small * (small * count) + (place ^ k) * small + to % small
-            pick = jnp.where(at == want, 1.0, 0.0).astype(BF16)
-            for g in range(groups):
-                outs[k][:, g * 128 : (g + 1) * 128] = jnp.dot(
-                    weight_ref[:, g * span : (g + 1) * span], pick, preferred_element_type=F32
-                ).astype(BF16)
-
-    return pl.pallas_call(
-        kernel,
-        out_shape=[jax.ShapeDtypeStruct((rows, columns // count), BF16)] * count,
-        cost_estimate=pl.CostEstimate(
-            flops=2 * weight.size * span, bytes_accessed=4 * weight.size, transcendentals=0
-        ),
-    )(weight)
+    parts = jnp.dot(
+        weight.reshape(rows * groups, span), one_hot(grouped, lane), preferred_element_type=F32
+    ).astype(BF16)
+    parts = parts.reshape(rows, groups, count, 128).transpose(2, 0, 1, 3)
+    parts = parts.reshape(count, rows, groups * 128)
+    return [
+        lax.dynamic_index_in_dim(parts, lax.axis_index(axis) ^ k, 0, keepdims=False)
+        for k in range(count)
+    ]
 
 
 def stem_backward(own, parts, stem_pre, grad_out, gain, extra):
@@ -363,9 +364,7 @@
         kernel,
         out_shape=jax.ShapeDtypeStruct((block + extra, channels), BF16),
         compiler_params=kernel_params(),
-        cost_estimate=pl.CostEstimate(
-            flops=30 * own.size, bytes_accessed=14 * own.size, transcendentals=0
-        ),
+        cost_estimate=costs(0.7),
     )(own, stem_pre, grad_out, gain, *parts)
 
 
@@ -375,9 +374,11 @@
     return (centered * inverse, inverse)
 
 
-def gather_parts(value, axis, chains):
+def gather_parts(value, axis, chains, first=None):
     if list(chains) == [(2, 2), (1, 2)]:
         far = swap(value, axis, 2)
+        if first is not None:
+            far = after(far, first)
         return [value, swap(value, axis, 1), far, swap(far, axis, 1)]
     return [value] + [swap(value, axis, k) for k in range(1, lax.axis_size(axis))]
 
@@ -386,75 +387,114 @@
     return [value] + [swap(value, axis, k) for k in range(1, lax.axis_size(axis))]
 
 
-def split_parts(parts, axis, stride, size, dim, cut):
+def split_parts(parts, axis, stride, size, dim, cuts):
     shape = parts[0].shape
     lead = shape[:dim] + (size,) + shape[dim:-2]
-    rows, width = shape[-2:]
-    chunks = (width - cut) // 128
+    rows = shape[-2]
 
     def kernel(*refs):
         place = (lax.axis_index(axis) // stride) % size
+        inner = (slice(None),) * (len(lead) - dim - 1)
         for k in range(size):
-            target = (slice(None),) * dim + (place ^ k,)
-            refs[size][target] = refs[k][..., :cut]
-            for q in range(chunks):
-                inner = (slice(None),) * (len(lead) - dim - 1) + (q,)
-                lanes = slice(cut + q * 128, cut + (q + 1) * 128)
-                refs[size + 1][target + inner] = refs[k][..., lanes]
+            target = (slice(None),) * dim + (place ^ k,) + inner
+            start = 0
+            for n, (width, pieces) in enumerate(cuts):
+                for q in range(pieces):
+                    refs[size + n][target + (q,)] = refs[k][..., start : start + width]
+                    start += width
 
     return pl.pallas_call(
         kernel,
         out_shape=[
-            jax.ShapeDtypeStruct(lead + (rows, cut), parts[0].dtype),
-            jax.ShapeDtypeStruct(lead + (chunks, rows, 128), parts[0].dtype),
+            jax.ShapeDtypeStruct(lead + (pieces, rows, width), parts[0].dtype)
+            for width, pieces in cuts
         ],
         compiler_params=kernel_params(),
-        cost_estimate=costs(0, 4 * size * parts[0].size),
+        cost_estimate=costs(1.0),
     )(*parts)
 
 
-def split_gather(value, axis, chains, cut):
-    for dim, (stride, size) in enumerate(chains):
+def split_rest(value, axis, chains, cuts):
+    for dim, (stride, size) in enumerate(chains[1:], 1):
         parts = [value] + [swap(value, axis, k * stride) for k in range(1, size)]
         if dim == len(chains) - 1:
-            left, beyond = split_parts(parts, axis, stride, size, dim, cut)
-        else:
-            value = place_parts(parts, axis, stride, size, dim)
-    return left.reshape((-1,) + left.shape[-2:]), beyond.reshape(-1, 128)
-
-
-def prepare(mel, owner, slot, stem, up, taps, gain_one, gain_two, dp_count, tm_count):
+            return split_parts(parts, axis, stride, size, dim, cuts)
+        value = place_parts(parts, axis, stride, size, dim)
+
+
+def iota(shape, dim):
+    return lax.broadcasted_iota(jnp.int32, shape, dim)
+
+
+def table(flags):
+    return jnp.where(flags, 1.0, 0.0).astype(BF16)
+
+
+def fetch(sources, held, sems):
+    copies = [
+        pltpu.make_async_copy(source, target, sems.at[k])
+        for k, (source, target) in enumerate(zip(sources, held))
+    ]
+    for copy in copies:
+        copy.start()
+    for copy in copies:
+        copy.wait()
+
+
+def fetching_call(kernel, inputs, out_shape, cost):
+    return pl.pallas_call(
+        kernel,
+        out_shape=out_shape,
+        in_specs=[pl.BlockSpec(memory_space=pl.ANY)] * len(inputs),
+        scratch_shapes=[pltpu.VMEM(value.shape, value.dtype) for value in inputs]
+        + [pltpu.SemaphoreType.DMA((len(inputs),))],
+        cost_estimate=cost,
+    )(*inputs)
+
+
+def up_columns(up, rows, tm_count):
+    span = 128 * tm_count
+    groups = up.shape[1] // span
+
+    def kernel(source, *refs):
+        up_parts, (up_ref, sems) = refs[:tm_count], refs[tm_count:]
+        fetch([source], [up_ref], sems)
+        place = lax.axis_index("tm")
+        at, to = iota((span, 128), 0), iota((span, 128), 1)
+        for k in range(tm_count):
+            want = to // rows * (rows * tm_count) + (place ^ k) * rows + to % rows
+            pick = table(at == want)
+            for g in range(groups):
+                up_parts[k][:, g * 128 : (g + 1) * 128] = jnp.dot(
+                    up_ref[:, g * span : (g + 1) * span], pick, preferred_element_type=F32
+                ).astype(BF16)
+
+    return fetching_call(
+        kernel,
+        (up,),
+        [jax.ShapeDtypeStruct((rows, up.shape[1] // tm_count), BF16)] * tm_count,
+        costs(1.5),
+    )
+
+
+def prepare(mel, owner, slot, stem, down, taps, gain_one, gain_two, dp_count):
     pieces, values = mel.shape
     capacity = max(2, 2 * pieces // dp_count)
     slots = dp_count * capacity
     stem_rows, channels = stem.shape
     rows, tap_count = taps.shape
     chunks = rows // stem_rows
-    span = 128 * tm_count
-    groups = up.shape[1] // span
+    beyond = channels + 128 * (chunks + 1)
     inputs = (
-        up, stem, taps, gain_one[None, :], gain_two[None, :], owner[None, :], slot[None, :], mel
+        stem, taps, gain_one[None, :], gain_two[None, :], owner[None, :], slot[None, :], mel, down
     )
     count = len(inputs)
 
     def kernel(*refs):
-        sent, pack, *up_parts = refs[count : count + 2 + tm_count]
-        held = refs[count + 2 + tm_count : -1]
-        copies = [
-            pltpu.make_async_copy(refs[k], held[k], refs[-1].at[k]) for k in range(count)
-        ]
-        for copy in copies:
-            copy.start()
-        up_ref, stem_ref, taps_ref, one_ref, two_ref, owner_ref, slot_ref, mel_ref = held
-
-        def iota(shape, dim):
-            return lax.broadcasted_iota(jnp.int32, shape, dim)
-
-        def table(flags):
-            return jnp.where(flags, 1.0, 0.0).astype(BF16)
-
-        for copy in copies:
-            copy.wait()
+        sent, pack = refs[count : count + 2]
+        held = refs[count + 2 : -1]
+        fetch(refs[:count], held, refs[-1])
+        stem_ref, taps_ref, one_ref, two_ref, owner_ref, slot_ref, mel_ref, down_ref = held
         pack[:, :channels] = stem_ref[...]
         lane = iota((rows, 128), 1)
         spread = table(lane % rows == iota((rows, 128), 0))
@@ -472,17 +512,8 @@
         for q in range(chunks):
             lanes = slice(channels + 128 * (q + 1), channels + 128 * (q + 2))
             pack[:, lanes] = small[q * stem_rows : (q + 1) * stem_rows].astype(BF16)
-
-        place = lax.axis_index("tm")
-        at = iota((span, 128), 0)
-        to = iota((span, 128), 1)
-        for k in range(tm_count):
-            want = to // rows * (rows * tm_count) + (place ^ k) * rows + to % rows
-            pick = table(at == want)
-            for g in range(groups):
-                up_parts[k][:, g * 128 : (g + 1) * 128] = jnp.dot(
-                    up_ref[:, g * span : (g + 1) * span], pick, preferred_element_type=F32
-                ).astype(BF16)
+            lanes = slice(beyond + channels * q, beyond + channels * (q + 1))
+            pack[:, lanes] = down_ref[q * stem_rows : (q + 1) * stem_rows, :]
 
         owners = jnp.broadcast_to(owner_ref[...].astype(F32), (pieces, pieces))
         earlier = iota((pieces, pieces), 0) < iota((pieces, pieces), 1)
@@ -496,19 +527,15 @@
         label = jnp.sum(jnp.where(chosen, labels, 0.0), axis=1, keepdims=True)
         sent[:, values:] = jnp.broadcast_to(label, (slots, 128)).astype(BF16)
 
-    outs = pl.pallas_call(
-        kernel,
-        out_shape=[
+    return fetching_call(
+        kernel,
+        inputs,
+        [
             jax.ShapeDtypeStruct((slots, values + 128), BF16),
-            jax.ShapeDtypeStruct((stem_rows, channels + 128 * (chunks + 1)), BF16),
-        ]
-        + [jax.ShapeDtypeStruct((rows, up.shape[1] // tm_count), BF16)] * tm_count,
-        in_specs=[pl.BlockSpec(memory_space=pl.ANY)] * count,
-        scratch_shapes=[pltpu.VMEM(value.shape, value.dtype) for value in inputs]
-        + [pltpu.SemaphoreType.DMA((count,))],
-        cost_estimate=costs(1 << 27, 2 << 20),
-    )(*inputs)
-    return outs[0], outs[1], list(outs[2:])
+            jax.ShapeDtypeStruct((stem_rows, beyond + channels * chunks), BF16),
+        ],
+        costs(2.0),
+    )
 
 
 def place_frames(arrived, pieces, features):
@@ -531,7 +558,7 @@
         kernel,
         out_shape=jax.ShapeDtypeStruct((pieces * steps, features), BF16),
         compiler_params=kernel_params(),
-        cost_estimate=costs(2 * arrived.size * pieces * steps, 4 * arrived.size),
+        cost_estimate=costs(0.6),
     )(arrived)
 
 
@@ -596,7 +623,7 @@
             jax.ShapeDtypeStruct((count, share + extra, block + extra), BF16),
         ],
         compiler_params=kernel_params(),
-        cost_estimate=costs(2 * frames.size * channels, 2 * stem_all.size + 4 * frames.size),
+        cost_estimate=costs(2.8),
     )(frames, stem_all)
 
 
@@ -627,7 +654,7 @@
             jax.ShapeDtypeStruct((length + 2 * PAD, held), F32),
         ],
         compiler_params=kernel_params(),
-        cost_estimate=costs(4 * normed.size * held, 2 * normed.size + 2 * up.size),
+        cost_estimate=costs(0.7),
     )(normed, up)
 
 
@@ -688,7 +715,7 @@
             pltpu.VMEM((TILE + 2 * PAD, 128), jnp.int32),
         ],
         compiler_params=kernel_params(),
-        cost_estimate=costs(4 * taps * gated.size, 8 * gated.size),
+        cost_estimate=costs(3.0),
     )(gated, small, segments)
 
 
@@ -734,7 +761,7 @@
             jax.ShapeDtypeStruct((1, held), F32),
         ],
         compiler_params=kernel_params(),
-        cost_estimate=costs(40 * conv.size, 20 * conv.size),
+        cost_estimate=costs(0.7),
     )(conv, turned, grad_act, *stats)
 
 
@@ -809,7 +836,7 @@
             pltpu.VMEM((TILE + 2 * PAD, 128), jnp.int32),
         ],
         compiler_params=kernel_params(),
-        cost_estimate=costs(8 * taps * hat.size, 24 * hat.size),
+        cost_estimate=costs(6.2),
     )(grad_hat, hat, inverse, gated, segments, linear, gate, turned, gain_term, *sums)
 
 
@@ -852,7 +879,7 @@
         kernel,
         out_shape=[jax.ShapeDtypeStruct((dp_count // size, height, channels), BF16)] * size,
         compiler_params=kernel_params(),
-        cost_estimate=costs(2 * turned.size * channels, 4 * count * width * channels),
+        cost_estimate=costs(1.2),
     )(turned, small, *parts)
 
 
@@ -891,7 +918,7 @@
             jax.ShapeDtypeStruct((1, rows), F32),
         ],
         compiler_params=kernel_params(),
-        cost_estimate=costs(1 << 24, 2 * count * parts[0].size),
+        cost_estimate=costs(1.2),
     )(*parts)
 
 
@@ -940,13 +967,18 @@
     features = stem_rows * dp_count * tm_count
     length = block * tm_count
 
+    sums_chains = ((4, 2), (2, 2), (1, 2))
+
+    by_parts = stem_rows % 16 == 0 and rows % 16 == 0 and dp_chains == ((2, 4), (1, 2))
     span = 128 * tm_count
     lane = jnp.arange(span, dtype=jnp.int32)
     grouped = (lane // rows) % tm_count * 128 + lane // (rows * tm_count) * rows + lane % rows
-    if stem_rows % 16 == 0 and rows % 16 == 0:
-        sent, pack, up_parts = prepare(
-            mel_pieces[0], dest_owner[0], dest_slot[0], stem_weight, up_weight, depth_kernel,
-            gain_pre, gain_post, dp_count, tm_count,
+    chunks = rows // stem_rows
+    if by_parts:
+        up_parts = up_columns(up_weight, rows, tm_count)
+        sent, pack = prepare(
+            mel_pieces[0], dest_owner[0], dest_slot[0], after(stem_weight, up_parts[0]),
+            down_weight, depth_kernel, gain_pre, gain_post, dp_count,
         )
     else:
         sent = order_pieces(mel_pieces[0], dest_owner[0], dest_slot[0], dp_count)
@@ -955,31 +987,49 @@
         small = jnp.concatenate(
             [depth_kernel, gain_post[:, None], jnp.zeros((rows, 128 - taps - 1), BF16)], axis=1
         )
-        small = [small[q : q + stem_rows] for q in range(0, rows, stem_rows)]
-        pack = jnp.concatenate([stem_weight, beside] + small, axis=1)
-
-    stem_mine, small_all = split_gather(pack, "dp", dp_chains, channels + 128)
+        folded = [
+            value[q : q + stem_rows]
+            for value in (small, down_weight)
+            for q in range(0, rows, stem_rows)
+        ]
+        pack = jnp.concatenate([stem_weight, beside] + folded, axis=1)
+
     up_parts = [up_parts[0]] + [swap(up_parts[k], "tm", k) for k in range(1, tm_count)]
     up_mine = place_parts(up_parts, "tm", 1, tm_count, 0).reshape(tm_count * rows, 2 * held)
-    up_near = gather_stage(up_mine, "dp", *dp_chains[0], 0)
-    up_full = gather_rest(up_near, "dp", dp_chains).reshape(channels, 2 * held)
-    down_near = gather_stage(after(down_weight, up_near), "dp", *dp_chains[0], 0)
-    down_full = gather_rest(down_near, "dp", dp_chains).reshape(held, channels)
-    stem_parts = gather_parts(stem_mine, "tm", tm_chains)
-    stem_all = place_parts(stem_parts, "tm", 1, tm_count, 1)
-    stem_all = stem_all.reshape(features, channels + 128)
+    pack_near = gather_stage(pack, "dp", *dp_chains[0], 0)
+    up_sides = swap_parts([up_mine] * dp_chains[0][1], "dp", dp_chains[0])
+    stem_mine, small_all, down_full = split_rest(
+        pack_near, "dp", dp_chains, ((channels + 128, 1), (128, chunks), (channels, chunks))
+    )
+    stem_mine = stem_mine.reshape(dp_count, stem_rows, channels + 128)
+    small_all = small_all.reshape(held, 128)
+    down_full = down_full.reshape(held, channels)
 
     pieces = mel_pieces.shape[1]
     capacity = max(2, 2 * pieces // dp_count)
     arrived = lax.all_to_all(
-        after(sent, up_mine, stem_mine).reshape(dp_count, capacity, -1), "dp", split_axis=0, concat_axis=0, tiled=True
+        after(sent, pack_near, up_sides[1]).reshape(dp_count, capacity, -1),
+        "dp",
+        split_axis=0,
+        concat_axis=0,
+        tiled=True,
     ).reshape(dp_count * capacity, -1)
-    frames = place_frames(arrived, pieces, features)
-    frames = place_parts(gather_parts(frames, "tm", tm_chains), "tm", 1, tm_count, 0)
-    frames = frames.reshape(length, features)
+    up_near = place_parts(up_sides, "dp", *dp_chains[0], 0)
+    frames = place_frames(after(arrived, up_near), pieces, features)
+    frame_parts = gather_parts(frames, "tm", tm_chains)
+    stem_parts = gather_parts(stem_mine, "tm", tm_chains, frames)
+    frames = place_parts(frame_parts, "tm", 1, tm_count, 0).reshape(length, features)
+    stem_all = place_parts(stem_parts, "tm", 1, tm_count, 1)
+    stem_all = stem_all.reshape(features, channels + 128)
+
     grad_out = out_grad[0]
-    grad_out_all = gather_parts(after(grad_out, stem_parts[2]), "tm", tm_chains)
-    grad_out_all = place_parts(grad_out_all, "tm", 1, tm_count, 0).reshape(length, channels)
+    grad_first = after(grad_out, stem_parts[2])
+    hierarchical = list(tm_chains) == [(2, 2), (1, 2)]
+    if hierarchical:
+        grad_parts = [grad_first, swap(grad_first, "tm", 1), swap(grad_first, "tm", 2)]
+    else:
+        grad_parts = gather_parts(grad_first, "tm", tm_chains)
+
     segments = jnp.pad(segment_ids[0], (PAD, PAD), constant_values=-1)
     segments = jnp.broadcast_to(segments[:, None], (length + 2 * PAD, 128))
 
@@ -987,82 +1037,74 @@
     normed, stem_pre, gain_one, frames_turned = stem_forward(
         frames, stem_all, tm_count, "tm", rows, extra
     )
+    up_full = gather_rest(up_near, "dp", dp_chains).reshape(channels, 2 * held)
+    grad_parts = lax.optimization_barrier((grad_parts, normed))[0]
+    if hierarchical:
+        grad_parts = grad_parts + [swap(grad_parts[2], "tm", 1)]
     linear, gate_sig, gated = up_forward(normed, up_full)
     conv, stats, turned = conv_forward(gated, small_all, segments, taps)
+    stats = swap_all(stats, "tm")
+    grad_parts = lax.optimization_barrier((grad_parts, conv))[0]
+    grad_out_all = place_parts(grad_parts, "tm", 1, tm_count, 0).reshape(length, channels)
     grad_act = lax.dot_general(
         grad_out_all, down_full, (((1,), (1,)), ((), ())), preferred_element_type=F32
     )
     activated, conv_hat, grad_hat, inverse, sums, gain_post_term = activate(
-        conv, swap_all(stats, "tm"), turned, grad_act, taps
+        conv, stats, turned, grad_act, taps
     )
     sums = swap_all(sums, "tm")
-    by_parts = stem_rows % 16 == 0 and rows % 16 == 0
     if by_parts:
-        down_terms = part_terms(activated, grad_out_all, "dp", dp_chains)
+        down_terms = part_terms(activated, grad_out_all, False, "dp", sums_chains)
+        normed_turned = turn(normed)
+        grad_hat = after(grad_hat, normed_turned)
     else:
         down_terms = [message_terms(activated, grad_out_all, dp_count, tm_count)]
-    y_own, *y_others = block_terms(activated, down_full, False, "tm", tm_count)
-    down_terms, y_others = lax.optimization_barrier((down_terms, y_others, *sums))[:2]
-    y_far, y_parts, y_passed = block_sum(y_others, "tm", tm_chains)
+    down_terms = lax.optimization_barrier((down_terms, *sums))[0]
     if by_parts:
-        down_parts = swap_parts(down_terms, "dp", dp_chains[-1])
-
-    grad_hat = after(grad_hat, *down_terms, y_passed)
+        down_parts = swap_parts(down_terms, "dp", sums_chains[-1])
+
+    grad_hat = after(grad_hat, *down_terms)
     grad_proj, kernel_term = conv_backward(
         grad_hat, conv_hat, inverse, sums, gated, segments, linear, gate_sig, turned, taps,
         gain_post_term,
     )
 
     own_terms, *other_terms = block_terms(
-        after(grad_proj, y_far), up_full, True, "tm", tm_count
-    )
-    small_term = kernel_term.reshape(taps + 1, dp_count, rows).transpose(1, 0, 2)
-    small_term = small_term.reshape(dp_count, (taps + 1) * rows)
-    small_term = jnp.pad(small_term, ((0, 0), (0, channels - (taps + 1) * rows)))
+        after(grad_proj, *down_parts[1:]) if by_parts else grad_proj, up_full, True, "tm", tm_count
+    )
     if by_parts:
-        up_terms = part_terms(after(normed, *other_terms), grad_proj, "dp", dp_chains)
+        up_terms = part_terms(
+            after(normed_turned, *other_terms), grad_proj, True, "dp", sums_chains
+        )
+        up_parts = swap_parts(up_terms, "dp", sums_chains[-1])
     else:
         up_terms = [message_terms(normed, grad_proj, dp_count, tm_count)]
     grad_far, grad_parts, grad_passed = block_sum(other_terms, "tm", tm_chains, up_terms[-1])
-    if by_parts:
-        down_parts = add_parts(
-            [after(down_parts[0], grad_passed)] + down_parts[1:], "dp", dp_chains[0]
-        )
-        down_parts = swap_parts(down_parts, "dp", dp_chains[0])
-        up_parts = reduce_parts(up_terms, "dp", dp_chains)
+    small_term = after(kernel_term, grad_passed)
+    small_term = small_term.reshape(taps + 1, dp_count, rows).transpose(1, 0, 2)
+    small_term = small_term.reshape(dp_count, (taps + 1) * rows)
+    small_term = jnp.pad(small_term, ((0, 0), (0, channels - (taps + 1) * rows)))
+    y_own, *y_others = block_terms(
+        after(activated, grad_passed), down_full, False, "tm", tm_count
+    )
     grad_stem_pre = stem_backward(
         own_terms, grad_parts + [grad_far], stem_pre, grad_out, gain_one, extra
     )
-    grad_stem_parts = gather_parts(grad_stem_pre, "tm", tm_chains)
-    y_out = finish_rows(after(stem_pre, grad_stem_pre), y_own, y_parts + [y_far])
+    if by_parts:
+        up_parts = join_parts(
+            [after(up_parts[0], grad_stem_pre)] + up_parts[1:], down_parts, "dp", sums_chains[1]
+        )
+        grad_stem_parts = gather_parts(grad_stem_pre, "tm", tm_chains, up_parts[-1])
+        up_parts = reduce_rest(up_parts, "dp", sums_chains[:2])
+    else:
+        grad_stem_parts = gather_parts(grad_stem_pre, "tm", tm_chains)
+    y_far, y_parts, _ = block_sum(y_others, "tm", tm_chains, grad_stem_parts[2])
     if by_parts:
         stem_terms = stem_message(
-            frames_turned, grad_stem_parts, small_term, "dp", dp_chains, stem_rows
-        )
-        stem_sums = reduce_parts(stem_terms, "dp", dp_chains)
-        down_parts = cut_columns([after(down_parts[0], grad_stem_pre)] + down_parts[1:], "tm")
-        down_parts = [down_parts[0]] + [
-            swap(part, "tm", k) for k, part in enumerate(down_parts[1:], 1)
-        ]
-        grad_down = stack_rows(down_parts, "tm")
-        up_parts = cut_columns(up_parts, "tm")
-        up_parts = [up_parts[0]] + [
-            swap(part, "tm", k) for k, part in enumerate(up_parts[1:], 1)
-        ]
-        grad_up = mix_columns(up_parts, "tm", rows)
+            frames_turned, grad_stem_parts, small_term, "dp", sums_chains, stem_rows
+        )
+        stem_sums = reduce_rest(stem_terms, "dp", sums_chains)
     else:
-        down_sums = lax.all_to_all(
-            down_terms[0], ("dp", "tm"), split_axis=0, concat_axis=0, tiled=True
-        )
-        grad_down = jnp.sum(
-            down_sums.reshape(dp_count, tm_count * rows, held).astype(F32), axis=0
-        )
-        up_sums = lax.all_to_all(
-            up_terms[0], ("dp", "tm"), split_axis=0, concat_axis=0, tiled=True
-        )
-        up_sums = up_sums.reshape(dp_count, tm_count, tm_count * rows, 128)
-        spread = one_hot(lane, grouped).reshape(tm_count, 128, span)
-        grad_up = jnp.einsum("ijab,jbc->ac", up_sums, spread, preferred_element_type=F32)
         stem_sum = sum(
             jnp.dot(frames_turned[k], grad_stem_parts[k], preferred_element_type=F32)
             for k in range(tm_count)
@@ -1076,6 +1118,24 @@
         stem_sums = [
             lax.all_to_all(stem_terms, "dp", split_axis=0, concat_axis=0, tiled=True)
         ]
+    if by_parts:
+        up_parts = cut_columns([after(up_parts[0], *stem_terms)] + up_parts[1:], "tm", tm_count * rows, rows)
+        up_parts = swap_all_parts(up_parts, "tm")
+        grad_up, grad_down = mix_columns(up_parts, "tm", tm_count * rows, rows)
+    else:
+        down_sums = lax.all_to_all(
+            down_terms[0], ("dp", "tm"), split_axis=0, concat_axis=0, tiled=True
+        )
+        grad_down = jnp.sum(
+            down_sums.reshape(dp_count, tm_count * rows, held).astype(F32), axis=0
+        )
+        up_sums = lax.all_to_all(
+            up_terms[0], ("dp", "tm"), split_axis=0, concat_axis=0, tiled=True
+        )
+        up_sums = up_sums.reshape(dp_count, tm_count, tm_count * rows, 128)
+        spread = one_hot(lane, grouped).reshape(tm_count, 128, span)
+        grad_up = jnp.einsum("ijab,jbc->ac", up_sums, spread, preferred_element_type=F32)
+    y_out = finish_rows(stem_pre, y_own, y_parts + [y_far])
     grad_stem, grad_kernel, grad_gain_post, grad_gain_pre = stem_finish(
         stem_sums, stem_rows, rows, taps, "tm"
     )

time: 154 us -> 132 us (0.86)
  starting transfers between devices: 54.7 us -> 44.5 us
  waiting for transfers between devices: 59.1 us -> 48.9 us
  Pallas kernels: 32.2 us -> 27 us
  local copies, waits for them, and re-layouts: 5.56 us -> 9.39 us
    ppermute x57 -> x45, waiting for transfers between devices: 59.1 us -> 40.2 us  [swap(): return lax.ppermute(value, axis, [(i, i ^ mask) for i in range(size)])]
    ppermute x57 -> x45, starting transfers between devices: 51.2 us -> 40.8 us  [swap(): return lax.ppermute(value, axis, [(i, i ^ mask) for i in range(size)])]
    all_to_all x1, waiting for transfers between devices: 0.01 us -> 8.68 us  [per_device(): lax.all_to_all(after(sent, pack_near, up_sides[1]).reshape(dp_count, capa...]
    pallas_call x2, Pallas kernels: 4.61 us -> 1.93 us  [part_terms(): pl.pallas_call(kernel, out_shape=[jax.ShapeDtypeStruct((total // size, ro...]
    unnamed x20 -> x42, local copies, waits for them, and re-layouts: 2.9 us -> 5.26 us
    reshape x2, local copies, waits for them, and re-layouts: 0.77 us -> 2.33 us  [per_device(): small_term = small_term.reshape(taps + 1, dp_count, rows).transpose(1, 0, 2)]
    pallas_call x6 -> x7, Pallas kernels: 4.32 us -> 5.85 us  [the longest x2 4.05 us: fetching_call(): pl.pallas_call(kernel, out_shape=out_shape, in_specs=[pl.BlockSpec(memory...]
  transfers between devices with their start and end apart: 58 -> 46, of which waited for: 23 -> 18; matrix products, arithmetic and copies ran while one was open for 2% -> 4% of each run, Pallas kernels for 17% -> 17%
where the time goes in v4:
time: 132 us; the launch traced here: 131 us
  waiting for transfers between devices  48.9 us (37%)
  starting transfers between devices  44.5 us (34%)
  Pallas kernels  27 us (20%)
  local copies, waits for them, and re-layouts  9.39 us (7%)
    ppermute x45, starting transfers between devices, swap(): return lax.ppermute(value, axis, [(i, i ^ mask) for i in range(size)])  40.8 us
    ppermute x45, waiting for transfers between devices, swap(): return lax.ppermute(value, axis, [(i, i ^ mask) for i in range(size)])  40.2 us
    all_to_all x1, waiting for transfers between devices, per_device(): lax.all_to_all(after(sent, pack_near, up_sides[1]).reshape(dp_count, capa...  8.68 us
    pallas_call x1, Pallas kernels, conv_backward(): pl.pallas_call(kernel, out_shape=[jax.ShapeDtypeStruct((length, 2 * held)...  6.18 us
    unnamed x42, local copies, waits for them, and re-layouts  5.26 us
    pallas_call x2, Pallas kernels, fetching_call(): pl.pallas_call(kernel, out_shape=out_shape, in_specs=[pl.BlockSpec(memory...  4.05 us
    all_to_all x1, starting transfers between devices, per_device(): lax.all_to_all(after(sent, pack_near, up_sides[1]).reshape(dp_count, capa...  3.75 us
    pallas_call x1, Pallas kernels, conv_forward(): pl.pallas_call(kernel, out_shape=[jax.ShapeDtypeStruct((length, held), F3...  2.97 us
  transfers between devices with their start and end apart: 46, of which 18 were waited for; matrix products, arithmetic and copies ran while one was open for 4% of the time, Pallas kernels for 17%

profile of v4, /device:TPU:0, one launch (start us, length us, event | category | flops | bytes accessed | tf_op | source)
XLA Modules:
  0.0 131.4 jit_solution(3127041980599969420)
XLA Ops:
  0.6 2.0 %shard_map.162 = (bf16[32,512]{1,0:T(8,128)(2,1)}, bf16[32,512]{1,0:T(8,128)(2,1)}, bf16[32,512]{1,0:T(8,128)(2,1)}, bf16[32,512]{1,0:T(8,128)(2,1)}) custom-call(bf16[32,2048]{1,0:T(8,128)(2,1)} %source.1), custom_call_target="tpu_custom_call" | custom-call | flops 30000001024 | bytes 65536 | tf_op jit(solution)/shard_map/pallas_call | solution.py:445
  3.1 2.6 %collective-permute-start.4 = (bf16[32,512]{1,0:T(8,128)(2,1)}, bf16[32,512]{1,0:T(8,128)(2,1)S(1)}, u32[]{:S(2)}, u32[]{:S(2)}) collective-permute-start(bf16[32,512]{1,0:T(8,128)(2,1)} %get-tuple-element.96), channel_id=1, source_target_pairs={{0,2},{1,3},{2,0},{3,1},{4,6},{5,7},{6,4},{7,5},{8,10},{9,11},{10,... | collective-permute-start | bytes 98312 | tf_op jit(solution)/shard_map/ppermute | solution.py:23
  5.8 2.1 %shard_map.163 = (bf16[64,2176]{1,0:T(8,128)(2,1)}, bf16[16,3456]{1,0:T(8,128)(2,1)}) custom-call(bf16[16,1024]{1,0:T(8,128)(2,1)} %refs_0_, bf16[32,31]{1,0:T(8,128)(2,1)} %refs_1_.1, bf16[1,32]{1,0:T(2,128)(2,1)} %bitcast.47, bf16[1,32]{1,0:T(2,128)(2,1)} %bitcast.48, s32[1,32]{1,0:T(1,128)} %refs_4_.1, s32[1,32]{1,0:T(1,128)} %refs_5_.1, ...), custom_call_target="tpu_custom_call" | custom-call | flops 40000000000 | bytes 65536 | tf_op jit(solution)/shard_map/pallas_call | solution.py:445
  7.9 3.9 %collective-permute-start.2 = (bf16[16,3456]{1,0:T(8,128)(2,1)}, bf16[16,3456]{1,0:T(8,128)(2,1)S(1)}, u32[]{:S(2)}, u32[]{:S(2)}) collective-permute-start(bf16[16,3456]{1,0:T(8,128)(2,1)} %get-tuple-element.94.refs_0_), channel_id=1, source_target_pairs={{0,24},{4,28},{8,16},{12,20},{16,8},{20,12},{24,0},{28,4},{1,25},{... | collective-permute-start | bytes 331784 | tf_op jit(solution)/shard_map/ppermute | solution.py:23
  13.1 3.8 %collective-permute-start.8 = (bf16[128,512]{1,0:T(8,128)(2,1)S(1)}, bf16[128,512]{1,0:T(8,128)(2,1)S(1)}, u32[]{:S(2)}, u32[]{:S(2)}) collective-permute-start(bf16[128,512]{1,0:T(8,128)(2,1)S(1)} %bitcast.35), channel_id=1, source_target_pairs={{0,24},{4,28},{8,16},{12,20},{16,8},{20,12},{24,0},{28,4},{1,25},{... | collective-permute-start | bytes 393224 | tf_op jit(solution)/shard_map/ppermute | solution.py:23
  16.9 4.0 %collective-permute-start.6 = (bf16[128,512]{1,0:T(8,128)(2,1)S(1)}, bf16[128,512]{1,0:T(8,128)(2,1)S(1)}, u32[]{:S(2)}, u32[]{:S(2)}) collective-permute-start(bf16[128,512]{1,0:T(8,128)(2,1)S(1)} %bitcast.37), channel_id=1, source_target_pairs={{0,8},{4,12},{8,0},{12,4},{16,24},{20,28},{24,16},{28,20},{1,9},{5... | collective-permute-start | bytes 393224 | tf_op jit(solution)/shard_map/ppermute | solution.py:23
  20.9 7.1 %collective-permute-done.1.refs_2_ = bf16[16,3456]{1,0:T(8,128)(2,1)S(1)} collective-permute-done((bf16[16,3456]{1,0:T(8,128)(2,1)}, bf16[16,3456]{1,0:T(8,128)(2,1)S(1)}, u32[]{:S(2)}, u32[]{:S(2)}) %collective-permute-start.1) | collective-permute-done | bytes 110624 | tf_op jit(solution)/shard_map/ppermute | solution.py:23
  29.6 3.8 %all-to-all-start = ((bf16[8,8,2176]{2,1,0:T(8,128)(2,1)}), bf16[8,8,2176]{2,1,0:T(8,128)(2,1)S(1)}, u32[]{:S(2)}, u32[]{:S(2)}) async-start(bf16[8,8,2176]{2,1,0:T(8,128)(2,1)} %bitcast.4), calls=%async_computation | async-start | bytes 557056 | tf_op jit(solution)/shard_map/all_to_all | solution.py:1010
  33.5 2.1 %collective-permute-start.16 = (bf16[4,128,512]{2,1,0:T(8,128)(2,1)S(1)}, bf16[4,128,512]{2,1,0:T(8,128)(2,1)S(1)}, u32[]{:S(2)}, u32[]{:S(2)}) collective-permute-start(bf16[4,128,512]{2,1,0:T(8,128)(2,1)S(1)} %shard_map.166.refs_0_), channel_id=1, source_target_pairs={{0,4},{4,0},{8,12},{12,8},{16,20},{20,16},{24,28},{28,24},{1,5},{5... | collective-permute-start | bytes 1572872 | tf_op jit(solution)/shard_map/ppermute | solution.py:23
  35.6 8.7 %all-to-all-done = bf16[8,8,2176]{2,1,0:T(8,128)(2,1)S(1)} async-done(((bf16[8,8,2176]{2,1,0:T(8,128)(2,1)}), bf16[8,8,2176]{2,1,0:T(8,128)(2,1)S(1)}, u32[]{:S(2)}, u32[]{:S(2)}) %all-to-all-start) | async-done | bytes 278560 | tf_op jit(solution)/shard_map/all_to_all | solution.py:1010
  47.4 2.3 %collective-permute-done.10.refs_2_ = bf16[128,512]{1,0:T(8,128)(2,1)S(1)} collective-permute-done((bf16[128,512]{1,0:T(8,128)(2,1)S(1)}, bf16[128,512]{1,0:T(8,128)(2,1)S(1)}, u32[]{:S(2)}, u32[]{:S(2)}) %collective-permute-start.10) | collective-permute-done | bytes 131104 | tf_op jit(solution)/shard_map/ppermute | solution.py:23
  49.6 3.8 %collective-permute-done.16.refs_1_ = bf16[4,128,512]{2,1,0:T(8,128)(2,1)S(1)} collective-permute-done((bf16[4,128,512]{2,1,0:T(8,128)(2,1)S(1)}, bf16[4,128,512]{2,1,0:T(8,128)(2,1)S(1)}, u32[]{:S(2)}, u32[]{:S(2)}) %collective-permute-start.16) | collective-permute-done | bytes 524320 | tf_op jit(solution)/shard_map/ppermute | solution.py:23
  53.5 1.6 %collective-permute-start.18 = (bf16[128,1024]{1,0:T(8,128)(2,1)S(1)}, bf16[128,1024]{1,0:T(8,128)(2,1)S(1)}, u32[]{:S(2)}, u32[]{:S(2)}) collective-permute-start(bf16[128,1024]{1,0:T(8,128)(2,1)S(1)} %bitcast.31), channel_id=1, source_target_pairs={{0,2},{1,3},{2,0},{3,1},{4,6},{5,7},{6,4},{7,5},{8,10},{9,11},{10,... | collective-permute-start | bytes 786440 | tf_op jit(solution)/shard_map/ppermute | solution.py:23
  57.2 2.7 %shard_map.171 = (bf16[512,1024]{1,0:T(8,128)(2,1)S(1)}, f32[128,1024]{1,0:T(8,128)S(1)}, f32[1,1024]{1,0:T(1,128)S(1)}, bf16[4,144,144]{2,1,0:T(8,128)(2,1)S(1)}) custom-call(bf16[512,512]{1,0:T(8,128)(2,1)S(1)} %bitcast.42, bf16[512,1152]{1,0:T(8,128)(2,1)S(1)} %bitcast.39), custom_call_target="tpu_custom_call" | custom-call | flops 56000000000 | bytes 65536 | tf_op jit(solution)/shard_map/pallas_call | solution.py:617
  61.1 3.0 %shard_map.174 = (f32[512,256]{1,0:T(8,128)S(1)}, f32[8,512]{1,0:T(8,128)S(1)}, f32[128,256]{1,0:T(8,128)S(1)}) custom-call(f32[544,256]{1,0:T(8,128)S(1)} %get-tuple-element.104.gated_ref, bf16[256,128]{1,0:T(8,128)(2,1)S(1)} %bitcast.43, s32[544,128]{1,0:T(8,128)S(1)} %broadcast_in_dim.17.seg_ref), custom_call_target="tpu_custom_call" | custom-call | flops 60000002048 | bytes 65536 | tf_op jit(solution)/shard_map/pallas_call | solution.py:706
  67.7 2.0 %collective-permute-done.21.refs_2_ = f32[8,512]{1,0:T(8,128)S(1)} collective-permute-done((f32[8,512]{1,0:T(8,128)S(1)}, f32[8,512]{1,0:T(8,128)S(1)}, u32[]{:S(2)}, u32[]{:S(2)}) %collective-permute-start.21) | collective-permute-done | bytes 16416 | tf_op jit(solution)/shard_map/ppermute | solution.py:23
  75.8 6.2 %shard_map.179 = (bf16[512,512]{1,0:T(8,128)(2,1)S(1)}, f32[32,256]{1,0:T(8,128)S(1)}) custom-call(f32[512,256]{1,0:T(8,128)S(1)} %get-tuple-element.126.grad_ref, f32[512,256]{1,0:T(8,128)S(1)} %get-tuple-element.127.hat_ref, f32[512,128]{1,0:T(8,128)S(1)} %get-tuple-element.128.inverse_ref, f32[544,256]{1,0:T(8,128)S(1)} %get-tuple-element.104.gated_ref, ...), custom_call_target="tpu_custom_call" | custom-call | flops 124000002048 | bytes 65536 | tf_op jit(solution)/shard_map/pallas_call | solution.py:825
  100.4 7.5 %collective-permute-done.32.refs_2_ = bf16[144,1024]{1,0:T(8,128)(2,1)S(1)} collective-permute-done((bf16[144,1024]{1,0:T(8,128)(2,1)S(1)}, bf16[144,1024]{1,0:T(8,128)(2,1)S(1)}, u32[]{:S(2)}, u32[]{:S(2)}) %collective-permute-start.32) | collective-permute-done | bytes 294944 | tf_op jit(solution)/shard_map/ppermute | solution.py:23
  109.4 2.1 %collective-permute-done.40.refs_1_ = bf16[2,192,512]{2,1,0:T(8,128)(2,1)S(1)} collective-permute-done((bf16[2,192,512]{2,1,0:T(8,128)(2,1)S(1)}, bf16[2,192,512]{2,1,0:T(8,128)(2,1)S(1)}, u32[]{:S(2)}, u32[]{:S(2)}) %collective-permute-start.40) | collective-permute-done | bytes 393248 | tf_op jit(solution)/shard_map/ppermute | solution.py:23
  113.7 3.0 %collective-permute-done.34.refs_1_ = bf16[128,1024]{1,0:T(8,128)(2,1)S(1)} collective-permute-done((bf16[128,1024]{1,0:T(8,128)(2,1)S(1)}, bf16[128,1024]{1,0:T(8,128)(2,1)S(1)}, u32[]{:S(2)}, u32[]{:S(2)}) %collective-permute-start.34) | collective-permute-done | bytes 262176 | tf_op jit(solution)/shard_map/ppermute | solution.py:23
  117.6 1.7 %collective-permute-done.37.refs_1_ = bf16[4,24,1024]{2,1,0:T(8,128)(2,1)S(1)} collective-permute-done((bf16[4,24,1024]{2,1,0:T(8,128)(2,1)S(1)}, bf16[4,24,1024]{2,1,0:T(8,128)(2,1)S(1)}, u32[]{:S(2)}, u32[]{:S(2)}) %collective-permute-start.37) | collective-permute-done | bytes 196640 | tf_op jit(solution)/shard_map/ppermute | solution.py:23
  120.0 3.1 %collective-permute-done.41.refs_1_ = bf16[1,192,512]{2,1,0:T(8,128)(2,1)S(1)} collective-permute-done((bf16[1,192,512]{2,1,0:T(8,128)(2,1)S(1)}, bf16[1,192,512]{2,1,0:T(8,128)(2,1)S(1)}, u32[]{:S(2)}, u32[]{:S(2)}) %collective-permute-start.41) | collective-permute-done | bytes 196640 | tf_op jit(solution)/shard_map/ppermute | solution.py:23
  123.4 1.8 %collective-permute-start.44 = (bf16[192,128]{1,0:T(8,128)(2,1)S(1)}, bf16[192,128]{1,0:T(8,128)(2,1)S(1)}, u32[]{:S(2)}, u32[]{:S(2)}) collective-permute-start(bf16[192,128]{1,0:T(8,128)(2,1)S(1)} %get-tuple-element.169), channel_id=1, source_target_pairs={{0,3},{1,2},{2,1},{3,0},{4,7},{5,6},{6,5},{7,4},{8,11},{9,10},{10,... | collective-permute-start | bytes 147464 | tf_op jit(solution)/shard_map/ppermute | solution.py:23
  126.0 1.9 %collective-permute-done.43.refs_2_ = bf16[192,128]{1,0:T(8,128)(2,1)S(1)} collective-permute-done((bf16[192,128]{1,0:T(8,128)(2,1)S(1)}, bf16[192,128]{1,0:T(8,128)(2,1)S(1)}, u32[]{:S(2)}, u32[]{:S(2)}) %collective-permute-start.43) | collective-permute-done | bytes 49184 | tf_op jit(solution)/shard_map/ppermute | solution.py:23
  (149 shorter events, 47.7 us)
Async XLA Ops:
  2.6 9.8 %collective-permute-start.3 = (bf16[32,512]{1,0:T(8,128)(2,1)}, bf16[32,512]{1,0:T(8,128)(2,1)S(1)}, u32[]{:S(2)}, u32[]{:S(2)}) collective-permute-start(bf16[32,512]{1,0:T(8,128)(2,1)} %get-tuple-element.95), channel_id=1, source_target_pairs={{0,1},{1,0},{2,3},{3,2},{4,5},{5,4},{6,7},{7,6},{8,9},{9,8},{10,11... | collective-permute-start | bytes 98312 | tf_op jit(solution)/shard_map/ppermute | solution.py:23
  3.1 10.0 %collective-permute-start.4 = (bf16[32,512]{1,0:T(8,128)(2,1)}, bf16[32,512]{1,0:T(8,128)(2,1)S(1)}, u32[]{:S(2)}, u32[]{:S(2)}) collective-permute-start(bf16[32,512]{1,0:T(8,128)(2,1)} %get-tuple-element.96), channel_id=1, source_target_pairs={{0,2},{1,3},{2,0},{3,1},{4,6},{5,7},{6,4},{7,5},{8,10},{9,11},{10,... | collective-permute-start | bytes 98312 | tf_op jit(solution)/shard_map/ppermute | solution.py:23
  5.7 7.4 %collective-permute-start.5 = (bf16[32,512]{1,0:T(8,128)(2,1)}, bf16[32,512]{1,0:T(8,128)(2,1)S(1)}, u32[]{:S(2)}, u32[]{:S(2)}) collective-permute-start(bf16[32,512]{1,0:T(8,128)(2,1)} %get-tuple-element.97), channel_id=1, source_target_pairs={{0,3},{1,2},{2,1},{3,0},{4,7},{5,6},{6,5},{7,4},{8,11},{9,10},{10,... | collective-permute-start | bytes 98312 | tf_op jit(solution)/shard_map/ppermute | solution.py:23
  7.9 9.1 %collective-permute-start.2 = (bf16[16,3456]{1,0:T(8,128)(2,1)}, bf16[16,3456]{1,0:T(8,128)(2,1)S(1)}, u32[]{:S(2)}, u32[]{:S(2)}) collective-permute-start(bf16[16,3456]{1,0:T(8,128)(2,1)} %get-tuple-element.94.refs_0_), channel_id=1, source_target_pairs={{0,24},{4,28},{8,16},{12,20},{16,8},{20,12},{24,0},{28,4},{1,25},{... | collective-permute-start | bytes 331784 | tf_op jit(solution)/shard_map/ppermute | solution.py:23
  11.8 16.3 %collective-permute-start.1 = (bf16[16,3456]{1,0:T(8,128)(2,1)}, bf16[16,3456]{1,0:T(8,128)(2,1)S(1)}, u32[]{:S(2)}, u32[]{:S(2)}) collective-permute-start(bf16[16,3456]{1,0:T(8,128)(2,1)} %get-tuple-element.94.refs_0_), channel_id=1, source_target_pairs={{0,16},{4,20},{8,24},{12,28},{16,0},{20,4},{24,8},{28,12},{1,17},{... | collective-permute-start | bytes 331784 | tf_op jit(solution)/shard_map/ppermute | solution.py:23
  12.4 15.6 %collective-permute-start = (bf16[16,3456]{1,0:T(8,128)(2,1)}, bf16[16,3456]{1,0:T(8,128)(2,1)S(1)}, u32[]{:S(2)}, u32[]{:S(2)}) collective-permute-start(bf16[16,3456]{1,0:T(8,128)(2,1)} %get-tuple-element.94.refs_0_), channel_id=1, source_target_pairs={{0,8},{4,12},{8,0},{12,4},{16,24},{20,28},{24,16},{28,20},{1,9},{5... | collective-permute-start | bytes 331784 | tf_op jit(solution)/shard_map/ppermute | solution.py:23
  13.1 20.3 %collective-permute-start.8 = (bf16[128,512]{1,0:T(8,128)(2,1)S(1)}, bf16[128,512]{1,0:T(8,128)(2,1)S(1)}, u32[]{:S(2)}, u32[]{:S(2)}) collective-permute-start(bf16[128,512]{1,0:T(8,128)(2,1)S(1)} %bitcast.35), channel_id=1, source_target_pairs={{0,24},{4,28},{8,16},{12,20},{16,8},{20,12},{24,0},{28,4},{1,25},{... | collective-permute-start | bytes 393224 | tf_op jit(solution)/shard_map/ppermute | solution.py:23
  16.9 16.5 %collective-permute-start.7 = (bf16[128,512]{1,0:T(8,128)(2,1)S(1)}, bf16[128,512]{1,0:T(8,128)(2,1)S(1)}, u32[]{:S(2)}, u32[]{:S(2)}) collective-permute-start(bf16[128,512]{1,0:T(8,128)(2,1)S(1)} %bitcast.36), channel_id=1, source_target_pairs={{0,16},{4,20},{8,24},{12,28},{16,0},{20,4},{24,8},{28,12},{1,17},{... | collective-permute-start | bytes 393224 | tf_op jit(solution)/shard_map/ppermute | solution.py:23
  16.9 12.7 %collective-permute-start.6 = (bf16[128,512]{1,0:T(8,128)(2,1)S(1)}, bf16[128,512]{1,0:T(8,128)(2,1)S(1)}, u32[]{:S(2)}, u32[]{:S(2)}) collective-permute-start(bf16[128,512]{1,0:T(8,128)(2,1)S(1)} %bitcast.37), channel_id=1, source_target_pairs={{0,8},{4,12},{8,0},{12,4},{16,24},{20,28},{24,16},{28,20},{1,9},{5... | collective-permute-start | bytes 393224 | tf_op jit(solution)/shard_map/ppermute | solution.py:23
  28.1 18.1 %collective-permute-start.12 = (bf16[4,16,3456]{2,1,0:T(8,128)(2,1)S(1)}, bf16[4,16,3456]{2,1,0:T(8,128)(2,1)S(1)}, u32[]{:S(2)}, u32[]{:S(2)}) collective-permute-start(bf16[4,16,3456]{2,1,0:T(8,128)(2,1)S(1)} %shard_map.164.refs_0_), channel_id=1, source_target_pairs={{0,4},{4,0},{8,12},{12,8},{16,20},{20,16},{24,28},{28,24},{1,5},{5... | collective-permute-start | bytes 1327112 | tf_op jit(solution)/shard_map/ppermute | solution.py:23
  29.6 14.6 %all-to-all-start = ((bf16[8,8,2176]{2,1,0:T(8,128)(2,1)}), bf16[8,8,2176]{2,1,0:T(8,128)(2,1)S(1)}, u32[]{:S(2)}, u32[]{:S(2)}) async-start(bf16[8,8,2176]{2,1,0:T(8,128)(2,1)} %bitcast.4), calls=%async_computation | async-start | bytes 557056 | tf_op jit(solution)/shard_map/all_to_all | solution.py:1010
  33.5 19.9 %collective-permute-start.16 = (bf16[4,128,512]{2,1,0:T(8,128)(2,1)S(1)}, bf16[4,128,512]{2,1,0:T(8,128)(2,1)S(1)}, u32[]{:S(2)}, u32[]{:S(2)}) collective-permute-start(bf16[4,128,512]{2,1,0:T(8,128)(2,1)S(1)} %shard_map.166.refs_0_), channel_id=1, source_target_pairs={{0,4},{4,0},{8,12},{12,8},{16,20},{20,16},{24,28},{28,24},{1,5},{5... | collective-permute-start | bytes 1572872 | tf_op jit(solution)/shard_map/ppermute | solution.py:23
  46.9 8.8 %collective-permute-start.13 = (bf16[8,16,1152]{2,1,0:T(8,128)(2,1)S(1)}, bf16[8,16,1152]{2,1,0:T(8,128)(2,1)S(1)}, u32[]{:S(2)}, u32[]{:S(2)}) collective-permute-start(bf16[8,16,1152]{2,1,0:T(8,128)(2,1)S(1)} %bitcast.29), channel_id=1, source_target_pairs={{0,1},{1,0},{2,3},{3,2},{4,5},{5,4},{6,7},{7,6},{8,9},{9,8},{10,11... | collective-permute-start | bytes 884744 | tf_op jit(solution)/shard_map/ppermute | solution.py:23
  46.9 8.3 %collective-permute-start.9 = (bf16[128,512]{1,0:T(8,128)(2,1)S(1)}, bf16[128,512]{1,0:T(8,128)(2,1)S(1)}, u32[]{:S(2)}, u32[]{:S(2)}) collective-permute-start(bf16[128,512]{1,0:T(8,128)(2,1)S(1)} %shard_map.167.refs_0_), channel_id=1, source_target_pairs={{0,1},{1,0},{2,3},{3,2},{4,5},{5,4},{6,7},{7,6},{8,9},{9,8},{10,11... | collective-permute-start | bytes 393224 | tf_op jit(solution)/shard_map/ppermute | solution.py:23
  74.3 7.7 %collective-permute-start.26 = (bf16[4,32,1024]{2,1,0:T(8,128)(2,1)S(1)}, bf16[4,32,1024]{2,1,0:T(8,128)(2,1)S(1)}, u32[]{:S(2)}, u32[]{:S(2)}) collective-permute-start(bf16[4,32,1024]{2,1,0:T(8,128)(2,1)S(1)} %get-tuple-element.125), channel_id=1, source_target_pairs={{0,4},{4,0},{8,12},{12,8},{16,20},{20,16},{24,28},{28,24},{1,5},{5... | collective-permute-start | bytes 786440 | tf_op jit(solution)/shard_map/ppermute | solution.py:23
  83.7 10.8 %collective-permute-start.30 = (bf16[128,1024]{1,0:T(8,128)(2,1)S(1)}, bf16[128,1024]{1,0:T(8,128)(2,1)S(1)}, u32[]{:S(2)}, u32[]{:S(2)}) collective-permute-start(bf16[128,1024]{1,0:T(8,128)(2,1)S(1)} %get-tuple-element.136), channel_id=1, source_target_pairs={{0,1},{1,0},{2,3},{3,2},{4,5},{5,4},{6,7},{7,6},{8,9},{9,8},{10,11... | collective-permute-start | bytes 786440 | tf_op jit(solution)/shard_map/ppermute | solution.py:23
  86.2 13.9 %collective-permute-start.33 = (bf16[4,128,512]{2,1,0:T(8,128)(2,1)S(1)}, bf16[4,128,512]{2,1,0:T(8,128)(2,1)S(1)}, u32[]{:S(2)}, u32[]{:S(2)}) collective-permute-start(bf16[4,128,512]{2,1,0:T(8,128)(2,1)S(1)} %get-tuple-element.138), channel_id=1, source_target_pairs={{0,4},{4,0},{8,12},{12,8},{16,20},{20,16},{24,28},{28,24},{1,5},{5... | collective-permute-start | bytes 1572872 | tf_op jit(solution)/shard_map/ppermute | solution.py:23
  87.7 8.0 %collective-permute-start.31 = (bf16[128,1024]{1,0:T(8,128)(2,1)S(1)}, bf16[128,1024]{1,0:T(8,128)(2,1)S(1)}, u32[]{:S(2)}, u32[]{:S(2)}) collective-permute-start(bf16[128,1024]{1,0:T(8,128)(2,1)S(1)} %shard_map.181), channel_id=1, source_target_pairs={{0,2},{1,3},{2,0},{3,1},{4,6},{5,7},{6,4},{7,5},{8,10},{9,11},{10,... | collective-permute-start | bytes 786440 | tf_op jit(solution)/shard_map/ppermute | solution.py:23
  93.9 19.7 %collective-permute-start.28 = (bf16[128,1024]{1,0:T(8,128)(2,1)S(1)}, bf16[128,1024]{1,0:T(8,128)(2,1)S(1)}, u32[]{:S(2)}, u32[]{:S(2)}) collective-permute-start(bf16[128,1024]{1,0:T(8,128)(2,1)S(1)} %get-tuple-element.142), channel_id=1, source_target_pairs={{0,1},{1,0},{2,3},{3,2},{4,5},{5,4},{6,7},{7,6},{8,9},{9,8},{10,11... | collective-permute-start | bytes 786440 | tf_op jit(solution)/shard_map/ppermute | solution.py:23
  98.5 13.3 %collective-permute-start.35 = (bf16[144,1024]{1,0:T(8,128)(2,1)S(1)}, bf16[144,1024]{1,0:T(8,128)(2,1)S(1)}, u32[]{:S(2)}, u32[]{:S(2)}) collective-permute-start(bf16[144,1024]{1,0:T(8,128)(2,1)S(1)} %shard_map.185.refs_0_), channel_id=1, source_target_pairs={{0,1},{1,0},{2,3},{3,2},{4,5},{5,4},{6,7},{7,6},{8,9},{9,8},{10,11... | collective-permute-start | bytes 884744 | tf_op jit(solution)/shard_map/ppermute | solution.py:23
  98.5 9.4 %collective-permute-start.32 = (bf16[144,1024]{1,0:T(8,128)(2,1)S(1)}, bf16[144,1024]{1,0:T(8,128)(2,1)S(1)}, u32[]{:S(2)}, u32[]{:S(2)}) collective-permute-start(bf16[144,1024]{1,0:T(8,128)(2,1)S(1)} %shard_map.185.refs_0_), channel_id=1, source_target_pairs={{0,2},{1,3},{2,0},{3,1},{4,6},{5,7},{6,4},{7,5},{8,10},{9,11},{10,... | collective-permute-start | bytes 884744 | tf_op jit(solution)/shard_map/ppermute | solution.py:23
  100.3 11.3 %collective-permute-start.40 = (bf16[2,192,512]{2,1,0:T(8,128)(2,1)S(1)}, bf16[2,192,512]{2,1,0:T(8,128)(2,1)S(1)}, u32[]{:S(2)}, u32[]{:S(2)}) collective-permute-start(bf16[2,192,512]{2,1,0:T(8,128)(2,1)S(1)} %get-tuple-element.149), channel_id=1, source_target_pairs={{0,8},{4,12},{8,0},{12,4},{16,24},{20,28},{24,16},{28,20},{1,9},{5... | collective-permute-start | bytes 1179656 | tf_op jit(solution)/shard_map/ppermute | solution.py:23
  108.0 8.7 %collective-permute-start.34 = (bf16[128,1024]{1,0:T(8,128)(2,1)S(1)}, bf16[128,1024]{1,0:T(8,128)(2,1)S(1)}, u32[]{:S(2)}, u32[]{:S(2)}) collective-permute-start(bf16[128,1024]{1,0:T(8,128)(2,1)S(1)} %shard_map.184), channel_id=1, source_target_pairs={{0,2},{1,3},{2,0},{3,1},{4,6},{5,7},{6,4},{7,5},{8,10},{9,11},{10,... | collective-permute-start | bytes 786440 | tf_op jit(solution)/shard_map/ppermute | solution.py:23
  111.6 11.4 %collective-permute-start.41 = (bf16[1,192,512]{2,1,0:T(8,128)(2,1)S(1)}, bf16[1,192,512]{2,1,0:T(8,128)(2,1)S(1)}, u32[]{:S(2)}, u32[]{:S(2)}) collective-permute-start(bf16[1,192,512]{2,1,0:T(8,128)(2,1)S(1)} %get-tuple-element.165), channel_id=1, source_target_pairs={{0,16},{4,20},{8,24},{12,28},{16,0},{20,4},{24,8},{28,12},{1,17},{... | collective-permute-start | bytes 589832 | tf_op jit(solution)/shard_map/ppermute | solution.py:23
  (43 other events, 199.4 us)

commit v5 on v4

--- a/solution.py
+++ b/solution.py
@@ -187,36 +187,6 @@
     )(left, right)
 
 
-def join_parts(first, second, axis, chain):
-    stride, size = chain
-    count = len(first)
-    lead, rows, columns = first[0].shape
-    _, below, wide = second[0].shape
-    folds = wide // columns
-
-    def kernel(*refs):
-        place = (lax.axis_index(axis) // stride) % size
-        outs = refs[2 * count :]
-        for a in range(lead // size):
-            for k in range(size):
-                at = a * size + (place ^ k)
-                total = sum(part[at].astype(F32) for part in refs[:count])
-                outs[k][a, :rows, :] = total.astype(BF16)
-                total = sum(part[at].astype(F32) for part in refs[count : 2 * count]).astype(BF16)
-                for f in range(folds):
-                    outs[k][a, rows + f * below : rows + (f + 1) * below, :] = total[
-                        :, f * columns : (f + 1) * columns
-                    ]
-
-    shape = (lead // size, rows + folds * below, columns)
-    return pl.pallas_call(
-        kernel,
-        out_shape=[jax.ShapeDtypeStruct(shape, BF16)] * size,
-        compiler_params=kernel_params(),
-        cost_estimate=costs(0.8),
-    )(*first, *second)
-
-
 def swap_all_parts(parts, axis):
     return [parts[0]] + [swap(part, axis, k) for k, part in enumerate(parts[1:], 1)]
 
@@ -253,36 +223,37 @@
     return parts
 
 
-def cut_columns(parts, axis, rows, below):
+def cut_columns(first, second, axis):
     count = lax.axis_size(axis)
-    _, height, columns = parts[0].shape
+    terms = len(first)
+    _, rows, columns = first[0].shape
+    _, below, wide = second[0].shape
     share = columns // count
-    folds = (height - rows) // below
-    wide = folds * columns // count
+    folds = wide // columns
 
     def kernel(*refs):
         place = lax.axis_index(axis)
-        total = sum(part[0].astype(F32) for part in refs[: len(parts)]).astype(BF16)
+        upper = sum(part[0].astype(F32) for part in refs[:terms]).astype(BF16)
+        lower = sum(part[0].astype(F32) for part in refs[terms : 2 * terms]).astype(BF16)
         for j in range(count):
-            fold, start = divmod(wide * j, columns)
             for k in range(count):
 
                 @pl.when(place ^ j == k)
                 def _():
-                    out = refs[len(parts) + k]
-                    out[:rows, :] = total[:rows, j * share : (j + 1) * share]
+                    out = refs[2 * terms + k]
+                    out[:rows, :] = upper[:, j * share : (j + 1) * share]
                     for f in range(folds):
-                        lanes = slice(start + f * share, start + (f + 1) * share)
-                        out[rows + f * below : rows + (f + 1) * below, :] = total[
-                            rows + fold * below : rows + (fold + 1) * below, lanes
+                        start = (j * folds + f) * share
+                        out[rows + f * below : rows + (f + 1) * below, :] = lower[
+                            :, start : start + share
                         ]
 
     return pl.pallas_call(
         kernel,
-        out_shape=[jax.ShapeDtypeStruct((height, share), BF16)] * count,
+        out_shape=[jax.ShapeDtypeStruct((rows + folds * below, share), BF16)] * count,
         compiler_params=kernel_params(),
         cost_estimate=costs(0.6),
-    )(*parts)
+    )(*first, *second)
 
 
 def mix_columns(parts, axis, rows, small):
@@ -671,6 +642,39 @@
     return turned[:, :1], turned[:, 1:2]
 
 
+def spread_segments(segments):
+    length = segments.shape[1]
+
+    def kernel(source, out):
+        edge = jnp.full((PAD, 128), -1.0, F32)
+        out[:PAD, :] = edge
+        out[PAD + length :, :] = edge
+        out[PAD : PAD + length, :] = jnp.broadcast_to(
+            source[...].astype(F32), (128, length)
+        ).T
+
+    return pl.pallas_call(
+        kernel,
+        out_shape=jax.ShapeDtypeStruct((length + 2 * PAD, 128), F32),
+        compiler_params=kernel_params(),
+        cost_estimate=costs(0.5),
+    )(segments)
+
+
+def multiply_turned(left, right):
+    def kernel(left_ref, right_ref, out):
+        out[...] = lax.dot_general(
+            left_ref[...], right_ref[...], (((1,), (1,)), ((), ())), preferred_element_type=F32
+        )
+
+    return pl.pallas_call(
+        kernel,
+        out_shape=jax.ShapeDtypeStruct((left.shape[0], right.shape[0]), F32),
+        compiler_params=kernel_params(),
+        cost_estimate=costs(0.6),
+    )(left, right)
+
+
 TILE = 64
 
 
@@ -712,7 +716,7 @@
         ],
         scratch_shapes=[
             pltpu.VMEM((TILE + 2 * PAD, held), F32),
-            pltpu.VMEM((TILE + 2 * PAD, 128), jnp.int32),
+            pltpu.VMEM((TILE + 2 * PAD, 128), F32),
         ],
         compiler_params=kernel_params(),
         cost_estimate=costs(3.0),
@@ -833,7 +837,7 @@
             pltpu.VMEM((taps, 8, held), F32),
             pltpu.VMEM((TILE + 2 * PAD, held), F32),
             pltpu.VMEM((TILE + 2 * PAD, held), F32),
-            pltpu.VMEM((TILE + 2 * PAD, 128), jnp.int32),
+            pltpu.VMEM((TILE + 2 * PAD, 128), F32),
         ],
         compiler_params=kernel_params(),
         cost_estimate=costs(6.2),
@@ -847,7 +851,10 @@
     channels = parts[0].shape[1]
     rows = dp_count * stem_rows
     own = channels // dp_count
-    height = stem_rows + 8
+    height = stem_rows + 16
+
+    folds = channels // small.shape[1]
+    below = small.shape[0] // folds
 
     def kernel(turned_ref, small_ref, *refs):
         outs = refs[count:]
@@ -855,6 +862,9 @@
         total = jnp.zeros((share, channels), F32)
         for k in range(count):
             total = total + jnp.dot(turned_ref[k], refs[k][...], preferred_element_type=F32)
+        lower = jnp.concatenate(
+            [small_ref[q * below : (q + 1) * below, :] for q in range(folds)], axis=1
+        )
         for i in range(dp_count):
             gain = jnp.concatenate(
                 [total[rows : rows + 1, i * own : (i + 1) * own], jnp.zeros((1, channels - own), F32)],
@@ -863,9 +873,9 @@
             block = jnp.concatenate(
                 [
                     total[i * stem_rows : (i + 1) * stem_rows],
-                    small_ref[i : i + 1, :],
+                    lower,
                     gain,
-                    jnp.zeros((6, channels), F32),
+                    jnp.zeros((7, channels), F32),
                 ],
                 axis=0,
             ).astype(BF16)
@@ -891,20 +901,29 @@
         stem, kernel_out, post, pre = refs[count:]
         total = sum(jnp.sum(part[...].astype(F32), axis=0) for part in refs[:count])
         stem[...] = total[:stem_rows]
-        lane = lax.broadcasted_iota(jnp.int32, (taps + 1, channels), 1)
-        tap = lax.broadcasted_iota(jnp.int32, (taps + 1, channels), 0)
-        spread = jnp.where(lane // rows == tap, total[stem_rows : stem_rows + 1], 0.0)
-        at = lax.broadcasted_iota(jnp.int32, (channels, rows), 0)
-        to = lax.broadcasted_iota(jnp.int32, (channels, rows), 1)
-        fold = jnp.where(at % rows == to, 1.0, 0.0)
-        table = jnp.dot(
-            spread, fold, preferred_element_type=F32, precision=lax.Precision.HIGHEST
-        )
-        kernel_out[...] = table.T[:, :taps]
-        post[...] = table[taps : taps + 1]
+        held = channels // lax.axis_size(axis)
+        below = (taps + 1) * held // channels
+        pick = iota((held, rows), 0) == iota((held, rows), 1) + lax.axis_index("dp") * rows
+        pick = jnp.where(pick, 1.0, 0.0)
+        lower = total[stem_rows : stem_rows + below]
+        rest = jnp.concatenate(
+            [
+                jnp.dot(
+                    lower[:, q * held : (q + 1) * held],
+                    pick,
+                    preferred_element_type=F32,
+                    precision=lax.Precision.HIGHEST,
+                )
+                for q in range(channels // held)
+            ],
+            axis=0,
+        )
+        kernel_out[...] = rest.T[:, :taps]
+        post[...] = rest[taps : taps + 1]
+        at, to = iota((channels, rows), 0), iota((channels, rows), 1)
         mine = lax.axis_index(axis) * rows
         own = jnp.where(at == to + mine, 1.0, 0.0)
-        line = jnp.broadcast_to(total[stem_rows + 1 : stem_rows + 2], (8, channels))
+        line = jnp.broadcast_to(total[stem_rows + below : stem_rows + below + 1], (8, channels))
         pre[...] = jnp.dot(
             line, own, preferred_element_type=F32, precision=lax.Precision.HIGHEST
         )[:1]
@@ -1008,7 +1027,7 @@
     pieces = mel_pieces.shape[1]
     capacity = max(2, 2 * pieces // dp_count)
     arrived = lax.all_to_all(
-        after(sent, pack_near, up_sides[1]).reshape(dp_count, capacity, -1),
+        after(sent, pack_near).reshape(dp_count, capacity, -1),
         "dp",
         split_axis=0,
         concat_axis=0,
@@ -1023,15 +1042,14 @@
     stem_all = stem_all.reshape(features, channels + 128)
 
     grad_out = out_grad[0]
-    grad_first = after(grad_out, stem_parts[2])
+    grad_first = after(grad_out, up_near)
     hierarchical = list(tm_chains) == [(2, 2), (1, 2)]
     if hierarchical:
         grad_parts = [grad_first, swap(grad_first, "tm", 1), swap(grad_first, "tm", 2)]
     else:
         grad_parts = gather_parts(grad_first, "tm", tm_chains)
 
-    segments = jnp.pad(segment_ids[0], (PAD, PAD), constant_values=-1)
-    segments = jnp.broadcast_to(segments[:, None], (length + 2 * PAD, 128))
+    segments = spread_segments(segment_ids)
 
     extra = 16
     normed, stem_pre, gain_one, frames_turned = stem_forward(
@@ -1046,9 +1064,7 @@
     stats = swap_all(stats, "tm")
     grad_parts = lax.optimization_barrier((grad_parts, conv))[0]
     grad_out_all = place_parts(grad_parts, "tm", 1, tm_count, 0).reshape(length, channels)
-    grad_act = lax.dot_general(
-        grad_out_all, down_full, (((1,), (1,)), ((), ())), preferred_element_type=F32
-    )
+    grad_act = multiply_turned(grad_out_all, down_full)
     activated, conv_hat, grad_hat, inverse, sums, gain_post_term = activate(
         conv, stats, turned, grad_act, taps
     )
@@ -1080,10 +1096,11 @@
     else:
         up_terms = [message_terms(normed, grad_proj, dp_count, tm_count)]
     grad_far, grad_parts, grad_passed = block_sum(other_terms, "tm", tm_chains, up_terms[-1])
-    small_term = after(kernel_term, grad_passed)
-    small_term = small_term.reshape(taps + 1, dp_count, rows).transpose(1, 0, 2)
-    small_term = small_term.reshape(dp_count, (taps + 1) * rows)
-    small_term = jnp.pad(small_term, ((0, 0), (0, channels - (taps + 1) * rows)))
+    if by_parts:
+        down_parts[0] = after(down_parts[0], grad_passed)
+        down_parts = add_parts(down_parts, "dp", sums_chains[1])
+        down_parts = swap_parts(down_parts, "dp", sums_chains[1])
+        own_terms = after(own_terms, *down_parts[1:])
     y_own, *y_others = block_terms(
         after(activated, grad_passed), down_full, False, "tm", tm_count
     )
@@ -1091,17 +1108,19 @@
         own_terms, grad_parts + [grad_far], stem_pre, grad_out, gain_one, extra
     )
     if by_parts:
-        up_parts = join_parts(
-            [after(up_parts[0], grad_stem_pre)] + up_parts[1:], down_parts, "dp", sums_chains[1]
-        )
-        grad_stem_parts = gather_parts(grad_stem_pre, "tm", tm_chains, up_parts[-1])
+        up_parts[0] = after(up_parts[0], grad_stem_pre)
+        up_parts = add_parts(up_parts, "dp", sums_chains[1])
+        down_parts[0] = after(down_parts[0], up_parts[-1])
+        down_parts = add_parts(down_parts, "dp", sums_chains[0])
+        down_parts = swap_parts(down_parts, "dp", sums_chains[0])
+        grad_stem_parts = gather_parts(grad_stem_pre, "tm", tm_chains, down_parts[0])
         up_parts = reduce_rest(up_parts, "dp", sums_chains[:2])
     else:
         grad_stem_parts = gather_parts(grad_stem_pre, "tm", tm_chains)
     y_far, y_parts, _ = block_sum(y_others, "tm", tm_chains, grad_stem_parts[2])
     if by_parts:
         stem_terms = stem_message(
-            frames_turned, grad_stem_parts, small_term, "dp", sums_chains, stem_rows
+            frames_turned, grad_stem_parts, kernel_term, "dp", sums_chains, stem_rows
         )
         stem_sums = reduce_rest(stem_terms, "dp", sums_chains)
     else:
@@ -1113,13 +1132,17 @@
         gain_term = stem_sum[share].reshape(dp_count, 1, tm_count * rows)
         gain_term = jnp.pad(gain_term, ((0, 0), (0, 0), (0, channels - tm_count * rows)))
         stem_terms = stem_sum[:share].reshape(dp_count, stem_rows, channels)
-        stem_terms = jnp.concatenate([stem_terms, small_term[:, None, :], gain_term], axis=1)
-        stem_terms = jnp.pad(stem_terms.astype(BF16), ((0, 0), (0, 6), (0, 0)))
+        folds = channels // held
+        small_term = kernel_term.reshape(folds, -1, held).transpose(1, 0, 2).reshape(-1, channels)
+        small_term = jnp.broadcast_to(small_term[None], (dp_count,) + small_term.shape)
+        stem_terms = jnp.concatenate([stem_terms, small_term, gain_term], axis=1)
+        stem_terms = jnp.pad(stem_terms.astype(BF16), ((0, 0), (0, 7), (0, 0)))
         stem_sums = [
             lax.all_to_all(stem_terms, "dp", split_axis=0, concat_axis=0, tiled=True)
         ]
     if by_parts:
-        up_parts = cut_columns([after(up_parts[0], *stem_terms)] + up_parts[1:], "tm", tm_count * rows, rows)
+        up_parts[0] = after(up_parts[0], *stem_terms)
+        up_parts = cut_columns(up_parts, down_parts, "tm")
         up_parts = swap_all_parts(up_parts, "tm")
         grad_up, grad_down = mix_columns(up_parts, "tm", tm_count * rows, rows)
     else:

time: 132 us -> 124 us (0.939)
  local copies, waits for them, and re-layouts: 9.39 us -> 0.52 us
  starting transfers between devices: 44.5 us -> 51.3 us
  waiting for transfers between devices: 48.9 us -> 43.5 us
    all_to_all x1, waiting for transfers between devices: 8.68 us -> 2.59 us  [per_device(): lax.all_to_all(after(sent, pack_near).reshape(dp_count, capacity, -1), 'd...]
    unnamed x42 -> x22, local copies, waits for them, and re-layouts: 5.26 us -> 0.52 us
    all_to_all x1, starting transfers between devices: 3.75 us -> 8.43 us  [per_device(): lax.all_to_all(after(sent, pack_near).reshape(dp_count, capacity, -1), 'd...]
    reshape x3 -> x0, local copies, waits for them, and re-layouts: 3.34 us -> none  [the longest x2 2.33 us: per_device(): small_term = small_term.reshape(taps + 1, dp_count, rows).transpose(1, 0, 2)]
    ppermute x45 -> x47, starting transfers between devices: 40.8 us -> 42.8 us  [swap(): return lax.ppermute(value, axis, [(i, i ^ mask) for i in range(size)])]
    ppermute x45 -> x47, waiting for transfers between devices: 40.2 us -> 40.9 us  [swap(): return lax.ppermute(value, axis, [(i, i ^ mask) for i in range(size)])]
  transfers between devices with their start and end apart: 46 -> 48, of which waited for: 18 -> 26; matrix products, arithmetic and copies ran while one was open for 4% -> 0% of each run, Pallas kernels for 17% -> 17%
where the time goes in v5:
time: 124 us
  starting transfers between devices  51.3 us (41%)
  waiting for transfers between devices  43.5 us (35%)
  Pallas kernels  27.4 us (22%)
    ppermute x47, starting transfers between devices, swap(): return lax.ppermute(value, axis, [(i, i ^ mask) for i in range(size)])  42.8 us
    ppermute x47, waiting for transfers between devices, swap(): return lax.ppermute(value, axis, [(i, i ^ mask) for i in range(size)])  40.9 us
    all_to_all x1, starting transfers between devices, per_device(): lax.all_to_all(after(sent, pack_near).reshape(dp_count, capacity, -1), 'd...  8.43 us
    pallas_call x1, Pallas kernels, conv_backward(): pl.pallas_call(kernel, out_shape=[jax.ShapeDtypeStruct((length, 2 * held)...  6.18 us
    pallas_call x2, Pallas kernels, fetching_call(): pl.pallas_call(kernel, out_shape=out_shape, in_specs=[pl.BlockSpec(memory...  4.05 us
    pallas_call x1, Pallas kernels, conv_forward(): pl.pallas_call(kernel, out_shape=[jax.ShapeDtypeStruct((length, held), F3...  2.98 us
    pallas_call x1, Pallas kernels, stem_forward(): pl.pallas_call(kernel, out_shape=[jax.ShapeDtypeStruct((length, channels)...  2.73 us
    all_to_all x1, waiting for transfers between devices, per_device(): lax.all_to_all(after(sent, pack_near).reshape(dp_count, capacity, -1), 'd...  2.59 us
  transfers between devices with their start and end apart: 48, of which 26 were waited for; matrix products, arithmetic and copies ran while one was open for 0% of the time, Pallas kernels for 17%

profile of v5, /device:TPU:0, one launch (start us, length us, event | category | flops | bytes accessed | tf_op | source)
XLA Modules:
  0.0 123.7 jit_solution(7686061658920389814)
XLA Ops:
  0.6 1.9 %shard_map.162 = (bf16[32,512]{1,0:T(8,128)(2,1)}, bf16[32,512]{1,0:T(8,128)(2,1)}, bf16[32,512]{1,0:T(8,128)(2,1)}, bf16[32,512]{1,0:T(8,128)(2,1)}) custom-call(bf16[32,2048]{1,0:T(8,128)(2,1)} %source.2), custom_call_target="tpu_custom_call" | custom-call | flops 30000001024 | bytes 65536 | tf_op jit(solution)/shard_map/pallas_call | solution.py:416
  2.6 2.1 %shard_map.163 = (bf16[64,2176]{1,0:T(8,128)(2,1)}, bf16[16,3456]{1,0:T(8,128)(2,1)}) custom-call(bf16[16,1024]{1,0:T(8,128)(2,1)} %refs_0_, bf16[32,31]{1,0:T(8,128)(2,1)} %refs_1_.1, bf16[1,32]{1,0:T(2,128)(2,1)} %bitcast.39, bf16[1,32]{1,0:T(2,128)(2,1)} %bitcast.40, s32[1,32]{1,0:T(1,128)} %refs_4_.1, s32[1,32]{1,0:T(1,128)} %refs_5_.1, ...), custom_call_target="tpu_custom_call" | custom-call | flops 40000000000 | bytes 65536 | tf_op jit(solution)/shard_map/pallas_call | solution.py:416
  4.7 5.1 %collective-permute-start.2 = (bf16[16,3456]{1,0:T(8,128)(2,1)}, bf16[16,3456]{1,0:T(8,128)(2,1)S(1)}, u32[]{:S(2)}, u32[]{:S(2)}) collective-permute-start(bf16[16,3456]{1,0:T(8,128)(2,1)} %get-tuple-element.100.refs_0_), channel_id=1, source_target_pairs={{0,24},{4,28},{8,16},{12,20},{16,8},{20,12},{24,0},{28,4},{1,25},{... | collective-permute-start | bytes 331784 | tf_op jit(solution)/shard_map/ppermute | solution.py:23
  9.9 1.6 %collective-permute-start.4 = (bf16[32,512]{1,0:T(8,128)(2,1)S(1)}, bf16[32,512]{1,0:T(8,128)(2,1)S(1)}, u32[]{:S(2)}, u32[]{:S(2)}) collective-permute-start(bf16[32,512]{1,0:T(8,128)(2,1)S(1)} %copy-done.9), channel_id=1, source_target_pairs={{0,2},{1,3},{2,0},{3,1},{4,6},{5,7},{6,4},{7,5},{8,10},{9,11},{10,... | collective-permute-start | bytes 98312 | tf_op jit(solution)/shard_map/ppermute | solution.py:23
  14.8 2.0 %collective-permute-start.8 = (bf16[128,512]{1,0:T(8,128)(2,1)S(1)}, bf16[128,512]{1,0:T(8,128)(2,1)S(1)}, u32[]{:S(2)}, u32[]{:S(2)}) collective-permute-start(bf16[128,512]{1,0:T(8,128)(2,1)S(1)} %bitcast.25), channel_id=1, source_target_pairs={{0,24},{4,28},{8,16},{12,20},{16,8},{20,12},{24,0},{28,4},{1,25},{... | collective-permute-start | bytes 393224 | tf_op jit(solution)/shard_map/ppermute | solution.py:23
  20.3 1.6 %collective-permute-start.12 = (bf16[4,16,3456]{2,1,0:T(8,128)(2,1)S(1)}, bf16[4,16,3456]{2,1,0:T(8,128)(2,1)S(1)}, u32[]{:S(2)}, u32[]{:S(2)}) collective-permute-start(bf16[4,16,3456]{2,1,0:T(8,128)(2,1)S(1)} %shard_map.164.refs_0_), channel_id=1, source_target_pairs={{0,4},{4,0},{8,12},{12,8},{16,20},{20,16},{24,28},{28,24},{1,5},{5... | collective-permute-start | bytes 1327112 | tf_op jit(solution)/shard_map/ppermute | solution.py:23
  21.8 8.4 %all-to-all-start = ((bf16[8,8,2176]{2,1,0:T(8,128)(2,1)}), bf16[8,8,2176]{2,1,0:T(8,128)(2,1)S(1)}, u32[]{:S(2)}, u32[]{:S(2)}) async-start(bf16[8,8,2176]{2,1,0:T(8,128)(2,1)} %bitcast.3), calls=%async_computation | async-start | bytes 557056 | tf_op jit(solution)/shard_map/all_to_all | solution.py:1029
  30.3 2.1 %collective-permute-done.7.refs_2_ = bf16[128,512]{1,0:T(8,128)(2,1)S(1)} collective-permute-done((bf16[128,512]{1,0:T(8,128)(2,1)S(1)}, bf16[128,512]{1,0:T(8,128)(2,1)S(1)}, u32[]{:S(2)}, u32[]{:S(2)}) %collective-permute-start.7) | collective-permute-done | bytes 131104 | tf_op jit(solution)/shard_map/ppermute | solution.py:23
  32.5 2.2 %collective-permute-start.18 = (bf16[128,1024]{1,0:T(8,128)(2,1)S(1)}, bf16[128,1024]{1,0:T(8,128)(2,1)S(1)}, u32[]{:S(2)}, u32[]{:S(2)}) collective-permute-start(bf16[128,1024]{1,0:T(8,128)(2,1)S(1)} %bitcast.21), channel_id=1, source_target_pairs={{0,2},{1,3},{2,0},{3,1},{4,6},{5,7},{6,4},{7,5},{8,10},{9,11},{10,... | collective-permute-start | bytes 786440 | tf_op jit(solution)/shard_map/ppermute | solution.py:23
  36.1 2.6 %all-to-all-done = bf16[8,8,2176]{2,1,0:T(8,128)(2,1)S(1)} async-done(((bf16[8,8,2176]{2,1,0:T(8,128)(2,1)}), bf16[8,8,2176]{2,1,0:T(8,128)(2,1)S(1)}, u32[]{:S(2)}, u32[]{:S(2)}) %all-to-all-start) | async-done | bytes 278560 | tf_op jit(solution)/shard_map/all_to_all | solution.py:1029
  39.1 2.4 %collective-permute-start.10 = (bf16[128,512]{1,0:T(8,128)(2,1)S(1)}, bf16[128,512]{1,0:T(8,128)(2,1)S(1)}, u32[]{:S(2)}, u32[]{:S(2)}) collective-permute-start(bf16[128,512]{1,0:T(8,128)(2,1)S(1)} %shard_map.167.refs_0_), channel_id=1, source_target_pairs={{0,2},{1,3},{2,0},{3,1},{4,6},{5,7},{6,4},{7,5},{8,10},{9,11},{10,... | collective-permute-start | bytes 393224 | tf_op jit(solution)/shard_map/ppermute | solution.py:23
  41.6 7.7 %collective-permute-done.16.refs_1_ = bf16[4,128,512]{2,1,0:T(8,128)(2,1)S(1)} collective-permute-done((bf16[4,128,512]{2,1,0:T(8,128)(2,1)S(1)}, bf16[4,128,512]{2,1,0:T(8,128)(2,1)S(1)}, u32[]{:S(2)}, u32[]{:S(2)}) %collective-permute-start.16) | collective-permute-done | bytes 524320 | tf_op jit(solution)/shard_map/ppermute | solution.py:23
  52.4 2.7 %shard_map.171 = (bf16[512,1024]{1,0:T(8,128)(2,1)S(1)}, f32[128,1024]{1,0:T(8,128)S(1)}, f32[1,1024]{1,0:T(1,128)S(1)}, bf16[4,144,144]{2,1,0:T(8,128)(2,1)S(1)}) custom-call(bf16[512,512]{1,0:T(8,128)(2,1)S(1)} %bitcast.36, bf16[512,1152]{1,0:T(8,128)(2,1)S(1)} %bitcast.29), custom_call_target="tpu_custom_call" | custom-call | flops 56000000000 | bytes 65536 | tf_op jit(solution)/shard_map/pallas_call | solution.py:588
  56.1 3.0 %shard_map.175 = (f32[512,256]{1,0:T(8,128)S(1)}, f32[8,512]{1,0:T(8,128)S(1)}, f32[128,256]{1,0:T(8,128)S(1)}) custom-call(f32[544,256]{1,0:T(8,128)S(1)} %get-tuple-element.110.gated_ref, bf16[256,128]{1,0:T(8,128)(2,1)S(1)} %bitcast.37, f32[544,128]{1,0:T(8,128)S(1)} %shard_map.174.seg_ref), custom_call_target="tpu_custom_call" | custom-call | flops 60000002048 | bytes 65536 | tf_op jit(solution)/shard_map/pallas_call | solution.py:710
  69.8 6.2 %shard_map.181 = (bf16[512,512]{1,0:T(8,128)(2,1)S(1)}, f32[32,256]{1,0:T(8,128)S(1)}) custom-call(f32[512,256]{1,0:T(8,128)S(1)} %get-tuple-element.132.grad_ref, f32[512,256]{1,0:T(8,128)S(1)} %get-tuple-element.133.hat_ref, f32[512,128]{1,0:T(8,128)S(1)} %get-tuple-element.134.inverse_ref, f32[544,256]{1,0:T(8,128)S(1)} %get-tuple-element.110.gated_ref, ...), custom_call_target="tpu_custom_call" | custom-call | flops 124000002048 | bytes 65536 | tf_op jit(solution)/shard_map/pallas_call | solution.py:829
  83.2 4.0 %collective-permute-done.30.refs_1_ = bf16[2,32,1024]{2,1,0:T(8,128)(2,1)S(1)} collective-permute-done((bf16[2,32,1024]{2,1,0:T(8,128)(2,1)S(1)}, bf16[2,32,1024]{2,1,0:T(8,128)(2,1)S(1)}, u32[]{:S(2)}, u32[]{:S(2)}) %collective-permute-start.30) | collective-permute-done | bytes 131104 | tf_op jit(solution)/shard_map/ppermute | solution.py:23
  87.3 1.7 %collective-permute-done.32.refs_1_ = bf16[128,1024]{1,0:T(8,128)(2,1)S(1)} collective-permute-done((bf16[128,1024]{1,0:T(8,128)(2,1)S(1)}, bf16[128,1024]{1,0:T(8,128)(2,1)S(1)}, u32[]{:S(2)}, u32[]{:S(2)}) %collective-permute-start.32) | collective-permute-done | bytes 262176 | tf_op jit(solution)/shard_map/ppermute | solution.py:23
  91.0 2.5 %collective-permute-done.34.refs_1_ = bf16[4,128,512]{2,1,0:T(8,128)(2,1)S(1)} collective-permute-done((bf16[4,128,512]{2,1,0:T(8,128)(2,1)S(1)}, bf16[4,128,512]{2,1,0:T(8,128)(2,1)S(1)}, u32[]{:S(2)}, u32[]{:S(2)}) %collective-permute-start.34) | collective-permute-done | bytes 524320 | tf_op jit(solution)/shard_map/ppermute | solution.py:23
  94.8 2.2 %collective-permute-start.43 = (bf16[1,32,1024]{2,1,0:T(8,128)(2,1)S(1)}, bf16[1,32,1024]{2,1,0:T(8,128)(2,1)S(1)}, u32[]{:S(2)}, u32[]{:S(2)}) collective-permute-start(bf16[1,32,1024]{2,1,0:T(8,128)(2,1)S(1)} %get-tuple-element.177), channel_id=1, source_target_pairs={{0,16},{4,20},{8,24},{12,28},{16,0},{20,4},{24,8},{28,12},{1,17},{... | collective-permute-start | bytes 196616 | tf_op jit(solution)/shard_map/ppermute | solution.py:23
  97.0 2.1 %collective-permute-done.33.refs_2_ = bf16[144,1024]{1,0:T(8,128)(2,1)S(1)} collective-permute-done((bf16[144,1024]{1,0:T(8,128)(2,1)S(1)}, bf16[144,1024]{1,0:T(8,128)(2,1)S(1)}, u32[]{:S(2)}, u32[]{:S(2)}) %collective-permute-start.33) | collective-permute-done | bytes 294944 | tf_op jit(solution)/shard_map/ppermute | solution.py:23
  99.2 3.5 %collective-permute-done.41.refs_1_ = bf16[2,128,512]{2,1,0:T(8,128)(2,1)S(1)} collective-permute-done((bf16[2,128,512]{2,1,0:T(8,128)(2,1)S(1)}, bf16[2,128,512]{2,1,0:T(8,128)(2,1)S(1)}, u32[]{:S(2)}, u32[]{:S(2)}) %collective-permute-start.41) | collective-permute-done | bytes 262176 | tf_op jit(solution)/shard_map/ppermute | solution.py:23
  106.2 4.0 %collective-permute-done.35.refs_1_ = bf16[128,1024]{1,0:T(8,128)(2,1)S(1)} collective-permute-done((bf16[128,1024]{1,0:T(8,128)(2,1)S(1)}, bf16[128,1024]{1,0:T(8,128)(2,1)S(1)}, u32[]{:S(2)}, u32[]{:S(2)}) %collective-permute-start.35) | collective-permute-done | bytes 262176 | tf_op jit(solution)/shard_map/ppermute | solution.py:23
  111.8 2.5 %collective-permute-start.39 = (bf16[2,32,1024]{2,1,0:T(8,128)(2,1)S(1)}, bf16[2,32,1024]{2,1,0:T(8,128)(2,1)S(1)}, u32[]{:S(2)}, u32[]{:S(2)}) collective-permute-start(bf16[2,32,1024]{2,1,0:T(8,128)(2,1)S(1)} %get-tuple-element.169), channel_id=1, source_target_pairs={{0,8},{4,12},{8,0},{12,4},{16,24},{20,28},{24,16},{28,20},{1,9},{5... | collective-permute-start | bytes 393224 | tf_op jit(solution)/shard_map/ppermute | solution.py:23
  120.5 2.1 %collective-permute-done.40.refs_1_ = bf16[1,32,1024]{2,1,0:T(8,128)(2,1)S(1)} collective-permute-done((bf16[1,32,1024]{2,1,0:T(8,128)(2,1)S(1)}, bf16[1,32,1024]{2,1,0:T(8,128)(2,1)S(1)}, u32[]{:S(2)}, u32[]{:S(2)}) %collective-permute-start.40) | collective-permute-done | bytes 65568 | tf_op jit(solution)/shard_map/ppermute | solution.py:23
  (131 shorter events, 46.3 us)
Async XLA Ops:
  4.7 13.2 %collective-permute-start.2 = (bf16[16,3456]{1,0:T(8,128)(2,1)}, bf16[16,3456]{1,0:T(8,128)(2,1)S(1)}, u32[]{:S(2)}, u32[]{:S(2)}) collective-permute-start(bf16[16,3456]{1,0:T(8,128)(2,1)} %get-tuple-element.100.refs_0_), channel_id=1, source_target_pairs={{0,24},{4,28},{8,16},{12,20},{16,8},{20,12},{24,0},{28,4},{1,25},{... | collective-permute-start | bytes 331784 | tf_op jit(solution)/shard_map/ppermute | solution.py:23
  9.9 10.0 %collective-permute-start.1 = (bf16[16,3456]{1,0:T(8,128)(2,1)}, bf16[16,3456]{1,0:T(8,128)(2,1)S(1)}, u32[]{:S(2)}, u32[]{:S(2)}) collective-permute-start(bf16[16,3456]{1,0:T(8,128)(2,1)} %get-tuple-element.100.refs_0_), channel_id=1, source_target_pairs={{0,16},{4,20},{8,24},{12,28},{16,0},{20,4},{24,8},{28,12},{1,17},{... | collective-permute-start | bytes 331784 | tf_op jit(solution)/shard_map/ppermute | solution.py:23
  12.4 7.9 %collective-permute-start = (bf16[16,3456]{1,0:T(8,128)(2,1)S(1)}, bf16[16,3456]{1,0:T(8,128)(2,1)S(1)}, u32[]{:S(2)}, u32[]{:S(2)}) collective-permute-start(bf16[16,3456]{1,0:T(8,128)(2,1)S(1)} %copy-done.1), channel_id=1, source_target_pairs={{0,8},{4,12},{8,0},{12,4},{16,24},{20,28},{24,16},{28,20},{1,9},{5... | collective-permute-start | bytes 331784 | tf_op jit(solution)/shard_map/ppermute | solution.py:23
  14.8 15.4 %collective-permute-start.8 = (bf16[128,512]{1,0:T(8,128)(2,1)S(1)}, bf16[128,512]{1,0:T(8,128)(2,1)S(1)}, u32[]{:S(2)}, u32[]{:S(2)}) collective-permute-start(bf16[128,512]{1,0:T(8,128)(2,1)S(1)} %bitcast.25), channel_id=1, source_target_pairs={{0,24},{4,28},{8,16},{12,20},{16,8},{20,12},{24,0},{28,4},{1,25},{... | collective-permute-start | bytes 393224 | tf_op jit(solution)/shard_map/ppermute | solution.py:23
  16.8 15.5 %collective-permute-start.7 = (bf16[128,512]{1,0:T(8,128)(2,1)S(1)}, bf16[128,512]{1,0:T(8,128)(2,1)S(1)}, u32[]{:S(2)}, u32[]{:S(2)}) collective-permute-start(bf16[128,512]{1,0:T(8,128)(2,1)S(1)} %bitcast.26), channel_id=1, source_target_pairs={{0,16},{4,20},{8,24},{12,28},{16,0},{20,4},{24,8},{28,12},{1,17},{... | collective-permute-start | bytes 393224 | tf_op jit(solution)/shard_map/ppermute | solution.py:23
  17.9 14.5 %collective-permute-start.6 = (bf16[128,512]{1,0:T(8,128)(2,1)S(1)}, bf16[128,512]{1,0:T(8,128)(2,1)S(1)}, u32[]{:S(2)}, u32[]{:S(2)}) collective-permute-start(bf16[128,512]{1,0:T(8,128)(2,1)S(1)} %bitcast.27), channel_id=1, source_target_pairs={{0,8},{4,12},{8,0},{12,4},{16,24},{20,28},{24,16},{28,20},{1,9},{5... | collective-permute-start | bytes 393224 | tf_op jit(solution)/shard_map/ppermute | solution.py:23
  20.3 21.2 %collective-permute-start.12 = (bf16[4,16,3456]{2,1,0:T(8,128)(2,1)S(1)}, bf16[4,16,3456]{2,1,0:T(8,128)(2,1)S(1)}, u32[]{:S(2)}, u32[]{:S(2)}) collective-permute-start(bf16[4,16,3456]{2,1,0:T(8,128)(2,1)S(1)} %shard_map.164.refs_0_), channel_id=1, source_target_pairs={{0,4},{4,0},{8,12},{12,8},{16,20},{20,16},{24,28},{28,24},{1,5},{5... | collective-permute-start | bytes 1327112 | tf_op jit(solution)/shard_map/ppermute | solution.py:23
  21.8 16.9 %all-to-all-start = ((bf16[8,8,2176]{2,1,0:T(8,128)(2,1)}), bf16[8,8,2176]{2,1,0:T(8,128)(2,1)S(1)}, u32[]{:S(2)}, u32[]{:S(2)}) async-start(bf16[8,8,2176]{2,1,0:T(8,128)(2,1)} %bitcast.3), calls=%async_computation | async-start | bytes 557056 | tf_op jit(solution)/shard_map/all_to_all | solution.py:1029
  32.5 22.6 %collective-permute-start.18 = (bf16[128,1024]{1,0:T(8,128)(2,1)S(1)}, bf16[128,1024]{1,0:T(8,128)(2,1)S(1)}, u32[]{:S(2)}, u32[]{:S(2)}) collective-permute-start(bf16[128,1024]{1,0:T(8,128)(2,1)S(1)} %bitcast.21), channel_id=1, source_target_pairs={{0,2},{1,3},{2,0},{3,1},{4,6},{5,7},{6,4},{7,5},{8,10},{9,11},{10,... | collective-permute-start | bytes 786440 | tf_op jit(solution)/shard_map/ppermute | solution.py:23
  34.6 20.5 %collective-permute-start.17 = (bf16[128,1024]{1,0:T(8,128)(2,1)S(1)}, bf16[128,1024]{1,0:T(8,128)(2,1)S(1)}, u32[]{:S(2)}, u32[]{:S(2)}) collective-permute-start(bf16[128,1024]{1,0:T(8,128)(2,1)S(1)} %bitcast.22), channel_id=1, source_target_pairs={{0,1},{1,0},{2,3},{3,2},{4,5},{5,4},{6,7},{7,6},{8,9},{9,8},{10,11... | collective-permute-start | bytes 786440 | tf_op jit(solution)/shard_map/ppermute | solution.py:23
  34.6 14.7 %collective-permute-start.16 = (bf16[4,128,512]{2,1,0:T(8,128)(2,1)S(1)}, bf16[4,128,512]{2,1,0:T(8,128)(2,1)S(1)}, u32[]{:S(2)}, u32[]{:S(2)}) collective-permute-start(bf16[4,128,512]{2,1,0:T(8,128)(2,1)S(1)} %shard_map.166.refs_0_), channel_id=1, source_target_pairs={{0,4},{4,0},{8,12},{12,8},{16,20},{20,16},{24,28},{28,24},{1,5},{5... | collective-permute-start | bytes 1572872 | tf_op jit(solution)/shard_map/ppermute | solution.py:23
  39.1 10.3 %collective-permute-start.10 = (bf16[128,512]{1,0:T(8,128)(2,1)S(1)}, bf16[128,512]{1,0:T(8,128)(2,1)S(1)}, u32[]{:S(2)}, u32[]{:S(2)}) collective-permute-start(bf16[128,512]{1,0:T(8,128)(2,1)S(1)} %shard_map.167.refs_0_), channel_id=1, source_target_pairs={{0,2},{1,3},{2,0},{3,1},{4,6},{5,7},{6,4},{7,5},{8,10},{9,11},{10,... | collective-permute-start | bytes 393224 | tf_op jit(solution)/shard_map/ppermute | solution.py:23
  41.5 8.4 %collective-permute-start.14 = (bf16[8,16,1152]{2,1,0:T(8,128)(2,1)S(1)}, bf16[8,16,1152]{2,1,0:T(8,128)(2,1)S(1)}, u32[]{:S(2)}, u32[]{:S(2)}) collective-permute-start(bf16[8,16,1152]{2,1,0:T(8,128)(2,1)S(1)} %bitcast.18), channel_id=1, source_target_pairs={{0,2},{1,3},{2,0},{3,1},{4,6},{5,7},{6,4},{7,5},{8,10},{9,11},{10,... | collective-permute-start | bytes 884744 | tf_op jit(solution)/shard_map/ppermute | solution.py:23
  68.5 8.5 %collective-permute-start.26 = (bf16[4,32,1024]{2,1,0:T(8,128)(2,1)S(1)}, bf16[4,32,1024]{2,1,0:T(8,128)(2,1)S(1)}, u32[]{:S(2)}, u32[]{:S(2)}) collective-permute-start(bf16[4,32,1024]{2,1,0:T(8,128)(2,1)S(1)} %get-tuple-element.131), channel_id=1, source_target_pairs={{0,4},{4,0},{8,12},{12,8},{16,20},{20,16},{24,28},{28,24},{1,5},{5... | collective-permute-start | bytes 786440 | tf_op jit(solution)/shard_map/ppermute | solution.py:23
  77.9 9.3 %collective-permute-start.31 = (bf16[128,1024]{1,0:T(8,128)(2,1)S(1)}, bf16[128,1024]{1,0:T(8,128)(2,1)S(1)}, u32[]{:S(2)}, u32[]{:S(2)}) collective-permute-start(bf16[128,1024]{1,0:T(8,128)(2,1)S(1)} %get-tuple-element.142), channel_id=1, source_target_pairs={{0,1},{1,0},{2,3},{3,2},{4,5},{5,4},{6,7},{7,6},{8,9},{9,8},{10,11... | collective-permute-start | bytes 786440 | tf_op jit(solution)/shard_map/ppermute | solution.py:23
  79.6 14.0 %collective-permute-start.34 = (bf16[4,128,512]{2,1,0:T(8,128)(2,1)S(1)}, bf16[4,128,512]{2,1,0:T(8,128)(2,1)S(1)}, u32[]{:S(2)}, u32[]{:S(2)}) collective-permute-start(bf16[4,128,512]{2,1,0:T(8,128)(2,1)S(1)} %get-tuple-element.144), channel_id=1, source_target_pairs={{0,4},{4,0},{8,12},{12,8},{16,20},{20,16},{24,28},{28,24},{1,5},{5... | collective-permute-start | bytes 1572872 | tf_op jit(solution)/shard_map/ppermute | solution.py:23
  80.9 8.1 %collective-permute-start.32 = (bf16[128,1024]{1,0:T(8,128)(2,1)S(1)}, bf16[128,1024]{1,0:T(8,128)(2,1)S(1)}, u32[]{:S(2)}, u32[]{:S(2)}) collective-permute-start(bf16[128,1024]{1,0:T(8,128)(2,1)S(1)} %shard_map.183), channel_id=1, source_target_pairs={{0,2},{1,3},{2,0},{3,1},{4,6},{5,7},{6,4},{7,5},{8,10},{9,11},{10,... | collective-permute-start | bytes 786440 | tf_op jit(solution)/shard_map/ppermute | solution.py:23
  83.1 23.0 %collective-permute-start.28 = (bf16[128,1024]{1,0:T(8,128)(2,1)S(1)}, bf16[128,1024]{1,0:T(8,128)(2,1)S(1)}, u32[]{:S(2)}, u32[]{:S(2)}) collective-permute-start(bf16[128,1024]{1,0:T(8,128)(2,1)S(1)} %get-tuple-element.148), channel_id=1, source_target_pairs={{0,1},{1,0},{2,3},{3,2},{4,5},{5,4},{6,7},{7,6},{8,9},{9,8},{10,11... | collective-permute-start | bytes 786440 | tf_op jit(solution)/shard_map/ppermute | solution.py:23
  89.6 13.9 %collective-permute-start.36 = (bf16[144,1024]{1,0:T(8,128)(2,1)S(1)}, bf16[144,1024]{1,0:T(8,128)(2,1)S(1)}, u32[]{:S(2)}, u32[]{:S(2)}) collective-permute-start(bf16[144,1024]{1,0:T(8,128)(2,1)S(1)} %shard_map.188.refs_0_), channel_id=1, source_target_pairs={{0,1},{1,0},{2,3},{3,2},{4,5},{5,4},{6,7},{7,6},{8,9},{9,8},{10,11... | collective-permute-start | bytes 884744 | tf_op jit(solution)/shard_map/ppermute | solution.py:23
  89.7 9.4 %collective-permute-start.33 = (bf16[144,1024]{1,0:T(8,128)(2,1)S(1)}, bf16[144,1024]{1,0:T(8,128)(2,1)S(1)}, u32[]{:S(2)}, u32[]{:S(2)}) collective-permute-start(bf16[144,1024]{1,0:T(8,128)(2,1)S(1)} %shard_map.188.refs_0_), channel_id=1, source_target_pairs={{0,2},{1,3},{2,0},{3,1},{4,6},{5,7},{6,4},{7,5},{8,10},{9,11},{10,... | collective-permute-start | bytes 884744 | tf_op jit(solution)/shard_map/ppermute | solution.py:23
  93.7 8.9 %collective-permute-start.41 = (bf16[2,128,512]{2,1,0:T(8,128)(2,1)S(1)}, bf16[2,128,512]{2,1,0:T(8,128)(2,1)S(1)}, u32[]{:S(2)}, u32[]{:S(2)}) collective-permute-start(bf16[2,128,512]{2,1,0:T(8,128)(2,1)S(1)} %get-tuple-element.159), channel_id=1, source_target_pairs={{0,8},{4,12},{8,0},{12,4},{16,24},{20,28},{24,16},{28,20},{1,9},{5... | collective-permute-start | bytes 786440 | tf_op jit(solution)/shard_map/ppermute | solution.py:23
  94.8 19.5 %collective-permute-start.43 = (bf16[1,32,1024]{2,1,0:T(8,128)(2,1)S(1)}, bf16[1,32,1024]{2,1,0:T(8,128)(2,1)S(1)}, u32[]{:S(2)}, u32[]{:S(2)}) collective-permute-start(bf16[1,32,1024]{2,1,0:T(8,128)(2,1)S(1)} %get-tuple-element.177), channel_id=1, source_target_pairs={{0,16},{4,20},{8,24},{12,28},{16,0},{20,4},{24,8},{28,12},{1,17},{... | collective-permute-start | bytes 196616 | tf_op jit(solution)/shard_map/ppermute | solution.py:23
  102.7 11.7 %collective-permute-start.42 = (bf16[1,128,512]{2,1,0:T(8,128)(2,1)S(1)}, bf16[1,128,512]{2,1,0:T(8,128)(2,1)S(1)}, u32[]{:S(2)}, u32[]{:S(2)}) collective-permute-start(bf16[1,128,512]{2,1,0:T(8,128)(2,1)S(1)} %get-tuple-element.176), channel_id=1, source_target_pairs={{0,16},{4,20},{8,24},{12,28},{16,0},{20,4},{24,8},{28,12},{1,17},{... | collective-permute-start | bytes 393224 | tf_op jit(solution)/shard_map/ppermute | solution.py:23
  103.5 6.7 %collective-permute-start.35 = (bf16[128,1024]{1,0:T(8,128)(2,1)S(1)}, bf16[128,1024]{1,0:T(8,128)(2,1)S(1)}, u32[]{:S(2)}, u32[]{:S(2)}) collective-permute-start(bf16[128,1024]{1,0:T(8,128)(2,1)S(1)} %shard_map.186), channel_id=1, source_target_pairs={{0,2},{1,3},{2,0},{3,1},{4,6},{5,7},{6,4},{7,5},{8,10},{9,11},{10,... | collective-permute-start | bytes 786440 | tf_op jit(solution)/shard_map/ppermute | solution.py:23
  (35 other events, 143.8 us)

commit v6 on v5

--- a/solution.py
+++ b/solution.py
@@ -53,7 +53,7 @@
         kernel,
         out_shape=jax.ShapeDtypeStruct(out_shape, parts[0].dtype),
         compiler_params=kernel_params(),
-        cost_estimate=costs(0.8),
+        cost_estimate=costs(2.74),
     )(*parts)
 
 
@@ -93,7 +93,7 @@
         + [jax.ShapeDtypeStruct((block, width), BF16)] * (count - 1),
         scratch_shapes=[pltpu.VMEM((count * block, width), F32)],
         compiler_params=kernel_params(),
-        cost_estimate=costs(1.2),
+        cost_estimate=costs(0.365),
     )(left, right)
 
 
@@ -116,7 +116,7 @@
         kernel,
         out_shape=jax.ShapeDtypeStruct(one.shape, BF16),
         compiler_params=kernel_params(),
-        cost_estimate=costs(0.5),
+        cost_estimate=costs(1.39),
     )(one, other)
 
 
@@ -133,7 +133,7 @@
         kernel,
         out_shape=jax.ShapeDtypeStruct(own.shape, BF16),
         compiler_params=kernel_params(),
-        cost_estimate=costs(0.6),
+        cost_estimate=costs(0.527),
     )(stem_pre, own, *parts)
 
 
@@ -148,7 +148,7 @@
         kernel,
         out_shape=jax.ShapeDtypeStruct((columns, rows), value.dtype),
         compiler_params=kernel_params(),
-        cost_estimate=costs(1.0),
+        cost_estimate=costs(2.02),
     )(value)
 
 
@@ -183,7 +183,7 @@
         kernel,
         out_shape=[jax.ShapeDtypeStruct((total // size, rows, columns), BF16)] * size,
         compiler_params=kernel_params(),
-        cost_estimate=costs(1.5),
+        cost_estimate=costs(0.818),
     )(left, right)
 
 
@@ -212,7 +212,7 @@
         kernel,
         out_shape=[jax.ShapeDtypeStruct(shape, BF16)] * size,
         compiler_params=kernel_params(),
-        cost_estimate=costs(0.6),
+        cost_estimate=costs(0.316),
     )(*parts)
 
 
@@ -252,7 +252,7 @@
         kernel,
         out_shape=[jax.ShapeDtypeStruct((rows + folds * below, share), BF16)] * count,
         compiler_params=kernel_params(),
-        cost_estimate=costs(0.6),
+        cost_estimate=costs(1.37),
     )(*first, *second)
 
 
@@ -285,7 +285,7 @@
             jax.ShapeDtypeStruct((count * small, folds * share), F32),
         ],
         compiler_params=kernel_params(),
-        cost_estimate=costs(0.8),
+        cost_estimate=costs(0.334),
     )(*parts)
 
 
@@ -335,7 +335,7 @@
         kernel,
         out_shape=jax.ShapeDtypeStruct((block + extra, channels), BF16),
         compiler_params=kernel_params(),
-        cost_estimate=costs(0.7),
+        cost_estimate=costs(0.391),
     )(own, stem_pre, grad_out, gain, *parts)
 
 
@@ -381,7 +381,7 @@
             for width, pieces in cuts
         ],
         compiler_params=kernel_params(),
-        cost_estimate=costs(1.0),
+        cost_estimate=costs(0.398),
     )(*parts)
 
 
@@ -444,7 +444,7 @@
         kernel,
         (up,),
         [jax.ShapeDtypeStruct((rows, up.shape[1] // tm_count), BF16)] * tm_count,
-        costs(1.5),
+        costs(0.761),
     )
 
 
@@ -505,7 +505,7 @@
             jax.ShapeDtypeStruct((slots, values + 128), BF16),
             jax.ShapeDtypeStruct((stem_rows, beyond + channels * chunks), BF16),
         ],
-        costs(2.0),
+        costs(7),
     )
 
 
@@ -529,7 +529,7 @@
         kernel,
         out_shape=jax.ShapeDtypeStruct((pieces * steps, features), BF16),
         compiler_params=kernel_params(),
-        cost_estimate=costs(0.6),
+        cost_estimate=costs(0.926),
     )(arrived)
 
 
@@ -594,7 +594,7 @@
             jax.ShapeDtypeStruct((count, share + extra, block + extra), BF16),
         ],
         compiler_params=kernel_params(),
-        cost_estimate=costs(2.8),
+        cost_estimate=costs(4.22),
     )(frames, stem_all)
 
 
@@ -625,7 +625,7 @@
             jax.ShapeDtypeStruct((length + 2 * PAD, held), F32),
         ],
         compiler_params=kernel_params(),
-        cost_estimate=costs(0.7),
+        cost_estimate=costs(0.396),
     )(normed, up)
 
 
@@ -657,7 +657,7 @@
         kernel,
         out_shape=jax.ShapeDtypeStruct((length + 2 * PAD, 128), F32),
         compiler_params=kernel_params(),
-        cost_estimate=costs(0.5),
+        cost_estimate=costs(0.877),
     )(segments)
 
 
@@ -671,7 +671,7 @@
         kernel,
         out_shape=jax.ShapeDtypeStruct((left.shape[0], right.shape[0]), F32),
         compiler_params=kernel_params(),
-        cost_estimate=costs(0.6),
+        cost_estimate=costs(0.594),
     )(left, right)
 
 
@@ -719,7 +719,7 @@
             pltpu.VMEM((TILE + 2 * PAD, 128), F32),
         ],
         compiler_params=kernel_params(),
-        cost_estimate=costs(3.0),
+        cost_estimate=costs(1.03),
     )(gated, small, segments)
 
 
@@ -765,7 +765,7 @@
             jax.ShapeDtypeStruct((1, held), F32),
         ],
         compiler_params=kernel_params(),
-        cost_estimate=costs(0.7),
+        cost_estimate=costs(0.416),
     )(conv, turned, grad_act, *stats)
 
 
@@ -840,7 +840,7 @@
             pltpu.VMEM((TILE + 2 * PAD, 128), F32),
         ],
         compiler_params=kernel_params(),
-        cost_estimate=costs(6.2),
+        cost_estimate=costs(4.02),
     )(grad_hat, hat, inverse, gated, segments, linear, gate, turned, gain_term, *sums)
 
 
@@ -889,7 +889,7 @@
         kernel,
         out_shape=[jax.ShapeDtypeStruct((dp_count // size, height, channels), BF16)] * size,
         compiler_params=kernel_params(),
-        cost_estimate=costs(1.2),
+        cost_estimate=costs(2.73),
     )(turned, small, *parts)
 
 
@@ -937,7 +937,7 @@
             jax.ShapeDtypeStruct((1, rows), F32),
         ],
         compiler_params=kernel_params(),
-        cost_estimate=costs(1.2),
+        cost_estimate=costs(0.614),
     )(*parts)
 
 
@@ -1100,7 +1100,7 @@
         down_parts[0] = after(down_parts[0], grad_passed)
         down_parts = add_parts(down_parts, "dp", sums_chains[1])
         down_parts = swap_parts(down_parts, "dp", sums_chains[1])
-        own_terms = after(own_terms, *down_parts[1:])
+        own_terms = own_terms
     y_own, *y_others = block_terms(
         after(activated, grad_passed), down_full, False, "tm", tm_count
     )

time: 124 us -> 124 us (level)
  waiting for transfers between devices: 43.5 us -> 40.9 us
  Pallas kernels: 27.4 us -> 29.5 us
    ppermute x47, waiting for transfers between devices: 40.9 us -> 38.2 us  [swap(): return lax.ppermute(value, axis, [(i, i ^ mask) for i in range(size)])]
  transfers between devices with their start and end apart: 48 -> 48, of which waited for: 26 -> 23; matrix products, arithmetic and copies ran while one was open for 0% -> 0% of each run, Pallas kernels for 17% -> 18%
where the time goes in v6:
time: 124 us; the launch traced here: 123 us
  starting transfers between devices  51.3 us (41%)
  waiting for transfers between devices  40.9 us (33%)
  Pallas kernels  29.5 us (24%)
    ppermute x47, starting transfers between devices, swap(): return lax.ppermute(value, axis, [(i, i ^ mask) for i in range(size)])  42.9 us
    ppermute x47, waiting for transfers between devices, swap(): return lax.ppermute(value, axis, [(i, i ^ mask) for i in range(size)])  38.2 us
    all_to_all x1, starting transfers between devices, per_device(): lax.all_to_all(after(sent, pack_near).reshape(dp_count, capacity, -1), 'd...  8.45 us
    pallas_call x1, Pallas kernels, conv_backward(): pl.pallas_call(kernel, out_shape=[jax.ShapeDtypeStruct((length, 2 * held)...  6.2 us
    pallas_call x2, Pallas kernels, fetching_call(): pl.pallas_call(kernel, out_shape=out_shape, in_specs=[pl.BlockSpec(memory...  4.05 us
    pallas_call x1, Pallas kernels, conv_forward(): pl.pallas_call(kernel, out_shape=[jax.ShapeDtypeStruct((length, held), F3...  2.98 us
    pallas_call x1, Pallas kernels, stem_forward(): pl.pallas_call(kernel, out_shape=[jax.ShapeDtypeStruct((length, channels)...  2.73 us
    all_to_all x1, waiting for transfers between devices, per_device(): lax.all_to_all(after(sent, pack_near).reshape(dp_count, capacity, -1), 'd...  2.63 us
  transfers between devices with their start and end apart: 48, of which 23 were waited for; matrix products, arithmetic and copies ran while one was open for 0% of the time, Pallas kernels for 18%

profile of v6, /device:TPU:0, one launch (start us, length us, event | category | flops | bytes accessed | tf_op | source)
XLA Modules:
  0.0 123.2 jit_solution(10448699051094611313)
XLA Ops:
  0.6 1.9 %shard_map.162 = (bf16[32,512]{1,0:T(8,128)(2,1)}, bf16[32,512]{1,0:T(8,128)(2,1)}, bf16[32,512]{1,0:T(8,128)(2,1)}, bf16[32,512]{1,0:T(8,128)(2,1)}) custom-call(bf16[32,2048]{1,0:T(8,128)(2,1)} %source.2), custom_call_target="tpu_custom_call" | custom-call | flops 15219999744 | bytes 65536 | tf_op jit(solution)/shard_map/pallas_call | solution.py:416
  2.6 2.1 %shard_map.163 = (bf16[64,2176]{1,0:T(8,128)(2,1)}, bf16[16,3456]{1,0:T(8,128)(2,1)}) custom-call(bf16[16,1024]{1,0:T(8,128)(2,1)} %refs_0_, bf16[32,31]{1,0:T(8,128)(2,1)} %refs_1_.1, bf16[1,32]{1,0:T(2,128)(2,1)} %bitcast.35, bf16[1,32]{1,0:T(2,128)(2,1)} %bitcast.36, s32[1,32]{1,0:T(1,128)} %refs_4_.1, s32[1,32]{1,0:T(1,128)} %refs_5_.1, ...), custom_call_target="tpu_custom_call" | custom-call | flops 140000002048 | bytes 65536 | tf_op jit(solution)/shard_map/pallas_call | solution.py:416
  4.7 5.1 %collective-permute-start.2 = (bf16[16,3456]{1,0:T(8,128)(2,1)}, bf16[16,3456]{1,0:T(8,128)(2,1)S(1)}, u32[]{:S(2)}, u32[]{:S(2)}) collective-permute-start(bf16[16,3456]{1,0:T(8,128)(2,1)} %get-tuple-element.99.refs_0_), channel_id=1, source_target_pairs={{0,24},{4,28},{8,16},{12,20},{16,8},{20,12},{24,0},{28,4},{1,25},{... | collective-permute-start | bytes 331784 | tf_op jit(solution)/shard_map/ppermute | solution.py:23
  9.9 1.6 %collective-permute-start.4 = (bf16[32,512]{1,0:T(8,128)(2,1)S(1)}, bf16[32,512]{1,0:T(8,128)(2,1)S(1)}, u32[]{:S(2)}, u32[]{:S(2)}) collective-permute-start(bf16[32,512]{1,0:T(8,128)(2,1)S(1)} %copy-done.6), channel_id=1, source_target_pairs={{0,2},{1,3},{2,0},{3,1},{4,6},{5,7},{6,4},{7,5},{8,10},{9,11},{10,... | collective-permute-start | bytes 98312 | tf_op jit(solution)/shard_map/ppermute | solution.py:23
  14.8 2.0 %collective-permute-start.8 = (bf16[128,512]{1,0:T(8,128)(2,1)S(1)}, bf16[128,512]{1,0:T(8,128)(2,1)S(1)}, u32[]{:S(2)}, u32[]{:S(2)}) collective-permute-start(bf16[128,512]{1,0:T(8,128)(2,1)S(1)} %bitcast.21), channel_id=1, source_target_pairs={{0,24},{4,28},{8,16},{12,20},{16,8},{20,12},{24,0},{28,4},{1,25},{... | collective-permute-start | bytes 393224 | tf_op jit(solution)/shard_map/ppermute | solution.py:23
  21.8 8.5 %all-to-all-start = ((bf16[8,8,2176]{2,1,0:T(8,128)(2,1)}), bf16[8,8,2176]{2,1,0:T(8,128)(2,1)S(1)}, u32[]{:S(2)}, u32[]{:S(2)}) async-start(bf16[8,8,2176]{2,1,0:T(8,128)(2,1)} %bitcast.3), calls=%async_computation | async-start | bytes 557056 | tf_op jit(solution)/shard_map/all_to_all | solution.py:1029
  30.3 2.1 %collective-permute-done.7.refs_2_ = bf16[128,512]{1,0:T(8,128)(2,1)S(1)} collective-permute-done((bf16[128,512]{1,0:T(8,128)(2,1)S(1)}, bf16[128,512]{1,0:T(8,128)(2,1)S(1)}, u32[]{:S(2)}, u32[]{:S(2)}) %collective-permute-start.7) | collective-permute-done | bytes 131104 | tf_op jit(solution)/shard_map/ppermute | solution.py:23
  32.5 2.2 %collective-permute-start.18 = (bf16[128,1024]{1,0:T(8,128)(2,1)}, bf16[128,1024]{1,0:T(8,128)(2,1)}, u32[]{:S(2)}, u32[]{:S(2)}) collective-permute-start(bf16[128,1024]{1,0:T(8,128)(2,1)} %bitcast.11.refs_0_.out_grad_ref), channel_id=1, source_target_pairs={{0,2},{1,3},{2,0},{3,1},{4,6},{5,7},{6,4},{7,5},{8,10},{9,11},{10,... | collective-permute-start | bytes 786440 | tf_op jit(solution)/shard_map/ppermute | solution.py:23
  36.1 2.6 %all-to-all-done = bf16[8,8,2176]{2,1,0:T(8,128)(2,1)S(1)} async-done(((bf16[8,8,2176]{2,1,0:T(8,128)(2,1)}), bf16[8,8,2176]{2,1,0:T(8,128)(2,1)S(1)}, u32[]{:S(2)}, u32[]{:S(2)}) %all-to-all-start) | async-done | bytes 278560 | tf_op jit(solution)/shard_map/all_to_all | solution.py:1029
  39.1 2.4 %collective-permute-start.10 = (bf16[128,512]{1,0:T(8,128)(2,1)S(1)}, bf16[128,512]{1,0:T(8,128)(2,1)S(1)}, u32[]{:S(2)}, u32[]{:S(2)}) collective-permute-start(bf16[128,512]{1,0:T(8,128)(2,1)S(1)} %shard_map.167.refs_0_), channel_id=1, source_target_pairs={{0,2},{1,3},{2,0},{3,1},{4,6},{5,7},{6,4},{7,5},{8,10},{9,11},{10,... | collective-permute-start | bytes 393224 | tf_op jit(solution)/shard_map/ppermute | solution.py:23
  41.6 7.7 %collective-permute-done.16.refs_1_ = bf16[4,128,512]{2,1,0:T(8,128)(2,1)S(1)} collective-permute-done((bf16[4,128,512]{2,1,0:T(8,128)(2,1)S(1)}, bf16[4,128,512]{2,1,0:T(8,128)(2,1)S(1)}, u32[]{:S(2)}, u32[]{:S(2)}) %collective-permute-start.16) | collective-permute-done | bytes 524320 | tf_op jit(solution)/shard_map/ppermute | solution.py:23
  52.4 2.7 %shard_map.171 = (bf16[512,1024]{1,0:T(8,128)(2,1)S(1)}, f32[128,1024]{1,0:T(8,128)S(1)}, f32[1,1024]{1,0:T(1,128)S(1)}, bf16[4,144,144]{2,1,0:T(8,128)(2,1)S(1)}) custom-call(bf16[512,512]{1,0:T(8,128)(2,1)S(1)} %bitcast.32, bf16[512,1152]{1,0:T(8,128)(2,1)S(1)} %bitcast.25), custom_call_target="tpu_custom_call" | custom-call | flops 84399996928 | bytes 65536 | tf_op jit(solution)/shard_map/pallas_call | solution.py:588
  56.5 3.0 %shard_map.175 = (f32[512,256]{1,0:T(8,128)S(1)}, f32[8,512]{1,0:T(8,128)S(1)}, f32[128,256]{1,0:T(8,128)S(1)}) custom-call(f32[544,256]{1,0:T(8,128)S(1)} %get-tuple-element.109.gated_ref, bf16[256,128]{1,0:T(8,128)(2,1)S(1)} %bitcast.33, f32[544,128]{1,0:T(8,128)S(1)} %shard_map.174.seg_ref), custom_call_target="tpu_custom_call" | custom-call | flops 20600000512 | bytes 65536 | tf_op jit(solution)/shard_map/pallas_call | solution.py:710
  69.8 6.2 %shard_map.181 = (bf16[512,512]{1,0:T(8,128)(2,1)S(1)}, f32[32,256]{1,0:T(8,128)S(1)}) custom-call(f32[512,256]{1,0:T(8,128)S(1)} %get-tuple-element.131.grad_ref, f32[512,256]{1,0:T(8,128)S(1)} %get-tuple-element.132.hat_ref, f32[512,128]{1,0:T(8,128)S(1)} %get-tuple-element.133.inverse_ref, f32[544,256]{1,0:T(8,128)S(1)} %get-tuple-element.109.gated_ref, ...), custom_call_target="tpu_custom_call" | custom-call | flops 80399998976 | bytes 65536 | tf_op jit(solution)/shard_map/pallas_call | solution.py:829
  83.4 5.6 %collective-permute-done.31.refs_1_ = bf16[128,1024]{1,0:T(8,128)(2,1)S(1)} collective-permute-done((bf16[128,1024]{1,0:T(8,128)(2,1)S(1)}, bf16[128,1024]{1,0:T(8,128)(2,1)S(1)}, u32[]{:S(2)}, u32[]{:S(2)}) %collective-permute-start.31) | collective-permute-done | bytes 262176 | tf_op jit(solution)/shard_map/ppermute | solution.py:23
  89.0 1.6 %shard_map.187.refs_0_ = bf16[144,1024]{1,0:T(8,128)(2,1)S(1)} custom-call(f32[128,1024]{1,0:T(8,128)S(1)} %get-tuple-element.150.own_ref, f32[128,1024]{1,0:T(8,128)S(1)} %get-tuple-element.107.pre_ref, bf16[128,1024]{1,0:T(8,128)(2,1)} %bitcast.11.refs_0_.out_grad_ref, f32[1,1024]{1,0:T(1,128)S(1)} %get-tuple-element.151.gain_ref, ...), custom_call_target="tpu_custom_call" | custom-call | flops 7820000256 | bytes 65536 | tf_op jit(solution)/shard_map/pallas_call | solution.py:334
  91.9 1.7 %collective-permute-done.33.refs_1_ = bf16[4,128,512]{2,1,0:T(8,128)(2,1)S(1)} collective-permute-done((bf16[4,128,512]{2,1,0:T(8,128)(2,1)S(1)}, bf16[4,128,512]{2,1,0:T(8,128)(2,1)S(1)}, u32[]{:S(2)}, u32[]{:S(2)}) %collective-permute-start.33) | collective-permute-done | bytes 524320 | tf_op jit(solution)/shard_map/ppermute | solution.py:23
  94.2 2.5 %collective-permute-start.43 = (bf16[1,32,1024]{2,1,0:T(8,128)(2,1)S(1)}, bf16[1,32,1024]{2,1,0:T(8,128)(2,1)S(1)}, u32[]{:S(2)}, u32[]{:S(2)}) collective-permute-start(bf16[1,32,1024]{2,1,0:T(8,128)(2,1)S(1)} %get-tuple-element.175), channel_id=1, source_target_pairs={{0,16},{4,20},{8,24},{12,28},{16,0},{20,4},{24,8},{28,12},{1,17},{... | collective-permute-start | bytes 196616 | tf_op jit(solution)/shard_map/ppermute | solution.py:23
  96.7 3.4 %collective-permute-done.32.refs_2_ = bf16[144,1024]{1,0:T(8,128)(2,1)S(1)} collective-permute-done((bf16[144,1024]{1,0:T(8,128)(2,1)S(1)}, bf16[144,1024]{1,0:T(8,128)(2,1)S(1)}, u32[]{:S(2)}, u32[]{:S(2)}) %collective-permute-start.32) | collective-permute-done | bytes 294944 | tf_op jit(solution)/shard_map/ppermute | solution.py:23
  100.1 2.5 %collective-permute-done.41.refs_1_ = bf16[2,128,512]{2,1,0:T(8,128)(2,1)S(1)} collective-permute-done((bf16[2,128,512]{2,1,0:T(8,128)(2,1)S(1)}, bf16[2,128,512]{2,1,0:T(8,128)(2,1)S(1)}, u32[]{:S(2)}, u32[]{:S(2)}) %collective-permute-start.41) | collective-permute-done | bytes 262176 | tf_op jit(solution)/shard_map/ppermute | solution.py:23
  106.2 3.6 %collective-permute-done.35.refs_1_ = bf16[128,1024]{1,0:T(8,128)(2,1)S(1)} collective-permute-done((bf16[128,1024]{1,0:T(8,128)(2,1)S(1)}, bf16[128,1024]{1,0:T(8,128)(2,1)S(1)}, u32[]{:S(2)}, u32[]{:S(2)}) %collective-permute-start.35) | collective-permute-done | bytes 262176 | tf_op jit(solution)/shard_map/ppermute | solution.py:23
  111.5 2.4 %collective-permute-start.39 = (bf16[2,32,1024]{2,1,0:T(8,128)(2,1)S(1)}, bf16[2,32,1024]{2,1,0:T(8,128)(2,1)S(1)}, u32[]{:S(2)}, u32[]{:S(2)}) collective-permute-start(bf16[2,32,1024]{2,1,0:T(8,128)(2,1)S(1)} %get-tuple-element.167), channel_id=1, source_target_pairs={{0,8},{4,12},{8,0},{12,4},{16,24},{20,28},{24,16},{28,20},{1,9},{5... | collective-permute-start | bytes 393224 | tf_op jit(solution)/shard_map/ppermute | solution.py:23
  116.9 1.6 %collective-permute-start.40 = (bf16[1,32,1024]{2,1,0:T(8,128)(2,1)S(1)}, bf16[1,32,1024]{2,1,0:T(8,128)(2,1)S(1)}, u32[]{:S(2)}, u32[]{:S(2)}) collective-permute-start(bf16[1,32,1024]{2,1,0:T(8,128)(2,1)S(1)} %get-tuple-element.169), channel_id=1, source_target_pairs={{0,16},{4,20},{8,24},{12,28},{16,0},{20,4},{24,8},{28,12},{1,17},{... | collective-permute-start | bytes 196616 | tf_op jit(solution)/shard_map/ppermute | solution.py:23
  120.0 2.1 %collective-permute-done.40.refs_1_ = bf16[1,32,1024]{2,1,0:T(8,128)(2,1)S(1)} collective-permute-done((bf16[1,32,1024]{2,1,0:T(8,128)(2,1)S(1)}, bf16[1,32,1024]{2,1,0:T(8,128)(2,1)S(1)}, u32[]{:S(2)}, u32[]{:S(2)}) %collective-permute-start.40) | collective-permute-done | bytes 65568 | tf_op jit(solution)/shard_map/ppermute | solution.py:23
  (125 shorter events, 45.2 us)
Async XLA Ops:
  4.7 13.2 %collective-permute-start.2 = (bf16[16,3456]{1,0:T(8,128)(2,1)}, bf16[16,3456]{1,0:T(8,128)(2,1)S(1)}, u32[]{:S(2)}, u32[]{:S(2)}) collective-permute-start(bf16[16,3456]{1,0:T(8,128)(2,1)} %get-tuple-element.99.refs_0_), channel_id=1, source_target_pairs={{0,24},{4,28},{8,16},{12,20},{16,8},{20,12},{24,0},{28,4},{1,25},{... | collective-permute-start | bytes 331784 | tf_op jit(solution)/shard_map/ppermute | solution.py:23
  9.9 10.0 %collective-permute-start.1 = (bf16[16,3456]{1,0:T(8,128)(2,1)}, bf16[16,3456]{1,0:T(8,128)(2,1)S(1)}, u32[]{:S(2)}, u32[]{:S(2)}) collective-permute-start(bf16[16,3456]{1,0:T(8,128)(2,1)} %get-tuple-element.99.refs_0_), channel_id=1, source_target_pairs={{0,16},{4,20},{8,24},{12,28},{16,0},{20,4},{24,8},{28,12},{1,17},{... | collective-permute-start | bytes 331784 | tf_op jit(solution)/shard_map/ppermute | solution.py:23
  12.4 7.9 %collective-permute-start = (bf16[16,3456]{1,0:T(8,128)(2,1)S(1)}, bf16[16,3456]{1,0:T(8,128)(2,1)S(1)}, u32[]{:S(2)}, u32[]{:S(2)}) collective-permute-start(bf16[16,3456]{1,0:T(8,128)(2,1)S(1)} %copy-done), channel_id=1, source_target_pairs={{0,8},{4,12},{8,0},{12,4},{16,24},{20,28},{24,16},{28,20},{1,9},{5... | collective-permute-start | bytes 331784 | tf_op jit(solution)/shard_map/ppermute | solution.py:23
  14.8 15.5 %collective-permute-start.8 = (bf16[128,512]{1,0:T(8,128)(2,1)S(1)}, bf16[128,512]{1,0:T(8,128)(2,1)S(1)}, u32[]{:S(2)}, u32[]{:S(2)}) collective-permute-start(bf16[128,512]{1,0:T(8,128)(2,1)S(1)} %bitcast.21), channel_id=1, source_target_pairs={{0,24},{4,28},{8,16},{12,20},{16,8},{20,12},{24,0},{28,4},{1,25},{... | collective-permute-start | bytes 393224 | tf_op jit(solution)/shard_map/ppermute | solution.py:23
  16.9 15.5 %collective-permute-start.7 = (bf16[128,512]{1,0:T(8,128)(2,1)S(1)}, bf16[128,512]{1,0:T(8,128)(2,1)S(1)}, u32[]{:S(2)}, u32[]{:S(2)}) collective-permute-start(bf16[128,512]{1,0:T(8,128)(2,1)S(1)} %bitcast.22), channel_id=1, source_target_pairs={{0,16},{4,20},{8,24},{12,28},{16,0},{20,4},{24,8},{28,12},{1,17},{... | collective-permute-start | bytes 393224 | tf_op jit(solution)/shard_map/ppermute | solution.py:23
  17.9 14.5 %collective-permute-start.6 = (bf16[128,512]{1,0:T(8,128)(2,1)S(1)}, bf16[128,512]{1,0:T(8,128)(2,1)S(1)}, u32[]{:S(2)}, u32[]{:S(2)}) collective-permute-start(bf16[128,512]{1,0:T(8,128)(2,1)S(1)} %bitcast.23), channel_id=1, source_target_pairs={{0,8},{4,12},{8,0},{12,4},{16,24},{20,28},{24,16},{28,20},{1,9},{5... | collective-permute-start | bytes 393224 | tf_op jit(solution)/shard_map/ppermute | solution.py:23
  20.3 21.2 %collective-permute-start.12 = (bf16[4,16,3456]{2,1,0:T(8,128)(2,1)S(1)}, bf16[4,16,3456]{2,1,0:T(8,128)(2,1)S(1)}, u32[]{:S(2)}, u32[]{:S(2)}) collective-permute-start(bf16[4,16,3456]{2,1,0:T(8,128)(2,1)S(1)} %shard_map.164.refs_0_), channel_id=1, source_target_pairs={{0,4},{4,0},{8,12},{12,8},{16,20},{20,16},{24,28},{28,24},{1,5},{5... | collective-permute-start | bytes 1327112 | tf_op jit(solution)/shard_map/ppermute | solution.py:23
  21.8 16.9 %all-to-all-start = ((bf16[8,8,2176]{2,1,0:T(8,128)(2,1)}), bf16[8,8,2176]{2,1,0:T(8,128)(2,1)S(1)}, u32[]{:S(2)}, u32[]{:S(2)}) async-start(bf16[8,8,2176]{2,1,0:T(8,128)(2,1)} %bitcast.3), calls=%async_computation | async-start | bytes 557056 | tf_op jit(solution)/shard_map/all_to_all | solution.py:1029
  32.5 23.0 %collective-permute-start.18 = (bf16[128,1024]{1,0:T(8,128)(2,1)}, bf16[128,1024]{1,0:T(8,128)(2,1)}, u32[]{:S(2)}, u32[]{:S(2)}) collective-permute-start(bf16[128,1024]{1,0:T(8,128)(2,1)} %bitcast.11.refs_0_.out_grad_ref), channel_id=1, source_target_pairs={{0,2},{1,3},{2,0},{3,1},{4,6},{5,7},{6,4},{7,5},{8,10},{9,11},{10,... | collective-permute-start | bytes 786440 | tf_op jit(solution)/shard_map/ppermute | solution.py:23
  34.6 20.9 %collective-permute-start.17 = (bf16[128,1024]{1,0:T(8,128)(2,1)}, bf16[128,1024]{1,0:T(8,128)(2,1)}, u32[]{:S(2)}, u32[]{:S(2)}) collective-permute-start(bf16[128,1024]{1,0:T(8,128)(2,1)} %bitcast.11.refs_0_.out_grad_ref), channel_id=1, source_target_pairs={{0,1},{1,0},{2,3},{3,2},{4,5},{5,4},{6,7},{7,6},{8,9},{9,8},{10,11... | collective-permute-start | bytes 786440 | tf_op jit(solution)/shard_map/ppermute | solution.py:23
  34.6 14.7 %collective-permute-start.16 = (bf16[4,128,512]{2,1,0:T(8,128)(2,1)S(1)}, bf16[4,128,512]{2,1,0:T(8,128)(2,1)S(1)}, u32[]{:S(2)}, u32[]{:S(2)}) collective-permute-start(bf16[4,128,512]{2,1,0:T(8,128)(2,1)S(1)} %shard_map.166.refs_0_), channel_id=1, source_target_pairs={{0,4},{4,0},{8,12},{12,8},{16,20},{20,16},{24,28},{28,24},{1,5},{5... | collective-permute-start | bytes 1572872 | tf_op jit(solution)/shard_map/ppermute | solution.py:23
  39.1 10.3 %collective-permute-start.10 = (bf16[128,512]{1,0:T(8,128)(2,1)S(1)}, bf16[128,512]{1,0:T(8,128)(2,1)S(1)}, u32[]{:S(2)}, u32[]{:S(2)}) collective-permute-start(bf16[128,512]{1,0:T(8,128)(2,1)S(1)} %shard_map.167.refs_0_), channel_id=1, source_target_pairs={{0,2},{1,3},{2,0},{3,1},{4,6},{5,7},{6,4},{7,5},{8,10},{9,11},{10,... | collective-permute-start | bytes 393224 | tf_op jit(solution)/shard_map/ppermute | solution.py:23
  41.5 8.4 %collective-permute-start.14 = (bf16[8,16,1152]{2,1,0:T(8,128)(2,1)S(1)}, bf16[8,16,1152]{2,1,0:T(8,128)(2,1)S(1)}, u32[]{:S(2)}, u32[]{:S(2)}) collective-permute-start(bf16[8,16,1152]{2,1,0:T(8,128)(2,1)S(1)} %bitcast.18), channel_id=1, source_target_pairs={{0,2},{1,3},{2,0},{3,1},{4,6},{5,7},{6,4},{7,5},{8,10},{9,11},{10,... | collective-permute-start | bytes 884744 | tf_op jit(solution)/shard_map/ppermute | solution.py:23
  68.5 8.4 %collective-permute-start.26 = (bf16[4,32,1024]{2,1,0:T(8,128)(2,1)S(1)}, bf16[4,32,1024]{2,1,0:T(8,128)(2,1)S(1)}, u32[]{:S(2)}, u32[]{:S(2)}) collective-permute-start(bf16[4,32,1024]{2,1,0:T(8,128)(2,1)S(1)} %get-tuple-element.130), channel_id=1, source_target_pairs={{0,4},{4,0},{8,12},{12,8},{16,20},{20,16},{24,28},{28,24},{1,5},{5... | collective-permute-start | bytes 786440 | tf_op jit(solution)/shard_map/ppermute | solution.py:23
  79.6 14.0 %collective-permute-start.33 = (bf16[4,128,512]{2,1,0:T(8,128)(2,1)S(1)}, bf16[4,128,512]{2,1,0:T(8,128)(2,1)S(1)}, u32[]{:S(2)}, u32[]{:S(2)}) collective-permute-start(bf16[4,128,512]{2,1,0:T(8,128)(2,1)S(1)} %get-tuple-element.143), channel_id=1, source_target_pairs={{0,4},{4,0},{8,12},{12,8},{16,20},{20,16},{24,28},{28,24},{1,5},{5... | collective-permute-start | bytes 1572872 | tf_op jit(solution)/shard_map/ppermute | solution.py:23
  80.9 8.1 %collective-permute-start.31 = (bf16[128,1024]{1,0:T(8,128)(2,1)S(1)}, bf16[128,1024]{1,0:T(8,128)(2,1)S(1)}, u32[]{:S(2)}, u32[]{:S(2)}) collective-permute-start(bf16[128,1024]{1,0:T(8,128)(2,1)S(1)} %shard_map.183), channel_id=1, source_target_pairs={{0,2},{1,3},{2,0},{3,1},{4,6},{5,7},{6,4},{7,5},{8,10},{9,11},{10,... | collective-permute-start | bytes 786440 | tf_op jit(solution)/shard_map/ppermute | solution.py:23
  82.1 12.0 %collective-permute-start.34 = (bf16[2,32,1024]{2,1,0:T(8,128)(2,1)S(1)}, bf16[2,32,1024]{2,1,0:T(8,128)(2,1)S(1)}, u32[]{:S(2)}, u32[]{:S(2)}) collective-permute-start(bf16[2,32,1024]{2,1,0:T(8,128)(2,1)S(1)} %get-tuple-element.158), channel_id=1, source_target_pairs={{0,8},{4,12},{8,0},{12,4},{16,24},{20,28},{24,16},{28,20},{1,9},{5... | collective-permute-start | bytes 393224 | tf_op jit(solution)/shard_map/ppermute | solution.py:23
  82.8 23.4 %collective-permute-start.28 = (bf16[128,1024]{1,0:T(8,128)(2,1)S(1)}, bf16[128,1024]{1,0:T(8,128)(2,1)S(1)}, u32[]{:S(2)}, u32[]{:S(2)}) collective-permute-start(bf16[128,1024]{1,0:T(8,128)(2,1)S(1)} %get-tuple-element.147), channel_id=1, source_target_pairs={{0,1},{1,0},{2,3},{3,2},{4,5},{5,4},{6,7},{7,6},{8,9},{9,8},{10,11... | collective-permute-start | bytes 786440 | tf_op jit(solution)/shard_map/ppermute | solution.py:23
  82.9 7.8 %collective-permute-start.29 = (bf16[128,1024]{1,0:T(8,128)(2,1)S(1)}, bf16[128,1024]{1,0:T(8,128)(2,1)S(1)}, u32[]{:S(2)}, u32[]{:S(2)}) collective-permute-start(bf16[128,1024]{1,0:T(8,128)(2,1)S(1)} %get-tuple-element.149), channel_id=1, source_target_pairs={{0,1},{1,0},{2,3},{3,2},{4,5},{5,4},{6,7},{7,6},{8,9},{9,8},{10,11... | collective-permute-start | bytes 786440 | tf_op jit(solution)/shard_map/ppermute | solution.py:23
  90.6 12.9 %collective-permute-start.36 = (bf16[144,1024]{1,0:T(8,128)(2,1)S(1)}, bf16[144,1024]{1,0:T(8,128)(2,1)S(1)}, u32[]{:S(2)}, u32[]{:S(2)}) collective-permute-start(bf16[144,1024]{1,0:T(8,128)(2,1)S(1)} %shard_map.187.refs_0_), channel_id=1, source_target_pairs={{0,1},{1,0},{2,3},{3,2},{4,5},{5,4},{6,7},{7,6},{8,9},{9,8},{10,11... | collective-permute-start | bytes 884744 | tf_op jit(solution)/shard_map/ppermute | solution.py:23
  90.6 9.4 %collective-permute-start.32 = (bf16[144,1024]{1,0:T(8,128)(2,1)S(1)}, bf16[144,1024]{1,0:T(8,128)(2,1)S(1)}, u32[]{:S(2)}, u32[]{:S(2)}) collective-permute-start(bf16[144,1024]{1,0:T(8,128)(2,1)S(1)} %shard_map.187.refs_0_), channel_id=1, source_target_pairs={{0,2},{1,3},{2,0},{3,1},{4,6},{5,7},{6,4},{7,5},{8,10},{9,11},{10,... | collective-permute-start | bytes 884744 | tf_op jit(solution)/shard_map/ppermute | solution.py:23
  93.7 8.9 %collective-permute-start.41 = (bf16[2,128,512]{2,1,0:T(8,128)(2,1)S(1)}, bf16[2,128,512]{2,1,0:T(8,128)(2,1)S(1)}, u32[]{:S(2)}, u32[]{:S(2)}) collective-permute-start(bf16[2,128,512]{2,1,0:T(8,128)(2,1)S(1)} %get-tuple-element.156), channel_id=1, source_target_pairs={{0,8},{4,12},{8,0},{12,4},{16,24},{20,28},{24,16},{28,20},{1,9},{5... | collective-permute-start | bytes 786440 | tf_op jit(solution)/shard_map/ppermute | solution.py:23
  94.2 19.7 %collective-permute-start.43 = (bf16[1,32,1024]{2,1,0:T(8,128)(2,1)S(1)}, bf16[1,32,1024]{2,1,0:T(8,128)(2,1)S(1)}, u32[]{:S(2)}, u32[]{:S(2)}) collective-permute-start(bf16[1,32,1024]{2,1,0:T(8,128)(2,1)S(1)} %get-tuple-element.175), channel_id=1, source_target_pairs={{0,16},{4,20},{8,24},{12,28},{16,0},{20,4},{24,8},{28,12},{1,17},{... | collective-permute-start | bytes 196616 | tf_op jit(solution)/shard_map/ppermute | solution.py:23
  102.7 11.2 %collective-permute-start.42 = (bf16[1,128,512]{2,1,0:T(8,128)(2,1)S(1)}, bf16[1,128,512]{2,1,0:T(8,128)(2,1)S(1)}, u32[]{:S(2)}, u32[]{:S(2)}) collective-permute-start(bf16[1,128,512]{2,1,0:T(8,128)(2,1)S(1)} %get-tuple-element.174), channel_id=1, source_target_pairs={{0,16},{4,20},{8,24},{12,28},{16,0},{20,4},{24,8},{28,12},{1,17},{... | collective-permute-start | bytes 393224 | tf_op jit(solution)/shard_map/ppermute | solution.py:23
  (32 other events, 139.2 us)

commit v7 on v6

--- a/solution.py
+++ b/solution.py
@@ -533,15 +533,11 @@
     )(arrived)
 
 
-def stem_forward(frames, stem_all, count, axis, rows, extra):
-    length = frames.shape[0]
-    features, width = stem_all.shape
-    channels = width - 128
-    block = length // count
-    stem_rows = features * rows // channels
-    share = features // count
-
-    def kernel(frames_ref, stem_ref, normed, pre_own, gain_out, turned):
+def turn_frames(frames, count, axis, stem_rows, extra):
+    length, features = frames.shape
+    block, share = length // count, features // count
+
+    def kernel(frames_ref, turned):
         place = lax.axis_index(axis)
         feature = lax.broadcasted_iota(jnp.int32, (features, share), 0)
         chosen = lax.broadcasted_iota(jnp.int32, (features, share), 1)
@@ -561,6 +557,24 @@
             turned[k, share:, :block] = jnp.zeros((extra, block), BF16)
             turned[k, :share, block:] = jnp.zeros((share, extra), BF16)
             turned[k, share:, block:] = corner
+
+    return pl.pallas_call(
+        kernel,
+        out_shape=jax.ShapeDtypeStruct((count, share + extra, block + extra), BF16),
+        compiler_params=kernel_params(),
+        cost_estimate=costs(1.0),
+    )(frames)
+
+
+def stem_forward(frames, stem_all, count, axis, rows):
+    length = frames.shape[0]
+    features, width = stem_all.shape
+    channels = width - 128
+    block = length // count
+    stem_rows = features * rows // channels
+
+    def kernel(frames_ref, stem_ref, normed, pre_own, gain_out):
+        place = lax.axis_index(axis)
         beside = stem_ref[:, channels:].astype(F32)
         gains = []
         for g in range(channels // 128):
@@ -591,7 +605,6 @@
             jax.ShapeDtypeStruct((length, channels), BF16),
             jax.ShapeDtypeStruct((block, channels), F32),
             jax.ShapeDtypeStruct((1, channels), F32),
-            jax.ShapeDtypeStruct((count, share + extra, block + extra), BF16),
         ],
         compiler_params=kernel_params(),
         cost_estimate=costs(4.22),
@@ -1052,9 +1065,8 @@
     segments = spread_segments(segment_ids)
 
     extra = 16
-    normed, stem_pre, gain_one, frames_turned = stem_forward(
-        frames, stem_all, tm_count, "tm", rows, extra
-    )
+    normed, stem_pre, gain_one = stem_forward(frames, stem_all, tm_count, "tm", rows)
+    frames_turned = turn_frames(after(frames, normed), tm_count, "tm", stem_rows, extra)
     up_full = gather_rest(up_near, "dp", dp_chains).reshape(channels, 2 * held)
     grad_parts = lax.optimization_barrier((grad_parts, normed))[0]
     if hierarchical:

time: 124 us -> 124 us (level)
  transfers between devices with their start and end apart: 48 -> 48, of which waited for: 23 -> 22; matrix products, arithmetic and copies ran while one was open for 0% -> 0% of each run, Pallas kernels for 18% -> 19%
where the time goes in v7:
time: 124 us
  starting transfers between devices  52.1 us (42%)
  waiting for transfers between devices  40.5 us (33%)
  Pallas kernels  29.8 us (24%)
    ppermute x47, starting transfers between devices, swap(): return lax.ppermute(value, axis, [(i, i ^ mask) for i in range(size)])  43.7 us
    ppermute x47, waiting for transfers between devices, swap(): return lax.ppermute(value, axis, [(i, i ^ mask) for i in range(size)])  37.9 us
    all_to_all x1, starting transfers between devices, per_device(): lax.all_to_all(after(sent, pack_near).reshape(dp_count, capacity, -1), 'd...  8.45 us
    pallas_call x1, Pallas kernels, conv_backward(): pl.pallas_call(kernel, out_shape=[jax.ShapeDtypeStruct((length, 2 * held)...  6.26 us
    pallas_call x2, Pallas kernels, fetching_call(): pl.pallas_call(kernel, out_shape=out_shape, in_specs=[pl.BlockSpec(memory...  4.05 us
    pallas_call x1, Pallas kernels, conv_forward(): pl.pallas_call(kernel, out_shape=[jax.ShapeDtypeStruct((length, held), F3...  3.05 us
    all_to_all x1, waiting for transfers between devices, per_device(): lax.all_to_all(after(sent, pack_near).reshape(dp_count, capacity, -1), 'd...  2.63 us
    pallas_call x1, Pallas kernels, stem_forward(): pl.pallas_call(kernel, out_shape=[jax.ShapeDtypeStruct((length, channels)...  2.53 us
  transfers between devices with their start and end apart: 48, of which 22 were waited for; matrix products, arithmetic and copies ran while one was open for 0% of the time, Pallas kernels for 19%

profile of v7, /device:TPU:0, one launch (start us, length us, event | category | flops | bytes accessed | tf_op | source)
XLA Modules:
  0.0 123.9 jit_solution(10715244278630995698)
XLA Ops:
  0.6 1.9 %shard_map.162 = (bf16[32,512]{1,0:T(8,128)(2,1)}, bf16[32,512]{1,0:T(8,128)(2,1)}, bf16[32,512]{1,0:T(8,128)(2,1)}, bf16[32,512]{1,0:T(8,128)(2,1)}) custom-call(bf16[32,2048]{1,0:T(8,128)(2,1)} %source.2), custom_call_target="tpu_custom_call" | custom-call | flops 15219999744 | bytes 65536 | tf_op jit(solution)/shard_map/pallas_call | solution.py:416
  2.6 2.1 %shard_map.163 = (bf16[64,2176]{1,0:T(8,128)(2,1)}, bf16[16,3456]{1,0:T(8,128)(2,1)}) custom-call(bf16[16,1024]{1,0:T(8,128)(2,1)} %refs_0_, bf16[32,31]{1,0:T(8,128)(2,1)} %refs_1_.1, bf16[1,32]{1,0:T(2,128)(2,1)} %bitcast.36, bf16[1,32]{1,0:T(2,128)(2,1)} %bitcast.37, s32[1,32]{1,0:T(1,128)} %refs_4_.1, s32[1,32]{1,0:T(1,128)} %refs_5_.1, ...), custom_call_target="tpu_custom_call" | custom-call | flops 140000002048 | bytes 65536 | tf_op jit(solution)/shard_map/pallas_call | solution.py:416
  4.7 5.1 %collective-permute-start.2 = (bf16[16,3456]{1,0:T(8,128)(2,1)}, bf16[16,3456]{1,0:T(8,128)(2,1)S(1)}, u32[]{:S(2)}, u32[]{:S(2)}) collective-permute-start(bf16[16,3456]{1,0:T(8,128)(2,1)} %get-tuple-element.99.refs_0_), channel_id=1, source_target_pairs={{0,24},{4,28},{8,16},{12,20},{16,8},{20,12},{24,0},{28,4},{1,25},{... | collective-permute-start | bytes 331784 | tf_op jit(solution)/shard_map/ppermute | solution.py:23
  9.9 1.6 %collective-permute-start.4 = (bf16[32,512]{1,0:T(8,128)(2,1)S(1)}, bf16[32,512]{1,0:T(8,128)(2,1)S(1)}, u32[]{:S(2)}, u32[]{:S(2)}) collective-permute-start(bf16[32,512]{1,0:T(8,128)(2,1)S(1)} %copy-done.6), channel_id=1, source_target_pairs={{0,2},{1,3},{2,0},{3,1},{4,6},{5,7},{6,4},{7,5},{8,10},{9,11},{10,... | collective-permute-start | bytes 98312 | tf_op jit(solution)/shard_map/ppermute | solution.py:23
  14.8 2.0 %collective-permute-start.8 = (bf16[128,512]{1,0:T(8,128)(2,1)S(1)}, bf16[128,512]{1,0:T(8,128)(2,1)S(1)}, u32[]{:S(2)}, u32[]{:S(2)}) collective-permute-start(bf16[128,512]{1,0:T(8,128)(2,1)S(1)} %bitcast.21), channel_id=1, source_target_pairs={{0,24},{4,28},{8,16},{12,20},{16,8},{20,12},{24,0},{28,4},{1,25},{... | collective-permute-start | bytes 393224 | tf_op jit(solution)/shard_map/ppermute | solution.py:23
  21.8 8.5 %all-to-all-start = ((bf16[8,8,2176]{2,1,0:T(8,128)(2,1)}), bf16[8,8,2176]{2,1,0:T(8,128)(2,1)S(1)}, u32[]{:S(2)}, u32[]{:S(2)}) async-start(bf16[8,8,2176]{2,1,0:T(8,128)(2,1)} %bitcast.3), calls=%async_computation | async-start | bytes 557056 | tf_op jit(solution)/shard_map/all_to_all | solution.py:1042
  30.3 2.1 %collective-permute-done.7.refs_2_ = bf16[128,512]{1,0:T(8,128)(2,1)S(1)} collective-permute-done((bf16[128,512]{1,0:T(8,128)(2,1)S(1)}, bf16[128,512]{1,0:T(8,128)(2,1)S(1)}, u32[]{:S(2)}, u32[]{:S(2)}) %collective-permute-start.7) | collective-permute-done | bytes 131104 | tf_op jit(solution)/shard_map/ppermute | solution.py:23
  32.5 2.2 %collective-permute-start.18 = (bf16[128,1024]{1,0:T(8,128)(2,1)}, bf16[128,1024]{1,0:T(8,128)(2,1)}, u32[]{:S(2)}, u32[]{:S(2)}) collective-permute-start(bf16[128,1024]{1,0:T(8,128)(2,1)} %bitcast.11.refs_0_.out_grad_ref), channel_id=1, source_target_pairs={{0,2},{1,3},{2,0},{3,1},{4,6},{5,7},{6,4},{7,5},{8,10},{9,11},{10,... | collective-permute-start | bytes 786440 | tf_op jit(solution)/shard_map/ppermute | solution.py:23
  36.1 2.6 %all-to-all-done = bf16[8,8,2176]{2,1,0:T(8,128)(2,1)S(1)} async-done(((bf16[8,8,2176]{2,1,0:T(8,128)(2,1)}), bf16[8,8,2176]{2,1,0:T(8,128)(2,1)S(1)}, u32[]{:S(2)}, u32[]{:S(2)}) %all-to-all-start) | async-done | bytes 278560 | tf_op jit(solution)/shard_map/all_to_all | solution.py:1042
  39.1 2.4 %collective-permute-start.10 = (bf16[128,512]{1,0:T(8,128)(2,1)S(1)}, bf16[128,512]{1,0:T(8,128)(2,1)S(1)}, u32[]{:S(2)}, u32[]{:S(2)}) collective-permute-start(bf16[128,512]{1,0:T(8,128)(2,1)S(1)} %shard_map.167.refs_0_), channel_id=1, source_target_pairs={{0,2},{1,3},{2,0},{3,1},{4,6},{5,7},{6,4},{7,5},{8,10},{9,11},{10,... | collective-permute-start | bytes 393224 | tf_op jit(solution)/shard_map/ppermute | solution.py:23
  41.6 7.7 %collective-permute-done.16.refs_1_ = bf16[4,128,512]{2,1,0:T(8,128)(2,1)S(1)} collective-permute-done((bf16[4,128,512]{2,1,0:T(8,128)(2,1)S(1)}, bf16[4,128,512]{2,1,0:T(8,128)(2,1)S(1)}, u32[]{:S(2)}, u32[]{:S(2)}) %collective-permute-start.16) | collective-permute-done | bytes 524320 | tf_op jit(solution)/shard_map/ppermute | solution.py:23
  52.4 2.5 %shard_map.171 = (bf16[512,1024]{1,0:T(8,128)(2,1)S(1)}, f32[128,1024]{1,0:T(8,128)S(1)}, f32[1,1024]{1,0:T(1,128)S(1)}) custom-call(bf16[512,512]{1,0:T(8,128)(2,1)S(1)} %bitcast.32, bf16[512,1152]{1,0:T(8,128)(2,1)S(1)} %bitcast.25), custom_call_target="tpu_custom_call" | custom-call | flops 84399996928 | bytes 65536 | tf_op jit(solution)/shard_map/pallas_call | solution.py:602
  56.1 3.0 %shard_map.175 = (f32[512,256]{1,0:T(8,128)S(1)}, f32[8,512]{1,0:T(8,128)S(1)}, f32[128,256]{1,0:T(8,128)S(1)}) custom-call(f32[544,256]{1,0:T(8,128)S(1)} %get-tuple-element.109.gated_ref, bf16[256,128]{1,0:T(8,128)(2,1)S(1)} %bitcast.34, f32[544,128]{1,0:T(8,128)S(1)} %shard_map.174.seg_ref), custom_call_target="tpu_custom_call" | custom-call | flops 20600000512 | bytes 65536 | tf_op jit(solution)/shard_map/pallas_call | solution.py:723
  71.0 6.3 %shard_map.181 = (bf16[512,512]{1,0:T(8,128)(2,1)S(1)}, f32[32,256]{1,0:T(8,128)S(1)}) custom-call(f32[512,256]{1,0:T(8,128)S(1)} %get-tuple-element.131.grad_ref, f32[512,256]{1,0:T(8,128)S(1)} %get-tuple-element.132.hat_ref, f32[512,128]{1,0:T(8,128)S(1)} %get-tuple-element.133.inverse_ref, f32[544,256]{1,0:T(8,128)S(1)} %get-tuple-element.109.gated_ref, ...), custom_call_target="tpu_custom_call" | custom-call | flops 80399998976 | bytes 65536 | tf_op jit(solution)/shard_map/pallas_call | solution.py:842
  84.0 5.2 %collective-permute-done.31.refs_1_ = bf16[128,1024]{1,0:T(8,128)(2,1)S(1)} collective-permute-done((bf16[128,1024]{1,0:T(8,128)(2,1)S(1)}, bf16[128,1024]{1,0:T(8,128)(2,1)S(1)}, u32[]{:S(2)}, u32[]{:S(2)}) %collective-permute-start.31) | collective-permute-done | bytes 262176 | tf_op jit(solution)/shard_map/ppermute | solution.py:23
  89.2 1.6 %shard_map.187.refs_0_ = bf16[144,1024]{1,0:T(8,128)(2,1)S(1)} custom-call(f32[128,1024]{1,0:T(8,128)S(1)} %get-tuple-element.150.own_ref, f32[128,1024]{1,0:T(8,128)S(1)} %get-tuple-element.107.pre_ref, bf16[128,1024]{1,0:T(8,128)(2,1)} %bitcast.11.refs_0_.out_grad_ref, f32[1,1024]{1,0:T(1,128)S(1)} %get-tuple-element.151.gain_ref, ...), custom_call_target="tpu_custom_call" | custom-call | flops 7820000256 | bytes 65536 | tf_op jit(solution)/shard_map/pallas_call | solution.py:334
  92.1 1.8 %collective-permute-done.33.refs_1_ = bf16[4,128,512]{2,1,0:T(8,128)(2,1)S(1)} collective-permute-done((bf16[4,128,512]{2,1,0:T(8,128)(2,1)S(1)}, bf16[4,128,512]{2,1,0:T(8,128)(2,1)S(1)}, u32[]{:S(2)}, u32[]{:S(2)}) %collective-permute-start.33) | collective-permute-done | bytes 524320 | tf_op jit(solution)/shard_map/ppermute | solution.py:23
  94.3 2.9 %collective-permute-start.43 = (bf16[1,32,1024]{2,1,0:T(8,128)(2,1)S(1)}, bf16[1,32,1024]{2,1,0:T(8,128)(2,1)S(1)}, u32[]{:S(2)}, u32[]{:S(2)}) collective-permute-start(bf16[1,32,1024]{2,1,0:T(8,128)(2,1)S(1)} %get-tuple-element.175), channel_id=1, source_target_pairs={{0,16},{4,20},{8,24},{12,28},{16,0},{20,4},{24,8},{28,12},{1,17},{... | collective-permute-start | bytes 196616 | tf_op jit(solution)/shard_map/ppermute | solution.py:23
  97.2 3.1 %collective-permute-done.32.refs_2_ = bf16[144,1024]{1,0:T(8,128)(2,1)S(1)} collective-permute-done((bf16[144,1024]{1,0:T(8,128)(2,1)S(1)}, bf16[144,1024]{1,0:T(8,128)(2,1)S(1)}, u32[]{:S(2)}, u32[]{:S(2)}) %collective-permute-start.32) | collective-permute-done | bytes 294944 | tf_op jit(solution)/shard_map/ppermute | solution.py:23
  100.3 2.6 %collective-permute-done.41.refs_1_ = bf16[2,128,512]{2,1,0:T(8,128)(2,1)S(1)} collective-permute-done((bf16[2,128,512]{2,1,0:T(8,128)(2,1)S(1)}, bf16[2,128,512]{2,1,0:T(8,128)(2,1)S(1)}, u32[]{:S(2)}, u32[]{:S(2)}) %collective-permute-start.41) | collective-permute-done | bytes 262176 | tf_op jit(solution)/shard_map/ppermute | solution.py:23
  106.4 4.1 %collective-permute-done.35.refs_1_ = bf16[128,1024]{1,0:T(8,128)(2,1)S(1)} collective-permute-done((bf16[128,1024]{1,0:T(8,128)(2,1)S(1)}, bf16[128,1024]{1,0:T(8,128)(2,1)S(1)}, u32[]{:S(2)}, u32[]{:S(2)}) %collective-permute-start.35) | collective-permute-done | bytes 262176 | tf_op jit(solution)/shard_map/ppermute | solution.py:23
  112.0 2.5 %collective-permute-start.39 = (bf16[2,32,1024]{2,1,0:T(8,128)(2,1)S(1)}, bf16[2,32,1024]{2,1,0:T(8,128)(2,1)S(1)}, u32[]{:S(2)}, u32[]{:S(2)}) collective-permute-start(bf16[2,32,1024]{2,1,0:T(8,128)(2,1)S(1)} %get-tuple-element.167), channel_id=1, source_target_pairs={{0,8},{4,12},{8,0},{12,4},{16,24},{20,28},{24,16},{28,20},{1,9},{5... | collective-permute-start | bytes 393224 | tf_op jit(solution)/shard_map/ppermute | solution.py:23
  117.6 1.8 %collective-permute-start.40 = (bf16[1,32,1024]{2,1,0:T(8,128)(2,1)S(1)}, bf16[1,32,1024]{2,1,0:T(8,128)(2,1)S(1)}, u32[]{:S(2)}, u32[]{:S(2)}) collective-permute-start(bf16[1,32,1024]{2,1,0:T(8,128)(2,1)S(1)} %get-tuple-element.169), channel_id=1, source_target_pairs={{0,16},{4,20},{8,24},{12,28},{16,0},{20,4},{24,8},{28,12},{1,17},{... | collective-permute-start | bytes 196616 | tf_op jit(solution)/shard_map/ppermute | solution.py:23
  120.7 2.1 %collective-permute-done.40.refs_1_ = bf16[1,32,1024]{2,1,0:T(8,128)(2,1)S(1)} collective-permute-done((bf16[1,32,1024]{2,1,0:T(8,128)(2,1)S(1)}, bf16[1,32,1024]{2,1,0:T(8,128)(2,1)S(1)}, u32[]{:S(2)}, u32[]{:S(2)}) %collective-permute-start.40) | collective-permute-done | bytes 65568 | tf_op jit(solution)/shard_map/ppermute | solution.py:23
  (126 shorter events, 45.2 us)
Async XLA Ops:
  4.7 13.2 %collective-permute-start.2 = (bf16[16,3456]{1,0:T(8,128)(2,1)}, bf16[16,3456]{1,0:T(8,128)(2,1)S(1)}, u32[]{:S(2)}, u32[]{:S(2)}) collective-permute-start(bf16[16,3456]{1,0:T(8,128)(2,1)} %get-tuple-element.99.refs_0_), channel_id=1, source_target_pairs={{0,24},{4,28},{8,16},{12,20},{16,8},{20,12},{24,0},{28,4},{1,25},{... | collective-permute-start | bytes 331784 | tf_op jit(solution)/shard_map/ppermute | solution.py:23
  9.9 10.0 %collective-permute-start.1 = (bf16[16,3456]{1,0:T(8,128)(2,1)}, bf16[16,3456]{1,0:T(8,128)(2,1)S(1)}, u32[]{:S(2)}, u32[]{:S(2)}) collective-permute-start(bf16[16,3456]{1,0:T(8,128)(2,1)} %get-tuple-element.99.refs_0_), channel_id=1, source_target_pairs={{0,16},{4,20},{8,24},{12,28},{16,0},{20,4},{24,8},{28,12},{1,17},{... | collective-permute-start | bytes 331784 | tf_op jit(solution)/shard_map/ppermute | solution.py:23
  12.4 7.9 %collective-permute-start = (bf16[16,3456]{1,0:T(8,128)(2,1)S(1)}, bf16[16,3456]{1,0:T(8,128)(2,1)S(1)}, u32[]{:S(2)}, u32[]{:S(2)}) collective-permute-start(bf16[16,3456]{1,0:T(8,128)(2,1)S(1)} %copy-done), channel_id=1, source_target_pairs={{0,8},{4,12},{8,0},{12,4},{16,24},{20,28},{24,16},{28,20},{1,9},{5... | collective-permute-start | bytes 331784 | tf_op jit(solution)/shard_map/ppermute | solution.py:23
  14.8 15.5 %collective-permute-start.8 = (bf16[128,512]{1,0:T(8,128)(2,1)S(1)}, bf16[128,512]{1,0:T(8,128)(2,1)S(1)}, u32[]{:S(2)}, u32[]{:S(2)}) collective-permute-start(bf16[128,512]{1,0:T(8,128)(2,1)S(1)} %bitcast.21), channel_id=1, source_target_pairs={{0,24},{4,28},{8,16},{12,20},{16,8},{20,12},{24,0},{28,4},{1,25},{... | collective-permute-start | bytes 393224 | tf_op jit(solution)/shard_map/ppermute | solution.py:23
  16.9 15.5 %collective-permute-start.7 = (bf16[128,512]{1,0:T(8,128)(2,1)S(1)}, bf16[128,512]{1,0:T(8,128)(2,1)S(1)}, u32[]{:S(2)}, u32[]{:S(2)}) collective-permute-start(bf16[128,512]{1,0:T(8,128)(2,1)S(1)} %bitcast.22), channel_id=1, source_target_pairs={{0,16},{4,20},{8,24},{12,28},{16,0},{20,4},{24,8},{28,12},{1,17},{... | collective-permute-start | bytes 393224 | tf_op jit(solution)/shard_map/ppermute | solution.py:23
  17.9 14.5 %collective-permute-start.6 = (bf16[128,512]{1,0:T(8,128)(2,1)S(1)}, bf16[128,512]{1,0:T(8,128)(2,1)S(1)}, u32[]{:S(2)}, u32[]{:S(2)}) collective-permute-start(bf16[128,512]{1,0:T(8,128)(2,1)S(1)} %bitcast.23), channel_id=1, source_target_pairs={{0,8},{4,12},{8,0},{12,4},{16,24},{20,28},{24,16},{28,20},{1,9},{5... | collective-permute-start | bytes 393224 | tf_op jit(solution)/shard_map/ppermute | solution.py:23
  20.3 21.2 %collective-permute-start.12 = (bf16[4,16,3456]{2,1,0:T(8,128)(2,1)S(1)}, bf16[4,16,3456]{2,1,0:T(8,128)(2,1)S(1)}, u32[]{:S(2)}, u32[]{:S(2)}) collective-permute-start(bf16[4,16,3456]{2,1,0:T(8,128)(2,1)S(1)} %shard_map.164.refs_0_), channel_id=1, source_target_pairs={{0,4},{4,0},{8,12},{12,8},{16,20},{20,16},{24,28},{28,24},{1,5},{5... | collective-permute-start | bytes 1327112 | tf_op jit(solution)/shard_map/ppermute | solution.py:23
  21.8 16.9 %all-to-all-start = ((bf16[8,8,2176]{2,1,0:T(8,128)(2,1)}), bf16[8,8,2176]{2,1,0:T(8,128)(2,1)S(1)}, u32[]{:S(2)}, u32[]{:S(2)}) async-start(bf16[8,8,2176]{2,1,0:T(8,128)(2,1)} %bitcast.3), calls=%async_computation | async-start | bytes 557056 | tf_op jit(solution)/shard_map/all_to_all | solution.py:1042
  32.5 28.6 %collective-permute-start.18 = (bf16[128,1024]{1,0:T(8,128)(2,1)}, bf16[128,1024]{1,0:T(8,128)(2,1)}, u32[]{:S(2)}, u32[]{:S(2)}) collective-permute-start(bf16[128,1024]{1,0:T(8,128)(2,1)} %bitcast.11.refs_0_.out_grad_ref), channel_id=1, source_target_pairs={{0,2},{1,3},{2,0},{3,1},{4,6},{5,7},{6,4},{7,5},{8,10},{9,11},{10,... | collective-permute-start | bytes 786440 | tf_op jit(solution)/shard_map/ppermute | solution.py:23
  34.6 26.4 %collective-permute-start.17 = (bf16[128,1024]{1,0:T(8,128)(2,1)}, bf16[128,1024]{1,0:T(8,128)(2,1)}, u32[]{:S(2)}, u32[]{:S(2)}) collective-permute-start(bf16[128,1024]{1,0:T(8,128)(2,1)} %bitcast.11.refs_0_.out_grad_ref), channel_id=1, source_target_pairs={{0,1},{1,0},{2,3},{3,2},{4,5},{5,4},{6,7},{7,6},{8,9},{9,8},{10,11... | collective-permute-start | bytes 786440 | tf_op jit(solution)/shard_map/ppermute | solution.py:23
  34.6 14.7 %collective-permute-start.16 = (bf16[4,128,512]{2,1,0:T(8,128)(2,1)S(1)}, bf16[4,128,512]{2,1,0:T(8,128)(2,1)S(1)}, u32[]{:S(2)}, u32[]{:S(2)}) collective-permute-start(bf16[4,128,512]{2,1,0:T(8,128)(2,1)S(1)} %shard_map.166.refs_0_), channel_id=1, source_target_pairs={{0,4},{4,0},{8,12},{12,8},{16,20},{20,16},{24,28},{28,24},{1,5},{5... | collective-permute-start | bytes 1572872 | tf_op jit(solution)/shard_map/ppermute | solution.py:23
  39.1 10.3 %collective-permute-start.10 = (bf16[128,512]{1,0:T(8,128)(2,1)S(1)}, bf16[128,512]{1,0:T(8,128)(2,1)S(1)}, u32[]{:S(2)}, u32[]{:S(2)}) collective-permute-start(bf16[128,512]{1,0:T(8,128)(2,1)S(1)} %shard_map.167.refs_0_), channel_id=1, source_target_pairs={{0,2},{1,3},{2,0},{3,1},{4,6},{5,7},{6,4},{7,5},{8,10},{9,11},{10,... | collective-permute-start | bytes 393224 | tf_op jit(solution)/shard_map/ppermute | solution.py:23
  41.5 8.4 %collective-permute-start.14 = (bf16[8,16,1152]{2,1,0:T(8,128)(2,1)S(1)}, bf16[8,16,1152]{2,1,0:T(8,128)(2,1)S(1)}, u32[]{:S(2)}, u32[]{:S(2)}) collective-permute-start(bf16[8,16,1152]{2,1,0:T(8,128)(2,1)S(1)} %bitcast.18), channel_id=1, source_target_pairs={{0,2},{1,3},{2,0},{3,1},{4,6},{5,7},{6,4},{7,5},{8,10},{9,11},{10,... | collective-permute-start | bytes 884744 | tf_op jit(solution)/shard_map/ppermute | solution.py:23
  69.7 7.5 %collective-permute-start.26 = (bf16[4,32,1024]{2,1,0:T(8,128)(2,1)S(1)}, bf16[4,32,1024]{2,1,0:T(8,128)(2,1)S(1)}, u32[]{:S(2)}, u32[]{:S(2)}) collective-permute-start(bf16[4,32,1024]{2,1,0:T(8,128)(2,1)S(1)} %get-tuple-element.130), channel_id=1, source_target_pairs={{0,4},{4,0},{8,12},{12,8},{16,20},{20,16},{24,28},{28,24},{1,5},{5... | collective-permute-start | bytes 786440 | tf_op jit(solution)/shard_map/ppermute | solution.py:23
  79.9 14.0 %collective-permute-start.33 = (bf16[4,128,512]{2,1,0:T(8,128)(2,1)S(1)}, bf16[4,128,512]{2,1,0:T(8,128)(2,1)S(1)}, u32[]{:S(2)}, u32[]{:S(2)}) collective-permute-start(bf16[4,128,512]{2,1,0:T(8,128)(2,1)S(1)} %get-tuple-element.143), channel_id=1, source_target_pairs={{0,4},{4,0},{8,12},{12,8},{16,20},{20,16},{24,28},{28,24},{1,5},{5... | collective-permute-start | bytes 1572872 | tf_op jit(solution)/shard_map/ppermute | solution.py:23
  81.1 8.1 %collective-permute-start.31 = (bf16[128,1024]{1,0:T(8,128)(2,1)S(1)}, bf16[128,1024]{1,0:T(8,128)(2,1)S(1)}, u32[]{:S(2)}, u32[]{:S(2)}) collective-permute-start(bf16[128,1024]{1,0:T(8,128)(2,1)S(1)} %shard_map.183), channel_id=1, source_target_pairs={{0,2},{1,3},{2,0},{3,1},{4,6},{5,7},{6,4},{7,5},{8,10},{9,11},{10,... | collective-permute-start | bytes 786440 | tf_op jit(solution)/shard_map/ppermute | solution.py:23
  82.3 12.0 %collective-permute-start.34 = (bf16[2,32,1024]{2,1,0:T(8,128)(2,1)S(1)}, bf16[2,32,1024]{2,1,0:T(8,128)(2,1)S(1)}, u32[]{:S(2)}, u32[]{:S(2)}) collective-permute-start(bf16[2,32,1024]{2,1,0:T(8,128)(2,1)S(1)} %get-tuple-element.158), channel_id=1, source_target_pairs={{0,8},{4,12},{8,0},{12,4},{16,24},{20,28},{24,16},{28,20},{1,9},{5... | collective-permute-start | bytes 393224 | tf_op jit(solution)/shard_map/ppermute | solution.py:23
  83.4 22.9 %collective-permute-start.28 = (bf16[128,1024]{1,0:T(8,128)(2,1)S(1)}, bf16[128,1024]{1,0:T(8,128)(2,1)S(1)}, u32[]{:S(2)}, u32[]{:S(2)}) collective-permute-start(bf16[128,1024]{1,0:T(8,128)(2,1)S(1)} %get-tuple-element.147), channel_id=1, source_target_pairs={{0,1},{1,0},{2,3},{3,2},{4,5},{5,4},{6,7},{7,6},{8,9},{9,8},{10,11... | collective-permute-start | bytes 786440 | tf_op jit(solution)/shard_map/ppermute | solution.py:23
  83.5 7.3 %collective-permute-start.29 = (bf16[128,1024]{1,0:T(8,128)(2,1)S(1)}, bf16[128,1024]{1,0:T(8,128)(2,1)S(1)}, u32[]{:S(2)}, u32[]{:S(2)}) collective-permute-start(bf16[128,1024]{1,0:T(8,128)(2,1)S(1)} %get-tuple-element.149), channel_id=1, source_target_pairs={{0,1},{1,0},{2,3},{3,2},{4,5},{5,4},{6,7},{7,6},{8,9},{9,8},{10,11... | collective-permute-start | bytes 786440 | tf_op jit(solution)/shard_map/ppermute | solution.py:23
  90.8 12.9 %collective-permute-start.36 = (bf16[144,1024]{1,0:T(8,128)(2,1)S(1)}, bf16[144,1024]{1,0:T(8,128)(2,1)S(1)}, u32[]{:S(2)}, u32[]{:S(2)}) collective-permute-start(bf16[144,1024]{1,0:T(8,128)(2,1)S(1)} %shard_map.187.refs_0_), channel_id=1, source_target_pairs={{0,1},{1,0},{2,3},{3,2},{4,5},{5,4},{6,7},{7,6},{8,9},{9,8},{10,11... | collective-permute-start | bytes 884744 | tf_op jit(solution)/shard_map/ppermute | solution.py:23
  90.9 9.4 %collective-permute-start.32 = (bf16[144,1024]{1,0:T(8,128)(2,1)S(1)}, bf16[144,1024]{1,0:T(8,128)(2,1)S(1)}, u32[]{:S(2)}, u32[]{:S(2)}) collective-permute-start(bf16[144,1024]{1,0:T(8,128)(2,1)S(1)} %shard_map.187.refs_0_), channel_id=1, source_target_pairs={{0,2},{1,3},{2,0},{3,1},{4,6},{5,7},{6,4},{7,5},{8,10},{9,11},{10,... | collective-permute-start | bytes 884744 | tf_op jit(solution)/shard_map/ppermute | solution.py:23
  94.0 8.9 %collective-permute-start.41 = (bf16[2,128,512]{2,1,0:T(8,128)(2,1)S(1)}, bf16[2,128,512]{2,1,0:T(8,128)(2,1)S(1)}, u32[]{:S(2)}, u32[]{:S(2)}) collective-permute-start(bf16[2,128,512]{2,1,0:T(8,128)(2,1)S(1)} %get-tuple-element.156), channel_id=1, source_target_pairs={{0,8},{4,12},{8,0},{12,4},{16,24},{20,28},{24,16},{28,20},{1,9},{5... | collective-permute-start | bytes 786440 | tf_op jit(solution)/shard_map/ppermute | solution.py:23
  94.3 20.3 %collective-permute-start.43 = (bf16[1,32,1024]{2,1,0:T(8,128)(2,1)S(1)}, bf16[1,32,1024]{2,1,0:T(8,128)(2,1)S(1)}, u32[]{:S(2)}, u32[]{:S(2)}) collective-permute-start(bf16[1,32,1024]{2,1,0:T(8,128)(2,1)S(1)} %get-tuple-element.175), channel_id=1, source_target_pairs={{0,16},{4,20},{8,24},{12,28},{16,0},{20,4},{24,8},{28,12},{1,17},{... | collective-permute-start | bytes 196616 | tf_op jit(solution)/shard_map/ppermute | solution.py:23
  103.0 11.6 %collective-permute-start.42 = (bf16[1,128,512]{2,1,0:T(8,128)(2,1)S(1)}, bf16[1,128,512]{2,1,0:T(8,128)(2,1)S(1)}, u32[]{:S(2)}, u32[]{:S(2)}) collective-permute-start(bf16[1,128,512]{2,1,0:T(8,128)(2,1)S(1)} %get-tuple-element.174), channel_id=1, source_target_pairs={{0,16},{4,20},{8,24},{12,28},{16,0},{20,4},{24,8},{28,12},{1,17},{... | collective-permute-start | bytes 393224 | tf_op jit(solution)/shard_map/ppermute | solution.py:23
  (32 other events, 139.0 us)
